TPU v7x, 32 devices: a whole 2x2x4 slice. The times are simulated.
32 devices in a mesh: proto: 8 (over y, x, core), batch: 4 (over z).
Axes of the slice: x: 2, y: 2, z: 4, core: 2. Of those that a mesh axis runs over, the one named last changes fastest.
Arguments:
- teacher_feats: bfloat16 [1024, 512], P('batch'), may hold values from -200 to 200
- student_feats: bfloat16 [1024, 512], P('batch'), may hold values from -200 to 200
- proto_weight: bfloat16 [512, 65536], P(None, 'proto'), may hold values from -40 to 40
Outputs:
- grad_weight: bfloat16 [512, 65536], P('batch', 'proto')
- grad_student: float32 [1024, 512], P('batch')
- loss: float32 [], replicated
All inputs are finite; a program needn't handle non-finite values.
Results may differ from a plain program's by a relative error of at most 0.012.
Values may be sent and summed in bfloat16 or wider, within the bound.
No kernel may reach another device: no remote copies, remote signals or barrier semaphores. Data moves between devices by JAX's collectives and lax.ppermute only.
A program may use at most 128 MiB of HBM per device.

v0:
```python
import functools
import math

import jax
import jax.numpy as jnp
from jax import lax
from jax.experimental import pallas as pl
from jax.experimental.pallas import tpu as pltpu
from jax.sharding import PartitionSpec as P

SWEEPS = 3
TEMP_TEACHER = 0.04
TEMP_STUDENT = 0.1
LOG2E = math.log2(math.e)
SCALE_TEACHER = LOG2E / TEMP_TEACHER
SCALE_STUDENT = LOG2E / TEMP_STUDENT
LANES = 128
WIDE = 1024
TILE = 256
F32 = jnp.float32
BF16 = jnp.bfloat16


def unit_rows(values):
    wide = values.astype(F32)
    length = jnp.sqrt(jnp.sum(wide * wide, axis=-1, keepdims=True) + 1e-06)
    return wide / length, length


def diagonal():
    shape = (LANES, LANES)
    return lax.broadcasted_iota(jnp.int32, shape, 0) == lax.broadcasted_iota(jnp.int32, shape, 1)


def to_column(row):
    spread = jnp.where(diagonal(), jnp.broadcast_to(row, (LANES, LANES)), 0.0)
    return jnp.sum(spread, axis=1, keepdims=True)


def to_row(column):
    spread = jnp.where(diagonal(), jnp.broadcast_to(column, (LANES, LANES)), 0.0)
    return jnp.sum(spread, axis=0, keepdims=True)


def spread_rows(ref, rows):
    for a in range(rows.shape[0]):
        ref[a * LANES : (a + 1) * LANES, :] = jnp.broadcast_to(
            to_column(rows[a : a + 1, :]), (LANES, LANES)
        )


def pack_rows(ref, columns):
    for a in range(columns.shape[0] // LANES):
        ref[a : a + 1, :] = to_row(columns[a * LANES : (a + 1) * LANES, :])


def lane_tiles(values):
    return [values[:, t * LANES : (t + 1) * LANES] for t in range(values.shape[1] // LANES)]


def fold(values):
    return functools.reduce(jnp.add, lane_tiles(values))


def column_sums(values):
    rows, cols = values.shape
    return jnp.sum(values.reshape(rows // 8, 8, cols), axis=0)


def nt_dot(a, b):
    return lax.dot_general(a, b, (((1,), (1,)), ((), ())), preferred_element_type=F32)


def add_up(values):
    return functools.reduce(jnp.add, values)


def repeat(out_ref):
    for p in range(1, out_ref.shape[0]):
        out_ref[p] = out_ref[0]


def chunk(k):
    return slice(k * WIDE, (k + 1) * WIDE)


def copies(source, target, sems, first=0, back=0, count=None):
    def chunks(ref):
        return ref.shape[0] if len(ref.shape) == 3 else ref.shape[1] // WIDE

    count = count or min(chunks(source), chunks(target))
    return [copy_of(source, target, sems, k, first, back) for k in range(count)]


def columns_of(k, first=0, count=WIDE):
    return pl.ds(pl.multiple_of(k * WIDE + first, LANES), count)


def copy_of(source, target, sems, k, first=0, back=0):
    def part(ref, k):
        return ref.at[k] if len(ref.shape) == 3 else ref.at[:, columns_of(k)]

    return pltpu.make_async_copy(part(source, first + k), part(target, back + k), sems.at[k])


def start(*lists):
    for each in zip(*lists):
        for copy in each:
            copy.start()


def wait(*lists):
    for each in lists:
        for copy in each:
            copy.wait()


def stats_kernel(
    t_hbm, s_hbm, w_hbm, t_out, s_out, t_unit, out_ref, back_ref,
    raw, w_ref, unit, exps, logits, top, total, raw_sem, w_sem, t_sem, s_sem,
):
    own = raw.shape[1]
    quarter = out_ref.shape[1] // 4
    chunks = exps.shape[1]
    halves = (slice(0, own), slice(own, 2 * own))
    loads = copies(w_hbm, w_ref, w_sem)
    raw_loads = [
        pltpu.make_async_copy(ref, raw.at[which], raw_sem.at[which])
        for which, ref in enumerate((t_hbm, s_hbm))
    ]
    start(raw_loads, loads[:2])
    start(loads[2:])
    top[...] = jnp.full(top.shape, -1e30, F32)
    total[...] = jnp.zeros(total.shape, F32)
    back_ref[...] = jnp.zeros(back_ref.shape, F32)
    wait(raw_loads)
    for which in range(2):
        unit[halves[which], :] = unit_rows(raw[which])[0].astype(BF16)
    t_unit[...] = unit[halves[0], :]

    @pl.loop(0, chunks)
    def _(k):
        copy_of(w_hbm, w_ref, w_sem, k).wait()
        for n in range(0, WIDE, TILE):
            here = columns_of(k, n, TILE)
            values = jnp.dot(unit[...], w_ref[:, here], preferred_element_type=F32)
            for half, scale in zip(halves, (SCALE_TEACHER, SCALE_STUDENT)):
                part = values[half, :] * scale
                logits[half, here] = part
                top[half, :] = functools.reduce(jnp.maximum, lane_tiles(part), top[half, :])

    peak = jnp.max(top[...], axis=1, keepdims=True)
    top[...] = jnp.broadcast_to(peak, top.shape)

    @pl.loop(0, chunks)
    def _(k):
        for which, (half, out, sem) in enumerate(zip(halves, (t_out, s_out), (t_sem, s_sem))):
            shift = top[half, :]
            for n in range(0, WIDE, TILE):
                tiles = lane_tiles(logits[half, columns_of(k, n, TILE)])
                tiles = [jnp.exp2(tile - shift) for tile in tiles]
                for t, tile in enumerate(tiles):
                    lanes = slice(n + t * LANES, n + (t + 1) * LANES)
                    exps[which, k, :, lanes] = tile.astype(BF16)
                total[half, :] += add_up(tiles)
            copy_of(exps.at[which], out, sem, k).start()
        back_ref[...] += nt_dot(exps[1, k], w_ref[:, columns_of(k)])

    sums = jnp.sum(total[...], axis=1, keepdims=True)
    for which, half in enumerate(halves):
        for k, column in enumerate((peak, sums)):
            first = (2 * which + k) * quarter
            pack_rows(out_ref.at[0, first : first + quarter], column[half, :])
    repeat(out_ref)
    wait(copies(exps.at[0], t_out, t_sem), copies(exps.at[1], s_out, s_sem))


def merged(stats_ref, which):
    parts, height, _ = stats_ref.shape
    quarter = height // 4
    first = 2 * which * quarter
    tops = [stats_ref[p, first : first + quarter, :] for p in range(parts)]
    top = functools.reduce(jnp.maximum, tops)
    sums = [
        stats_ref[p, first + quarter : first + 2 * quarter, :] * jnp.exp2(tops[p] - top)
        for p in range(parts)
    ]
    return top + jnp.log2(add_up(sums))


def column_pass(exp_hbm, exp_ref, sem, weight, out_ref):
    height = WIDE // LANES

    @pl.loop(0, exp_ref.shape[0])
    def _(k):
        copy_of(exp_hbm, exp_ref, sem, k).wait()
        sums = jnp.zeros((8, WIDE), F32)
        for g in range(0, exp_ref.shape[1], 16):
            shift = weight[g : g + 16, :]
            tiles = lane_tiles(exp_ref[k, g : g + 16, :].astype(F32))
            sums = sums + column_sums(jnp.concatenate([tile * shift for tile in tiles], axis=1))
        sums = jnp.sum(sums, axis=0, keepdims=True)
        block = jnp.concatenate(lane_tiles(sums), axis=0)
        for g in range(out_ref.shape[0]):
            out_ref[g, pl.ds(pl.multiple_of(k * height, height), height), :] = block


def first_column_kernel(place_ref, stats_ref, exp_hbm, *refs):
    factor_ref, out_ref, weight, exp_ref, sem = refs[-5:]
    start(copies(exp_hbm, exp_ref, sem))
    quarter = stats_ref.shape[1] // 4
    height = out_ref.shape[1] - 8
    own = stats_ref[pl.ds(place_ref[1], 1)][0]
    factor_ref[...] = jnp.zeros(factor_ref.shape, F32)
    rows = []
    for which in range(2):
        log_sum = merged(stats_ref, which)
        here = slice(which * quarter, (which + 1) * quarter)
        factor_ref[here, :] = jnp.exp2(
            own[2 * which * quarter : (2 * which + 1) * quarter, :] - log_sum
        )
        rows.append(log_sum)
    rows.append(jnp.zeros((8 - 2 * quarter, LANES), F32))
    logs = jnp.concatenate(rows, axis=0)
    for g in range(out_ref.shape[0]):
        out_ref[g, height:, :] = logs
    spread_rows(weight, factor_ref[:quarter, :])
    column_pass(exp_hbm, exp_ref, sem, weight, out_ref)


def column_kernel(sums_ref, factor_ref, exp_hbm, *refs):
    out_ref, weight, exp_ref, sem = refs[-4:]
    start(copies(exp_hbm, exp_ref, sem))
    quarter = weight.shape[0] // LANES
    scale = 1.0 / add_up([sums_ref[p, :quarter, :] for p in range(sums_ref.shape[0])])
    spread_rows(weight, scale * factor_ref[:quarter, :])
    column_pass(exp_hbm, exp_ref, sem, weight, out_ref)


def column_scales(cols_ref, height):
    return 1.0 / add_up([cols_ref[g, :height, :] for g in range(cols_ref.shape[0])])


def chunk_scales(scales, k):
    height = WIDE // LANES
    return scales[pl.ds(pl.multiple_of(k * height, height), height), :]


def add_row_sums(rows, values, scale):
    for g in range(0, values.shape[0], 32):
        total = rows[g : g + 32, :]
        for t, tile in enumerate(lane_tiles(values[g : g + 32, :].astype(F32))):
            total = total + tile * scale[t : t + 1, :]
        rows[g : g + 32, :] = total


def row_kernel(cols_ref, factor_ref, exp_hbm, *refs):
    out_ref, scales, rows, exp_ref, sem = refs[-5:]
    start(copies(exp_hbm, exp_ref, sem))
    scales[...] = column_scales(cols_ref, scales.shape[0])
    rows[...] = jnp.zeros(rows.shape, F32)
    quarter = rows.shape[0] // LANES
    out_ref[0] = jnp.zeros(out_ref.shape[1:], F32)

    @pl.loop(0, exp_ref.shape[0])
    def _(k):
        copy_of(exp_hbm, exp_ref, sem, k).wait()
        add_row_sums(rows, exp_ref.at[k], chunk_scales(scales, k))

    pack_rows(out_ref.at[0, :quarter], jnp.sum(rows[...], axis=1, keepdims=True))
    out_ref[0, :quarter, :] = out_ref[0, :quarter, :] * factor_ref[:quarter, :]
    repeat(out_ref)


def relative(place_ref, g, groups):
    return pl.ds(lax.rem(place_ref[0] + g, groups), 1)


def relative_logs(place_ref, logs_ref, lse, which, shift=0.0):
    groups = logs_ref.shape[0]
    own = lse.shape[0] // (groups - 1)
    quarter = own // LANES
    height = logs_ref.shape[1] - 8
    for g in range(1, groups):
        there = logs_ref[relative(place_ref, g, groups)][0]
        first = height + which * quarter
        spread_rows(lse.at[(g - 1) * own : g * own], there[first : first + quarter, :] - shift)


def student_rows_kernel(protos, place_ref, factor_ref, own_ref, *refs):
    unit_ref, feat_ref, scaled_ref, turned = refs[-4:]
    own = own_ref.shape[0]
    groups = turned.shape[1] // own
    raw = refs[: groups - 1]
    quarter, feats = own // LANES, feat_ref.shape[0]
    for g in range(groups):
        half = unit_rows((raw[g - 1] if g else own_ref)[...])[0].astype(BF16)
        if g:
            unit_ref[(g - 1) * own : g * own, :] = half
        half = half.astype(F32)
        for a in range(0, own, LANES):
            first = g * own + a
            turned[:, first : first + LANES] = jnp.transpose(half[a : a + LANES, :]).astype(BF16)
    feat = turned[pl.ds(pl.multiple_of(place_ref[0] * feats, feats), feats), :]
    feat_ref[...] = feat
    for a in range(quarter):
        lanes = slice(a * LANES, (a + 1) * LANES)
        factor = factor_ref[quarter + a : quarter + a + 1, :] * protos
        scaled_ref[:, lanes] = (feat[:, lanes].astype(F32) * factor).astype(BF16)


def probabilities(unit, w_ref, k, lse, scale, use):
    for n in range(0, WIDE, TILE):
        logits = jnp.dot(
            unit[...], w_ref[:, columns_of(k, n, TILE)], preferred_element_type=F32
        )
        shift = lse[...]
        use(n, [jnp.exp2(tile * scale - shift) for tile in lane_tiles(logits)])


def student_kernel(
    log_protos, first, place_ref, logs_ref, unit, feat_ref, scaled_ref, exp_hbm, w_hbm, *refs
):
    grad_hbm, token_ref, lse, prob, exp_ref, w_ref, grad, exp_sem, w_sem, grad_sem = refs[-10:]
    own, count = exp_ref.shape[1], exp_ref.shape[0]
    exp_loads = copies(exp_hbm, exp_ref, exp_sem, first, 0, count)
    w_loads = copies(w_hbm, w_ref, w_sem, first, 0, count)
    start(w_loads, exp_loads)
    token_ref[...] = jnp.zeros(token_ref.shape, F32)
    relative_logs(place_ref, logs_ref, lse, 1, log_protos)

    @pl.loop(0, count)
    def _(k):
        copy_of(w_hbm, w_ref, w_sem, k, first).wait()

        def use(n, tiles):
            for t, tile in enumerate(tiles):
                prob[:, n + t * LANES : n + (t + 1) * LANES] = tile.astype(BF16)

        probabilities(unit, w_ref, k, lse, SCALE_STUDENT, use)
        copy_of(exp_hbm, exp_ref, exp_sem, k, first).wait()
        values = jnp.dot(scaled_ref[...], exp_ref[k], preferred_element_type=F32)
        values = values + jnp.dot(feat_ref[:, own:], prob[...], preferred_element_type=F32)
        grad[:, columns_of(k)] = values.astype(BF16)
        copy_of(grad, grad_hbm, grad_sem, k).start()

    wait(copies(grad, grad_hbm, grad_sem))


def as_three(value):
    high = value.astype(BF16)
    rest = value - high.astype(F32)
    middle = rest.astype(BF16)
    return high, middle, (rest - middle.astype(F32)).astype(BF16)


def last_kernel(groups, place_ref, logs_ref, cols_ref, factor_ref, own_ref, student_ref, exp_hbm, w_hbm, *refs):
    units = refs[: groups - 1]
    (
        prob_hbm, scale_ref, out_ref, unit, lse, rows, own_rows, back, scaled, sums, prob_ref,
        exp_ref, w_ref, prob_sem, exp_sem, w_sem,
    ) = refs[-16:]
    w_loads, exp_loads = copies(w_hbm, w_ref, w_sem), copies(exp_hbm, exp_ref, exp_sem)
    start(w_loads, exp_loads)
    slots, others, _ = prob_ref.shape
    own, chunks = exp_ref.shape[1], exp_ref.shape[0]
    tiles = (own + others) // LANES
    quarter = own // LANES
    scale_ref[...] = column_scales(cols_ref, scale_ref.shape[0])
    rows[...] = jnp.zeros(rows.shape, F32)
    own_rows[...] = jnp.zeros(own_rows.shape, F32)
    back[...] = jnp.zeros(back.shape, F32)
    relative_logs(place_ref, logs_ref, lse, 0)
    for g in range(groups - 1):
        unit[g * own : (g + 1) * own, :] = units[g][...]
    partner = slice((groups // 2 - 1) * own, groups // 2 * own)

    def store(k):
        return pltpu.make_async_copy(prob_ref.at[lax.rem(k, slots)], prob_hbm.at[k], prob_sem.at[k])

    @pl.loop(0, chunks)
    def _(k):
        copy_of(w_hbm, w_ref, w_sem, k).wait()
        slot = lax.rem(k, slots)
        scale = chunk_scales(scale_ref, k)

        @pl.when(k >= slots)
        def _():
            store(k - slots).wait()

        def use(n, tiles):
            for t, tile in enumerate(tiles):
                prob_ref[slot, :, n + t * LANES : n + (t + 1) * LANES] = tile.astype(BF16)
            first = n // LANES
            tiles = [tile * scale[first + t : first + t + 1, :] for t, tile in enumerate(tiles)]
            rows[...] += add_up(tiles)
            for t, tile in enumerate(tiles):
                scaled[:, n + t * LANES : n + (t + 1) * LANES] = tile[partner, :].astype(BF16)

        probabilities(unit, w_ref, k, lse, SCALE_TEACHER, use)
        store(k).start()
        back[...] += nt_dot(scaled[...], w_ref[:, columns_of(k)])
        copy_of(exp_hbm, exp_ref, exp_sem, k).wait()
        add_row_sums(own_rows, exp_ref.at[k], scale)

    sums[...] = jnp.zeros(sums.shape, F32)
    pack_rows(sums.at[:quarter], jnp.sum(own_rows[...], axis=1, keepdims=True))
    sums[:quarter, :] = sums[:quarter, :] * factor_ref[:quarter, :]
    pack_rows(sums.at[quarter:tiles], jnp.sum(rows[...], axis=1, keepdims=True))
    half = unit_rows(own_ref[...])[0].astype(BF16).astype(F32)
    inner = jnp.sum(half * back[...], axis=1, keepdims=True)
    pack_rows(sums.at[tiles : tiles + quarter], inner)
    parts = out_ref.shape[0]
    share = own // parts
    protos = 1.0 * out_ref.shape[0] * w_ref.shape[1]
    student = []
    for a in range(quarter):
        factor = to_column(factor_ref[quarter + a : quarter + a + 1, :] * protos)
        student.append(student_ref[a * LANES : (a + 1) * LANES, :] * factor)
    student = jnp.concatenate(student, axis=0).astype(BF16)
    terms = list(as_three(sums[...]))
    terms.append(jnp.zeros((sums.shape[0], out_ref.shape[2] - 3 * LANES), BF16))
    terms = jnp.concatenate(terms, axis=1)
    for p in range(parts):
        here = slice(p * share, (p + 1) * share)
        out_ref[p] = jnp.concatenate(
            [student[here, :], back[here, :].astype(BF16), terms], axis=0
        )
    for k in range(max(0, chunks - slots), chunks):
        store(k).wait()


def total_sums(message_ref, first):
    parts = message_ref.shape[0]
    each = [
        add_up([t.astype(F32) for t in lane_tiles(message_ref[p, first:, : 3 * LANES])[::-1]])
        for p in range(parts)
    ]
    return add_up(each)


def rows_kernel(tiles, protos, place_ref, s_ref, message_ref, logs_ref, *refs):
    out_ref, loss_ref, sums_ref, weight = refs[-4:]
    parts = message_ref.shape[0]
    share, own = out_ref.shape[1], weight.shape[0]
    quarter = own // LANES
    first = tiles // 2
    totals = total_sums(message_ref, 2 * share)
    sums_ref[...] = totals
    scale = 1.0 / totals[first : first + quarter, :]
    spread_rows(weight, scale)
    mine = pl.ds(pl.multiple_of(place_ref[1] * share, share), share)
    total = add_up([message_ref[p, :share, :].astype(F32) for p in range(parts)])
    paired = add_up([message_ref[p, share : 2 * share, :].astype(F32) for p in range(parts)])
    total = total - paired * (weight[mine, :1] * protos)
    unit, length = unit_rows(s_ref[mine, :])
    out_ref[0] = (total - unit * jnp.sum(unit * total, axis=-1, keepdims=True)) / length
    repeat(out_ref)
    height = logs_ref.shape[1] - 8
    logs = logs_ref[pl.ds(place_ref[0], 1)][0][height + quarter : height + 2 * quarter, :]
    terms = logs / LOG2E - totals[tiles : tiles + quarter, :] * scale / TEMP_STUDENT
    loss_ref[...] = jnp.broadcast_to(jnp.sum(terms), loss_ref.shape)


def grad_kernel(counts, protos, exp_hbm, prob_hbm, feat_ref, scale_ref, sums_ref, factor_ref, *refs):
    parts = refs[: len(counts)]
    out_hbm, scaled, exp_ref, prob_ref, part_ref, out, exp_sem, prob_sem, part_sem, sem = refs[-10:]
    exp_loads = copies(exp_hbm, exp_ref, exp_sem)
    prob_loads = copies(prob_hbm, prob_ref, prob_sem)
    part_loads, first = [], 0
    for count, part in zip(counts, parts):
        part_loads += copies(part, part_ref, part_sem.at[first : first + count], 0, first)
        first += count
    start(exp_loads, prob_loads, part_loads)
    own = exp_ref.shape[1]
    tiles = (own + prob_ref.shape[1]) // LANES
    rows = protos / sums_ref[:tiles, :]
    for a in range(tiles):
        other = (a + tiles // 2) % tiles
        feat = feat_ref[:, other * LANES : (other + 1) * LANES].astype(F32)
        row = rows[a : a + 1, :]
        if a < own // LANES:
            row = row * factor_ref[a : a + 1, :]
        scaled[:, a * LANES : (a + 1) * LANES] = (feat * row).astype(BF16)
    stores = copies(out, out_hbm, sem)
    for k, store in enumerate(stores):
        exp_loads[k].wait()
        prob_loads[k].wait()
        paired = jnp.dot(scaled[:, :own], exp_ref[k], preferred_element_type=F32)
        paired = paired + jnp.dot(
            scaled[:, own:], prob_ref[k], preferred_element_type=F32
        )
        part_loads[k].wait()
        for t, tile in enumerate(lane_tiles(paired)):
            lanes = slice(k * WIDE + t * LANES, k * WIDE + (t + 1) * LANES)
            scale = scale_ref[lanes.start // LANES : lanes.stop // LANES, :]
            out[:, lanes] = (part_ref[:, lanes].astype(F32) - tile * scale).astype(BF16)
        store.start()
    for store in stores:
        store.wait()


SMEM = pl.BlockSpec(memory_space=pltpu.SMEM)
VMEM = pl.BlockSpec(memory_space=pltpu.VMEM)
ANY = pl.BlockSpec(memory_space=pl.ANY)


def params(nbytes):
    return pltpu.CompilerParams(vmem_limit_bytes=int(nbytes) + 8 * 2**20)


def cost(flops, nbytes, exps=0):
    return pl.CostEstimate(flops=int(flops), bytes_accessed=int(nbytes), transcendentals=int(exps))


def exchange(value, axis):
    return lax.all_to_all(value, axis, 0, 0)


def following(value, axis):
    n = lax.axis_size(axis)
    return [lax.ppermute(value, axis, [(i, (i - s) % n) for i in range(n)]) for s in range(1, n)]


def tree_sum(value, axis):
    n = lax.axis_size(axis)
    values = [value] + [
        lax.ppermute(value, axis, [(i, i ^ s) for i in range(n)]) for s in range(1, n)
    ]
    while len(values) > 1:
        values = [a + b for a, b in zip(values[::2], values[1::2])]
    return values[0]


def local(teacher_feats, student_feats, proto_weight):
    parts, groups = lax.axis_size("proto"), lax.axis_size("batch")
    own, width = teacher_feats.shape
    local_protos = proto_weight.shape[1]
    rows = own * groups
    others = rows - own
    protos = local_protos * parts
    feats = width // groups
    share = own // parts
    tiles = rows // LANES
    height = local_protos // LANES
    chunks = local_protos // WIDE
    place = jnp.stack([lax.axis_index("batch"), lax.axis_index("proto")]).astype(jnp.int32)
    struct = jax.ShapeDtypeStruct
    weight_bytes = 2 * width * local_protos
    exp_bytes = 2 * own * local_protos
    others_bytes = 2 * others * local_protos
    spread = pltpu.VMEM((own, LANES), F32)
    w_buffer = pltpu.VMEM((width, local_protos), BF16)
    exp_buffer = pltpu.VMEM((chunks, own, WIDE), BF16)
    sems = pltpu.SemaphoreType.DMA((chunks,))
    log_protos = math.log2(protos)
    token = struct((8, LANES), F32)

    def far(value):
        return pltpu.with_memory_space_constraint(value, pltpu.HBM)

    weight = far(proto_weight)
    s_all = following(student_feats, "batch")

    exps = pltpu.HBM((chunks, own, WIDE), BF16)
    t_exp, s_exp, t_unit, stats, back_student = pl.pallas_call(
        stats_kernel,
        in_specs=[ANY] * 3,
        out_specs=[ANY, ANY, VMEM, VMEM, VMEM],
        out_shape=[
            exps,
            exps,
            struct((own, width), BF16),
            struct((parts, 4 * own // LANES, LANES), F32),
            struct((own, width), F32),
        ],
        scratch_shapes=[
            pltpu.VMEM((2, own, width), BF16),
            w_buffer,
            pltpu.VMEM((2 * own, width), BF16),
            pltpu.VMEM((2, chunks, own, WIDE), BF16),
            pltpu.VMEM((2 * own, local_protos), F32),
            pltpu.VMEM((2 * own, LANES), F32),
            pltpu.VMEM((2 * own, LANES), F32),
            pltpu.SemaphoreType.DMA((2,)),
            sems, sems, sems,
        ],
        compiler_params=params(weight_bytes + 6 * exp_bytes),
        cost_estimate=cost(4 * own * width * local_protos, weight_bytes),
        name="own_rows",
    )(far(teacher_feats), far(student_feats), weight)
    t_exp, s_exp = far(t_exp), far(s_exp)
    t_all = following(t_unit, "batch")

    stats = exchange(stats, "proto")

    first_shape = (groups, height + 8, LANES)
    factor, cols = pl.pallas_call(
        first_column_kernel,
        in_specs=[SMEM, VMEM, ANY] + [ANY] * (groups - 1),
        out_specs=[VMEM, VMEM],
        out_shape=[token, struct(first_shape, F32)],
        scratch_shapes=[spread, exp_buffer, sems],
        compiler_params=params(exp_bytes),
        cost_estimate=cost(2 * own * local_protos, exp_bytes),
        name="first_columns",
    )(place, stats, t_exp, *s_all)

    unit, feat, scaled = pl.pallas_call(
        functools.partial(student_rows_kernel, float(protos)),
        in_specs=[SMEM, VMEM, VMEM] + [VMEM] * (groups - 1) + [ANY],
        out_specs=[VMEM] * 3,
        out_shape=[
            struct((others, width), BF16), struct((feats, rows), BF16), struct((feats, own), BF16),
        ],
        scratch_shapes=[pltpu.VMEM((width, rows), BF16)],
        compiler_params=params(2 * rows * width),
        cost_estimate=cost(8 * rows * width, 2 * rows * width),
        name="student_rows",
    )(place, factor, student_feats, *s_all, cols)
    cols = exchange(cols, "batch")
    logs = cols

    counts = [c * chunks // 8 for c in (1, 1, 1, 1, 4)]
    grad_parts = []

    def student_piece(before):
        turn = len(grad_parts)
        first, count = sum(counts[:turn]), counts[turn]
        grad_part, done = pl.pallas_call(
            functools.partial(student_kernel, log_protos, first),
            in_specs=[SMEM] + [VMEM] * 4 + [ANY] * 3,
            out_specs=[ANY, VMEM],
            out_shape=[pltpu.HBM((feats, count * WIDE), BF16), token],
            scratch_shapes=[
                pltpu.VMEM((others, LANES), F32),
                pltpu.VMEM((others, WIDE), BF16),
                pltpu.VMEM((count, own, WIDE), BF16),
                pltpu.VMEM((width, count * WIDE), BF16),
                pltpu.VMEM((feats, count * WIDE), BF16),
            ]
            + [pltpu.SemaphoreType.DMA((count,))] * 3,
            compiler_params=params(16 * 2**20),
            cost_estimate=cost(2.5 * rows * width * WIDE * count, 2 * width * WIDE * count),
            name="student_side",
        )(place, logs, unit, feat, scaled, s_exp, weight, before)
        grad_parts.append(far(grad_part))
        return done

    done = unit
    for turn in range(SWEEPS - 1):
        late = t_all if turn == 0 else []
        sums = pl.pallas_call(
            row_kernel,
            in_specs=[VMEM, VMEM, ANY, ANY],
            out_specs=VMEM,
            out_shape=struct((parts, 8, LANES), F32),
            scratch_shapes=[pltpu.VMEM((height, LANES), F32), spread, exp_buffer, sems],
            compiler_params=params(exp_bytes),
            cost_estimate=cost(2 * own * local_protos, exp_bytes),
            name="rows",
        )(cols, factor, t_exp, done)
        done = student_piece(sums)
        sums = exchange(sums, "proto")
        cols = pl.pallas_call(
            column_kernel,
            in_specs=[VMEM, VMEM, ANY, ANY] + [ANY] * len(late),
            out_specs=VMEM,
            out_shape=struct((groups, height, LANES), F32),
            scratch_shapes=[spread, exp_buffer, sems],
            compiler_params=params(exp_bytes),
            cost_estimate=cost(2 * own * local_protos, exp_bytes),
            name="columns",
        )(sums, factor, t_exp, done, *late)
        done = student_piece(cols)
        cols = exchange(cols, "batch")

    sum_rows = -(-(tiles + own // LANES) // 16) * 16
    message_shape = (parts, 2 * share + sum_rows, width)
    prob, col_scale, message = pl.pallas_call(
        functools.partial(last_kernel, groups),
        in_specs=[SMEM] + [VMEM] * 5 + [ANY] * 2 + [VMEM] * (groups - 1) + [ANY],
        out_specs=[ANY, VMEM, VMEM],
        out_shape=[
            pltpu.HBM((chunks, others, WIDE), BF16),
            struct((height, LANES), F32),
            struct(message_shape, BF16),
        ],
        scratch_shapes=[
            pltpu.VMEM((others, width), BF16),
            pltpu.VMEM((others, LANES), F32),
            pltpu.VMEM((others, LANES), F32),
            spread,
            pltpu.VMEM((own, width), F32),
            pltpu.VMEM((own, WIDE), BF16),
            pltpu.VMEM((sum_rows, LANES), F32),
            pltpu.VMEM((min(chunks, 3), others, WIDE), BF16),
            exp_buffer,
            w_buffer,
            sems, sems, sems,
        ],
        compiler_params=params(20 * 2**20 + weight_bytes + exp_bytes),
        cost_estimate=cost(2 * rows * width * local_protos, others_bytes),
        name="last_rows",
    )(
        place, logs, cols, factor, student_feats, back_student, t_exp, weight, *t_all, done,
    )
    done = student_piece(message)
    message = exchange(message, "proto")

    grad_rows, loss_part, sums = pl.pallas_call(
        functools.partial(rows_kernel, tiles, float(protos)),
        in_specs=[SMEM] + [VMEM] * 3 + [ANY],
        out_specs=[VMEM] * 3,
        out_shape=[struct((parts, share, width), F32), token, struct((sum_rows, LANES), F32)],
        scratch_shapes=[spread],
        compiler_params=params(0),
        name="row_grads",
    )(place, student_feats, message, logs, done)
    grad_rows = exchange(grad_rows, "proto").reshape(own, width)
    loss = tree_sum(loss_part, "batch")[0, 0] / rows

    grad_weight = pl.pallas_call(
        functools.partial(grad_kernel, counts, float(protos)),
        in_specs=[ANY] * 2 + [VMEM] * 4 + [ANY] * len(counts),
        out_specs=ANY,
        out_shape=struct((feats, local_protos), BF16),
        scratch_shapes=[
            pltpu.VMEM((feats, rows), BF16),
            exp_buffer,
            pltpu.VMEM((chunks, others, WIDE), BF16),
            pltpu.VMEM((feats, local_protos), BF16),
            pltpu.VMEM((feats, local_protos), BF16),
            sems, sems, sems, sems,
        ],
        compiler_params=params(exp_bytes + others_bytes + 4 * feats * local_protos),
        cost_estimate=cost(2 * feats * rows * local_protos, others_bytes),
        name="weight_grads",
    )(t_exp, far(prob), feat, col_scale, sums, factor, *grad_parts)
    return grad_weight, grad_rows, loss


def solution(mesh):
    return jax.shard_map(
        local,
        mesh=mesh,
        in_specs=(P("batch", None), P("batch", None), P(None, "proto")),
        out_specs=(P("batch", "proto"), P("batch", None), P()),
        check_vma=False,
    )
```

profile of v0, /device:TPU:0, one launch (start us, length us, event | category | flops | bytes accessed | tf_op | source)
XLA Modules:
  0.0 160.6 jit_solution(962997164734877815)
XLA Ops:
  0.6 3.1 %collective-permute-start.2 = (bf16[256,512]{1,0:T(8,128)(2,1)}, bf16[256,512]{1,0:T(8,128)(2,1)S(1)}, u32[]{:S(2)}, u32[]{:S(2)}) collective-permute-start(bf16[256,512]{1,0:T(8,128)(2,1)} %s_ref.1), channel_id=1, source_target_pairs={{0,1},{1,2},{2,3},{3,0},{4,5},{5,6},{6,7},{7,4},{8,9},{9,10},{10,1... | collective-permute-start | bytes 786440 | tf_op jit(solution)/shard_map/ppermute | solution.py:522
  7.6 17.5 %own_rows.1 = (bf16[8,256,1024]{2,1,0:T(8,128)(2,1)}, bf16[8,256,1024]{2,1,0:T(8,128)(2,1)}, bf16[256,512]{1,0:T(8,128)(2,1)S(1)}, f32[8,8,128]{2,1,0:T(8,128)}, f32[256,512]{1,0:T(8,128)S(1)}) custom-call(bf16[256,512]{1,0:T(8,128)(2,1)} %t_hbm.1, bf16[256,512]{1,0:T(8,128)(2,1)} %s_ref.1, bf16[512,8192]{1,0:T(8,128)(2,1)} %w_hbm.13), custom_call_target="tpu_custom_call" | custom-call | flops 4294967296 | bytes 8388608 | tf_op jit(solution)/shard_map/own_rows/pallas_call | solution.py:566
  25.2 3.9 %all-to-all-start = ((f32[8,8,128]{2,1,0:T(8,128)}), f32[8,8,128]{2,1,0:T(8,128)S(1)}, u32[]{:S(2)}, u32[]{:S(2)}) async-start(f32[8,8,128]{2,1,0:T(8,128)} %get-tuple-element.30), calls=%async_computation | async-start | bytes 65536 | tf_op jit(solution)/shard_map/all_to_all | solution.py:517
  29.1 4.8 %all-to-all-done.stats_ref = f32[8,8,128]{2,1,0:T(8,128)S(1)} async-done(((f32[8,8,128]{2,1,0:T(8,128)}), f32[8,8,128]{2,1,0:T(8,128)S(1)}, u32[]{:S(2)}, u32[]{:S(2)}) %all-to-all-start) | async-done | bytes 32800 | tf_op jit(solution)/shard_map/all_to_all | solution.py:517
  33.9 3.6 %first_columns.1 = (f32[8,128]{1,0:T(8,128)S(1)}, f32[4,72,128]{2,1,0:T(8,128)}) custom-call(s32[2]{0:T(128)S(1)} %pad_add_fusion.place_ref, f32[8,8,128]{2,1,0:T(8,128)S(1)} %all-to-all-done.stats_ref, bf16[8,256,1024]{2,1,0:T(8,128)(2,1)} %get-tuple-element.29.exp_hbm, bf16[256,512]{1,0:T(8,128)(2,1)S(1)} %collective-permute-done.refs_0_, ...), custom_call_target="tpu_custom_call" | custom-call | flops 4194304 | bytes 4194304 | tf_op jit(solution)/shard_map/first_columns/pallas_call | solution.py:598
  37.5 3.3 %all-to-all-start.1 = ((f32[4,72,128]{2,1,0:T(8,128)}), f32[4,72,128]{2,1,0:T(8,128)S(1)}, u32[]{:S(2)}, u32[]{:S(2)}) async-start(f32[4,72,128]{2,1,0:T(8,128)} %get-tuple-element.31.refs_3_), calls=%async_computation.1 | async-start | bytes 294912 | tf_op jit(solution)/shard_map/all_to_all | solution.py:517
  48.0 11.0 %all-to-all-done.1.cols_ref.logs_ref = f32[4,72,128]{2,1,0:T(8,128)S(1)} async-done(((f32[4,72,128]{2,1,0:T(8,128)}), f32[4,72,128]{2,1,0:T(8,128)S(1)}, u32[]{:S(2)}, u32[]{:S(2)}) %all-to-all-start.1) | async-done | bytes 147488 | tf_op jit(solution)/shard_map/all_to_all | solution.py:517
  59.1 3.1 %rows.2.refs_0_ = f32[8,8,128]{2,1,0:T(8,128)} custom-call(f32[4,72,128]{2,1,0:T(8,128)S(1)} %all-to-all-done.1.cols_ref.logs_ref, f32[8,128]{1,0:T(8,128)S(1)} %get-tuple-element.32.factor_ref, bf16[8,256,1024]{2,1,0:T(8,128)(2,1)} %get-tuple-element.29.exp_hbm, bf16[768,512]{1,0:T(8,128)(2,1)S(1)} %get-tuple-element.33.refs_0_.unit), custom_call_target="tpu_custom_call" | custom-call | flops 4194304 | bytes 4194304 | tf_op jit(solution)/shard_map/rows/pallas_call | solution.py:653
  62.1 3.4 %all-to-all-start.2 = ((f32[8,8,128]{2,1,0:T(8,128)}), f32[8,8,128]{2,1,0:T(8,128)S(1)}, u32[]{:S(2)}, u32[]{:S(2)}) async-start(f32[8,8,128]{2,1,0:T(8,128)} %rows.2.refs_0_), calls=%async_computation.2 | async-start | bytes 65536 | tf_op jit(solution)/shard_map/all_to_all | solution.py:517
  65.5 4.0 %student_side.5 = (bf16[128,1024]{1,0:T(8,128)(2,1)}, f32[8,128]{1,0:T(8,128)S(1)}) custom-call(s32[2]{0:T(128)S(1)} %pad_add_fusion.place_ref, f32[4,72,128]{2,1,0:T(8,128)S(1)} %all-to-all-done.1.cols_ref.logs_ref, bf16[768,512]{1,0:T(8,128)(2,1)S(1)} %get-tuple-element.33.refs_0_.unit, bf16[128,1024]{1,0:T(8,128)(2,1)S(1)} %get-tuple-element.34.feat_ref, ...), custom_call_target="tpu_custom_call" | custom-call | flops 1342177280 | bytes 1048576 | tf_op jit(solution)/shard_map/student_side/pallas_call | solution.py:630
  70.3 3.0 %columns.2.refs_0_ = f32[4,64,128]{2,1,0:T(8,128)} custom-call(f32[8,8,128]{2,1,0:T(8,128)S(1)} %all-to-all-done.2.sums_ref, f32[8,128]{1,0:T(8,128)S(1)} %get-tuple-element.32.factor_ref, bf16[8,256,1024]{2,1,0:T(8,128)(2,1)} %get-tuple-element.29.exp_hbm, f32[8,128]{1,0:T(8,128)S(1)} %get-tuple-element.37.refs_0_, ...), custom_call_target="tpu_custom_call" | custom-call | flops 4194304 | bytes 4194304 | tf_op jit(solution)/shard_map/columns/pallas_call | solution.py:665
  73.3 3.3 %all-to-all-start.3 = ((f32[4,64,128]{2,1,0:T(8,128)}), f32[4,64,128]{2,1,0:T(8,128)S(1)}, u32[]{:S(2)}, u32[]{:S(2)}) async-start(f32[4,64,128]{2,1,0:T(8,128)} %columns.2.refs_0_), calls=%async_computation.3 | async-start | bytes 262144 | tf_op jit(solution)/shard_map/all_to_all | solution.py:517
  76.6 4.0 %student_side.6 = (bf16[128,1024]{1,0:T(8,128)(2,1)}, f32[8,128]{1,0:T(8,128)S(1)}) custom-call(s32[2]{0:T(128)S(1)} %pad_add_fusion.place_ref, f32[4,72,128]{2,1,0:T(8,128)S(1)} %all-to-all-done.1.cols_ref.logs_ref, bf16[768,512]{1,0:T(8,128)(2,1)S(1)} %get-tuple-element.33.refs_0_.unit, bf16[128,1024]{1,0:T(8,128)(2,1)S(1)} %get-tuple-element.34.feat_ref, ...), custom_call_target="tpu_custom_call" | custom-call | flops 1342177280 | bytes 1048576 | tf_op jit(solution)/shard_map/student_side/pallas_call | solution.py:630
  82.7 3.1 %rows.3.refs_0_ = f32[8,8,128]{2,1,0:T(8,128)} custom-call(f32[4,64,128]{2,1,0:T(8,128)S(1)} %all-to-all-done.3.cols_ref, f32[8,128]{1,0:T(8,128)S(1)} %get-tuple-element.32.factor_ref, bf16[8,256,1024]{2,1,0:T(8,128)(2,1)} %get-tuple-element.29.exp_hbm, f32[8,128]{1,0:T(8,128)S(1)} %get-tuple-element.39.refs_0_), custom_call_target="tpu_custom_call" | custom-call | flops 4194304 | bytes 4194304 | tf_op jit(solution)/shard_map/rows/pallas_call | solution.py:653
  85.7 3.7 %all-to-all-start.4 = ((f32[8,8,128]{2,1,0:T(8,128)}), f32[8,8,128]{2,1,0:T(8,128)S(1)}, u32[]{:S(2)}, u32[]{:S(2)}) async-start(f32[8,8,128]{2,1,0:T(8,128)} %rows.3.refs_0_), calls=%async_computation.4 | async-start | bytes 65536 | tf_op jit(solution)/shard_map/all_to_all | solution.py:517
  89.5 4.0 %student_side.7 = (bf16[128,1024]{1,0:T(8,128)(2,1)}, f32[8,128]{1,0:T(8,128)S(1)}) custom-call(s32[2]{0:T(128)S(1)} %pad_add_fusion.place_ref, f32[4,72,128]{2,1,0:T(8,128)S(1)} %all-to-all-done.1.cols_ref.logs_ref, bf16[768,512]{1,0:T(8,128)(2,1)S(1)} %get-tuple-element.33.refs_0_.unit, bf16[128,1024]{1,0:T(8,128)(2,1)S(1)} %get-tuple-element.34.feat_ref, ...), custom_call_target="tpu_custom_call" | custom-call | flops 1342177280 | bytes 1048576 | tf_op jit(solution)/shard_map/student_side/pallas_call | solution.py:630
  94.3 3.0 %columns.3.refs_0_ = f32[4,64,128]{2,1,0:T(8,128)} custom-call(f32[8,8,128]{2,1,0:T(8,128)S(1)} %all-to-all-done.4.sums_ref, f32[8,128]{1,0:T(8,128)S(1)} %get-tuple-element.32.factor_ref, bf16[8,256,1024]{2,1,0:T(8,128)(2,1)} %get-tuple-element.29.exp_hbm, f32[8,128]{1,0:T(8,128)S(1)} %get-tuple-element.40.refs_0_), custom_call_target="tpu_custom_call" | custom-call | flops 4194304 | bytes 4194304 | tf_op jit(solution)/shard_map/columns/pallas_call | solution.py:665
  97.3 3.3 %all-to-all-start.5 = ((f32[4,64,128]{2,1,0:T(8,128)}), f32[4,64,128]{2,1,0:T(8,128)S(1)}, u32[]{:S(2)}, u32[]{:S(2)}) async-start(f32[4,64,128]{2,1,0:T(8,128)} %columns.3.refs_0_), calls=%async_computation.5 | async-start | bytes 262144 | tf_op jit(solution)/shard_map/all_to_all | solution.py:517
  100.7 4.0 %student_side.8 = (bf16[128,1024]{1,0:T(8,128)(2,1)}, f32[8,128]{1,0:T(8,128)S(1)}) custom-call(s32[2]{0:T(128)S(1)} %pad_add_fusion.place_ref, f32[4,72,128]{2,1,0:T(8,128)S(1)} %all-to-all-done.1.cols_ref.logs_ref, bf16[768,512]{1,0:T(8,128)(2,1)S(1)} %get-tuple-element.33.refs_0_.unit, bf16[128,1024]{1,0:T(8,128)(2,1)S(1)} %get-tuple-element.34.feat_ref, ...), custom_call_target="tpu_custom_call" | custom-call | flops 1342177280 | bytes 1048576 | tf_op jit(solution)/shard_map/student_side/pallas_call | solution.py:630
  106.7 17.9 %last_rows.1 = (bf16[8,768,1024]{2,1,0:T(8,128)(2,1)}, f32[64,128]{1,0:T(8,128)S(1)}, bf16[8,80,512]{2,1,0:T(8,128)(2,1)}) custom-call(s32[2]{0:T(128)S(1)} %pad_add_fusion.place_ref, f32[4,72,128]{2,1,0:T(8,128)S(1)} %all-to-all-done.1.cols_ref.logs_ref, f32[4,64,128]{2,1,0:T(8,128)S(1)} %all-to-all-done.5.cols_ref, ...), custom_call_target="tpu_custom_call" | custom-call | flops 8589934592 | bytes 12582912 | tf_op jit(solution)/shard_map/last_rows/pallas_call | solution.py:680
  124.6 3.9 %all-to-all-start.6 = ((bf16[8,80,512]{2,1,0:T(8,128)(2,1)}), bf16[8,80,512]{2,1,0:T(8,128)(2,1)S(1)}, u32[]{:S(2)}, u32[]{:S(2)}) async-start(bf16[8,80,512]{2,1,0:T(8,128)(2,1)} %get-tuple-element.45.refs_0_), calls=%async_computation.6 | async-start | bytes 1310720 | tf_op jit(solution)/shard_map/all_to_all | solution.py:517
  128.4 8.5 %student_side.9 = (bf16[128,4096]{1,0:T(8,128)(2,1)}, f32[8,128]{1,0:T(8,128)S(1)}) custom-call(s32[2]{0:T(128)S(1)} %pad_add_fusion.place_ref, f32[4,72,128]{2,1,0:T(8,128)S(1)} %all-to-all-done.1.cols_ref.logs_ref, bf16[768,512]{1,0:T(8,128)(2,1)S(1)} %get-tuple-element.33.refs_0_.unit, bf16[128,1024]{1,0:T(8,128)(2,1)S(1)} %get-tuple-element.34.feat_ref, ...), custom_call_target="tpu_custom_call" | custom-call | flops 5368709120 | bytes 4194304 | tf_op jit(solution)/shard_map/student_side/pallas_call | solution.py:630
  141.3 3.5 %all-to-all-start.7 = ((f32[8,32,512]{2,1,0:T(8,128)}), f32[8,32,512]{2,1,0:T(8,128)S(1)}, u32[]{:S(2)}, u32[]{:S(2)}) async-start(f32[8,32,512]{2,1,0:T(8,128)} %get-tuple-element.53), calls=%async_computation.7 | async-start | bytes 1048576 | tf_op jit(solution)/shard_map/all_to_all | solution.py:517
  149.2 8.3 %weight_grads.1 = bf16[128,8192]{1,0:T(8,128)(2,1)} custom-call(bf16[8,256,1024]{2,1,0:T(8,128)(2,1)} %get-tuple-element.29.exp_hbm, bf16[8,768,1024]{2,1,0:T(8,128)(2,1)} %get-tuple-element.43.prob_hbm, bf16[128,1024]{1,0:T(8,128)(2,1)S(1)} %get-tuple-element.34.feat_ref, f32[64,128]{1,0:T(8,128)S(1)} %get-tuple-element.44.scale_ref, ...), custom_call_target="tpu_custom_call" | custom-call | flops 2147483648 | bytes 12582912 | tf_op jit(solution)/shard_map/weight_grads/pallas_call | solution.py:723
  (35 shorter events, 27.0 us)
Async XLA Ops:
  0.6 33.3 %collective-permute-start.2 = (bf16[256,512]{1,0:T(8,128)(2,1)}, bf16[256,512]{1,0:T(8,128)(2,1)S(1)}, u32[]{:S(2)}, u32[]{:S(2)}) collective-permute-start(bf16[256,512]{1,0:T(8,128)(2,1)} %s_ref.1), channel_id=1, source_target_pairs={{0,1},{1,2},{2,3},{3,0},{4,5},{5,6},{6,7},{7,4},{8,9},{9,10},{10,1... | collective-permute-start | bytes 786440 | tf_op jit(solution)/shard_map/ppermute | solution.py:522
  3.7 30.2 %collective-permute-start.1 = (bf16[256,512]{1,0:T(8,128)(2,1)}, bf16[256,512]{1,0:T(8,128)(2,1)S(1)}, u32[]{:S(2)}, u32[]{:S(2)}) collective-permute-start(bf16[256,512]{1,0:T(8,128)(2,1)} %s_ref.1), channel_id=1, source_target_pairs={{0,2},{1,3},{2,0},{3,1},{4,6},{5,7},{6,4},{7,5},{8,10},{9,11},{10,... | collective-permute-start | bytes 786440 | tf_op jit(solution)/shard_map/ppermute | solution.py:522
  6.3 27.6 %collective-permute-start = (bf16[256,512]{1,0:T(8,128)(2,1)}, bf16[256,512]{1,0:T(8,128)(2,1)S(1)}, u32[]{:S(2)}, u32[]{:S(2)}) collective-permute-start(bf16[256,512]{1,0:T(8,128)(2,1)} %s_ref.1), channel_id=1, source_target_pairs={{0,3},{1,0},{2,1},{3,2},{4,7},{5,4},{6,5},{7,6},{8,11},{9,8},{10,9... | collective-permute-start | bytes 786440 | tf_op jit(solution)/shard_map/ppermute | solution.py:522
  25.2 15.7 %copy-start.1 = (f32[256,512]{1,0:T(8,128)}, f32[256,512]{1,0:T(8,128)S(1)}, u32[]{:S(2)}) copy-start(f32[256,512]{1,0:T(8,128)S(1)} %get-tuple-element.41.student_ref) | copy-start | bytes 1572868
  25.2 21.5 %copy-start = (bf16[256,512]{1,0:T(8,128)(2,1)S(1)}, bf16[256,512]{1,0:T(8,128)(2,1)}, u32[]{:S(2)}) copy-start(bf16[256,512]{1,0:T(8,128)(2,1)} %s_ref.1) | copy-start | bytes 786436
  25.2 8.7 %all-to-all-start = ((f32[8,8,128]{2,1,0:T(8,128)}), f32[8,8,128]{2,1,0:T(8,128)S(1)}, u32[]{:S(2)}, u32[]{:S(2)}) async-start(f32[8,8,128]{2,1,0:T(8,128)} %get-tuple-element.30), calls=%async_computation | async-start | bytes 65536 | tf_op jit(solution)/shard_map/all_to_all | solution.py:517
  37.5 21.6 %all-to-all-start.1 = ((f32[4,72,128]{2,1,0:T(8,128)}), f32[4,72,128]{2,1,0:T(8,128)S(1)}, u32[]{:S(2)}, u32[]{:S(2)}) async-start(f32[4,72,128]{2,1,0:T(8,128)} %get-tuple-element.31.refs_3_), calls=%async_computation.1 | async-start | bytes 294912 | tf_op jit(solution)/shard_map/all_to_all | solution.py:517
  40.9 28.6 %collective-permute-start.5 = (bf16[256,512]{1,0:T(8,128)(2,1)S(1)}, bf16[256,512]{1,0:T(8,128)(2,1)S(1)}, u32[]{:S(2)}, u32[]{:S(2)}) collective-permute-start(bf16[256,512]{1,0:T(8,128)(2,1)S(1)} %get-tuple-element.38), channel_id=1, source_target_pairs={{0,1},{1,2},{2,3},{3,0},{4,5},{5,6},{6,7},{7,4},{8,9},{9,10},{10,1... | collective-permute-start | bytes 786440 | tf_op jit(solution)/shard_map/ppermute | solution.py:522
  42.8 26.6 %collective-permute-start.4 = (bf16[256,512]{1,0:T(8,128)(2,1)S(1)}, bf16[256,512]{1,0:T(8,128)(2,1)S(1)}, u32[]{:S(2)}, u32[]{:S(2)}) collective-permute-start(bf16[256,512]{1,0:T(8,128)(2,1)S(1)} %get-tuple-element.38), channel_id=1, source_target_pairs={{0,2},{1,3},{2,0},{3,1},{4,6},{5,7},{6,4},{7,5},{8,10},{9,11},{10,... | collective-permute-start | bytes 786440 | tf_op jit(solution)/shard_map/ppermute | solution.py:522
  45.2 24.3 %collective-permute-start.3 = (bf16[256,512]{1,0:T(8,128)(2,1)S(1)}, bf16[256,512]{1,0:T(8,128)(2,1)S(1)}, u32[]{:S(2)}, u32[]{:S(2)}) collective-permute-start(bf16[256,512]{1,0:T(8,128)(2,1)S(1)} %get-tuple-element.38), channel_id=1, source_target_pairs={{0,3},{1,0},{2,1},{3,2},{4,7},{5,4},{6,5},{7,6},{8,11},{9,8},{10,9... | collective-permute-start | bytes 786440 | tf_op jit(solution)/shard_map/ppermute | solution.py:522
  62.1 8.1 %all-to-all-start.2 = ((f32[8,8,128]{2,1,0:T(8,128)}), f32[8,8,128]{2,1,0:T(8,128)S(1)}, u32[]{:S(2)}, u32[]{:S(2)}) async-start(f32[8,8,128]{2,1,0:T(8,128)} %rows.2.refs_0_), calls=%async_computation.2 | async-start | bytes 65536 | tf_op jit(solution)/shard_map/all_to_all | solution.py:517
  73.3 9.4 %all-to-all-start.3 = ((f32[4,64,128]{2,1,0:T(8,128)}), f32[4,64,128]{2,1,0:T(8,128)S(1)}, u32[]{:S(2)}, u32[]{:S(2)}) async-start(f32[4,64,128]{2,1,0:T(8,128)} %columns.2.refs_0_), calls=%async_computation.3 | async-start | bytes 262144 | tf_op jit(solution)/shard_map/all_to_all | solution.py:517
  85.7 8.6 %all-to-all-start.4 = ((f32[8,8,128]{2,1,0:T(8,128)}), f32[8,8,128]{2,1,0:T(8,128)S(1)}, u32[]{:S(2)}, u32[]{:S(2)}) async-start(f32[8,8,128]{2,1,0:T(8,128)} %rows.3.refs_0_), calls=%async_computation.4 | async-start | bytes 65536 | tf_op jit(solution)/shard_map/all_to_all | solution.py:517
  97.3 9.4 %all-to-all-start.5 = ((f32[4,64,128]{2,1,0:T(8,128)}), f32[4,64,128]{2,1,0:T(8,128)S(1)}, u32[]{:S(2)}, u32[]{:S(2)}) async-start(f32[4,64,128]{2,1,0:T(8,128)} %columns.3.refs_0_), calls=%async_computation.5 | async-start | bytes 262144 | tf_op jit(solution)/shard_map/all_to_all | solution.py:517
  100.6 6.1 %copy-start.2 = (f32[256,512]{1,0:T(8,128)S(1)}, f32[256,512]{1,0:T(8,128)}, u32[]{:S(2)}) copy-start(f32[256,512]{1,0:T(8,128)} %copy-done.1) | copy-start | bytes 1572868
  124.6 15.0 %all-to-all-start.6 = ((bf16[8,80,512]{2,1,0:T(8,128)(2,1)}), bf16[8,80,512]{2,1,0:T(8,128)(2,1)S(1)}, u32[]{:S(2)}, u32[]{:S(2)}) async-start(bf16[8,80,512]{2,1,0:T(8,128)(2,1)} %get-tuple-element.45.refs_0_), calls=%async_computation.6 | async-start | bytes 1310720 | tf_op jit(solution)/shard_map/all_to_all | solution.py:517
  141.3 17.4 %all-to-all-start.7 = ((f32[8,32,512]{2,1,0:T(8,128)}), f32[8,32,512]{2,1,0:T(8,128)S(1)}, u32[]{:S(2)}, u32[]{:S(2)}) async-start(f32[8,32,512]{2,1,0:T(8,128)} %get-tuple-element.53), calls=%async_computation.7 | async-start | bytes 1048576 | tf_op jit(solution)/shard_map/all_to_all | solution.py:517
  144.8 12.7 %collective-permute-start.8 = (f32[8,128]{1,0:T(8,128)S(1)}, f32[8,128]{1,0:T(8,128)S(1)}, u32[]{:S(2)}, u32[]{:S(2)}) collective-permute-start(f32[8,128]{1,0:T(8,128)S(1)} %get-tuple-element.54), channel_id=1, source_target_pairs={{0,3},{1,2},{2,1},{3,0},{4,7},{5,6},{6,5},{7,4},{8,11},{9,10},{10,... | collective-permute-start | bytes 12296 | tf_op jit(solution)/shard_map/ppermute | solution.py:528
  146.5 11.0 %collective-permute-start.7 = (f32[8,128]{1,0:T(8,128)S(1)}, f32[8,128]{1,0:T(8,128)S(1)}, u32[]{:S(2)}, u32[]{:S(2)}) collective-permute-start(f32[8,128]{1,0:T(8,128)S(1)} %get-tuple-element.54), channel_id=1, source_target_pairs={{0,2},{1,3},{2,0},{3,1},{4,6},{5,7},{6,4},{7,5},{8,10},{9,11},{10,... | collective-permute-start | bytes 12296 | tf_op jit(solution)/shard_map/ppermute | solution.py:528
  147.3 10.2 %collective-permute-start.6 = (f32[8,128]{1,0:T(8,128)S(1)}, f32[8,128]{1,0:T(8,128)S(1)}, u32[]{:S(2)}, u32[]{:S(2)}) collective-permute-start(f32[8,128]{1,0:T(8,128)S(1)} %get-tuple-element.54), channel_id=1, source_target_pairs={{0,1},{1,0},{2,3},{3,2},{4,5},{5,4},{6,7},{7,6},{8,9},{9,8},{10,11... | collective-permute-start | bytes 12296 | tf_op jit(solution)/shard_map/ppermute | solution.py:528
where the time goes:
time: 162 us; the launch traced here: 161 us
  Pallas kernels  86.7 us (54%)
  starting transfers between devices  45.6 us (28%)
  waiting for transfers between devices  24.2 us (15%)
  between operations  2.67 us (2%)
    all_to_all x8, starting transfers between devices, exchange(): return lax.all_to_all(value, axis, 0, 0)  28.3 us
    pallas_call x5, Pallas kernels, student_piece(): pl.pallas_call(functools.partial(student_kernel, log_protos, first), in_s...  24.4 us
    all_to_all x8, waiting for transfers between devices, exchange(): return lax.all_to_all(value, axis, 0, 0)  24.2 us
    pallas_call x1, Pallas kernels, local(): pl.pallas_call(functools.partial(last_kernel, groups), in_specs=[SMEM] +...  17.9 us
    pallas_call x1, Pallas kernels, local(): pl.pallas_call(stats_kernel, in_specs=[ANY] * 3, out_specs=[ANY, ANY, VME...  17.5 us
    ppermute x6, starting transfers between devices, following(): lax.ppermute(value, axis, [(i, (i - s) % n) for i in range(n)])  12.8 us
    pallas_call x1, Pallas kernels, local(): pl.pallas_call(functools.partial(grad_kernel, counts, float(protos)), in_...  8.27 us
    pallas_call x2, Pallas kernels, local(): pl.pallas_call(row_kernel, in_specs=[VMEM, VMEM, ANY, ANY], out_specs=VME...  6.13 us
  transfers between devices with their start and end apart: 17, of which 7 were waited for; matrix products, arithmetic and copies ran while one was open for 0% of the time, Pallas kernels for 34%

commit v1 on v0

--- a/solution.py
+++ b/solution.py
@@ -116,7 +116,7 @@
 
 
 def stats_kernel(
-    t_hbm, s_hbm, w_hbm, t_out, s_out, t_unit, out_ref, back_ref,
+    t_hbm, s_hbm, w_hbm, t_out, s_out, out_ref,
     raw, w_ref, unit, exps, logits, top, total, raw_sem, w_sem, t_sem, s_sem,
 ):
     own = raw.shape[1]
@@ -132,11 +132,9 @@
     start(loads[2:])
     top[...] = jnp.full(top.shape, -1e30, F32)
     total[...] = jnp.zeros(total.shape, F32)
-    back_ref[...] = jnp.zeros(back_ref.shape, F32)
     wait(raw_loads)
     for which in range(2):
         unit[halves[which], :] = unit_rows(raw[which])[0].astype(BF16)
-    t_unit[...] = unit[halves[0], :]
 
     @pl.loop(0, chunks)
     def _(k):
@@ -164,7 +162,6 @@
                     exps[which, k, :, lanes] = tile.astype(BF16)
                 total[half, :] += add_up(tiles)
             copy_of(exps.at[which], out, sem, k).start()
-        back_ref[...] += nt_dot(exps[1, k], w_ref[:, columns_of(k)])
 
     sums = jnp.sum(total[...], axis=1, keepdims=True)
     for which, half in enumerate(halves):
@@ -272,6 +269,17 @@
     repeat(out_ref)
 
 
+def own_back_kernel(before_ref, exp_hbm, w_hbm, back_ref, exp_ref, w_ref, exp_sem, w_sem):
+    start(copies(exp_hbm, exp_ref, exp_sem), copies(w_hbm, w_ref, w_sem))
+    back_ref[...] = jnp.zeros(back_ref.shape, F32)
+
+    @pl.loop(0, exp_ref.shape[0])
+    def _(k):
+        copy_of(exp_hbm, exp_ref, exp_sem, k).wait()
+        copy_of(w_hbm, w_ref, w_sem, k).wait()
+        back_ref[...] += nt_dot(exp_ref[k], w_ref[:, columns_of(k)])
+
+
 def relative(place_ref, g, groups):
     return pl.ds(lax.rem(place_ref[0] + g, groups), 1)
 
@@ -287,8 +295,9 @@
         spread_rows(lse.at[(g - 1) * own : g * own], there[first : first + quarter, :] - shift)
 
 
-def student_rows_kernel(protos, place_ref, factor_ref, own_ref, *refs):
-    unit_ref, feat_ref, scaled_ref, turned = refs[-4:]
+def student_rows_kernel(protos, place_ref, factor_ref, t_ref, own_ref, *refs):
+    unit_ref, feat_ref, scaled_ref, t_unit, turned = refs[-5:]
+    t_unit[...] = unit_rows(t_ref[...])[0].astype(BF16)
     own = own_ref.shape[0]
     groups = turned.shape[1] // own
     raw = refs[: groups - 1]
@@ -321,7 +330,7 @@
 def student_kernel(
     log_protos, first, place_ref, logs_ref, unit, feat_ref, scaled_ref, exp_hbm, w_hbm, *refs
 ):
-    grad_hbm, token_ref, lse, prob, exp_ref, w_ref, grad, exp_sem, w_sem, grad_sem = refs[-10:]
+    grad, token_ref, lse, prob, exp_ref, w_ref, exp_sem, w_sem = refs[-8:]
     own, count = exp_ref.shape[1], exp_ref.shape[0]
     exp_loads = copies(exp_hbm, exp_ref, exp_sem, first, 0, count)
     w_loads = copies(w_hbm, w_ref, w_sem, first, 0, count)
@@ -342,9 +351,6 @@
         values = jnp.dot(scaled_ref[...], exp_ref[k], preferred_element_type=F32)
         values = values + jnp.dot(feat_ref[:, own:], prob[...], preferred_element_type=F32)
         grad[:, columns_of(k)] = values.astype(BF16)
-        copy_of(grad, grad_hbm, grad_sem, k).start()
-
-    wait(copies(grad, grad_hbm, grad_sem))
 
 
 def as_three(value):
@@ -464,14 +470,11 @@
 
 def grad_kernel(counts, protos, exp_hbm, prob_hbm, feat_ref, scale_ref, sums_ref, factor_ref, *refs):
     parts = refs[: len(counts)]
-    out_hbm, scaled, exp_ref, prob_ref, part_ref, out, exp_sem, prob_sem, part_sem, sem = refs[-10:]
+    out_hbm, scaled, exp_ref, prob_ref, out, exp_sem, prob_sem, sem = refs[-8:]
     exp_loads = copies(exp_hbm, exp_ref, exp_sem)
     prob_loads = copies(prob_hbm, prob_ref, prob_sem)
-    part_loads, first = [], 0
-    for count, part in zip(counts, parts):
-        part_loads += copies(part, part_ref, part_sem.at[first : first + count], 0, first)
-        first += count
-    start(exp_loads, prob_loads, part_loads)
+    start(exp_loads, prob_loads)
+    where = [(part, k) for count, part in zip(counts, parts) for k in range(count)]
     own = exp_ref.shape[1]
     tiles = (own + prob_ref.shape[1]) // LANES
     rows = protos / sums_ref[:tiles, :]
@@ -490,11 +493,12 @@
         paired = paired + jnp.dot(
             scaled[:, own:], prob_ref[k], preferred_element_type=F32
         )
-        part_loads[k].wait()
+        part, there = where[k]
         for t, tile in enumerate(lane_tiles(paired)):
             lanes = slice(k * WIDE + t * LANES, k * WIDE + (t + 1) * LANES)
             scale = scale_ref[lanes.start // LANES : lanes.stop // LANES, :]
-            out[:, lanes] = (part_ref[:, lanes].astype(F32) - tile * scale).astype(BF16)
+            own_part = part[:, there * WIDE + t * LANES : there * WIDE + (t + 1) * LANES]
+            out[:, lanes] = (own_part.astype(F32) - tile * scale).astype(BF16)
         store.start()
     for store in stores:
         store.wait()
@@ -563,16 +567,14 @@
     s_all = following(student_feats, "batch")
 
     exps = pltpu.HBM((chunks, own, WIDE), BF16)
-    t_exp, s_exp, t_unit, stats, back_student = pl.pallas_call(
+    t_exp, s_exp, stats = pl.pallas_call(
         stats_kernel,
         in_specs=[ANY] * 3,
-        out_specs=[ANY, ANY, VMEM, VMEM, VMEM],
+        out_specs=[ANY, ANY, VMEM],
         out_shape=[
             exps,
             exps,
-            struct((own, width), BF16),
             struct((parts, 4 * own // LANES, LANES), F32),
-            struct((own, width), F32),
         ],
         scratch_shapes=[
             pltpu.VMEM((2, own, width), BF16),
@@ -590,34 +592,46 @@
         name="own_rows",
     )(far(teacher_feats), far(student_feats), weight)
     t_exp, s_exp = far(t_exp), far(s_exp)
-    t_all = following(t_unit, "batch")
+
+    back_student = pl.pallas_call(
+        own_back_kernel,
+        in_specs=[ANY] * 3,
+        out_specs=VMEM,
+        out_shape=struct((own, width), F32),
+        scratch_shapes=[exp_buffer, w_buffer, sems, sems],
+        compiler_params=params(weight_bytes + exp_bytes),
+        cost_estimate=cost(2 * own * width * local_protos, weight_bytes),
+        name="own_back",
+    )(stats, s_exp, weight)
 
     stats = exchange(stats, "proto")
 
     first_shape = (groups, height + 8, LANES)
     factor, cols = pl.pallas_call(
         first_column_kernel,
-        in_specs=[SMEM, VMEM, ANY] + [ANY] * (groups - 1),
+        in_specs=[SMEM, VMEM, ANY, ANY] + [ANY] * (groups - 1),
         out_specs=[VMEM, VMEM],
         out_shape=[token, struct(first_shape, F32)],
         scratch_shapes=[spread, exp_buffer, sems],
         compiler_params=params(exp_bytes),
         cost_estimate=cost(2 * own * local_protos, exp_bytes),
         name="first_columns",
-    )(place, stats, t_exp, *s_all)
-
-    unit, feat, scaled = pl.pallas_call(
+    )(place, stats, t_exp, back_student, *s_all)
+
+    unit, feat, scaled, t_unit = pl.pallas_call(
         functools.partial(student_rows_kernel, float(protos)),
-        in_specs=[SMEM, VMEM, VMEM] + [VMEM] * (groups - 1) + [ANY],
-        out_specs=[VMEM] * 3,
+        in_specs=[SMEM, VMEM, VMEM, VMEM] + [VMEM] * (groups - 1) + [ANY],
+        out_specs=[VMEM] * 4,
         out_shape=[
             struct((others, width), BF16), struct((feats, rows), BF16), struct((feats, own), BF16),
+            struct((own, width), BF16),
         ],
         scratch_shapes=[pltpu.VMEM((width, rows), BF16)],
         compiler_params=params(2 * rows * width),
         cost_estimate=cost(8 * rows * width, 2 * rows * width),
         name="student_rows",
-    )(place, factor, student_feats, *s_all, cols)
+    )(place, factor, teacher_feats, student_feats, *s_all, cols)
+    t_all = following(t_unit, "batch")
     cols = exchange(cols, "batch")
     logs = cols
 
@@ -630,48 +644,47 @@
         grad_part, done = pl.pallas_call(
             functools.partial(student_kernel, log_protos, first),
             in_specs=[SMEM] + [VMEM] * 4 + [ANY] * 3,
-            out_specs=[ANY, VMEM],
-            out_shape=[pltpu.HBM((feats, count * WIDE), BF16), token],
+            out_specs=[VMEM, VMEM],
+            out_shape=[struct((feats, count * WIDE), BF16), token],
             scratch_shapes=[
                 pltpu.VMEM((others, LANES), F32),
                 pltpu.VMEM((others, WIDE), BF16),
                 pltpu.VMEM((count, own, WIDE), BF16),
                 pltpu.VMEM((width, count * WIDE), BF16),
-                pltpu.VMEM((feats, count * WIDE), BF16),
             ]
-            + [pltpu.SemaphoreType.DMA((count,))] * 3,
+            + [pltpu.SemaphoreType.DMA((count,))] * 2,
             compiler_params=params(16 * 2**20),
             cost_estimate=cost(2.5 * rows * width * WIDE * count, 2 * width * WIDE * count),
             name="student_side",
         )(place, logs, unit, feat, scaled, s_exp, weight, before)
-        grad_parts.append(far(grad_part))
+        grad_parts.append(grad_part)
         return done
 
     done = unit
     for turn in range(SWEEPS - 1):
-        late = t_all if turn == 0 else []
+        late = t_all if turn == 1 else []
         sums = pl.pallas_call(
             row_kernel,
-            in_specs=[VMEM, VMEM, ANY, ANY],
+            in_specs=[VMEM, VMEM, ANY, ANY] + [ANY] * len(late),
             out_specs=VMEM,
             out_shape=struct((parts, 8, LANES), F32),
             scratch_shapes=[pltpu.VMEM((height, LANES), F32), spread, exp_buffer, sems],
             compiler_params=params(exp_bytes),
             cost_estimate=cost(2 * own * local_protos, exp_bytes),
             name="rows",
-        )(cols, factor, t_exp, done)
+        )(cols, factor, t_exp, done, *late)
         done = student_piece(sums)
         sums = exchange(sums, "proto")
         cols = pl.pallas_call(
             column_kernel,
-            in_specs=[VMEM, VMEM, ANY, ANY] + [ANY] * len(late),
+            in_specs=[VMEM, VMEM, ANY, ANY],
             out_specs=VMEM,
             out_shape=struct((groups, height, LANES), F32),
             scratch_shapes=[spread, exp_buffer, sems],
             compiler_params=params(exp_bytes),
             cost_estimate=cost(2 * own * local_protos, exp_bytes),
             name="columns",
-        )(sums, factor, t_exp, done, *late)
+        )(sums, factor, t_exp, done)
         done = student_piece(cols)
         cols = exchange(cols, "batch")
 
@@ -722,7 +735,7 @@
 
     grad_weight = pl.pallas_call(
         functools.partial(grad_kernel, counts, float(protos)),
-        in_specs=[ANY] * 2 + [VMEM] * 4 + [ANY] * len(counts),
+        in_specs=[ANY] * 2 + [VMEM] * (4 + len(counts)),
         out_specs=ANY,
         out_shape=struct((feats, local_protos), BF16),
         scratch_shapes=[
@@ -730,8 +743,7 @@
             exp_buffer,
             pltpu.VMEM((chunks, others, WIDE), BF16),
             pltpu.VMEM((feats, local_protos), BF16),
-            pltpu.VMEM((feats, local_protos), BF16),
-            sems, sems, sems, sems,
+            sems, sems, sems,
         ],
         compiler_params=params(exp_bytes + others_bytes + 4 * feats * local_protos),
         cost_estimate=cost(2 * feats * rows * local_protos, others_bytes),

time: 162 us -> 154 us (0.951)
  waiting for transfers between devices: 24.2 us -> 11.1 us
  local copies, waits for them, and re-layouts: 1.33 us -> 5.42 us
    all_to_all x8, waiting for transfers between devices: 24.2 us -> 11.1 us  [exchange(): return lax.all_to_all(value, axis, 0, 0)]
    pallas_call x5 -> x6, Pallas kernels: 15.7 us -> 21.1 us  [the longest x2 6.12 us: local(): pl.pallas_call(row_kernel, in_specs=[VMEM, VMEM, ANY, ANY] + [ANY] * len(...]
    unnamed x7 -> x17, local copies, waits for them, and re-layouts: 0.81 us -> 4.91 us
    pallas_call x5, Pallas kernels: 24.4 us -> 20.8 us  [student_piece(): pl.pallas_call(functools.partial(student_kernel, log_protos, first), in_s...]
    pallas_call x1, Pallas kernels: 17.5 us -> 15.5 us  [local(): pl.pallas_call(stats_kernel, in_specs=[ANY] * 3, out_specs=[ANY, ANY, VME...]
  transfers between devices with their start and end apart: 17 -> 17, of which waited for: 7 -> 5; matrix products, arithmetic and copies ran while one was open for 0% -> 0% of each run, Pallas kernels for 34% -> 38%
where the time goes in v1:
time: 154 us; the launch traced here: 153 us
  Pallas kernels  86.8 us (56%)
  starting transfers between devices  46.4 us (30%)
  waiting for transfers between devices  11.1 us (7%)
  local copies, waits for them, and re-layouts  5.42 us (4%)
  between operations  2.72 us (2%)
    all_to_all x8, starting transfers between devices, exchange(): return lax.all_to_all(value, axis, 0, 0)  29.1 us
    pallas_call x5, Pallas kernels, student_piece(): pl.pallas_call(functools.partial(student_kernel, log_protos, first), in_s...  20.8 us
    pallas_call x1, Pallas kernels, local(): pl.pallas_call(functools.partial(last_kernel, groups), in_specs=[SMEM] +...  17.9 us
    pallas_call x1, Pallas kernels, local(): pl.pallas_call(stats_kernel, in_specs=[ANY] * 3, out_specs=[ANY, ANY, VME...  15.5 us
    ppermute x6, starting transfers between devices, following(): lax.ppermute(value, axis, [(i, (i - s) % n) for i in range(n)])  12.8 us
    all_to_all x8, waiting for transfers between devices, exchange(): return lax.all_to_all(value, axis, 0, 0)  11.1 us
    pallas_call x1, Pallas kernels, local(): pl.pallas_call(functools.partial(grad_kernel, counts, float(protos)), in_...  7.68 us
    pallas_call x2, Pallas kernels, local(): pl.pallas_call(row_kernel, in_specs=[VMEM, VMEM, ANY, ANY] + [ANY] * len(...  6.12 us
  transfers between devices with their start and end apart: 17, of which 5 were waited for; matrix products, arithmetic and copies ran while one was open for 0% of the time, Pallas kernels for 38%

profile of v1, /device:TPU:0, one launch (start us, length us, event | category | flops | bytes accessed | tf_op | source)
XLA Modules:
  0.0 152.5 jit_solution(14464813153699813374)
XLA Ops:
  0.6 3.1 %collective-permute-start.2 = (bf16[256,512]{1,0:T(8,128)(2,1)}, bf16[256,512]{1,0:T(8,128)(2,1)S(1)}, u32[]{:S(2)}, u32[]{:S(2)}) collective-permute-start(bf16[256,512]{1,0:T(8,128)(2,1)} %s_ref.1), channel_id=1, source_target_pairs={{0,1},{1,2},{2,3},{3,0},{4,5},{5,6},{6,7},{7,4},{8,9},{9,10},{10,1... | collective-permute-start | bytes 786440 | tf_op jit(solution)/shard_map/ppermute | solution.py:526
  7.6 15.5 %own_rows.1 = (bf16[8,256,1024]{2,1,0:T(8,128)(2,1)}, bf16[8,256,1024]{2,1,0:T(8,128)(2,1)}, f32[8,8,128]{2,1,0:T(8,128)}) custom-call(bf16[256,512]{1,0:T(8,128)(2,1)} %t_ref.1, bf16[256,512]{1,0:T(8,128)(2,1)} %s_ref.1, bf16[512,8192]{1,0:T(8,128)(2,1)} %w_hbm.15), custom_call_target="tpu_custom_call" | custom-call | flops 4294967296 | bytes 8388608 | tf_op jit(solution)/shard_map/own_rows/pallas_call | solution.py:570
  23.2 3.7 %all-to-all-start = ((f32[8,8,128]{2,1,0:T(8,128)}), f32[8,8,128]{2,1,0:T(8,128)S(1)}, u32[]{:S(2)}, u32[]{:S(2)}) async-start(f32[8,8,128]{2,1,0:T(8,128)} %get-tuple-element.29.before_ref), calls=%async_computation | async-start | bytes 65536 | tf_op jit(solution)/shard_map/all_to_all | solution.py:521
  26.9 5.5 %own_back.1.refs_0_.student_ref = f32[256,512]{1,0:T(8,128)S(1)} custom-call(f32[8,8,128]{2,1,0:T(8,128)} %get-tuple-element.29.before_ref, bf16[8,256,1024]{2,1,0:T(8,128)(2,1)} %get-tuple-element.30.exp_hbm, bf16[512,8192]{1,0:T(8,128)(2,1)} %w_hbm.15), custom_call_target="tpu_custom_call" | custom-call | flops 2147483648 | bytes 8388608 | tf_op jit(solution)/shard_map/own_back/pallas_call | solution.py:596
  32.5 3.6 %first_columns.1 = (f32[8,128]{1,0:T(8,128)S(1)}, f32[4,72,128]{2,1,0:T(8,128)}) custom-call(s32[2]{0:T(128)S(1)} %pad_add_fusion.place_ref, f32[8,8,128]{2,1,0:T(8,128)S(1)} %all-to-all-done.stats_ref, bf16[8,256,1024]{2,1,0:T(8,128)(2,1)} %get-tuple-element.28.exp_hbm, f32[256,512]{1,0:T(8,128)S(1)} %own_back.1.refs_0_.student_ref, ...), custom_call_target="tpu_custom_call" | custom-call | flops 4194304 | bytes 4194304 | tf_op jit(solution)/shard_map/first_columns/pallas_call | solution.py:610
  36.1 3.3 %all-to-all-start.1 = ((f32[4,72,128]{2,1,0:T(8,128)}), f32[4,72,128]{2,1,0:T(8,128)S(1)}, u32[]{:S(2)}, u32[]{:S(2)}) async-start(f32[4,72,128]{2,1,0:T(8,128)} %get-tuple-element.31.refs_3_), calls=%async_computation.1 | async-start | bytes 294912 | tf_op jit(solution)/shard_map/all_to_all | solution.py:521
  47.4 3.1 %rows.2.refs_0_ = f32[8,8,128]{2,1,0:T(8,128)} custom-call(f32[4,72,128]{2,1,0:T(8,128)S(1)} %all-to-all-done.1.cols_ref.logs_ref, f32[8,128]{1,0:T(8,128)S(1)} %get-tuple-element.32.factor_ref, bf16[8,256,1024]{2,1,0:T(8,128)(2,1)} %get-tuple-element.28.exp_hbm, bf16[768,512]{1,0:T(8,128)(2,1)S(1)} %get-tuple-element.33.refs_0_.unit), custom_call_target="tpu_custom_call" | custom-call | flops 4194304 | bytes 4194304 | tf_op jit(solution)/shard_map/rows/pallas_call | solution.py:666
  50.4 4.2 %all-to-all-start.2 = ((f32[8,8,128]{2,1,0:T(8,128)}), f32[8,8,128]{2,1,0:T(8,128)S(1)}, u32[]{:S(2)}, u32[]{:S(2)}) async-start(f32[8,8,128]{2,1,0:T(8,128)} %rows.2.refs_0_), calls=%async_computation.2 | async-start | bytes 65536 | tf_op jit(solution)/shard_map/all_to_all | solution.py:521
  54.7 3.3 %student_side.5 = (bf16[128,1024]{1,0:T(8,128)(2,1)S(1)}, f32[8,128]{1,0:T(8,128)S(1)}) custom-call(s32[2]{0:T(128)S(1)} %pad_add_fusion.place_ref, f32[4,72,128]{2,1,0:T(8,128)S(1)} %all-to-all-done.1.cols_ref.logs_ref, bf16[768,512]{1,0:T(8,128)(2,1)S(1)} %get-tuple-element.33.refs_0_.unit, bf16[128,1024]{1,0:T(8,128)(2,1)S(1)} %get-tuple-element.34.feat_ref, ...), custom_call_target="tpu_custom_call" | custom-call | flops 1342177280 | bytes 1048576 | tf_op jit(solution)/shard_map/student_side/pallas_call | solution.py:644
  59.5 3.0 %columns.2.refs_0_ = f32[4,64,128]{2,1,0:T(8,128)} custom-call(f32[8,8,128]{2,1,0:T(8,128)S(1)} %all-to-all-done.2.sums_ref, f32[8,128]{1,0:T(8,128)S(1)} %get-tuple-element.32.factor_ref, bf16[8,256,1024]{2,1,0:T(8,128)(2,1)} %get-tuple-element.28.exp_hbm, f32[8,128]{1,0:T(8,128)S(1)} %get-tuple-element.36.refs_0_), custom_call_target="tpu_custom_call" | custom-call | flops 4194304 | bytes 4194304 | tf_op jit(solution)/shard_map/columns/pallas_call | solution.py:678
  62.5 3.3 %all-to-all-start.3 = ((f32[4,64,128]{2,1,0:T(8,128)}), f32[4,64,128]{2,1,0:T(8,128)S(1)}, u32[]{:S(2)}, u32[]{:S(2)}) async-start(f32[4,64,128]{2,1,0:T(8,128)} %columns.2.refs_0_), calls=%async_computation.3 | async-start | bytes 262144 | tf_op jit(solution)/shard_map/all_to_all | solution.py:521
  65.8 3.3 %student_side.6 = (bf16[128,1024]{1,0:T(8,128)(2,1)S(1)}, f32[8,128]{1,0:T(8,128)S(1)}) custom-call(s32[2]{0:T(128)S(1)} %pad_add_fusion.place_ref, f32[4,72,128]{2,1,0:T(8,128)S(1)} %all-to-all-done.1.cols_ref.logs_ref, bf16[768,512]{1,0:T(8,128)(2,1)S(1)} %get-tuple-element.33.refs_0_.unit, bf16[128,1024]{1,0:T(8,128)(2,1)S(1)} %get-tuple-element.34.feat_ref, ...), custom_call_target="tpu_custom_call" | custom-call | flops 1342177280 | bytes 1048576 | tf_op jit(solution)/shard_map/student_side/pallas_call | solution.py:644
  69.2 3.0 %all-to-all-done.3.cols_ref = f32[4,64,128]{2,1,0:T(8,128)S(1)} async-done(((f32[4,64,128]{2,1,0:T(8,128)}), f32[4,64,128]{2,1,0:T(8,128)S(1)}, u32[]{:S(2)}, u32[]{:S(2)}) %all-to-all-start.3) | async-done | bytes 131104 | tf_op jit(solution)/shard_map/all_to_all | solution.py:521
  72.2 3.1 %rows.3.refs_0_ = f32[8,8,128]{2,1,0:T(8,128)} custom-call(f32[4,64,128]{2,1,0:T(8,128)S(1)} %all-to-all-done.3.cols_ref, f32[8,128]{1,0:T(8,128)S(1)} %get-tuple-element.32.factor_ref, bf16[8,256,1024]{2,1,0:T(8,128)(2,1)} %get-tuple-element.28.exp_hbm, f32[8,128]{1,0:T(8,128)S(1)} %get-tuple-element.37.refs_0_, ...), custom_call_target="tpu_custom_call" | custom-call | flops 4194304 | bytes 4194304 | tf_op jit(solution)/shard_map/rows/pallas_call | solution.py:666
  75.2 3.9 %all-to-all-start.4 = ((f32[8,8,128]{2,1,0:T(8,128)}), f32[8,8,128]{2,1,0:T(8,128)S(1)}, u32[]{:S(2)}, u32[]{:S(2)}) async-start(f32[8,8,128]{2,1,0:T(8,128)} %rows.3.refs_0_), calls=%async_computation.4 | async-start | bytes 65536 | tf_op jit(solution)/shard_map/all_to_all | solution.py:521
  79.1 3.3 %student_side.7 = (bf16[128,1024]{1,0:T(8,128)(2,1)S(1)}, f32[8,128]{1,0:T(8,128)S(1)}) custom-call(s32[2]{0:T(128)S(1)} %pad_add_fusion.place_ref, f32[4,72,128]{2,1,0:T(8,128)S(1)} %all-to-all-done.1.cols_ref.logs_ref, bf16[768,512]{1,0:T(8,128)(2,1)S(1)} %get-tuple-element.33.refs_0_.unit, bf16[128,1024]{1,0:T(8,128)(2,1)S(1)} %get-tuple-element.34.feat_ref, ...), custom_call_target="tpu_custom_call" | custom-call | flops 1342177280 | bytes 1048576 | tf_op jit(solution)/shard_map/student_side/pallas_call | solution.py:644
  84.0 3.0 %columns.3.refs_0_ = f32[4,64,128]{2,1,0:T(8,128)} custom-call(f32[8,8,128]{2,1,0:T(8,128)S(1)} %all-to-all-done.4.sums_ref, f32[8,128]{1,0:T(8,128)S(1)} %get-tuple-element.32.factor_ref, bf16[8,256,1024]{2,1,0:T(8,128)(2,1)} %get-tuple-element.28.exp_hbm, f32[8,128]{1,0:T(8,128)S(1)} %get-tuple-element.39.refs_0_), custom_call_target="tpu_custom_call" | custom-call | flops 4194304 | bytes 4194304 | tf_op jit(solution)/shard_map/columns/pallas_call | solution.py:678
  87.0 3.5 %all-to-all-start.5 = ((f32[4,64,128]{2,1,0:T(8,128)}), f32[4,64,128]{2,1,0:T(8,128)S(1)}, u32[]{:S(2)}, u32[]{:S(2)}) async-start(f32[4,64,128]{2,1,0:T(8,128)} %columns.3.refs_0_), calls=%async_computation.5 | async-start | bytes 262144 | tf_op jit(solution)/shard_map/all_to_all | solution.py:521
  90.5 3.3 %student_side.8 = (bf16[128,1024]{1,0:T(8,128)(2,1)S(1)}, f32[8,128]{1,0:T(8,128)S(1)}) custom-call(s32[2]{0:T(128)S(1)} %pad_add_fusion.place_ref, f32[4,72,128]{2,1,0:T(8,128)S(1)} %all-to-all-done.1.cols_ref.logs_ref, bf16[768,512]{1,0:T(8,128)(2,1)S(1)} %get-tuple-element.33.refs_0_.unit, bf16[128,1024]{1,0:T(8,128)(2,1)S(1)} %get-tuple-element.34.feat_ref, ...), custom_call_target="tpu_custom_call" | custom-call | flops 1342177280 | bytes 1048576 | tf_op jit(solution)/shard_map/student_side/pallas_call | solution.py:644
  98.3 17.9 %last_rows.1 = (bf16[8,768,1024]{2,1,0:T(8,128)(2,1)}, f32[64,128]{1,0:T(8,128)S(1)}, bf16[8,80,512]{2,1,0:T(8,128)(2,1)}) custom-call(s32[2]{0:T(128)S(1)} %pad_add_fusion.place_ref, f32[4,72,128]{2,1,0:T(8,128)S(1)} %all-to-all-done.1.cols_ref.logs_ref, f32[4,64,128]{2,1,0:T(8,128)S(1)} %all-to-all-done.5.cols_ref, ...), custom_call_target="tpu_custom_call" | custom-call | flops 8589934592 | bytes 12582912 | tf_op jit(solution)/shard_map/last_rows/pallas_call | solution.py:693
  116.2 3.6 %all-to-all-start.6 = ((bf16[8,80,512]{2,1,0:T(8,128)(2,1)}), bf16[8,80,512]{2,1,0:T(8,128)(2,1)S(1)}, u32[]{:S(2)}, u32[]{:S(2)}) async-start(bf16[8,80,512]{2,1,0:T(8,128)(2,1)} %get-tuple-element.43.refs_0_), calls=%async_computation.6 | async-start | bytes 1310720 | tf_op jit(solution)/shard_map/all_to_all | solution.py:521
  119.7 7.7 %student_side.9 = (bf16[128,4096]{1,0:T(8,128)(2,1)S(1)}, f32[8,128]{1,0:T(8,128)S(1)}) custom-call(s32[2]{0:T(128)S(1)} %pad_add_fusion.place_ref, f32[4,72,128]{2,1,0:T(8,128)S(1)} %all-to-all-done.1.cols_ref.logs_ref, bf16[768,512]{1,0:T(8,128)(2,1)S(1)} %get-tuple-element.33.refs_0_.unit, bf16[128,1024]{1,0:T(8,128)(2,1)S(1)} %get-tuple-element.34.feat_ref, ...), custom_call_target="tpu_custom_call" | custom-call | flops 5368709120 | bytes 4194304 | tf_op jit(solution)/shard_map/student_side/pallas_call | solution.py:644
  132.5 3.5 %all-to-all-start.7 = ((f32[8,32,512]{2,1,0:T(8,128)}), f32[8,32,512]{2,1,0:T(8,128)S(1)}, u32[]{:S(2)}, u32[]{:S(2)}) async-start(f32[8,32,512]{2,1,0:T(8,128)} %get-tuple-element.51), calls=%async_computation.7 | async-start | bytes 1048576 | tf_op jit(solution)/shard_map/all_to_all | solution.py:521
  141.7 7.7 %weight_grads.1 = bf16[128,8192]{1,0:T(8,128)(2,1)} custom-call(bf16[8,256,1024]{2,1,0:T(8,128)(2,1)} %get-tuple-element.28.exp_hbm, bf16[8,768,1024]{2,1,0:T(8,128)(2,1)} %get-tuple-element.41.prob_hbm, bf16[128,1024]{1,0:T(8,128)(2,1)S(1)} %get-tuple-element.34.feat_ref, f32[64,128]{1,0:T(8,128)S(1)} %get-tuple-element.42.scale_ref, ...), custom_call_target="tpu_custom_call" | custom-call | flops 2147483648 | bytes 12582912 | tf_op jit(solution)/shard_map/weight_grads/pallas_call | solution.py:736
  (46 shorter events, 31.5 us)
Async XLA Ops:
  0.6 31.9 %collective-permute-start.2 = (bf16[256,512]{1,0:T(8,128)(2,1)}, bf16[256,512]{1,0:T(8,128)(2,1)S(1)}, u32[]{:S(2)}, u32[]{:S(2)}) collective-permute-start(bf16[256,512]{1,0:T(8,128)(2,1)} %s_ref.1), channel_id=1, source_target_pairs={{0,1},{1,2},{2,3},{3,0},{4,5},{5,6},{6,7},{7,4},{8,9},{9,10},{10,1... | collective-permute-start | bytes 786440 | tf_op jit(solution)/shard_map/ppermute | solution.py:526
  3.7 28.8 %collective-permute-start.1 = (bf16[256,512]{1,0:T(8,128)(2,1)}, bf16[256,512]{1,0:T(8,128)(2,1)S(1)}, u32[]{:S(2)}, u32[]{:S(2)}) collective-permute-start(bf16[256,512]{1,0:T(8,128)(2,1)} %s_ref.1), channel_id=1, source_target_pairs={{0,2},{1,3},{2,0},{3,1},{4,6},{5,7},{6,4},{7,5},{8,10},{9,11},{10,... | collective-permute-start | bytes 786440 | tf_op jit(solution)/shard_map/ppermute | solution.py:526
  6.3 26.2 %collective-permute-start = (bf16[256,512]{1,0:T(8,128)(2,1)}, bf16[256,512]{1,0:T(8,128)(2,1)S(1)}, u32[]{:S(2)}, u32[]{:S(2)}) collective-permute-start(bf16[256,512]{1,0:T(8,128)(2,1)} %s_ref.1), channel_id=1, source_target_pairs={{0,3},{1,0},{2,1},{3,2},{4,7},{5,4},{6,5},{7,6},{8,11},{9,8},{10,9... | collective-permute-start | bytes 786440 | tf_op jit(solution)/shard_map/ppermute | solution.py:526
  23.2 9.3 %all-to-all-start = ((f32[8,8,128]{2,1,0:T(8,128)}), f32[8,8,128]{2,1,0:T(8,128)S(1)}, u32[]{:S(2)}, u32[]{:S(2)}) async-start(f32[8,8,128]{2,1,0:T(8,128)} %get-tuple-element.29.before_ref), calls=%async_computation | async-start | bytes 65536 | tf_op jit(solution)/shard_map/all_to_all | solution.py:521
  32.4 7.1 %copy-start = (bf16[256,512]{1,0:T(8,128)(2,1)S(1)}, bf16[256,512]{1,0:T(8,128)(2,1)}, u32[]{:S(2)}) copy-start(bf16[256,512]{1,0:T(8,128)(2,1)} %s_ref.1) | copy-start | bytes 786436
  32.4 7.1 %copy-start.7 = (bf16[256,512]{1,0:T(8,128)(2,1)S(1)}, bf16[256,512]{1,0:T(8,128)(2,1)}, u32[]{:S(2)}) copy-start(bf16[256,512]{1,0:T(8,128)(2,1)} %t_ref.1) | copy-start | bytes 786436
  36.1 11.3 %all-to-all-start.1 = ((f32[4,72,128]{2,1,0:T(8,128)}), f32[4,72,128]{2,1,0:T(8,128)S(1)}, u32[]{:S(2)}, u32[]{:S(2)}) async-start(f32[4,72,128]{2,1,0:T(8,128)} %get-tuple-element.31.refs_3_), calls=%async_computation.1 | async-start | bytes 294912 | tf_op jit(solution)/shard_map/all_to_all | solution.py:521
  41.6 27.5 %collective-permute-start.5 = (bf16[256,512]{1,0:T(8,128)(2,1)}, bf16[256,512]{1,0:T(8,128)(2,1)S(1)}, u32[]{:S(2)}, u32[]{:S(2)}) collective-permute-start(bf16[256,512]{1,0:T(8,128)(2,1)} %get-tuple-element.38), channel_id=1, source_target_pairs={{0,1},{1,2},{2,3},{3,0},{4,5},{5,6},{6,7},{7,4},{8,9},{9,10},{10,1... | collective-permute-start | bytes 786440 | tf_op jit(solution)/shard_map/ppermute | solution.py:526
  43.5 25.6 %collective-permute-start.4 = (bf16[256,512]{1,0:T(8,128)(2,1)}, bf16[256,512]{1,0:T(8,128)(2,1)S(1)}, u32[]{:S(2)}, u32[]{:S(2)}) collective-permute-start(bf16[256,512]{1,0:T(8,128)(2,1)} %get-tuple-element.38), channel_id=1, source_target_pairs={{0,2},{1,3},{2,0},{3,1},{4,6},{5,7},{6,4},{7,5},{8,10},{9,11},{10,... | collective-permute-start | bytes 786440 | tf_op jit(solution)/shard_map/ppermute | solution.py:526
  45.9 23.2 %collective-permute-start.3 = (bf16[256,512]{1,0:T(8,128)(2,1)}, bf16[256,512]{1,0:T(8,128)(2,1)S(1)}, u32[]{:S(2)}, u32[]{:S(2)}) collective-permute-start(bf16[256,512]{1,0:T(8,128)(2,1)} %get-tuple-element.38), channel_id=1, source_target_pairs={{0,3},{1,0},{2,1},{3,2},{4,7},{5,4},{6,5},{7,6},{8,11},{9,8},{10,9... | collective-permute-start | bytes 786440 | tf_op jit(solution)/shard_map/ppermute | solution.py:526
  50.4 9.1 %all-to-all-start.2 = ((f32[8,8,128]{2,1,0:T(8,128)}), f32[8,8,128]{2,1,0:T(8,128)S(1)}, u32[]{:S(2)}, u32[]{:S(2)}) async-start(f32[8,8,128]{2,1,0:T(8,128)} %rows.2.refs_0_), calls=%async_computation.2 | async-start | bytes 65536 | tf_op jit(solution)/shard_map/all_to_all | solution.py:521
  62.5 9.7 %all-to-all-start.3 = ((f32[4,64,128]{2,1,0:T(8,128)}), f32[4,64,128]{2,1,0:T(8,128)S(1)}, u32[]{:S(2)}, u32[]{:S(2)}) async-start(f32[4,64,128]{2,1,0:T(8,128)} %columns.2.refs_0_), calls=%async_computation.3 | async-start | bytes 262144 | tf_op jit(solution)/shard_map/all_to_all | solution.py:521
  69.1 6.1 %copy-start.3 = (bf16[256,512]{1,0:T(8,128)(2,1)}, bf16[256,512]{1,0:T(8,128)(2,1)S(1)}, u32[]{:S(2)}) copy-start(bf16[256,512]{1,0:T(8,128)(2,1)S(1)} %collective-permute-done.4.refs_2_.refs_1_) | copy-start | bytes 786436
  69.1 13.3 %copy-start.5 = (bf16[256,512]{1,0:T(8,128)(2,1)}, bf16[256,512]{1,0:T(8,128)(2,1)S(1)}, u32[]{:S(2)}) copy-start(bf16[256,512]{1,0:T(8,128)(2,1)S(1)} %collective-permute-done.3.refs_1_.refs_0_) | copy-start | bytes 786436
  75.2 8.8 %all-to-all-start.4 = ((f32[8,8,128]{2,1,0:T(8,128)}), f32[8,8,128]{2,1,0:T(8,128)S(1)}, u32[]{:S(2)}, u32[]{:S(2)}) async-start(f32[8,8,128]{2,1,0:T(8,128)} %rows.3.refs_0_), calls=%async_computation.4 | async-start | bytes 65536 | tf_op jit(solution)/shard_map/all_to_all | solution.py:521
  87.0 9.4 %all-to-all-start.5 = ((f32[4,64,128]{2,1,0:T(8,128)}), f32[4,64,128]{2,1,0:T(8,128)S(1)}, u32[]{:S(2)}, u32[]{:S(2)}) async-start(f32[4,64,128]{2,1,0:T(8,128)} %columns.3.refs_0_), calls=%async_computation.5 | async-start | bytes 262144 | tf_op jit(solution)/shard_map/all_to_all | solution.py:521
  96.4 1.0 copy-start.4
  116.2 14.6 %all-to-all-start.6 = ((bf16[8,80,512]{2,1,0:T(8,128)(2,1)}), bf16[8,80,512]{2,1,0:T(8,128)(2,1)S(1)}, u32[]{:S(2)}, u32[]{:S(2)}) async-start(bf16[8,80,512]{2,1,0:T(8,128)(2,1)} %get-tuple-element.43.refs_0_), calls=%async_computation.6 | async-start | bytes 1310720 | tf_op jit(solution)/shard_map/all_to_all | solution.py:521
  127.5 1.0 copy-start.1
  132.5 18.1 %all-to-all-start.7 = ((f32[8,32,512]{2,1,0:T(8,128)}), f32[8,32,512]{2,1,0:T(8,128)S(1)}, u32[]{:S(2)}, u32[]{:S(2)}) async-start(f32[8,32,512]{2,1,0:T(8,128)} %get-tuple-element.51), calls=%async_computation.7 | async-start | bytes 1048576 | tf_op jit(solution)/shard_map/all_to_all | solution.py:521
  136.0 13.4 %collective-permute-start.8 = (f32[8,128]{1,0:T(8,128)S(1)}, f32[8,128]{1,0:T(8,128)S(1)}, u32[]{:S(2)}, u32[]{:S(2)}) collective-permute-start(f32[8,128]{1,0:T(8,128)S(1)} %get-tuple-element.52), channel_id=1, source_target_pairs={{0,3},{1,2},{2,1},{3,0},{4,7},{5,6},{6,5},{7,4},{8,11},{9,10},{10,... | collective-permute-start | bytes 12296 | tf_op jit(solution)/shard_map/ppermute | solution.py:532
  137.7 11.7 %collective-permute-start.7 = (f32[8,128]{1,0:T(8,128)S(1)}, f32[8,128]{1,0:T(8,128)S(1)}, u32[]{:S(2)}, u32[]{:S(2)}) collective-permute-start(f32[8,128]{1,0:T(8,128)S(1)} %get-tuple-element.52), channel_id=1, source_target_pairs={{0,2},{1,3},{2,0},{3,1},{4,6},{5,7},{6,4},{7,5},{8,10},{9,11},{10,... | collective-permute-start | bytes 12296 | tf_op jit(solution)/shard_map/ppermute | solution.py:532
  138.6 10.8 %collective-permute-start.6 = (f32[8,128]{1,0:T(8,128)S(1)}, f32[8,128]{1,0:T(8,128)S(1)}, u32[]{:S(2)}, u32[]{:S(2)}) collective-permute-start(f32[8,128]{1,0:T(8,128)S(1)} %get-tuple-element.52), channel_id=1, source_target_pairs={{0,1},{1,0},{2,3},{3,2},{4,5},{5,4},{6,7},{7,6},{8,9},{9,8},{10,11... | collective-permute-start | bytes 12296 | tf_op jit(solution)/shard_map/ppermute | solution.py:532
  140.4 1.2 copy-start.2
  (1 other events, 0.9 us)

commit v2 on v1

--- a/solution.py
+++ b/solution.py
@@ -107,6 +107,10 @@
     for each in zip(*lists):
         for copy in each:
             copy.start()
+
+
+def whole_copies(pairs, sems):
+    return [pltpu.make_async_copy(a, b, sems.at[i]) for i, (a, b) in enumerate(pairs)]
 
 
 def wait(*lists):
@@ -295,8 +299,11 @@
         spread_rows(lse.at[(g - 1) * own : g * own], there[first : first + quarter, :] - shift)
 
 
-def student_rows_kernel(protos, place_ref, factor_ref, t_ref, own_ref, *refs):
-    unit_ref, feat_ref, scaled_ref, t_unit, turned = refs[-5:]
+def student_rows_kernel(protos, place_ref, factor_ref, t_hbm, own_hbm, *refs):
+    unit_ref, feat_ref, scaled_ref, t_unit, turned, t_ref, own_ref, sems = refs[-8:]
+    loads = whole_copies([(t_hbm, t_ref), (own_hbm, own_ref)], sems)
+    start(loads)
+    wait(loads)
     t_unit[...] = unit_rows(t_ref[...])[0].astype(BF16)
     own = own_ref.shape[0]
     groups = turned.shape[1] // own
@@ -328,10 +335,13 @@
 
 
 def student_kernel(
-    log_protos, first, place_ref, logs_ref, unit, feat_ref, scaled_ref, exp_hbm, w_hbm, *refs
+    log_protos, first, count, place_ref, logs_ref, unit, feat_ref, scaled_ref, exp_hbm, w_hbm, *refs
 ):
-    grad, token_ref, lse, prob, exp_ref, w_ref, exp_sem, w_sem = refs[-8:]
-    own, count = exp_ref.shape[1], exp_ref.shape[0]
+    if count > 1:
+        grad_hbm, token_ref, lse, prob, exp_ref, w_ref, exp_sem, w_sem, grad, grad_sem = refs[-10:]
+    else:
+        grad, token_ref, lse, prob, exp_ref, w_ref, exp_sem, w_sem = refs[-8:]
+    own = exp_ref.shape[1]
     exp_loads = copies(exp_hbm, exp_ref, exp_sem, first, 0, count)
     w_loads = copies(w_hbm, w_ref, w_sem, first, 0, count)
     start(w_loads, exp_loads)
@@ -351,6 +361,11 @@
         values = jnp.dot(scaled_ref[...], exp_ref[k], preferred_element_type=F32)
         values = values + jnp.dot(feat_ref[:, own:], prob[...], preferred_element_type=F32)
         grad[:, columns_of(k)] = values.astype(BF16)
+        if count > 1:
+            copy_of(grad, grad_hbm, grad_sem, k).start()
+
+    if count > 1:
+        wait(copies(grad, grad_hbm, grad_sem))
 
 
 def as_three(value):
@@ -360,16 +375,22 @@
     return high, middle, (rest - middle.astype(F32)).astype(BF16)
 
 
-def last_kernel(groups, place_ref, logs_ref, cols_ref, factor_ref, own_ref, student_ref, exp_hbm, w_hbm, *refs):
+def last_kernel(groups, place_ref, logs_ref, cols_ref, factor_ref, own_hbm, student_hbm, exp_hbm, w_hbm, *refs):
     units = refs[: groups - 1]
     (
         prob_hbm, scale_ref, out_ref, unit, lse, rows, own_rows, back, scaled, sums, prob_ref,
-        exp_ref, w_ref, prob_sem, exp_sem, w_sem,
-    ) = refs[-16:]
+        exp_ref, w_ref, own_ref, student_ref, prob_sem, exp_sem, w_sem, sem,
+    ) = refs[-19:]
+    own = own_ref.shape[0]
+    pairs = [(units[g], unit.at[g * own : (g + 1) * own]) for g in range(groups - 1)]
+    loads = whole_copies(pairs + [(own_hbm, own_ref), (student_hbm, student_ref)], sem)
     w_loads, exp_loads = copies(w_hbm, w_ref, w_sem), copies(exp_hbm, exp_ref, exp_sem)
-    start(w_loads, exp_loads)
+    start(w_loads[:1])
+    start(loads)
+    start(w_loads[1:])
+    start(exp_loads)
     slots, others, _ = prob_ref.shape
-    own, chunks = exp_ref.shape[1], exp_ref.shape[0]
+    chunks = exp_ref.shape[0]
     tiles = (own + others) // LANES
     quarter = own // LANES
     scale_ref[...] = column_scales(cols_ref, scale_ref.shape[0])
@@ -377,8 +398,7 @@
     own_rows[...] = jnp.zeros(own_rows.shape, F32)
     back[...] = jnp.zeros(back.shape, F32)
     relative_logs(place_ref, logs_ref, lse, 0)
-    for g in range(groups - 1):
-        unit[g * own : (g + 1) * own, :] = units[g][...]
+    wait(loads)
     partner = slice((groups // 2 - 1) * own, groups // 2 * own)
 
     def store(k):
@@ -445,21 +465,24 @@
     return add_up(each)
 
 
-def rows_kernel(tiles, protos, place_ref, s_ref, message_ref, logs_ref, *refs):
-    out_ref, loss_ref, sums_ref, weight = refs[-4:]
+def rows_kernel(tiles, protos, place_ref, s_hbm, message_ref, logs_ref, *refs):
+    out_ref, loss_ref, sums_ref, weight, s_ref, sem = refs[-6:]
     parts = message_ref.shape[0]
     share, own = out_ref.shape[1], weight.shape[0]
+    mine = pl.ds(pl.multiple_of(place_ref[1] * share, share), share)
+    load = pltpu.make_async_copy(s_hbm.at[mine], s_ref, sem)
+    load.start()
     quarter = own // LANES
     first = tiles // 2
     totals = total_sums(message_ref, 2 * share)
     sums_ref[...] = totals
     scale = 1.0 / totals[first : first + quarter, :]
     spread_rows(weight, scale)
-    mine = pl.ds(pl.multiple_of(place_ref[1] * share, share), share)
     total = add_up([message_ref[p, :share, :].astype(F32) for p in range(parts)])
     paired = add_up([message_ref[p, share : 2 * share, :].astype(F32) for p in range(parts)])
     total = total - paired * (weight[mine, :1] * protos)
-    unit, length = unit_rows(s_ref[mine, :])
+    load.wait()
+    unit, length = unit_rows(s_ref[...])
     out_ref[0] = (total - unit * jnp.sum(unit * total, axis=-1, keepdims=True)) / length
     repeat(out_ref)
     height = logs_ref.shape[1] - 8
@@ -470,10 +493,15 @@
 
 def grad_kernel(counts, protos, exp_hbm, prob_hbm, feat_ref, scale_ref, sums_ref, factor_ref, *refs):
     parts = refs[: len(counts)]
-    out_hbm, scaled, exp_ref, prob_ref, out, exp_sem, prob_sem, sem = refs[-8:]
+    out_hbm, scaled, exp_ref, prob_ref, out, last_ref, exp_sem, prob_sem, sem, last_sem = refs[-10:]
+    last_load = pltpu.make_async_copy(parts[-1], last_ref, last_sem)
+    parts = parts[:-1] + (last_ref,)
     exp_loads = copies(exp_hbm, exp_ref, exp_sem)
     prob_loads = copies(prob_hbm, prob_ref, prob_sem)
-    start(exp_loads, prob_loads)
+    early = sum(counts[:-1])
+    start(exp_loads[:early], prob_loads[:early])
+    last_load.start()
+    start(exp_loads[early:], prob_loads[early:])
     where = [(part, k) for count, part in zip(counts, parts) for k in range(count)]
     own = exp_ref.shape[1]
     tiles = (own + prob_ref.shape[1]) // LANES
@@ -494,6 +522,8 @@
             scaled[:, own:], prob_ref[k], preferred_element_type=F32
         )
         part, there = where[k]
+        if part is last_ref and there == 0:
+            last_load.wait()
         for t, tile in enumerate(lane_tiles(paired)):
             lanes = slice(k * WIDE + t * LANES, k * WIDE + (t + 1) * LANES)
             scale = scale_ref[lanes.start // LANES : lanes.stop // LANES, :]
@@ -564,6 +594,7 @@
         return pltpu.with_memory_space_constraint(value, pltpu.HBM)
 
     weight = far(proto_weight)
+    teacher_rows, student_rows = far(teacher_feats), far(student_feats)
     s_all = following(student_feats, "batch")
 
     exps = pltpu.HBM((chunks, own, WIDE), BF16)
@@ -590,7 +621,7 @@
         compiler_params=params(weight_bytes + 6 * exp_bytes),
         cost_estimate=cost(4 * own * width * local_protos, weight_bytes),
         name="own_rows",
-    )(far(teacher_feats), far(student_feats), weight)
+    )(teacher_rows, student_rows, weight)
     t_exp, s_exp = far(t_exp), far(s_exp)
 
     back_student = pl.pallas_call(
@@ -620,17 +651,22 @@
 
     unit, feat, scaled, t_unit = pl.pallas_call(
         functools.partial(student_rows_kernel, float(protos)),
-        in_specs=[SMEM, VMEM, VMEM, VMEM] + [VMEM] * (groups - 1) + [ANY],
+        in_specs=[SMEM, VMEM, ANY, ANY] + [VMEM] * (groups - 1) + [ANY],
         out_specs=[VMEM] * 4,
         out_shape=[
             struct((others, width), BF16), struct((feats, rows), BF16), struct((feats, own), BF16),
             struct((own, width), BF16),
         ],
-        scratch_shapes=[pltpu.VMEM((width, rows), BF16)],
+        scratch_shapes=[
+            pltpu.VMEM((width, rows), BF16),
+            pltpu.VMEM((own, width), BF16),
+            pltpu.VMEM((own, width), BF16),
+            pltpu.SemaphoreType.DMA((2,)),
+        ],
         compiler_params=params(2 * rows * width),
         cost_estimate=cost(8 * rows * width, 2 * rows * width),
         name="student_rows",
-    )(place, factor, teacher_feats, student_feats, *s_all, cols)
+    )(place, factor, teacher_rows, student_rows, *s_all, cols)
     t_all = following(t_unit, "batch")
     cols = exchange(cols, "batch")
     logs = cols
@@ -642,22 +678,26 @@
         turn = len(grad_parts)
         first, count = sum(counts[:turn]), counts[turn]
         grad_part, done = pl.pallas_call(
-            functools.partial(student_kernel, log_protos, first),
+            functools.partial(student_kernel, log_protos, first, count),
             in_specs=[SMEM] + [VMEM] * 4 + [ANY] * 3,
-            out_specs=[VMEM, VMEM],
-            out_shape=[struct((feats, count * WIDE), BF16), token],
+            out_specs=[ANY if count > 1 else VMEM, VMEM],
+            out_shape=[
+                (pltpu.HBM if count > 1 else struct)((feats, count * WIDE), BF16), token,
+            ],
             scratch_shapes=[
                 pltpu.VMEM((others, LANES), F32),
                 pltpu.VMEM((others, WIDE), BF16),
                 pltpu.VMEM((count, own, WIDE), BF16),
                 pltpu.VMEM((width, count * WIDE), BF16),
             ]
-            + [pltpu.SemaphoreType.DMA((count,))] * 2,
+            + [pltpu.SemaphoreType.DMA((count,))] * 2
+            + ([pltpu.VMEM((feats, count * WIDE), BF16)] if count > 1 else [])
+            + ([pltpu.SemaphoreType.DMA((count,))] if count > 1 else []),
             compiler_params=params(16 * 2**20),
             cost_estimate=cost(2.5 * rows * width * WIDE * count, 2 * width * WIDE * count),
             name="student_side",
         )(place, logs, unit, feat, scaled, s_exp, weight, before)
-        grad_parts.append(grad_part)
+        grad_parts.append(far(grad_part) if count > 1 else grad_part)
         return done
 
     done = unit
@@ -692,7 +732,7 @@
     message_shape = (parts, 2 * share + sum_rows, width)
     prob, col_scale, message = pl.pallas_call(
         functools.partial(last_kernel, groups),
-        in_specs=[SMEM] + [VMEM] * 5 + [ANY] * 2 + [VMEM] * (groups - 1) + [ANY],
+        in_specs=[SMEM] + [VMEM] * 3 + [ANY] * (4 + groups),
         out_specs=[ANY, VMEM, VMEM],
         out_shape=[
             pltpu.HBM((chunks, others, WIDE), BF16),
@@ -710,32 +750,36 @@
             pltpu.VMEM((min(chunks, 3), others, WIDE), BF16),
             exp_buffer,
             w_buffer,
+            pltpu.VMEM((own, width), BF16),
+            pltpu.VMEM((own, width), F32),
             sems, sems, sems,
+            pltpu.SemaphoreType.DMA((groups + 1,)),
         ],
         compiler_params=params(20 * 2**20 + weight_bytes + exp_bytes),
         cost_estimate=cost(2 * rows * width * local_protos, others_bytes),
         name="last_rows",
     )(
-        place, logs, cols, factor, student_feats, back_student, t_exp, weight, *t_all, done,
+        place, logs, cols, factor, student_rows, far(back_student), t_exp, weight,
+        *[far(x) for x in t_all], done,
     )
     done = student_piece(message)
     message = exchange(message, "proto")
 
     grad_rows, loss_part, sums = pl.pallas_call(
         functools.partial(rows_kernel, tiles, float(protos)),
-        in_specs=[SMEM] + [VMEM] * 3 + [ANY],
+        in_specs=[SMEM, ANY, VMEM, VMEM, ANY],
         out_specs=[VMEM] * 3,
         out_shape=[struct((parts, share, width), F32), token, struct((sum_rows, LANES), F32)],
-        scratch_shapes=[spread],
+        scratch_shapes=[spread, pltpu.VMEM((share, width), BF16), pltpu.SemaphoreType.DMA],
         compiler_params=params(0),
         name="row_grads",
-    )(place, student_feats, message, logs, done)
+    )(place, student_rows, message, logs, done)
     grad_rows = exchange(grad_rows, "proto").reshape(own, width)
     loss = tree_sum(loss_part, "batch")[0, 0] / rows
 
     grad_weight = pl.pallas_call(
         functools.partial(grad_kernel, counts, float(protos)),
-        in_specs=[ANY] * 2 + [VMEM] * (4 + len(counts)),
+        in_specs=[ANY] * 2 + [VMEM] * (3 + len(counts)) + [ANY],
         out_specs=ANY,
         out_shape=struct((feats, local_protos), BF16),
         scratch_shapes=[
@@ -743,7 +787,9 @@
             exp_buffer,
             pltpu.VMEM((chunks, others, WIDE), BF16),
             pltpu.VMEM((feats, local_protos), BF16),
+            pltpu.VMEM((feats, counts[-1] * WIDE), BF16),
             sems, sems, sems,
+            pltpu.SemaphoreType.DMA,
         ],
         compiler_params=params(exp_bytes + others_bytes + 4 * feats * local_protos),
         cost_estimate=cost(2 * feats * rows * local_protos, others_bytes),

time: 154 us -> 156 us (1.013)
  Pallas kernels: 86.8 us -> 92.8 us
  local copies, waits for them, and re-layouts: 5.42 us -> 1.33 us
    unnamed x17 -> x9, local copies, waits for them, and re-layouts: 4.91 us -> 0.81 us
    pallas_call x1, Pallas kernels: 17.9 us -> 20.9 us  [local(): pl.pallas_call(functools.partial(last_kernel, groups), in_specs=[SMEM] +...]
  transfers between devices with their start and end apart: 17 -> 17, of which waited for: 5 -> 5; matrix products, arithmetic and copies ran while one was open for 0% -> 0% of each run, Pallas kernels for 38% -> 39%
where the time goes in v2:
time: 156 us; the launch traced here: 154 us
  Pallas kernels  92.8 us (59%)
  starting transfers between devices  46.2 us (30%)
  waiting for transfers between devices  11.3 us (7%)
  between operations  2.73 us (2%)
    all_to_all x8, starting transfers between devices, exchange(): return lax.all_to_all(value, axis, 0, 0)  28.9 us
    pallas_call x5, Pallas kernels, student_piece(): pl.pallas_call(functools.partial(student_kernel, log_protos, first, count...  21.6 us
    pallas_call x1, Pallas kernels, local(): pl.pallas_call(functools.partial(last_kernel, groups), in_specs=[SMEM] +...  20.9 us
    pallas_call x1, Pallas kernels, local(): pl.pallas_call(stats_kernel, in_specs=[ANY] * 3, out_specs=[ANY, ANY, VME...  15.5 us
    ppermute x6, starting transfers between devices, following(): lax.ppermute(value, axis, [(i, (i - s) % n) for i in range(n)])  12.9 us
    all_to_all x8, waiting for transfers between devices, exchange(): return lax.all_to_all(value, axis, 0, 0)  11.3 us
    pallas_call x1, Pallas kernels, local(): pl.pallas_call(functools.partial(grad_kernel, counts, float(protos)), in_...  8.25 us
    pallas_call x2, Pallas kernels, local(): pl.pallas_call(row_kernel, in_specs=[VMEM, VMEM, ANY, ANY] + [ANY] * len(...  6.12 us
  transfers between devices with their start and end apart: 17, of which 5 were waited for; matrix products, arithmetic and copies ran while one was open for 0% of the time, Pallas kernels for 39%

profile of v2, /device:TPU:0, one launch (start us, length us, event | category | flops | bytes accessed | tf_op | source)
XLA Modules:
  0.0 154.5 jit_solution(10029505333591539799)
XLA Ops:
  0.6 3.1 %collective-permute-start.2 = (bf16[256,512]{1,0:T(8,128)(2,1)}, bf16[256,512]{1,0:T(8,128)(2,1)S(1)}, u32[]{:S(2)}, u32[]{:S(2)}) collective-permute-start(bf16[256,512]{1,0:T(8,128)(2,1)} %s_hbm.3), channel_id=1, source_target_pairs={{0,1},{1,2},{2,3},{3,0},{4,5},{5,6},{6,7},{7,4},{8,9},{9,10},{10,1... | collective-permute-start | bytes 786440 | tf_op jit(solution)/shard_map/ppermute | solution.py:556
  7.6 15.5 %own_rows.1 = (bf16[8,256,1024]{2,1,0:T(8,128)(2,1)}, bf16[8,256,1024]{2,1,0:T(8,128)(2,1)}, f32[8,8,128]{2,1,0:T(8,128)}) custom-call(bf16[256,512]{1,0:T(8,128)(2,1)} %t_hbm.3, bf16[256,512]{1,0:T(8,128)(2,1)} %s_hbm.3, bf16[512,8192]{1,0:T(8,128)(2,1)} %w_hbm.15), custom_call_target="tpu_custom_call" | custom-call | flops 4294967296 | bytes 8388608 | tf_op jit(solution)/shard_map/own_rows/pallas_call | solution.py:601
  23.2 3.7 %all-to-all-start = ((f32[8,8,128]{2,1,0:T(8,128)}), f32[8,8,128]{2,1,0:T(8,128)S(1)}, u32[]{:S(2)}, u32[]{:S(2)}) async-start(f32[8,8,128]{2,1,0:T(8,128)} %get-tuple-element.29.before_ref), calls=%async_computation | async-start | bytes 65536 | tf_op jit(solution)/shard_map/all_to_all | solution.py:551
  26.9 5.5 %own_back.1.refs_0_.student_hbm = f32[256,512]{1,0:T(8,128)S(1)} custom-call(f32[8,8,128]{2,1,0:T(8,128)} %get-tuple-element.29.before_ref, bf16[8,256,1024]{2,1,0:T(8,128)(2,1)} %get-tuple-element.30.exp_hbm, bf16[512,8192]{1,0:T(8,128)(2,1)} %w_hbm.15), custom_call_target="tpu_custom_call" | custom-call | flops 2147483648 | bytes 8388608 | tf_op jit(solution)/shard_map/own_back/pallas_call | solution.py:627
  32.5 3.6 %first_columns.1 = (f32[8,128]{1,0:T(8,128)S(1)}, f32[4,72,128]{2,1,0:T(8,128)}) custom-call(s32[2]{0:T(128)S(1)} %pad_add_fusion.place_ref, f32[8,8,128]{2,1,0:T(8,128)S(1)} %all-to-all-done.stats_ref, bf16[8,256,1024]{2,1,0:T(8,128)(2,1)} %get-tuple-element.28.exp_hbm, f32[256,512]{1,0:T(8,128)S(1)} %own_back.1.refs_0_.student_hbm, ...), custom_call_target="tpu_custom_call" | custom-call | flops 4194304 | bytes 4194304 | tf_op jit(solution)/shard_map/first_columns/pallas_call | solution.py:641
  36.1 3.3 %all-to-all-start.1 = ((f32[4,72,128]{2,1,0:T(8,128)}), f32[4,72,128]{2,1,0:T(8,128)S(1)}, u32[]{:S(2)}, u32[]{:S(2)}) async-start(f32[4,72,128]{2,1,0:T(8,128)} %get-tuple-element.31.refs_3_), calls=%async_computation.1 | async-start | bytes 294912 | tf_op jit(solution)/shard_map/all_to_all | solution.py:551
  39.4 3.1 %student_rows.1 = (bf16[768,512]{1,0:T(8,128)(2,1)S(1)}, bf16[128,1024]{1,0:T(8,128)(2,1)S(1)}, bf16[128,256]{1,0:T(8,128)(2,1)S(1)}, bf16[256,512]{1,0:T(8,128)(2,1)}) custom-call(s32[2]{0:T(128)S(1)} %pad_add_fusion.place_ref, f32[8,128]{1,0:T(8,128)S(1)} %get-tuple-element.32.factor_ref, bf16[256,512]{1,0:T(8,128)(2,1)} %t_hbm.3, bf16[256,512]{1,0:T(8,128)(2,1)} %s_hbm.3, ...), custom_call_target="tpu_custom_call" | custom-call | flops 4194304 | bytes 1048576 | tf_op jit(solution)/shard_map/student_rows/pallas_call | solution.py:652
  48.4 3.1 %rows.2.refs_0_ = f32[8,8,128]{2,1,0:T(8,128)} custom-call(f32[4,72,128]{2,1,0:T(8,128)S(1)} %all-to-all-done.1.cols_ref.logs_ref, f32[8,128]{1,0:T(8,128)S(1)} %get-tuple-element.32.factor_ref, bf16[8,256,1024]{2,1,0:T(8,128)(2,1)} %get-tuple-element.28.exp_hbm, bf16[768,512]{1,0:T(8,128)(2,1)S(1)} %get-tuple-element.33.refs_0_.unit), custom_call_target="tpu_custom_call" | custom-call | flops 4194304 | bytes 4194304 | tf_op jit(solution)/shard_map/rows/pallas_call | solution.py:706
  51.5 4.2 %all-to-all-start.2 = ((f32[8,8,128]{2,1,0:T(8,128)}), f32[8,8,128]{2,1,0:T(8,128)S(1)}, u32[]{:S(2)}, u32[]{:S(2)}) async-start(f32[8,8,128]{2,1,0:T(8,128)} %rows.2.refs_0_), calls=%async_computation.2 | async-start | bytes 65536 | tf_op jit(solution)/shard_map/all_to_all | solution.py:551
  55.7 3.3 %student_side.5 = (bf16[128,1024]{1,0:T(8,128)(2,1)S(1)}, f32[8,128]{1,0:T(8,128)S(1)}) custom-call(s32[2]{0:T(128)S(1)} %pad_add_fusion.place_ref, f32[4,72,128]{2,1,0:T(8,128)S(1)} %all-to-all-done.1.cols_ref.logs_ref, bf16[768,512]{1,0:T(8,128)(2,1)S(1)} %get-tuple-element.33.refs_0_.unit, bf16[128,1024]{1,0:T(8,128)(2,1)S(1)} %get-tuple-element.34.feat_ref, ...), custom_call_target="tpu_custom_call" | custom-call | flops 1342177280 | bytes 1048576 | tf_op jit(solution)/shard_map/student_side/pallas_call | solution.py:680
  63.5 3.3 %all-to-all-start.3 = ((f32[4,64,128]{2,1,0:T(8,128)}), f32[4,64,128]{2,1,0:T(8,128)S(1)}, u32[]{:S(2)}, u32[]{:S(2)}) async-start(f32[4,64,128]{2,1,0:T(8,128)} %columns.2.refs_0_), calls=%async_computation.3 | async-start | bytes 262144 | tf_op jit(solution)/shard_map/all_to_all | solution.py:551
  66.9 3.3 %student_side.6 = (bf16[128,1024]{1,0:T(8,128)(2,1)S(1)}, f32[8,128]{1,0:T(8,128)S(1)}) custom-call(s32[2]{0:T(128)S(1)} %pad_add_fusion.place_ref, f32[4,72,128]{2,1,0:T(8,128)S(1)} %all-to-all-done.1.cols_ref.logs_ref, bf16[768,512]{1,0:T(8,128)(2,1)S(1)} %get-tuple-element.33.refs_0_.unit, bf16[128,1024]{1,0:T(8,128)(2,1)S(1)} %get-tuple-element.34.feat_ref, ...), custom_call_target="tpu_custom_call" | custom-call | flops 1342177280 | bytes 1048576 | tf_op jit(solution)/shard_map/student_side/pallas_call | solution.py:680
  70.2 3.0 %all-to-all-done.3.cols_ref = f32[4,64,128]{2,1,0:T(8,128)S(1)} async-done(((f32[4,64,128]{2,1,0:T(8,128)}), f32[4,64,128]{2,1,0:T(8,128)S(1)}, u32[]{:S(2)}, u32[]{:S(2)}) %all-to-all-start.3) | async-done | bytes 131104 | tf_op jit(solution)/shard_map/all_to_all | solution.py:551
  73.2 3.1 %rows.3.refs_0_ = f32[8,8,128]{2,1,0:T(8,128)} custom-call(f32[4,64,128]{2,1,0:T(8,128)S(1)} %all-to-all-done.3.cols_ref, f32[8,128]{1,0:T(8,128)S(1)} %get-tuple-element.32.factor_ref, bf16[8,256,1024]{2,1,0:T(8,128)(2,1)} %get-tuple-element.28.exp_hbm, f32[8,128]{1,0:T(8,128)S(1)} %get-tuple-element.37.refs_0_, ...), custom_call_target="tpu_custom_call" | custom-call | flops 4194304 | bytes 4194304 | tf_op jit(solution)/shard_map/rows/pallas_call | solution.py:706
  76.3 3.7 %all-to-all-start.4 = ((f32[8,8,128]{2,1,0:T(8,128)}), f32[8,8,128]{2,1,0:T(8,128)S(1)}, u32[]{:S(2)}, u32[]{:S(2)}) async-start(f32[8,8,128]{2,1,0:T(8,128)} %rows.3.refs_0_), calls=%async_computation.4 | async-start | bytes 65536 | tf_op jit(solution)/shard_map/all_to_all | solution.py:551
  80.0 3.3 %student_side.7 = (bf16[128,1024]{1,0:T(8,128)(2,1)S(1)}, f32[8,128]{1,0:T(8,128)S(1)}) custom-call(s32[2]{0:T(128)S(1)} %pad_add_fusion.place_ref, f32[4,72,128]{2,1,0:T(8,128)S(1)} %all-to-all-done.1.cols_ref.logs_ref, bf16[768,512]{1,0:T(8,128)(2,1)S(1)} %get-tuple-element.33.refs_0_.unit, bf16[128,1024]{1,0:T(8,128)(2,1)S(1)} %get-tuple-element.34.feat_ref, ...), custom_call_target="tpu_custom_call" | custom-call | flops 1342177280 | bytes 1048576 | tf_op jit(solution)/shard_map/student_side/pallas_call | solution.py:680
  84.8 3.0 %columns.3.refs_0_ = f32[4,64,128]{2,1,0:T(8,128)} custom-call(f32[8,8,128]{2,1,0:T(8,128)S(1)} %all-to-all-done.4.sums_ref, f32[8,128]{1,0:T(8,128)S(1)} %get-tuple-element.32.factor_ref, bf16[8,256,1024]{2,1,0:T(8,128)(2,1)} %get-tuple-element.28.exp_hbm, f32[8,128]{1,0:T(8,128)S(1)} %get-tuple-element.39.refs_0_), custom_call_target="tpu_custom_call" | custom-call | flops 4194304 | bytes 4194304 | tf_op jit(solution)/shard_map/columns/pallas_call | solution.py:718
  87.8 3.5 %all-to-all-start.5 = ((f32[4,64,128]{2,1,0:T(8,128)}), f32[4,64,128]{2,1,0:T(8,128)S(1)}, u32[]{:S(2)}, u32[]{:S(2)}) async-start(f32[4,64,128]{2,1,0:T(8,128)} %columns.3.refs_0_), calls=%async_computation.5 | async-start | bytes 262144 | tf_op jit(solution)/shard_map/all_to_all | solution.py:551
  91.3 3.3 %student_side.8 = (bf16[128,1024]{1,0:T(8,128)(2,1)S(1)}, f32[8,128]{1,0:T(8,128)S(1)}) custom-call(s32[2]{0:T(128)S(1)} %pad_add_fusion.place_ref, f32[4,72,128]{2,1,0:T(8,128)S(1)} %all-to-all-done.1.cols_ref.logs_ref, bf16[768,512]{1,0:T(8,128)(2,1)S(1)} %get-tuple-element.33.refs_0_.unit, bf16[128,1024]{1,0:T(8,128)(2,1)S(1)} %get-tuple-element.34.feat_ref, ...), custom_call_target="tpu_custom_call" | custom-call | flops 1342177280 | bytes 1048576 | tf_op jit(solution)/shard_map/student_side/pallas_call | solution.py:680
  97.2 20.9 %last_rows.1 = (bf16[8,768,1024]{2,1,0:T(8,128)(2,1)}, f32[64,128]{1,0:T(8,128)S(1)}, bf16[8,80,512]{2,1,0:T(8,128)(2,1)}) custom-call(s32[2]{0:T(128)S(1)} %pad_add_fusion.place_ref, f32[4,72,128]{2,1,0:T(8,128)S(1)} %all-to-all-done.1.cols_ref.logs_ref, f32[4,64,128]{2,1,0:T(8,128)S(1)} %all-to-all-done.5.cols_ref, ...), custom_call_target="tpu_custom_call" | custom-call | flops 8589934592 | bytes 12582912 | tf_op jit(solution)/shard_map/last_rows/pallas_call | solution.py:733
  118.1 3.6 %all-to-all-start.6 = ((bf16[8,80,512]{2,1,0:T(8,128)(2,1)}), bf16[8,80,512]{2,1,0:T(8,128)(2,1)S(1)}, u32[]{:S(2)}, u32[]{:S(2)}) async-start(bf16[8,80,512]{2,1,0:T(8,128)(2,1)} %get-tuple-element.43.refs_0_), calls=%async_computation.6 | async-start | bytes 1310720 | tf_op jit(solution)/shard_map/all_to_all | solution.py:551
  121.7 8.5 %student_side.9 = (bf16[128,4096]{1,0:T(8,128)(2,1)}, f32[8,128]{1,0:T(8,128)S(1)}) custom-call(s32[2]{0:T(128)S(1)} %pad_add_fusion.place_ref, f32[4,72,128]{2,1,0:T(8,128)S(1)} %all-to-all-done.1.cols_ref.logs_ref, bf16[768,512]{1,0:T(8,128)(2,1)S(1)} %get-tuple-element.33.refs_0_.unit, bf16[128,1024]{1,0:T(8,128)(2,1)S(1)} %get-tuple-element.34.feat_ref, ...), custom_call_target="tpu_custom_call" | custom-call | flops 5368709120 | bytes 4194304 | tf_op jit(solution)/shard_map/student_side/pallas_call | solution.py:680
  135.1 3.5 %all-to-all-start.7 = ((f32[8,32,512]{2,1,0:T(8,128)}), f32[8,32,512]{2,1,0:T(8,128)S(1)}, u32[]{:S(2)}, u32[]{:S(2)}) async-start(f32[8,32,512]{2,1,0:T(8,128)} %get-tuple-element.51), calls=%async_computation.7 | async-start | bytes 1048576 | tf_op jit(solution)/shard_map/all_to_all | solution.py:551
  143.1 8.2 %weight_grads.1 = bf16[128,8192]{1,0:T(8,128)(2,1)} custom-call(bf16[8,256,1024]{2,1,0:T(8,128)(2,1)} %get-tuple-element.28.exp_hbm, bf16[8,768,1024]{2,1,0:T(8,128)(2,1)} %get-tuple-element.41.prob_hbm, bf16[128,1024]{1,0:T(8,128)(2,1)S(1)} %get-tuple-element.34.feat_ref, f32[64,128]{1,0:T(8,128)S(1)} %get-tuple-element.42.scale_ref, ...), custom_call_target="tpu_custom_call" | custom-call | flops 2147483648 | bytes 12582912 | tf_op jit(solution)/shard_map/weight_grads/pallas_call | solution.py:780
  (38 shorter events, 29.3 us)
Async XLA Ops:
  0.6 31.9 %collective-permute-start.2 = (bf16[256,512]{1,0:T(8,128)(2,1)}, bf16[256,512]{1,0:T(8,128)(2,1)S(1)}, u32[]{:S(2)}, u32[]{:S(2)}) collective-permute-start(bf16[256,512]{1,0:T(8,128)(2,1)} %s_hbm.3), channel_id=1, source_target_pairs={{0,1},{1,2},{2,3},{3,0},{4,5},{5,6},{6,7},{7,4},{8,9},{9,10},{10,1... | collective-permute-start | bytes 786440 | tf_op jit(solution)/shard_map/ppermute | solution.py:556
  3.7 28.8 %collective-permute-start.1 = (bf16[256,512]{1,0:T(8,128)(2,1)}, bf16[256,512]{1,0:T(8,128)(2,1)S(1)}, u32[]{:S(2)}, u32[]{:S(2)}) collective-permute-start(bf16[256,512]{1,0:T(8,128)(2,1)} %s_hbm.3), channel_id=1, source_target_pairs={{0,2},{1,3},{2,0},{3,1},{4,6},{5,7},{6,4},{7,5},{8,10},{9,11},{10,... | collective-permute-start | bytes 786440 | tf_op jit(solution)/shard_map/ppermute | solution.py:556
  6.3 26.2 %collective-permute-start = (bf16[256,512]{1,0:T(8,128)(2,1)}, bf16[256,512]{1,0:T(8,128)(2,1)S(1)}, u32[]{:S(2)}, u32[]{:S(2)}) collective-permute-start(bf16[256,512]{1,0:T(8,128)(2,1)} %s_hbm.3), channel_id=1, source_target_pairs={{0,3},{1,0},{2,1},{3,2},{4,7},{5,4},{6,5},{7,6},{8,11},{9,8},{10,9... | collective-permute-start | bytes 786440 | tf_op jit(solution)/shard_map/ppermute | solution.py:556
  23.2 9.3 %all-to-all-start = ((f32[8,8,128]{2,1,0:T(8,128)}), f32[8,8,128]{2,1,0:T(8,128)S(1)}, u32[]{:S(2)}, u32[]{:S(2)}) async-start(f32[8,8,128]{2,1,0:T(8,128)} %get-tuple-element.29.before_ref), calls=%async_computation | async-start | bytes 65536 | tf_op jit(solution)/shard_map/all_to_all | solution.py:551
  32.4 19.1 %copy-start = (f32[256,512]{1,0:T(8,128)}, f32[256,512]{1,0:T(8,128)S(1)}, u32[]{:S(2)}) copy-start(f32[256,512]{1,0:T(8,128)S(1)} %own_back.1.refs_0_.student_hbm) | copy-start | bytes 1572868
  36.1 12.4 %all-to-all-start.1 = ((f32[4,72,128]{2,1,0:T(8,128)}), f32[4,72,128]{2,1,0:T(8,128)S(1)}, u32[]{:S(2)}, u32[]{:S(2)}) async-start(f32[4,72,128]{2,1,0:T(8,128)} %get-tuple-element.31.refs_3_), calls=%async_computation.1 | async-start | bytes 294912 | tf_op jit(solution)/shard_map/all_to_all | solution.py:551
  42.6 27.6 %collective-permute-start.5 = (bf16[256,512]{1,0:T(8,128)(2,1)}, bf16[256,512]{1,0:T(8,128)(2,1)S(1)}, u32[]{:S(2)}, u32[]{:S(2)}) collective-permute-start(bf16[256,512]{1,0:T(8,128)(2,1)} %get-tuple-element.38), channel_id=1, source_target_pairs={{0,1},{1,2},{2,3},{3,0},{4,5},{5,6},{6,7},{7,4},{8,9},{9,10},{10,1... | collective-permute-start | bytes 786440 | tf_op jit(solution)/shard_map/ppermute | solution.py:556
  44.6 25.6 %collective-permute-start.4 = (bf16[256,512]{1,0:T(8,128)(2,1)}, bf16[256,512]{1,0:T(8,128)(2,1)S(1)}, u32[]{:S(2)}, u32[]{:S(2)}) collective-permute-start(bf16[256,512]{1,0:T(8,128)(2,1)} %get-tuple-element.38), channel_id=1, source_target_pairs={{0,2},{1,3},{2,0},{3,1},{4,6},{5,7},{6,4},{7,5},{8,10},{9,11},{10,... | collective-permute-start | bytes 786440 | tf_op jit(solution)/shard_map/ppermute | solution.py:556
  47.0 23.2 %collective-permute-start.3 = (bf16[256,512]{1,0:T(8,128)(2,1)}, bf16[256,512]{1,0:T(8,128)(2,1)S(1)}, u32[]{:S(2)}, u32[]{:S(2)}) collective-permute-start(bf16[256,512]{1,0:T(8,128)(2,1)} %get-tuple-element.38), channel_id=1, source_target_pairs={{0,3},{1,0},{2,1},{3,2},{4,7},{5,4},{6,5},{7,6},{8,11},{9,8},{10,9... | collective-permute-start | bytes 786440 | tf_op jit(solution)/shard_map/ppermute | solution.py:556
  51.5 9.1 %all-to-all-start.2 = ((f32[8,8,128]{2,1,0:T(8,128)}), f32[8,8,128]{2,1,0:T(8,128)S(1)}, u32[]{:S(2)}, u32[]{:S(2)}) async-start(f32[8,8,128]{2,1,0:T(8,128)} %rows.2.refs_0_), calls=%async_computation.2 | async-start | bytes 65536 | tf_op jit(solution)/shard_map/all_to_all | solution.py:551
  63.5 9.7 %all-to-all-start.3 = ((f32[4,64,128]{2,1,0:T(8,128)}), f32[4,64,128]{2,1,0:T(8,128)S(1)}, u32[]{:S(2)}, u32[]{:S(2)}) async-start(f32[4,64,128]{2,1,0:T(8,128)} %columns.2.refs_0_), calls=%async_computation.3 | async-start | bytes 262144 | tf_op jit(solution)/shard_map/all_to_all | solution.py:551
  70.2 13.1 %copy-start.1 = (bf16[256,512]{1,0:T(8,128)(2,1)}, bf16[256,512]{1,0:T(8,128)(2,1)S(1)}, u32[]{:S(2)}) copy-start(bf16[256,512]{1,0:T(8,128)(2,1)S(1)} %collective-permute-done.5.refs_3_.refs_2_) | copy-start | bytes 786436
  70.2 13.1 %copy-start.2 = (bf16[256,512]{1,0:T(8,128)(2,1)}, bf16[256,512]{1,0:T(8,128)(2,1)S(1)}, u32[]{:S(2)}) copy-start(bf16[256,512]{1,0:T(8,128)(2,1)S(1)} %collective-permute-done.4.refs_2_.refs_1_) | copy-start | bytes 786436
  70.2 6.1 %copy-start.3 = (bf16[256,512]{1,0:T(8,128)(2,1)}, bf16[256,512]{1,0:T(8,128)(2,1)S(1)}, u32[]{:S(2)}) copy-start(bf16[256,512]{1,0:T(8,128)(2,1)S(1)} %collective-permute-done.3.refs_1_.refs_0_) | copy-start | bytes 786436
  76.3 8.5 %all-to-all-start.4 = ((f32[8,8,128]{2,1,0:T(8,128)}), f32[8,8,128]{2,1,0:T(8,128)S(1)}, u32[]{:S(2)}, u32[]{:S(2)}) async-start(f32[8,8,128]{2,1,0:T(8,128)} %rows.3.refs_0_), calls=%async_computation.4 | async-start | bytes 65536 | tf_op jit(solution)/shard_map/all_to_all | solution.py:551
  87.8 9.4 %all-to-all-start.5 = ((f32[4,64,128]{2,1,0:T(8,128)}), f32[4,64,128]{2,1,0:T(8,128)S(1)}, u32[]{:S(2)}, u32[]{:S(2)}) async-start(f32[4,64,128]{2,1,0:T(8,128)} %columns.3.refs_0_), calls=%async_computation.5 | async-start | bytes 262144 | tf_op jit(solution)/shard_map/all_to_all | solution.py:551
  118.1 14.6 %all-to-all-start.6 = ((bf16[8,80,512]{2,1,0:T(8,128)(2,1)}), bf16[8,80,512]{2,1,0:T(8,128)(2,1)S(1)}, u32[]{:S(2)}, u32[]{:S(2)}) async-start(bf16[8,80,512]{2,1,0:T(8,128)(2,1)} %get-tuple-element.43.refs_0_), calls=%async_computation.6 | async-start | bytes 1310720 | tf_op jit(solution)/shard_map/all_to_all | solution.py:551
  135.1 17.4 %all-to-all-start.7 = ((f32[8,32,512]{2,1,0:T(8,128)}), f32[8,32,512]{2,1,0:T(8,128)S(1)}, u32[]{:S(2)}, u32[]{:S(2)}) async-start(f32[8,32,512]{2,1,0:T(8,128)} %get-tuple-element.51), calls=%async_computation.7 | async-start | bytes 1048576 | tf_op jit(solution)/shard_map/all_to_all | solution.py:551
  138.6 12.7 %collective-permute-start.8 = (f32[8,128]{1,0:T(8,128)S(1)}, f32[8,128]{1,0:T(8,128)S(1)}, u32[]{:S(2)}, u32[]{:S(2)}) collective-permute-start(f32[8,128]{1,0:T(8,128)S(1)} %get-tuple-element.52), channel_id=1, source_target_pairs={{0,3},{1,2},{2,1},{3,0},{4,7},{5,6},{6,5},{7,4},{8,11},{9,10},{10,... | collective-permute-start | bytes 12296 | tf_op jit(solution)/shard_map/ppermute | solution.py:562
  140.3 11.1 %collective-permute-start.7 = (f32[8,128]{1,0:T(8,128)S(1)}, f32[8,128]{1,0:T(8,128)S(1)}, u32[]{:S(2)}, u32[]{:S(2)}) collective-permute-start(f32[8,128]{1,0:T(8,128)S(1)} %get-tuple-element.52), channel_id=1, source_target_pairs={{0,2},{1,3},{2,0},{3,1},{4,6},{5,7},{6,4},{7,5},{8,10},{9,11},{10,... | collective-permute-start | bytes 12296 | tf_op jit(solution)/shard_map/ppermute | solution.py:562
  141.2 10.1 %collective-permute-start.6 = (f32[8,128]{1,0:T(8,128)S(1)}, f32[8,128]{1,0:T(8,128)S(1)}, u32[]{:S(2)}, u32[]{:S(2)}) collective-permute-start(f32[8,128]{1,0:T(8,128)S(1)} %get-tuple-element.52), channel_id=1, source_target_pairs={{0,1},{1,0},{2,3},{3,2},{4,5},{5,4},{6,7},{7,6},{8,9},{9,8},{10,11... | collective-permute-start | bytes 12296 | tf_op jit(solution)/shard_map/ppermute | solution.py:562

commit v3 on v1

--- a/solution.py
+++ b/solution.py
@@ -107,6 +107,10 @@
     for each in zip(*lists):
         for copy in each:
             copy.start()
+
+
+def whole_copies(pairs, sems):
+    return [pltpu.make_async_copy(a, b, sems.at[i]) for i, (a, b) in enumerate(pairs)]
 
 
 def wait(*lists):
@@ -234,8 +238,8 @@
     column_pass(exp_hbm, exp_ref, sem, weight, out_ref)
 
 
-def column_scales(cols_ref, height):
-    return 1.0 / add_up([cols_ref[g, :height, :] for g in range(cols_ref.shape[0])])
+def column_scales(cols, height):
+    return 1.0 / add_up([ref[g, :height, :] for ref in cols for g in range(ref.shape[0])])
 
 
 def chunk_scales(scales, k):
@@ -251,10 +255,11 @@
         rows[g : g + 32, :] = total
 
 
-def row_kernel(cols_ref, factor_ref, exp_hbm, *refs):
+def row_kernel(count, *refs):
+    cols, (factor_ref, exp_hbm) = refs[:count], refs[count : count + 2]
     out_ref, scales, rows, exp_ref, sem = refs[-5:]
     start(copies(exp_hbm, exp_ref, sem))
-    scales[...] = column_scales(cols_ref, scales.shape[0])
+    scales[...] = column_scales(cols, scales.shape[0])
     rows[...] = jnp.zeros(rows.shape, F32)
     quarter = rows.shape[0] // LANES
     out_ref[0] = jnp.zeros(out_ref.shape[1:], F32)
@@ -280,19 +285,12 @@
         back_ref[...] += nt_dot(exp_ref[k], w_ref[:, columns_of(k)])
 
 
-def relative(place_ref, g, groups):
-    return pl.ds(lax.rem(place_ref[0] + g, groups), 1)
-
-
-def relative_logs(place_ref, logs_ref, lse, which, shift=0.0):
-    groups = logs_ref.shape[0]
-    own = lse.shape[0] // (groups - 1)
+def relative_logs(logs, lse, which, shift=0.0):
+    own = lse.shape[0] // (len(logs) - 1)
     quarter = own // LANES
-    height = logs_ref.shape[1] - 8
-    for g in range(1, groups):
-        there = logs_ref[relative(place_ref, g, groups)][0]
-        first = height + which * quarter
-        spread_rows(lse.at[(g - 1) * own : g * own], there[first : first + quarter, :] - shift)
+    for g, ref in enumerate(logs[1:]):
+        first = ref.shape[1] - 8 + which * quarter
+        spread_rows(lse.at[g * own : (g + 1) * own], ref[0, first : first + quarter, :] - shift)
 
 
 def student_rows_kernel(protos, place_ref, factor_ref, t_ref, own_ref, *refs):
@@ -328,15 +326,16 @@
 
 
 def student_kernel(
-    log_protos, first, place_ref, logs_ref, unit, feat_ref, scaled_ref, exp_hbm, w_hbm, *refs
+    log_protos, first, groups, unit, feat_ref, scaled_ref, exp_hbm, w_hbm, *refs
 ):
+    logs = refs[:groups]
     grad, token_ref, lse, prob, exp_ref, w_ref, exp_sem, w_sem = refs[-8:]
     own, count = exp_ref.shape[1], exp_ref.shape[0]
     exp_loads = copies(exp_hbm, exp_ref, exp_sem, first, 0, count)
     w_loads = copies(w_hbm, w_ref, w_sem, first, 0, count)
     start(w_loads, exp_loads)
     token_ref[...] = jnp.zeros(token_ref.shape, F32)
-    relative_logs(place_ref, logs_ref, lse, 1, log_protos)
+    relative_logs(logs, lse, 1, log_protos)
 
     @pl.loop(0, count)
     def _(k):
@@ -360,23 +359,26 @@
     return high, middle, (rest - middle.astype(F32)).astype(BF16)
 
 
-def last_kernel(groups, place_ref, logs_ref, cols_ref, factor_ref, own_ref, student_ref, exp_hbm, w_hbm, *refs):
-    units = refs[: groups - 1]
+def last_kernel(groups, factor_ref, own_hbm, student_hbm, exp_hbm, w_hbm, *refs):
+    units, refs = refs[: groups - 1], refs[groups - 1 :]
+    logs, cols, refs = refs[:groups], refs[groups : 2 * groups], refs[2 * groups :]
     (
         prob_hbm, scale_ref, out_ref, unit, lse, rows, own_rows, back, scaled, sums, prob_ref,
-        exp_ref, w_ref, prob_sem, exp_sem, w_sem,
-    ) = refs[-16:]
+        exp_ref, w_ref, own_ref, student_ref, prob_sem, exp_sem, w_sem, sem,
+    ) = refs[-19:]
     w_loads, exp_loads = copies(w_hbm, w_ref, w_sem), copies(exp_hbm, exp_ref, exp_sem)
+    late_loads = whole_copies([(own_hbm, own_ref), (student_hbm, student_ref)], sem)
     start(w_loads, exp_loads)
+    start(late_loads)
     slots, others, _ = prob_ref.shape
     own, chunks = exp_ref.shape[1], exp_ref.shape[0]
     tiles = (own + others) // LANES
     quarter = own // LANES
-    scale_ref[...] = column_scales(cols_ref, scale_ref.shape[0])
+    scale_ref[...] = column_scales(cols, scale_ref.shape[0])
     rows[...] = jnp.zeros(rows.shape, F32)
     own_rows[...] = jnp.zeros(own_rows.shape, F32)
     back[...] = jnp.zeros(back.shape, F32)
-    relative_logs(place_ref, logs_ref, lse, 0)
+    relative_logs(logs, lse, 0)
     for g in range(groups - 1):
         unit[g * own : (g + 1) * own, :] = units[g][...]
     partner = slice((groups // 2 - 1) * own, groups // 2 * own)
@@ -413,6 +415,7 @@
     pack_rows(sums.at[:quarter], jnp.sum(own_rows[...], axis=1, keepdims=True))
     sums[:quarter, :] = sums[:quarter, :] * factor_ref[:quarter, :]
     pack_rows(sums.at[quarter:tiles], jnp.sum(rows[...], axis=1, keepdims=True))
+    wait(late_loads)
     half = unit_rows(own_ref[...])[0].astype(BF16).astype(F32)
     inner = jnp.sum(half * back[...], axis=1, keepdims=True)
     pack_rows(sums.at[tiles : tiles + quarter], inner)
@@ -445,25 +448,28 @@
     return add_up(each)
 
 
-def rows_kernel(tiles, protos, place_ref, s_ref, message_ref, logs_ref, *refs):
-    out_ref, loss_ref, sums_ref, weight = refs[-4:]
+def rows_kernel(tiles, protos, place_ref, s_hbm, message_ref, logs_ref, *refs):
+    out_ref, loss_ref, sums_ref, weight, s_ref, sem = refs[-6:]
     parts = message_ref.shape[0]
     share, own = out_ref.shape[1], weight.shape[0]
+    mine = pl.ds(pl.multiple_of(place_ref[1] * share, share), share)
+    load = pltpu.make_async_copy(s_hbm.at[mine], s_ref, sem)
+    load.start()
     quarter = own // LANES
     first = tiles // 2
     totals = total_sums(message_ref, 2 * share)
     sums_ref[...] = totals
     scale = 1.0 / totals[first : first + quarter, :]
     spread_rows(weight, scale)
-    mine = pl.ds(pl.multiple_of(place_ref[1] * share, share), share)
     total = add_up([message_ref[p, :share, :].astype(F32) for p in range(parts)])
     paired = add_up([message_ref[p, share : 2 * share, :].astype(F32) for p in range(parts)])
     total = total - paired * (weight[mine, :1] * protos)
-    unit, length = unit_rows(s_ref[mine, :])
+    load.wait()
+    unit, length = unit_rows(s_ref[...])
     out_ref[0] = (total - unit * jnp.sum(unit * total, axis=-1, keepdims=True)) / length
     repeat(out_ref)
     height = logs_ref.shape[1] - 8
-    logs = logs_ref[pl.ds(place_ref[0], 1)][0][height + quarter : height + 2 * quarter, :]
+    logs = logs_ref[0, height + quarter : height + 2 * quarter, :]
     terms = logs / LOG2E - totals[tiles : tiles + quarter, :] * scale / TEMP_STUDENT
     loss_ref[...] = jnp.broadcast_to(jnp.sum(terms), loss_ref.shape)
 
@@ -564,6 +570,7 @@
         return pltpu.with_memory_space_constraint(value, pltpu.HBM)
 
     weight = far(proto_weight)
+    teacher_rows, student_rows = far(teacher_feats), far(student_feats)
     s_all = following(student_feats, "batch")
 
     exps = pltpu.HBM((chunks, own, WIDE), BF16)
@@ -590,7 +597,7 @@
         compiler_params=params(weight_bytes + 6 * exp_bytes),
         cost_estimate=cost(4 * own * width * local_protos, weight_bytes),
         name="own_rows",
-    )(far(teacher_feats), far(student_feats), weight)
+    )(teacher_rows, student_rows, weight)
     t_exp, s_exp = far(t_exp), far(s_exp)
 
     back_student = pl.pallas_call(
@@ -606,7 +613,7 @@
 
     stats = exchange(stats, "proto")
 
-    first_shape = (groups, height + 8, LANES)
+    first_shape = (1, height + 8, LANES)
     factor, cols = pl.pallas_call(
         first_column_kernel,
         in_specs=[SMEM, VMEM, ANY, ANY] + [ANY] * (groups - 1),
@@ -632,7 +639,7 @@
         name="student_rows",
     )(place, factor, teacher_feats, student_feats, *s_all, cols)
     t_all = following(t_unit, "batch")
-    cols = exchange(cols, "batch")
+    cols = [cols] + following(cols, "batch")
     logs = cols
 
     counts = [c * chunks // 8 for c in (1, 1, 1, 1, 4)]
@@ -642,8 +649,8 @@
         turn = len(grad_parts)
         first, count = sum(counts[:turn]), counts[turn]
         grad_part, done = pl.pallas_call(
-            functools.partial(student_kernel, log_protos, first),
-            in_specs=[SMEM] + [VMEM] * 4 + [ANY] * 3,
+            functools.partial(student_kernel, log_protos, first, groups),
+            in_specs=[VMEM] * 3 + [ANY] * 2 + [VMEM] * groups + [ANY],
             out_specs=[VMEM, VMEM],
             out_shape=[struct((feats, count * WIDE), BF16), token],
             scratch_shapes=[
@@ -656,7 +663,7 @@
             compiler_params=params(16 * 2**20),
             cost_estimate=cost(2.5 * rows * width * WIDE * count, 2 * width * WIDE * count),
             name="student_side",
-        )(place, logs, unit, feat, scaled, s_exp, weight, before)
+        )(unit, feat, scaled, s_exp, weight, *logs, before)
         grad_parts.append(grad_part)
         return done
 
@@ -664,35 +671,39 @@
     for turn in range(SWEEPS - 1):
         late = t_all if turn == 1 else []
         sums = pl.pallas_call(
-            row_kernel,
-            in_specs=[VMEM, VMEM, ANY, ANY] + [ANY] * len(late),
+            functools.partial(row_kernel, len(cols)),
+            in_specs=[VMEM] * (len(cols) + 1) + [ANY] * (2 + len(late)),
             out_specs=VMEM,
             out_shape=struct((parts, 8, LANES), F32),
             scratch_shapes=[pltpu.VMEM((height, LANES), F32), spread, exp_buffer, sems],
             compiler_params=params(exp_bytes),
             cost_estimate=cost(2 * own * local_protos, exp_bytes),
             name="rows",
-        )(cols, factor, t_exp, done, *late)
+        )(*cols, factor, t_exp, done, *late)
         done = student_piece(sums)
         sums = exchange(sums, "proto")
+        middle = turn < SWEEPS - 2
         cols = pl.pallas_call(
             column_kernel,
             in_specs=[VMEM, VMEM, ANY, ANY],
             out_specs=VMEM,
-            out_shape=struct((groups, height, LANES), F32),
+            out_shape=struct((groups if middle else 1, height, LANES), F32),
             scratch_shapes=[spread, exp_buffer, sems],
             compiler_params=params(exp_bytes),
             cost_estimate=cost(2 * own * local_protos, exp_bytes),
             name="columns",
         )(sums, factor, t_exp, done)
         done = student_piece(cols)
-        cols = exchange(cols, "batch")
+        if middle:
+            cols = [exchange(cols, "batch")]
+        else:
+            cols = [cols] + following(cols, "batch")
 
     sum_rows = -(-(tiles + own // LANES) // 16) * 16
     message_shape = (parts, 2 * share + sum_rows, width)
     prob, col_scale, message = pl.pallas_call(
         functools.partial(last_kernel, groups),
-        in_specs=[SMEM] + [VMEM] * 5 + [ANY] * 2 + [VMEM] * (groups - 1) + [ANY],
+        in_specs=[VMEM] + [ANY] * 4 + [VMEM] * (3 * groups - 1) + [ANY],
         out_specs=[ANY, VMEM, VMEM],
         out_shape=[
             pltpu.HBM((chunks, others, WIDE), BF16),
@@ -710,26 +721,29 @@
             pltpu.VMEM((min(chunks, 3), others, WIDE), BF16),
             exp_buffer,
             w_buffer,
+            pltpu.VMEM((own, width), BF16),
+            pltpu.VMEM((own, width), F32),
             sems, sems, sems,
+            pltpu.SemaphoreType.DMA((2,)),
         ],
         compiler_params=params(20 * 2**20 + weight_bytes + exp_bytes),
         cost_estimate=cost(2 * rows * width * local_protos, others_bytes),
         name="last_rows",
     )(
-        place, logs, cols, factor, student_feats, back_student, t_exp, weight, *t_all, done,
+        factor, student_rows, far(back_student), t_exp, weight, *t_all, *logs, *cols, done,
     )
     done = student_piece(message)
     message = exchange(message, "proto")
 
     grad_rows, loss_part, sums = pl.pallas_call(
         functools.partial(rows_kernel, tiles, float(protos)),
-        in_specs=[SMEM] + [VMEM] * 3 + [ANY],
+        in_specs=[SMEM, ANY, VMEM, VMEM, ANY],
         out_specs=[VMEM] * 3,
         out_shape=[struct((parts, share, width), F32), token, struct((sum_rows, LANES), F32)],
-        scratch_shapes=[spread],
+        scratch_shapes=[spread, pltpu.VMEM((share, width), BF16), pltpu.SemaphoreType.DMA],
         compiler_params=params(0),
         name="row_grads",
-    )(place, student_feats, message, logs, done)
+    )(place, student_rows, message, logs[0], done)
     grad_rows = exchange(grad_rows, "proto").reshape(own, width)
     loss = tree_sum(loss_part, "batch")[0, 0] / rows
 

time: 154 us -> 149 us (0.968)
  Pallas kernels: 86.8 us -> 84.1 us
    all_to_all x8 -> x6, starting transfers between devices: 29.1 us -> 21.7 us  [exchange(): return lax.all_to_all(value, axis, 0, 0)]
    ppermute x6 -> x12, starting transfers between devices: 12.8 us -> 19.7 us  [following(): lax.ppermute(value, axis, [(i, (i - s) % n) for i in range(n)])]
    pallas_call x8, Pallas kernels: 44.8 us -> 42.8 us  [the longest x5 18.9 us: student_piece(): pl.pallas_call(functools.partial(student_kernel, log_protos, first, group...]
    unnamed x17 -> x15, local copies, waits for them, and re-layouts: 4.91 us -> 4.1 us
    all_to_all x8 -> x6, waiting for transfers between devices: 11.1 us -> 10.3 us  [exchange(): return lax.all_to_all(value, axis, 0, 0)]
  transfers between devices with their start and end apart: 17 -> 21, of which waited for: 5 -> 4; matrix products, arithmetic and copies ran while one was open for 0% -> 0% of each run, Pallas kernels for 38% -> 38%
where the time goes in v3:
time: 149 us; the launch traced here: 148 us
  Pallas kernels  84.1 us (56%)
  starting transfers between devices  45.9 us (31%)
  waiting for transfers between devices  10.4 us (7%)
  local copies, waits for them, and re-layouts  4.62 us (3%)
  between operations  2.68 us (2%)
    all_to_all x6, starting transfers between devices, exchange(): return lax.all_to_all(value, axis, 0, 0)  21.7 us
    ppermute x12, starting transfers between devices, following(): lax.ppermute(value, axis, [(i, (i - s) % n) for i in range(n)])  19.7 us
    pallas_call x5, Pallas kernels, student_piece(): pl.pallas_call(functools.partial(student_kernel, log_protos, first, group...  18.9 us
    pallas_call x1, Pallas kernels, local(): pl.pallas_call(functools.partial(last_kernel, groups), in_specs=[VMEM] +...  17.7 us
    pallas_call x1, Pallas kernels, local(): pl.pallas_call(stats_kernel, in_specs=[ANY] * 3, out_specs=[ANY, ANY, VME...  15.5 us
    all_to_all x6, waiting for transfers between devices, exchange(): return lax.all_to_all(value, axis, 0, 0)  10.3 us
    pallas_call x1, Pallas kernels, local(): pl.pallas_call(functools.partial(grad_kernel, counts, float(protos)), in_...  7.68 us
    pallas_call x2, Pallas kernels, local(): pl.pallas_call(functools.partial(row_kernel, len(cols)), in_specs=[VMEM]...  6.11 us
  transfers between devices with their start and end apart: 21, of which 4 were waited for; matrix products, arithmetic and copies ran while one was open for 0% of the time, Pallas kernels for 38%

profile of v3, /device:TPU:0, one launch (start us, length us, event | category | flops | bytes accessed | tf_op | source)
XLA Modules:
  0.0 147.7 jit_solution(14743557644827028505)
XLA Ops:
  0.6 3.1 %collective-permute-start.2 = (bf16[256,512]{1,0:T(8,128)(2,1)}, bf16[256,512]{1,0:T(8,128)(2,1)S(1)}, u32[]{:S(2)}, u32[]{:S(2)}) collective-permute-start(bf16[256,512]{1,0:T(8,128)(2,1)} %s_hbm.3), channel_id=1, source_target_pairs={{0,1},{1,2},{2,3},{3,0},{4,5},{5,6},{6,7},{7,4},{8,9},{9,10},{10,1... | collective-permute-start | bytes 786440 | tf_op jit(solution)/shard_map/ppermute | solution.py:532
  7.6 15.5 %own_rows.1 = (bf16[8,256,1024]{2,1,0:T(8,128)(2,1)}, bf16[8,256,1024]{2,1,0:T(8,128)(2,1)}, f32[8,8,128]{2,1,0:T(8,128)}) custom-call(bf16[256,512]{1,0:T(8,128)(2,1)} %t_ref.1, bf16[256,512]{1,0:T(8,128)(2,1)} %s_hbm.3, bf16[512,8192]{1,0:T(8,128)(2,1)} %w_hbm.15), custom_call_target="tpu_custom_call" | custom-call | flops 4294967296 | bytes 8388608 | tf_op jit(solution)/shard_map/own_rows/pallas_call | solution.py:577
  23.2 3.7 %all-to-all-start = ((f32[8,8,128]{2,1,0:T(8,128)}), f32[8,8,128]{2,1,0:T(8,128)S(1)}, u32[]{:S(2)}, u32[]{:S(2)}) async-start(f32[8,8,128]{2,1,0:T(8,128)} %get-tuple-element.29.before_ref), calls=%async_computation | async-start | bytes 65536 | tf_op jit(solution)/shard_map/all_to_all | solution.py:527
  26.9 5.5 %own_back.1.refs_0_.student_hbm = f32[256,512]{1,0:T(8,128)S(1)} custom-call(f32[8,8,128]{2,1,0:T(8,128)} %get-tuple-element.29.before_ref, bf16[8,256,1024]{2,1,0:T(8,128)(2,1)} %get-tuple-element.30.exp_hbm, bf16[512,8192]{1,0:T(8,128)(2,1)} %w_hbm.15), custom_call_target="tpu_custom_call" | custom-call | flops 2147483648 | bytes 8388608 | tf_op jit(solution)/shard_map/own_back/pallas_call | solution.py:603
  32.5 2.9 %first_columns.1 = (f32[8,128]{1,0:T(8,128)S(1)}, f32[1,72,128]{2,1,0:T(8,128)S(1)}) custom-call(s32[2]{0:T(128)S(1)} %pad_add_fusion.place_ref, f32[8,8,128]{2,1,0:T(8,128)S(1)} %all-to-all-done.stats_ref, bf16[8,256,1024]{2,1,0:T(8,128)(2,1)} %get-tuple-element.28.exp_hbm.refs_5_.refs_2_, f32[256,512]{1,0:T(8,128)S(1)} %own_back.1.refs_0_.student_hbm, ...), custom_call_target="tpu_custom_call" | custom-call | flops 4194304 | bytes 4194304 | tf_op jit(solution)/shard_map/first_columns/pallas_call | solution.py:617
  36.5 2.8 %collective-permute-start.6 = (f32[1,72,128]{2,1,0:T(8,128)S(1)}, f32[1,72,128]{2,1,0:T(8,128)S(1)}, u32[]{:S(2)}, u32[]{:S(2)}) collective-permute-start(f32[1,72,128]{2,1,0:T(8,128)S(1)} %get-tuple-element.32.refs_3_.refs_0_.logs_ref), channel_id=1, source_target_pairs={{0,3},{1,0},{2,1},{3,2},{4,7},{5,4},{6,5},{7,6},{8,11},{9,8},{10,9... | collective-permute-start | bytes 110600 | tf_op jit(solution)/shard_map/ppermute | solution.py:532
  43.5 2.9 %collective-permute-start.3 = (bf16[256,512]{1,0:T(8,128)(2,1)}, bf16[256,512]{1,0:T(8,128)(2,1)S(1)}, u32[]{:S(2)}, u32[]{:S(2)}) collective-permute-start(bf16[256,512]{1,0:T(8,128)(2,1)} %get-tuple-element.33), channel_id=1, source_target_pairs={{0,3},{1,0},{2,1},{3,2},{4,7},{5,4},{6,5},{7,6},{8,11},{9,8},{10,9... | collective-permute-start | bytes 786440 | tf_op jit(solution)/shard_map/ppermute | solution.py:532
  46.4 3.0 %rows.2.refs_4_ = f32[8,8,128]{2,1,0:T(8,128)} custom-call(f32[1,72,128]{2,1,0:T(8,128)S(1)} %get-tuple-element.32.refs_3_.refs_0_.logs_ref, f32[1,72,128]{2,1,0:T(8,128)S(1)} %collective-permute-done.6.refs_1_.refs_4_, f32[1,72,128]{2,1,0:T(8,128)S(1)} %collective-permute-done.7.refs_2_.refs_5_, f32[1,72,128]{2,1,0:T(8,128)S(1)} %collective-permute-done.8.refs_3_.refs_6_, ...), custom_call_target="tpu_custom_call" | custom-call | flops 4194304 | bytes 4194304 | tf_op jit(solution)/shard_map/rows/pallas_call | solution.py:673
  49.5 4.2 %all-to-all-start.1 = ((f32[8,8,128]{2,1,0:T(8,128)}), f32[8,8,128]{2,1,0:T(8,128)S(1)}, u32[]{:S(2)}, u32[]{:S(2)}) async-start(f32[8,8,128]{2,1,0:T(8,128)} %rows.2.refs_4_), calls=%async_computation.1 | async-start | bytes 65536 | tf_op jit(solution)/shard_map/all_to_all | solution.py:527
  53.7 2.9 %student_side.5 = (bf16[128,1024]{1,0:T(8,128)(2,1)S(1)}, f32[8,128]{1,0:T(8,128)S(1)}) custom-call(bf16[768,512]{1,0:T(8,128)(2,1)S(1)} %get-tuple-element.34.refs_6_.unit, bf16[128,1024]{1,0:T(8,128)(2,1)S(1)} %get-tuple-element.35.feat_ref, bf16[128,256]{1,0:T(8,128)(2,1)S(1)} %get-tuple-element.36.scaled_ref, ...), custom_call_target="tpu_custom_call" | custom-call | flops 1342177280 | bytes 1048576 | tf_op jit(solution)/shard_map/student_side/pallas_call | solution.py:651
  58.5 3.0 %columns.2.refs_4_ = f32[4,64,128]{2,1,0:T(8,128)} custom-call(f32[8,8,128]{2,1,0:T(8,128)S(1)} %all-to-all-done.1.sums_ref, f32[8,128]{1,0:T(8,128)S(1)} %get-tuple-element.31.factor_ref.refs_4_.refs_1_, bf16[8,256,1024]{2,1,0:T(8,128)(2,1)} %get-tuple-element.28.exp_hbm.refs_5_.refs_2_, f32[8,128]{1,0:T(8,128)S(1)} %get-tuple-element.37.refs_0_), custom_call_target="tpu_custom_call" | custom-call | flops 4194304 | bytes 4194304 | tf_op jit(solution)/shard_map/columns/pallas_call | solution.py:686
  61.5 3.3 %all-to-all-start.2 = ((f32[4,64,128]{2,1,0:T(8,128)}), f32[4,64,128]{2,1,0:T(8,128)S(1)}, u32[]{:S(2)}, u32[]{:S(2)}) async-start(f32[4,64,128]{2,1,0:T(8,128)} %columns.2.refs_4_), calls=%async_computation.2 | async-start | bytes 262144 | tf_op jit(solution)/shard_map/all_to_all | solution.py:527
  64.8 2.9 %student_side.6 = (bf16[128,1024]{1,0:T(8,128)(2,1)S(1)}, f32[8,128]{1,0:T(8,128)S(1)}) custom-call(bf16[768,512]{1,0:T(8,128)(2,1)S(1)} %get-tuple-element.34.refs_6_.unit, bf16[128,1024]{1,0:T(8,128)(2,1)S(1)} %get-tuple-element.35.feat_ref, bf16[128,256]{1,0:T(8,128)(2,1)S(1)} %get-tuple-element.36.scaled_ref, ...), custom_call_target="tpu_custom_call" | custom-call | flops 1342177280 | bytes 1048576 | tf_op jit(solution)/shard_map/student_side/pallas_call | solution.py:651
  67.7 3.4 %all-to-all-done.2.refs_0_ = f32[4,64,128]{2,1,0:T(8,128)S(1)} async-done(((f32[4,64,128]{2,1,0:T(8,128)}), f32[4,64,128]{2,1,0:T(8,128)S(1)}, u32[]{:S(2)}, u32[]{:S(2)}) %all-to-all-start.2) | async-done | bytes 131104 | tf_op jit(solution)/shard_map/all_to_all | solution.py:527
  71.2 3.1 %rows.3.refs_4_ = f32[8,8,128]{2,1,0:T(8,128)} custom-call(f32[4,64,128]{2,1,0:T(8,128)S(1)} %all-to-all-done.2.refs_0_, f32[8,128]{1,0:T(8,128)S(1)} %get-tuple-element.31.factor_ref.refs_4_.refs_1_, bf16[8,256,1024]{2,1,0:T(8,128)(2,1)} %get-tuple-element.28.exp_hbm.refs_5_.refs_2_, f32[8,128]{1,0:T(8,128)S(1)} %get-tuple-element.38.refs_3_, ...), custom_call_target="tpu_custom_call" | custom-call | flops 4194304 | bytes 4194304 | tf_op jit(solution)/shard_map/rows/pallas_call | solution.py:673
  74.3 3.4 %all-to-all-start.3 = ((f32[8,8,128]{2,1,0:T(8,128)}), f32[8,8,128]{2,1,0:T(8,128)S(1)}, u32[]{:S(2)}, u32[]{:S(2)}) async-start(f32[8,8,128]{2,1,0:T(8,128)} %rows.3.refs_4_), calls=%async_computation.3 | async-start | bytes 65536 | tf_op jit(solution)/shard_map/all_to_all | solution.py:527
  77.6 2.9 %student_side.7 = (bf16[128,1024]{1,0:T(8,128)(2,1)S(1)}, f32[8,128]{1,0:T(8,128)S(1)}) custom-call(bf16[768,512]{1,0:T(8,128)(2,1)S(1)} %get-tuple-element.34.refs_6_.unit, bf16[128,1024]{1,0:T(8,128)(2,1)S(1)} %get-tuple-element.35.feat_ref, bf16[128,256]{1,0:T(8,128)(2,1)S(1)} %get-tuple-element.36.scaled_ref, ...), custom_call_target="tpu_custom_call" | custom-call | flops 1342177280 | bytes 1048576 | tf_op jit(solution)/shard_map/student_side/pallas_call | solution.py:651
  88.7 2.9 %student_side.8 = (bf16[128,1024]{1,0:T(8,128)(2,1)S(1)}, f32[8,128]{1,0:T(8,128)S(1)}) custom-call(bf16[768,512]{1,0:T(8,128)(2,1)S(1)} %get-tuple-element.34.refs_6_.unit, bf16[128,1024]{1,0:T(8,128)(2,1)S(1)} %get-tuple-element.35.feat_ref, bf16[128,256]{1,0:T(8,128)(2,1)S(1)} %get-tuple-element.36.scaled_ref, ...), custom_call_target="tpu_custom_call" | custom-call | flops 1342177280 | bytes 1048576 | tf_op jit(solution)/shard_map/student_side/pallas_call | solution.py:651
  92.3 17.7 %last_rows.1 = (bf16[8,768,1024]{2,1,0:T(8,128)(2,1)}, f32[64,128]{1,0:T(8,128)S(1)}, bf16[8,80,512]{2,1,0:T(8,128)(2,1)}) custom-call(f32[8,128]{1,0:T(8,128)S(1)} %get-tuple-element.31.factor_ref.refs_4_.refs_1_, bf16[256,512]{1,0:T(8,128)(2,1)} %s_hbm.3, f32[256,512]{1,0:T(8,128)} %copy-done, ...), custom_call_target="tpu_custom_call" | custom-call | flops 8589934592 | bytes 12582912 | tf_op jit(solution)/shard_map/last_rows/pallas_call | solution.py:704
  110.0 3.6 %all-to-all-start.4 = ((bf16[8,80,512]{2,1,0:T(8,128)(2,1)}), bf16[8,80,512]{2,1,0:T(8,128)(2,1)S(1)}, u32[]{:S(2)}, u32[]{:S(2)}) async-start(bf16[8,80,512]{2,1,0:T(8,128)(2,1)} %get-tuple-element.43.refs_4_), calls=%async_computation.4 | async-start | bytes 1310720 | tf_op jit(solution)/shard_map/all_to_all | solution.py:527
  113.6 7.4 %student_side.9 = (bf16[128,4096]{1,0:T(8,128)(2,1)S(1)}, f32[8,128]{1,0:T(8,128)S(1)}) custom-call(bf16[768,512]{1,0:T(8,128)(2,1)S(1)} %get-tuple-element.34.refs_6_.unit, bf16[128,1024]{1,0:T(8,128)(2,1)S(1)} %get-tuple-element.35.feat_ref, bf16[128,256]{1,0:T(8,128)(2,1)S(1)} %get-tuple-element.36.scaled_ref, ...), custom_call_target="tpu_custom_call" | custom-call | flops 5368709120 | bytes 4194304 | tf_op jit(solution)/shard_map/student_side/pallas_call | solution.py:651
  121.0 3.7 %all-to-all-done.4.message_ref = bf16[8,80,512]{2,1,0:T(8,128)(2,1)S(1)} async-done(((bf16[8,80,512]{2,1,0:T(8,128)(2,1)}), bf16[8,80,512]{2,1,0:T(8,128)(2,1)S(1)}, u32[]{:S(2)}, u32[]{:S(2)}) %all-to-all-start.4) | async-done | bytes 655392 | tf_op jit(solution)/shard_map/all_to_all | solution.py:527
  127.0 3.5 %all-to-all-start.5 = ((f32[8,32,512]{2,1,0:T(8,128)}), f32[8,32,512]{2,1,0:T(8,128)S(1)}, u32[]{:S(2)}, u32[]{:S(2)}) async-start(f32[8,32,512]{2,1,0:T(8,128)} %get-tuple-element.51), calls=%async_computation.5 | async-start | bytes 1048576 | tf_op jit(solution)/shard_map/all_to_all | solution.py:527
  136.9 7.7 %weight_grads.1 = bf16[128,8192]{1,0:T(8,128)(2,1)} custom-call(bf16[8,256,1024]{2,1,0:T(8,128)(2,1)} %get-tuple-element.28.exp_hbm.refs_5_.refs_2_, bf16[8,768,1024]{2,1,0:T(8,128)(2,1)} %get-tuple-element.41.prob_hbm, bf16[128,1024]{1,0:T(8,128)(2,1)S(1)} %get-tuple-element.35.feat_ref, f32[64,128]{1,0:T(8,128)S(1)} %get-tuple-element.42.scale_ref, ...), custom_call_target="tpu_custom_call" | custom-call | flops 2147483648 | bytes 12582912 | tf_op jit(solution)/shard_map/weight_grads/pallas_call | solution.py:750
  (52 shorter events, 30.0 us)
Async XLA Ops:
  0.6 31.9 %collective-permute-start.2 = (bf16[256,512]{1,0:T(8,128)(2,1)}, bf16[256,512]{1,0:T(8,128)(2,1)S(1)}, u32[]{:S(2)}, u32[]{:S(2)}) collective-permute-start(bf16[256,512]{1,0:T(8,128)(2,1)} %s_hbm.3), channel_id=1, source_target_pairs={{0,1},{1,2},{2,3},{3,0},{4,5},{5,6},{6,7},{7,4},{8,9},{9,10},{10,1... | collective-permute-start | bytes 786440 | tf_op jit(solution)/shard_map/ppermute | solution.py:532
  3.7 28.8 %collective-permute-start.1 = (bf16[256,512]{1,0:T(8,128)(2,1)}, bf16[256,512]{1,0:T(8,128)(2,1)S(1)}, u32[]{:S(2)}, u32[]{:S(2)}) collective-permute-start(bf16[256,512]{1,0:T(8,128)(2,1)} %s_hbm.3), channel_id=1, source_target_pairs={{0,2},{1,3},{2,0},{3,1},{4,6},{5,7},{6,4},{7,5},{8,10},{9,11},{10,... | collective-permute-start | bytes 786440 | tf_op jit(solution)/shard_map/ppermute | solution.py:532
  6.3 26.2 %collective-permute-start = (bf16[256,512]{1,0:T(8,128)(2,1)}, bf16[256,512]{1,0:T(8,128)(2,1)S(1)}, u32[]{:S(2)}, u32[]{:S(2)}) collective-permute-start(bf16[256,512]{1,0:T(8,128)(2,1)} %s_hbm.3), channel_id=1, source_target_pairs={{0,3},{1,0},{2,1},{3,2},{4,7},{5,4},{6,5},{7,6},{8,11},{9,8},{10,9... | collective-permute-start | bytes 786440 | tf_op jit(solution)/shard_map/ppermute | solution.py:532
  23.2 9.3 %all-to-all-start = ((f32[8,8,128]{2,1,0:T(8,128)}), f32[8,8,128]{2,1,0:T(8,128)S(1)}, u32[]{:S(2)}, u32[]{:S(2)}) async-start(f32[8,8,128]{2,1,0:T(8,128)} %get-tuple-element.29.before_ref), calls=%async_computation | async-start | bytes 65536 | tf_op jit(solution)/shard_map/all_to_all | solution.py:527
  32.4 17.1 %copy-start = (f32[256,512]{1,0:T(8,128)}, f32[256,512]{1,0:T(8,128)S(1)}, u32[]{:S(2)}) copy-start(f32[256,512]{1,0:T(8,128)S(1)} %own_back.1.refs_0_.student_hbm) | copy-start | bytes 1572868
  32.4 6.9 %copy-start.1 = (bf16[256,512]{1,0:T(8,128)(2,1)S(1)}, bf16[256,512]{1,0:T(8,128)(2,1)}, u32[]{:S(2)}) copy-start(bf16[256,512]{1,0:T(8,128)(2,1)} %s_hbm.3) | copy-start | bytes 786436
  32.4 6.9 %copy-start.6 = (bf16[256,512]{1,0:T(8,128)(2,1)S(1)}, bf16[256,512]{1,0:T(8,128)(2,1)}, u32[]{:S(2)}) copy-start(bf16[256,512]{1,0:T(8,128)(2,1)} %t_ref.1) | copy-start | bytes 786436
  35.5 8.0 %collective-permute-start.8 = (f32[1,72,128]{2,1,0:T(8,128)S(1)}, f32[1,72,128]{2,1,0:T(8,128)S(1)}, u32[]{:S(2)}, u32[]{:S(2)}) collective-permute-start(f32[1,72,128]{2,1,0:T(8,128)S(1)} %get-tuple-element.32.refs_3_.refs_0_.logs_ref), channel_id=1, source_target_pairs={{0,1},{1,2},{2,3},{3,0},{4,5},{5,6},{6,7},{7,4},{8,9},{9,10},{10,1... | collective-permute-start | bytes 110600 | tf_op jit(solution)/shard_map/ppermute | solution.py:532
  36.2 10.2 %collective-permute-start.7 = (f32[1,72,128]{2,1,0:T(8,128)S(1)}, f32[1,72,128]{2,1,0:T(8,128)S(1)}, u32[]{:S(2)}, u32[]{:S(2)}) collective-permute-start(f32[1,72,128]{2,1,0:T(8,128)S(1)} %get-tuple-element.32.refs_3_.refs_0_.logs_ref), channel_id=1, source_target_pairs={{0,2},{1,3},{2,0},{3,1},{4,6},{5,7},{6,4},{7,5},{8,10},{9,11},{10,... | collective-permute-start | bytes 110600 | tf_op jit(solution)/shard_map/ppermute | solution.py:532
  36.5 9.9 %collective-permute-start.6 = (f32[1,72,128]{2,1,0:T(8,128)S(1)}, f32[1,72,128]{2,1,0:T(8,128)S(1)}, u32[]{:S(2)}, u32[]{:S(2)}) collective-permute-start(f32[1,72,128]{2,1,0:T(8,128)S(1)} %get-tuple-element.32.refs_3_.refs_0_.logs_ref), channel_id=1, source_target_pairs={{0,3},{1,0},{2,1},{3,2},{4,7},{5,4},{6,5},{7,6},{8,11},{9,8},{10,9... | collective-permute-start | bytes 110600 | tf_op jit(solution)/shard_map/ppermute | solution.py:532
  41.4 29.8 %collective-permute-start.5 = (bf16[256,512]{1,0:T(8,128)(2,1)}, bf16[256,512]{1,0:T(8,128)(2,1)S(1)}, u32[]{:S(2)}, u32[]{:S(2)}) collective-permute-start(bf16[256,512]{1,0:T(8,128)(2,1)} %get-tuple-element.33), channel_id=1, source_target_pairs={{0,1},{1,2},{2,3},{3,0},{4,5},{5,6},{6,7},{7,4},{8,9},{9,10},{10,1... | collective-permute-start | bytes 786440 | tf_op jit(solution)/shard_map/ppermute | solution.py:532
  42.0 29.2 %collective-permute-start.4 = (bf16[256,512]{1,0:T(8,128)(2,1)}, bf16[256,512]{1,0:T(8,128)(2,1)S(1)}, u32[]{:S(2)}, u32[]{:S(2)}) collective-permute-start(bf16[256,512]{1,0:T(8,128)(2,1)} %get-tuple-element.33), channel_id=1, source_target_pairs={{0,2},{1,3},{2,0},{3,1},{4,6},{5,7},{6,4},{7,5},{8,10},{9,11},{10,... | collective-permute-start | bytes 786440 | tf_op jit(solution)/shard_map/ppermute | solution.py:532
  43.5 27.7 %collective-permute-start.3 = (bf16[256,512]{1,0:T(8,128)(2,1)}, bf16[256,512]{1,0:T(8,128)(2,1)S(1)}, u32[]{:S(2)}, u32[]{:S(2)}) collective-permute-start(bf16[256,512]{1,0:T(8,128)(2,1)} %get-tuple-element.33), channel_id=1, source_target_pairs={{0,3},{1,0},{2,1},{3,2},{4,7},{5,4},{6,5},{7,6},{8,11},{9,8},{10,9... | collective-permute-start | bytes 786440 | tf_op jit(solution)/shard_map/ppermute | solution.py:532
  49.5 9.0 %all-to-all-start.1 = ((f32[8,8,128]{2,1,0:T(8,128)}), f32[8,8,128]{2,1,0:T(8,128)S(1)}, u32[]{:S(2)}, u32[]{:S(2)}) async-start(f32[8,8,128]{2,1,0:T(8,128)} %rows.2.refs_4_), calls=%async_computation.1 | async-start | bytes 65536 | tf_op jit(solution)/shard_map/all_to_all | solution.py:527
  61.5 9.7 %all-to-all-start.2 = ((f32[4,64,128]{2,1,0:T(8,128)}), f32[4,64,128]{2,1,0:T(8,128)S(1)}, u32[]{:S(2)}, u32[]{:S(2)}) async-start(f32[4,64,128]{2,1,0:T(8,128)} %columns.2.refs_4_), calls=%async_computation.2 | async-start | bytes 262144 | tf_op jit(solution)/shard_map/all_to_all | solution.py:527
  74.3 8.2 %all-to-all-start.3 = ((f32[8,8,128]{2,1,0:T(8,128)}), f32[8,8,128]{2,1,0:T(8,128)S(1)}, u32[]{:S(2)}, u32[]{:S(2)}) async-start(f32[8,8,128]{2,1,0:T(8,128)} %rows.3.refs_4_), calls=%async_computation.3 | async-start | bytes 65536 | tf_op jit(solution)/shard_map/all_to_all | solution.py:527
  84.8 7.5 %collective-permute-start.11 = (f32[1,64,128]{2,1,0:T(8,128)S(1)}, f32[1,64,128]{2,1,0:T(8,128)S(1)}, u32[]{:S(2)}, u32[]{:S(2)}) collective-permute-start(f32[1,64,128]{2,1,0:T(8,128)S(1)} %columns.3.refs_4_.refs_7_), channel_id=1, source_target_pairs={{0,1},{1,2},{2,3},{3,0},{4,5},{5,6},{6,7},{7,4},{8,9},{9,10},{10,1... | collective-permute-start | bytes 98312 | tf_op jit(solution)/shard_map/ppermute | solution.py:532
  85.7 6.6 %collective-permute-start.10 = (f32[1,64,128]{2,1,0:T(8,128)S(1)}, f32[1,64,128]{2,1,0:T(8,128)S(1)}, u32[]{:S(2)}, u32[]{:S(2)}) collective-permute-start(f32[1,64,128]{2,1,0:T(8,128)S(1)} %columns.3.refs_4_.refs_7_), channel_id=1, source_target_pairs={{0,2},{1,3},{2,0},{3,1},{4,6},{5,7},{6,4},{7,5},{8,10},{9,11},{10,... | collective-permute-start | bytes 98312 | tf_op jit(solution)/shard_map/ppermute | solution.py:532
  87.0 5.3 %collective-permute-start.9 = (f32[1,64,128]{2,1,0:T(8,128)S(1)}, f32[1,64,128]{2,1,0:T(8,128)S(1)}, u32[]{:S(2)}, u32[]{:S(2)}) collective-permute-start(f32[1,64,128]{2,1,0:T(8,128)S(1)} %columns.3.refs_4_.refs_7_), channel_id=1, source_target_pairs={{0,3},{1,0},{2,1},{3,2},{4,7},{5,4},{6,5},{7,6},{8,11},{9,8},{10,9... | collective-permute-start | bytes 98312 | tf_op jit(solution)/shard_map/ppermute | solution.py:532
  110.0 14.6 %all-to-all-start.4 = ((bf16[8,80,512]{2,1,0:T(8,128)(2,1)}), bf16[8,80,512]{2,1,0:T(8,128)(2,1)S(1)}, u32[]{:S(2)}, u32[]{:S(2)}) async-start(bf16[8,80,512]{2,1,0:T(8,128)(2,1)} %get-tuple-element.43.refs_4_), calls=%async_computation.4 | async-start | bytes 1310720 | tf_op jit(solution)/shard_map/all_to_all | solution.py:527
  127.0 18.8 %all-to-all-start.5 = ((f32[8,32,512]{2,1,0:T(8,128)}), f32[8,32,512]{2,1,0:T(8,128)S(1)}, u32[]{:S(2)}, u32[]{:S(2)}) async-start(f32[8,32,512]{2,1,0:T(8,128)} %get-tuple-element.51), calls=%async_computation.5 | async-start | bytes 1048576 | tf_op jit(solution)/shard_map/all_to_all | solution.py:527
  130.5 14.0 %collective-permute-start.14 = (f32[8,128]{1,0:T(8,128)S(1)}, f32[8,128]{1,0:T(8,128)S(1)}, u32[]{:S(2)}, u32[]{:S(2)}) collective-permute-start(f32[8,128]{1,0:T(8,128)S(1)} %get-tuple-element.52), channel_id=1, source_target_pairs={{0,3},{1,2},{2,1},{3,0},{4,7},{5,6},{6,5},{7,4},{8,11},{9,10},{10,... | collective-permute-start | bytes 12296 | tf_op jit(solution)/shard_map/ppermute | solution.py:538
  132.7 11.9 %collective-permute-start.13 = (f32[8,128]{1,0:T(8,128)S(1)}, f32[8,128]{1,0:T(8,128)S(1)}, u32[]{:S(2)}, u32[]{:S(2)}) collective-permute-start(f32[8,128]{1,0:T(8,128)S(1)} %get-tuple-element.52), channel_id=1, source_target_pairs={{0,2},{1,3},{2,0},{3,1},{4,6},{5,7},{6,4},{7,5},{8,10},{9,11},{10,... | collective-permute-start | bytes 12296 | tf_op jit(solution)/shard_map/ppermute | solution.py:538
  132.9 11.7 %collective-permute-start.12 = (f32[8,128]{1,0:T(8,128)S(1)}, f32[8,128]{1,0:T(8,128)S(1)}, u32[]{:S(2)}, u32[]{:S(2)}) collective-permute-start(f32[8,128]{1,0:T(8,128)S(1)} %get-tuple-element.52), channel_id=1, source_target_pairs={{0,1},{1,0},{2,3},{3,2},{4,5},{5,4},{6,7},{7,6},{8,9},{9,8},{10,11... | collective-permute-start | bytes 12296 | tf_op jit(solution)/shard_map/ppermute | solution.py:538
  (4 other events, 3.3 us)

commit v4 on v3

--- a/solution.py
+++ b/solution.py
@@ -326,11 +326,14 @@
 
 
 def student_kernel(
-    log_protos, first, groups, unit, feat_ref, scaled_ref, exp_hbm, w_hbm, *refs
+    log_protos, first, count, groups, unit, feat_ref, scaled_ref, exp_hbm, w_hbm, *refs
 ):
     logs = refs[:groups]
-    grad, token_ref, lse, prob, exp_ref, w_ref, exp_sem, w_sem = refs[-8:]
-    own, count = exp_ref.shape[1], exp_ref.shape[0]
+    if count > 1:
+        grad_hbm, token_ref, lse, prob, exp_ref, w_ref, exp_sem, w_sem, grad, grad_sem = refs[-10:]
+    else:
+        grad, token_ref, lse, prob, exp_ref, w_ref, exp_sem, w_sem = refs[-8:]
+    own = exp_ref.shape[1]
     exp_loads = copies(exp_hbm, exp_ref, exp_sem, first, 0, count)
     w_loads = copies(w_hbm, w_ref, w_sem, first, 0, count)
     start(w_loads, exp_loads)
@@ -350,6 +353,11 @@
         values = jnp.dot(scaled_ref[...], exp_ref[k], preferred_element_type=F32)
         values = values + jnp.dot(feat_ref[:, own:], prob[...], preferred_element_type=F32)
         grad[:, columns_of(k)] = values.astype(BF16)
+        if count > 1:
+            copy_of(grad, grad_hbm, grad_sem, k).start()
+
+    if count > 1:
+        wait(copies(grad, grad_hbm, grad_sem))
 
 
 def as_three(value):
@@ -474,12 +482,25 @@
     loss_ref[...] = jnp.broadcast_to(jnp.sum(terms), loss_ref.shape)
 
 
-def grad_kernel(counts, protos, exp_hbm, prob_hbm, feat_ref, scale_ref, sums_ref, factor_ref, *refs):
-    parts = refs[: len(counts)]
-    out_hbm, scaled, exp_ref, prob_ref, out, exp_sem, prob_sem, sem = refs[-8:]
+def grad_kernel(
+    counts, protos, rows_all, exp_hbm, prob_hbm, feat_ref, scale_ref, sums_ref, factor_ref, *refs
+):
+    parts, losses = refs[: len(counts)], refs[len(counts) : -11]
+    (
+        out_hbm, loss_ref, scaled, exp_ref, prob_ref, out, last_ref, exp_sem, prob_sem, sem, last_sem,
+    ) = refs[-11:]
+    last_load = pltpu.make_async_copy(parts[-1], last_ref, last_sem)
+    parts = (*parts[:-1], last_ref)
     exp_loads = copies(exp_hbm, exp_ref, exp_sem)
     prob_loads = copies(prob_hbm, prob_ref, prob_sem)
-    start(exp_loads, prob_loads)
+    early = sum(counts[:-1])
+    start(exp_loads[:early], prob_loads[:early])
+    last_load.start()
+    start(exp_loads[early:], prob_loads[early:])
+    losses = [ref[0:1, 0:1] for ref in losses]
+    while len(losses) > 1:
+        losses = [a + b for a, b in zip(losses[::2], losses[1::2])]
+    loss_ref[...] = losses[0] / rows_all
     where = [(part, k) for count, part in zip(counts, parts) for k in range(count)]
     own = exp_ref.shape[1]
     tiles = (own + prob_ref.shape[1]) // LANES
@@ -500,6 +521,8 @@
             scaled[:, own:], prob_ref[k], preferred_element_type=F32
         )
         part, there = where[k]
+        if part is last_ref and there == 0:
+            last_load.wait()
         for t, tile in enumerate(lane_tiles(paired)):
             lanes = slice(k * WIDE + t * LANES, k * WIDE + (t + 1) * LANES)
             scale = scale_ref[lanes.start // LANES : lanes.stop // LANES, :]
@@ -532,14 +555,11 @@
     return [lax.ppermute(value, axis, [(i, (i - s) % n) for i in range(n)]) for s in range(1, n)]
 
 
-def tree_sum(value, axis):
+def swapped(value, axis):
     n = lax.axis_size(axis)
-    values = [value] + [
+    return [value] + [
         lax.ppermute(value, axis, [(i, i ^ s) for i in range(n)]) for s in range(1, n)
     ]
-    while len(values) > 1:
-        values = [a + b for a, b in zip(values[::2], values[1::2])]
-    return values[0]
 
 
 def local(teacher_feats, student_feats, proto_weight):
@@ -649,22 +669,26 @@
         turn = len(grad_parts)
         first, count = sum(counts[:turn]), counts[turn]
         grad_part, done = pl.pallas_call(
-            functools.partial(student_kernel, log_protos, first, groups),
+            functools.partial(student_kernel, log_protos, first, count, groups),
             in_specs=[VMEM] * 3 + [ANY] * 2 + [VMEM] * groups + [ANY],
-            out_specs=[VMEM, VMEM],
-            out_shape=[struct((feats, count * WIDE), BF16), token],
+            out_specs=[ANY if count > 1 else VMEM, VMEM],
+            out_shape=[
+                (pltpu.HBM if count > 1 else struct)((feats, count * WIDE), BF16), token,
+            ],
             scratch_shapes=[
                 pltpu.VMEM((others, LANES), F32),
                 pltpu.VMEM((others, WIDE), BF16),
                 pltpu.VMEM((count, own, WIDE), BF16),
                 pltpu.VMEM((width, count * WIDE), BF16),
             ]
-            + [pltpu.SemaphoreType.DMA((count,))] * 2,
+            + [pltpu.SemaphoreType.DMA((count,))] * 2
+            + ([pltpu.VMEM((feats, count * WIDE), BF16)] if count > 1 else [])
+            + ([pltpu.SemaphoreType.DMA((count,))] if count > 1 else []),
             compiler_params=params(16 * 2**20),
             cost_estimate=cost(2.5 * rows * width * WIDE * count, 2 * width * WIDE * count),
             name="student_side",
         )(unit, feat, scaled, s_exp, weight, *logs, before)
-        grad_parts.append(grad_part)
+        grad_parts.append(far(grad_part) if count > 1 else grad_part)
         return done
 
     done = unit
@@ -682,22 +706,18 @@
         )(*cols, factor, t_exp, done, *late)
         done = student_piece(sums)
         sums = exchange(sums, "proto")
-        middle = turn < SWEEPS - 2
         cols = pl.pallas_call(
             column_kernel,
             in_specs=[VMEM, VMEM, ANY, ANY],
             out_specs=VMEM,
-            out_shape=struct((groups if middle else 1, height, LANES), F32),
+            out_shape=struct((1, height, LANES), F32),
             scratch_shapes=[spread, exp_buffer, sems],
             compiler_params=params(exp_bytes),
             cost_estimate=cost(2 * own * local_protos, exp_bytes),
             name="columns",
         )(sums, factor, t_exp, done)
         done = student_piece(cols)
-        if middle:
-            cols = [exchange(cols, "batch")]
-        else:
-            cols = [cols] + following(cols, "batch")
+        cols = [cols] + following(cols, "batch")
 
     sum_rows = -(-(tiles + own // LANES) // 16) * 16
     message_shape = (parts, 2 * share + sum_rows, width)
@@ -745,25 +765,27 @@
         name="row_grads",
     )(place, student_rows, message, logs[0], done)
     grad_rows = exchange(grad_rows, "proto").reshape(own, width)
-    loss = tree_sum(loss_part, "batch")[0, 0] / rows
-
-    grad_weight = pl.pallas_call(
-        functools.partial(grad_kernel, counts, float(protos)),
-        in_specs=[ANY] * 2 + [VMEM] * (4 + len(counts)),
-        out_specs=ANY,
-        out_shape=struct((feats, local_protos), BF16),
+    losses = swapped(loss_part, "batch")
+
+    grad_weight, loss = pl.pallas_call(
+        functools.partial(grad_kernel, counts, float(protos), float(rows)),
+        in_specs=[ANY] * 2 + [VMEM] * (3 + len(counts)) + [ANY] + [VMEM] * groups,
+        out_specs=[ANY, VMEM],
+        out_shape=[struct((feats, local_protos), BF16), struct((1, 1), F32)],
         scratch_shapes=[
             pltpu.VMEM((feats, rows), BF16),
             exp_buffer,
             pltpu.VMEM((chunks, others, WIDE), BF16),
             pltpu.VMEM((feats, local_protos), BF16),
+            pltpu.VMEM((feats, counts[-1] * WIDE), BF16),
             sems, sems, sems,
+            pltpu.SemaphoreType.DMA,
         ],
         compiler_params=params(exp_bytes + others_bytes + 4 * feats * local_protos),
         cost_estimate=cost(2 * feats * rows * local_protos, others_bytes),
         name="weight_grads",
-    )(t_exp, far(prob), feat, col_scale, sums, factor, *grad_parts)
-    return grad_weight, grad_rows, loss
+    )(t_exp, far(prob), feat, col_scale, sums, factor, *grad_parts, *losses)
+    return grad_weight, grad_rows, loss.reshape(())
 
 
 def solution(mesh):

time: 149 us -> 151 us (1.013)
  waiting for transfers between devices: 10.4 us -> 15.7 us
  local copies, waits for them, and re-layouts: 4.62 us -> 0.83 us
  between operations: 2.68 us -> 0.9 us
    ppermute x12 -> x15, waiting for transfers between devices: 0.03 us -> 5.94 us  [following(): lax.ppermute(value, axis, [(i, (i - s) % n) for i in range(n)])]
    ppermute x12 -> x15, starting transfers between devices: 19.7 us -> 23.8 us  [following(): lax.ppermute(value, axis, [(i, (i - s) % n) for i in range(n)])]
    all_to_all x6 -> x5, waiting for transfers between devices: 10.3 us -> 6.84 us  [exchange(): return lax.all_to_all(value, axis, 0, 0)]
    unnamed x15 -> x11, local copies, waits for them, and re-layouts: 4.1 us -> 0.83 us
    ppermute x3, waiting for transfers between devices: 0.01 us -> 2.87 us  [swapped(): lax.ppermute(value, axis, [(i, i ^ s) for i in range(n)])]
    all_to_all x6 -> x5, starting transfers between devices: 21.7 us -> 19 us  [exchange(): return lax.all_to_all(value, axis, 0, 0)]
    pallas_call x6, Pallas kernels: 26.6 us -> 28.4 us  [the longest x5 19.7 us: student_piece(): pl.pallas_call(functools.partial(student_kernel, log_protos, first, count...]
  transfers between devices with their start and end apart: 21 -> 23, of which waited for: 4 -> 8; matrix products, arithmetic and copies ran while one was open for 0% -> 0% of each run, Pallas kernels for 38% -> 38%
where the time goes in v4:
time: 151 us; the launch traced here: 150 us
  Pallas kernels  85.3 us (56%)
  starting transfers between devices  47.2 us (31%)
  waiting for transfers between devices  15.7 us (10%)
    ppermute x15, starting transfers between devices, following(): lax.ppermute(value, axis, [(i, (i - s) % n) for i in range(n)])  23.8 us
    pallas_call x5, Pallas kernels, student_piece(): pl.pallas_call(functools.partial(student_kernel, log_protos, first, count...  19.7 us
    all_to_all x5, starting transfers between devices, exchange(): return lax.all_to_all(value, axis, 0, 0)  19 us
    pallas_call x1, Pallas kernels, local(): pl.pallas_call(functools.partial(last_kernel, groups), in_specs=[VMEM] +...  17.7 us
    pallas_call x1, Pallas kernels, local(): pl.pallas_call(stats_kernel, in_specs=[ANY] * 3, out_specs=[ANY, ANY, VME...  15.5 us
    pallas_call x1, Pallas kernels, local(): pl.pallas_call(functools.partial(grad_kernel, counts, float(protos), floa...  8.75 us
    all_to_all x5, waiting for transfers between devices, exchange(): return lax.all_to_all(value, axis, 0, 0)  6.84 us
    pallas_call x2, Pallas kernels, local(): pl.pallas_call(functools.partial(row_kernel, len(cols)), in_specs=[VMEM]...  6.19 us
  transfers between devices with their start and end apart: 23, of which 8 were waited for; matrix products, arithmetic and copies ran while one was open for 0% of the time, Pallas kernels for 38%

profile of v4, /device:TPU:0, one launch (start us, length us, event | category | flops | bytes accessed | tf_op | source)
XLA Modules:
  0.0 150.0 jit_solution(16744742799181928743)
XLA Ops:
  0.6 3.1 %collective-permute-start.2 = (bf16[256,512]{1,0:T(8,128)(2,1)}, bf16[256,512]{1,0:T(8,128)(2,1)S(1)}, u32[]{:S(2)}, u32[]{:S(2)}) collective-permute-start(bf16[256,512]{1,0:T(8,128)(2,1)} %s_hbm.3), channel_id=1, source_target_pairs={{0,1},{1,2},{2,3},{3,0},{4,5},{5,6},{6,7},{7,4},{8,9},{9,10},{10,1... | collective-permute-start | bytes 786440 | tf_op jit(solution)/shard_map/ppermute | solution.py:555
  3.7 2.6 %collective-permute-start.1 = (bf16[256,512]{1,0:T(8,128)(2,1)}, bf16[256,512]{1,0:T(8,128)(2,1)S(1)}, u32[]{:S(2)}, u32[]{:S(2)}) collective-permute-start(bf16[256,512]{1,0:T(8,128)(2,1)} %s_hbm.3), channel_id=1, source_target_pairs={{0,2},{1,3},{2,0},{3,1},{4,6},{5,7},{6,4},{7,5},{8,10},{9,11},{10,... | collective-permute-start | bytes 786440 | tf_op jit(solution)/shard_map/ppermute | solution.py:555
  7.6 15.5 %own_rows.1 = (bf16[8,256,1024]{2,1,0:T(8,128)(2,1)}, bf16[8,256,1024]{2,1,0:T(8,128)(2,1)}, f32[8,8,128]{2,1,0:T(8,128)}) custom-call(bf16[256,512]{1,0:T(8,128)(2,1)} %t_ref.1, bf16[256,512]{1,0:T(8,128)(2,1)} %s_hbm.3, bf16[512,8192]{1,0:T(8,128)(2,1)} %w_hbm.15), custom_call_target="tpu_custom_call" | custom-call | flops 4294967296 | bytes 8388608 | tf_op jit(solution)/shard_map/own_rows/pallas_call | solution.py:597
  23.2 3.7 %all-to-all-start = ((f32[8,8,128]{2,1,0:T(8,128)}), f32[8,8,128]{2,1,0:T(8,128)S(1)}, u32[]{:S(2)}, u32[]{:S(2)}) async-start(f32[8,8,128]{2,1,0:T(8,128)} %get-tuple-element.31.before_ref), calls=%async_computation | async-start | bytes 65536 | tf_op jit(solution)/shard_map/all_to_all | solution.py:550
  26.9 5.5 %own_back.1.refs_0_.student_hbm = f32[256,512]{1,0:T(8,128)S(1)} custom-call(f32[8,8,128]{2,1,0:T(8,128)} %get-tuple-element.31.before_ref, bf16[8,256,1024]{2,1,0:T(8,128)(2,1)} %get-tuple-element.32.exp_hbm, bf16[512,8192]{1,0:T(8,128)(2,1)} %w_hbm.15), custom_call_target="tpu_custom_call" | custom-call | flops 2147483648 | bytes 8388608 | tf_op jit(solution)/shard_map/own_back/pallas_call | solution.py:623
  32.5 2.9 %first_columns.1 = (f32[8,128]{1,0:T(8,128)S(1)}, f32[1,72,128]{2,1,0:T(8,128)S(1)}) custom-call(s32[2]{0:T(128)S(1)} %pad_add_fusion.place_ref, f32[8,8,128]{2,1,0:T(8,128)S(1)} %all-to-all-done.stats_ref, bf16[8,256,1024]{2,1,0:T(8,128)(2,1)} %get-tuple-element.30.exp_hbm.refs_5_, f32[256,512]{1,0:T(8,128)S(1)} %own_back.1.refs_0_.student_hbm, ...), custom_call_target="tpu_custom_call" | custom-call | flops 4194304 | bytes 4194304 | tf_op jit(solution)/shard_map/first_columns/pallas_call | solution.py:637
  36.5 2.8 %collective-permute-start.6 = (f32[1,72,128]{2,1,0:T(8,128)S(1)}, f32[1,72,128]{2,1,0:T(8,128)S(1)}, u32[]{:S(2)}, u32[]{:S(2)}) collective-permute-start(f32[1,72,128]{2,1,0:T(8,128)S(1)} %get-tuple-element.34.refs_3_.refs_0_.logs_ref), channel_id=1, source_target_pairs={{0,3},{1,0},{2,1},{3,2},{4,7},{5,4},{6,5},{7,6},{8,11},{9,8},{10,9... | collective-permute-start | bytes 110600 | tf_op jit(solution)/shard_map/ppermute | solution.py:555
  43.5 2.9 %collective-permute-start.3 = (bf16[256,512]{1,0:T(8,128)(2,1)}, bf16[256,512]{1,0:T(8,128)(2,1)S(1)}, u32[]{:S(2)}, u32[]{:S(2)}) collective-permute-start(bf16[256,512]{1,0:T(8,128)(2,1)} %get-tuple-element.35), channel_id=1, source_target_pairs={{0,3},{1,0},{2,1},{3,2},{4,7},{5,4},{6,5},{7,6},{8,11},{9,8},{10,9... | collective-permute-start | bytes 786440 | tf_op jit(solution)/shard_map/ppermute | solution.py:555
  46.4 3.0 %rows.2.refs_4_ = f32[8,8,128]{2,1,0:T(8,128)} custom-call(f32[1,72,128]{2,1,0:T(8,128)S(1)} %get-tuple-element.34.refs_3_.refs_0_.logs_ref, f32[1,72,128]{2,1,0:T(8,128)S(1)} %collective-permute-done.6.refs_1_.refs_4_, f32[1,72,128]{2,1,0:T(8,128)S(1)} %collective-permute-done.7.refs_2_.refs_5_, f32[1,72,128]{2,1,0:T(8,128)S(1)} %collective-permute-done.8.refs_3_.refs_6_, ...), custom_call_target="tpu_custom_call" | custom-call | flops 4194304 | bytes 4194304 | tf_op jit(solution)/shard_map/rows/pallas_call | solution.py:697
  49.5 4.2 %all-to-all-start.1 = ((f32[8,8,128]{2,1,0:T(8,128)}), f32[8,8,128]{2,1,0:T(8,128)S(1)}, u32[]{:S(2)}, u32[]{:S(2)}) async-start(f32[8,8,128]{2,1,0:T(8,128)} %rows.2.refs_4_), calls=%async_computation.1 | async-start | bytes 65536 | tf_op jit(solution)/shard_map/all_to_all | solution.py:550
  53.7 2.9 %student_side.5 = (bf16[128,1024]{1,0:T(8,128)(2,1)S(1)}, f32[8,128]{1,0:T(8,128)S(1)}) custom-call(bf16[768,512]{1,0:T(8,128)(2,1)S(1)} %get-tuple-element.36.refs_6_.unit, bf16[128,1024]{1,0:T(8,128)(2,1)S(1)} %get-tuple-element.37.feat_ref, bf16[128,256]{1,0:T(8,128)(2,1)S(1)} %get-tuple-element.38.scaled_ref, ...), custom_call_target="tpu_custom_call" | custom-call | flops 1342177280 | bytes 1048576 | tf_op jit(solution)/shard_map/student_side/pallas_call | solution.py:671
  61.9 4.8 %collective-permute-done.11.refs_3_ = f32[1,64,128]{2,1,0:T(8,128)S(1)} collective-permute-done((f32[1,64,128]{2,1,0:T(8,128)S(1)}, f32[1,64,128]{2,1,0:T(8,128)S(1)}, u32[]{:S(2)}, u32[]{:S(2)}) %collective-permute-start.11) | collective-permute-done | bytes 32800 | tf_op jit(solution)/shard_map/ppermute | solution.py:555
  66.7 2.9 %student_side.6 = (bf16[128,1024]{1,0:T(8,128)(2,1)S(1)}, f32[8,128]{1,0:T(8,128)S(1)}) custom-call(bf16[768,512]{1,0:T(8,128)(2,1)S(1)} %get-tuple-element.36.refs_6_.unit, bf16[128,1024]{1,0:T(8,128)(2,1)S(1)} %get-tuple-element.37.feat_ref, bf16[128,256]{1,0:T(8,128)(2,1)S(1)} %get-tuple-element.38.scaled_ref, ...), custom_call_target="tpu_custom_call" | custom-call | flops 1342177280 | bytes 1048576 | tf_op jit(solution)/shard_map/student_side/pallas_call | solution.py:671
  70.7 3.1 %rows.3.refs_4_ = f32[8,8,128]{2,1,0:T(8,128)} custom-call(f32[1,64,128]{2,1,0:T(8,128)S(1)} %columns.2.refs_4_.refs_0_, f32[1,64,128]{2,1,0:T(8,128)S(1)} %collective-permute-done.9.refs_1_, f32[1,64,128]{2,1,0:T(8,128)S(1)} %collective-permute-done.10.refs_2_, f32[1,64,128]{2,1,0:T(8,128)S(1)} %collective-permute-done.11.refs_3_, ...), custom_call_target="tpu_custom_call" | custom-call | flops 4194304 | bytes 4194304 | tf_op jit(solution)/shard_map/rows/pallas_call | solution.py:697
  73.9 4.0 %all-to-all-start.2 = ((f32[8,8,128]{2,1,0:T(8,128)}), f32[8,8,128]{2,1,0:T(8,128)S(1)}, u32[]{:S(2)}, u32[]{:S(2)}) async-start(f32[8,8,128]{2,1,0:T(8,128)} %rows.3.refs_4_), calls=%async_computation.2 | async-start | bytes 65536 | tf_op jit(solution)/shard_map/all_to_all | solution.py:550
  77.9 2.9 %student_side.7 = (bf16[128,1024]{1,0:T(8,128)(2,1)S(1)}, f32[8,128]{1,0:T(8,128)S(1)}) custom-call(bf16[768,512]{1,0:T(8,128)(2,1)S(1)} %get-tuple-element.36.refs_6_.unit, bf16[128,1024]{1,0:T(8,128)(2,1)S(1)} %get-tuple-element.37.feat_ref, bf16[128,256]{1,0:T(8,128)(2,1)S(1)} %get-tuple-element.38.scaled_ref, ...), custom_call_target="tpu_custom_call" | custom-call | flops 1342177280 | bytes 1048576 | tf_op jit(solution)/shard_map/student_side/pallas_call | solution.py:671
  92.0 2.9 %student_side.8 = (bf16[128,1024]{1,0:T(8,128)(2,1)S(1)}, f32[8,128]{1,0:T(8,128)S(1)}) custom-call(bf16[768,512]{1,0:T(8,128)(2,1)S(1)} %get-tuple-element.36.refs_6_.unit, bf16[128,1024]{1,0:T(8,128)(2,1)S(1)} %get-tuple-element.37.feat_ref, bf16[128,256]{1,0:T(8,128)(2,1)S(1)} %get-tuple-element.38.scaled_ref, ...), custom_call_target="tpu_custom_call" | custom-call | flops 1342177280 | bytes 1048576 | tf_op jit(solution)/shard_map/student_side/pallas_call | solution.py:671
  94.9 17.7 %last_rows.1 = (bf16[8,768,1024]{2,1,0:T(8,128)(2,1)}, f32[64,128]{1,0:T(8,128)S(1)}, bf16[8,80,512]{2,1,0:T(8,128)(2,1)}) custom-call(f32[8,128]{1,0:T(8,128)S(1)} %get-tuple-element.33.factor_ref.refs_4_, bf16[256,512]{1,0:T(8,128)(2,1)} %s_hbm.3, f32[256,512]{1,0:T(8,128)} %copy-done, bf16[8,256,1024]{2,1,0:T(8,128)(2,1)} %get-tuple-element.30.exp_hbm.refs_5_, ...), custom_call_target="tpu_custom_call" | custom-call | flops 8589934592 | bytes 12582912 | tf_op jit(solution)/shard_map/last_rows/pallas_call | solution.py:724
  112.6 3.6 %all-to-all-start.3 = ((bf16[8,80,512]{2,1,0:T(8,128)(2,1)}), bf16[8,80,512]{2,1,0:T(8,128)(2,1)S(1)}, u32[]{:S(2)}, u32[]{:S(2)}) async-start(bf16[8,80,512]{2,1,0:T(8,128)(2,1)} %get-tuple-element.45.refs_4_), calls=%async_computation.3 | async-start | bytes 1310720 | tf_op jit(solution)/shard_map/all_to_all | solution.py:550
  116.2 8.1 %student_side.9 = (bf16[128,4096]{1,0:T(8,128)(2,1)}, f32[8,128]{1,0:T(8,128)S(1)}) custom-call(bf16[768,512]{1,0:T(8,128)(2,1)S(1)} %get-tuple-element.36.refs_6_.unit, bf16[128,1024]{1,0:T(8,128)(2,1)S(1)} %get-tuple-element.37.feat_ref, bf16[128,256]{1,0:T(8,128)(2,1)S(1)} %get-tuple-element.38.scaled_ref, ...), custom_call_target="tpu_custom_call" | custom-call | flops 5368709120 | bytes 4194304 | tf_op jit(solution)/shard_map/student_side/pallas_call | solution.py:671
  124.3 2.9 %all-to-all-done.3.message_ref = bf16[8,80,512]{2,1,0:T(8,128)(2,1)S(1)} async-done(((bf16[8,80,512]{2,1,0:T(8,128)(2,1)}), bf16[8,80,512]{2,1,0:T(8,128)(2,1)S(1)}, u32[]{:S(2)}, u32[]{:S(2)}) %all-to-all-start.3) | async-done | bytes 655392 | tf_op jit(solution)/shard_map/all_to_all | solution.py:550
  129.6 3.5 %all-to-all-start.4 = ((f32[8,32,512]{2,1,0:T(8,128)}), f32[8,32,512]{2,1,0:T(8,128)S(1)}, u32[]{:S(2)}, u32[]{:S(2)}) async-start(f32[8,32,512]{2,1,0:T(8,128)} %get-tuple-element.55), calls=%async_computation.4 | async-start | bytes 1048576 | tf_op jit(solution)/shard_map/all_to_all | solution.py:550
  133.1 2.8 %collective-permute-start.17 = (f32[8,128]{1,0:T(8,128)S(1)}, f32[8,128]{1,0:T(8,128)S(1)}, u32[]{:S(2)}, u32[]{:S(2)}) collective-permute-start(f32[8,128]{1,0:T(8,128)S(1)} %get-tuple-element.53.refs_5_), channel_id=1, source_target_pairs={{0,3},{1,2},{2,1},{3,0},{4,7},{5,6},{6,5},{7,4},{8,11},{9,10},{10,... | collective-permute-start | bytes 12296 | tf_op jit(solution)/shard_map/ppermute | solution.py:561
  140.4 8.8 %weight_grads.1 = (bf16[128,8192]{1,0:T(8,128)(2,1)}, f32[1,1]{1,0:T(1,128)}) custom-call(bf16[8,256,1024]{2,1,0:T(8,128)(2,1)} %get-tuple-element.30.exp_hbm.refs_5_, bf16[8,768,1024]{2,1,0:T(8,128)(2,1)} %get-tuple-element.43.prob_hbm, bf16[128,1024]{1,0:T(8,128)(2,1)S(1)} %get-tuple-element.37.feat_ref, f32[64,128]{1,0:T(8,128)S(1)} %get-tuple-element.44.scale_ref, ...), custom_call_target="tpu_custom_call" | custom-call | flops 2147483648 | bytes 12582912 | tf_op jit(solution)/shard_map/weight_grads/pallas_call | solution.py:770
  (50 shorter events, 31.9 us)
Async XLA Ops:
  0.6 31.9 %collective-permute-start.2 = (bf16[256,512]{1,0:T(8,128)(2,1)}, bf16[256,512]{1,0:T(8,128)(2,1)S(1)}, u32[]{:S(2)}, u32[]{:S(2)}) collective-permute-start(bf16[256,512]{1,0:T(8,128)(2,1)} %s_hbm.3), channel_id=1, source_target_pairs={{0,1},{1,2},{2,3},{3,0},{4,5},{5,6},{6,7},{7,4},{8,9},{9,10},{10,1... | collective-permute-start | bytes 786440 | tf_op jit(solution)/shard_map/ppermute | solution.py:555
  3.7 28.8 %collective-permute-start.1 = (bf16[256,512]{1,0:T(8,128)(2,1)}, bf16[256,512]{1,0:T(8,128)(2,1)S(1)}, u32[]{:S(2)}, u32[]{:S(2)}) collective-permute-start(bf16[256,512]{1,0:T(8,128)(2,1)} %s_hbm.3), channel_id=1, source_target_pairs={{0,2},{1,3},{2,0},{3,1},{4,6},{5,7},{6,4},{7,5},{8,10},{9,11},{10,... | collective-permute-start | bytes 786440 | tf_op jit(solution)/shard_map/ppermute | solution.py:555
  6.3 26.2 %collective-permute-start = (bf16[256,512]{1,0:T(8,128)(2,1)}, bf16[256,512]{1,0:T(8,128)(2,1)S(1)}, u32[]{:S(2)}, u32[]{:S(2)}) collective-permute-start(bf16[256,512]{1,0:T(8,128)(2,1)} %s_hbm.3), channel_id=1, source_target_pairs={{0,3},{1,0},{2,1},{3,2},{4,7},{5,4},{6,5},{7,6},{8,11},{9,8},{10,9... | collective-permute-start | bytes 786440 | tf_op jit(solution)/shard_map/ppermute | solution.py:555
  23.2 9.3 %all-to-all-start = ((f32[8,8,128]{2,1,0:T(8,128)}), f32[8,8,128]{2,1,0:T(8,128)S(1)}, u32[]{:S(2)}, u32[]{:S(2)}) async-start(f32[8,8,128]{2,1,0:T(8,128)} %get-tuple-element.31.before_ref), calls=%async_computation | async-start | bytes 65536 | tf_op jit(solution)/shard_map/all_to_all | solution.py:550
  32.4 17.1 %copy-start = (f32[256,512]{1,0:T(8,128)}, f32[256,512]{1,0:T(8,128)S(1)}, u32[]{:S(2)}) copy-start(f32[256,512]{1,0:T(8,128)S(1)} %own_back.1.refs_0_.student_hbm) | copy-start | bytes 1572868
  35.5 8.0 %collective-permute-start.8 = (f32[1,72,128]{2,1,0:T(8,128)S(1)}, f32[1,72,128]{2,1,0:T(8,128)S(1)}, u32[]{:S(2)}, u32[]{:S(2)}) collective-permute-start(f32[1,72,128]{2,1,0:T(8,128)S(1)} %get-tuple-element.34.refs_3_.refs_0_.logs_ref), channel_id=1, source_target_pairs={{0,1},{1,2},{2,3},{3,0},{4,5},{5,6},{6,7},{7,4},{8,9},{9,10},{10,1... | collective-permute-start | bytes 110600 | tf_op jit(solution)/shard_map/ppermute | solution.py:555
  36.2 10.2 %collective-permute-start.7 = (f32[1,72,128]{2,1,0:T(8,128)S(1)}, f32[1,72,128]{2,1,0:T(8,128)S(1)}, u32[]{:S(2)}, u32[]{:S(2)}) collective-permute-start(f32[1,72,128]{2,1,0:T(8,128)S(1)} %get-tuple-element.34.refs_3_.refs_0_.logs_ref), channel_id=1, source_target_pairs={{0,2},{1,3},{2,0},{3,1},{4,6},{5,7},{6,4},{7,5},{8,10},{9,11},{10,... | collective-permute-start | bytes 110600 | tf_op jit(solution)/shard_map/ppermute | solution.py:555
  36.5 9.9 %collective-permute-start.6 = (f32[1,72,128]{2,1,0:T(8,128)S(1)}, f32[1,72,128]{2,1,0:T(8,128)S(1)}, u32[]{:S(2)}, u32[]{:S(2)}) collective-permute-start(f32[1,72,128]{2,1,0:T(8,128)S(1)} %get-tuple-element.34.refs_3_.refs_0_.logs_ref), channel_id=1, source_target_pairs={{0,3},{1,0},{2,1},{3,2},{4,7},{5,4},{6,5},{7,6},{8,11},{9,8},{10,9... | collective-permute-start | bytes 110600 | tf_op jit(solution)/shard_map/ppermute | solution.py:555
  41.4 29.3 %collective-permute-start.5 = (bf16[256,512]{1,0:T(8,128)(2,1)}, bf16[256,512]{1,0:T(8,128)(2,1)S(1)}, u32[]{:S(2)}, u32[]{:S(2)}) collective-permute-start(bf16[256,512]{1,0:T(8,128)(2,1)} %get-tuple-element.35), channel_id=1, source_target_pairs={{0,1},{1,2},{2,3},{3,0},{4,5},{5,6},{6,7},{7,4},{8,9},{9,10},{10,1... | collective-permute-start | bytes 786440 | tf_op jit(solution)/shard_map/ppermute | solution.py:555
  42.0 28.7 %collective-permute-start.4 = (bf16[256,512]{1,0:T(8,128)(2,1)}, bf16[256,512]{1,0:T(8,128)(2,1)S(1)}, u32[]{:S(2)}, u32[]{:S(2)}) collective-permute-start(bf16[256,512]{1,0:T(8,128)(2,1)} %get-tuple-element.35), channel_id=1, source_target_pairs={{0,2},{1,3},{2,0},{3,1},{4,6},{5,7},{6,4},{7,5},{8,10},{9,11},{10,... | collective-permute-start | bytes 786440 | tf_op jit(solution)/shard_map/ppermute | solution.py:555
  43.5 27.2 %collective-permute-start.3 = (bf16[256,512]{1,0:T(8,128)(2,1)}, bf16[256,512]{1,0:T(8,128)(2,1)S(1)}, u32[]{:S(2)}, u32[]{:S(2)}) collective-permute-start(bf16[256,512]{1,0:T(8,128)(2,1)} %get-tuple-element.35), channel_id=1, source_target_pairs={{0,3},{1,0},{2,1},{3,2},{4,7},{5,4},{6,5},{7,6},{8,11},{9,8},{10,9... | collective-permute-start | bytes 786440 | tf_op jit(solution)/shard_map/ppermute | solution.py:555
  49.5 9.0 %all-to-all-start.1 = ((f32[8,8,128]{2,1,0:T(8,128)}), f32[8,8,128]{2,1,0:T(8,128)S(1)}, u32[]{:S(2)}, u32[]{:S(2)}) async-start(f32[8,8,128]{2,1,0:T(8,128)} %rows.2.refs_4_), calls=%async_computation.1 | async-start | bytes 65536 | tf_op jit(solution)/shard_map/all_to_all | solution.py:550
  60.8 5.8 %collective-permute-start.11 = (f32[1,64,128]{2,1,0:T(8,128)S(1)}, f32[1,64,128]{2,1,0:T(8,128)S(1)}, u32[]{:S(2)}, u32[]{:S(2)}) collective-permute-start(f32[1,64,128]{2,1,0:T(8,128)S(1)} %columns.2.refs_4_.refs_0_), channel_id=1, source_target_pairs={{0,1},{1,2},{2,3},{3,0},{4,5},{5,6},{6,7},{7,4},{8,9},{9,10},{10,1... | collective-permute-start | bytes 98312 | tf_op jit(solution)/shard_map/ppermute | solution.py:555
  60.9 9.4 %collective-permute-start.10 = (f32[1,64,128]{2,1,0:T(8,128)S(1)}, f32[1,64,128]{2,1,0:T(8,128)S(1)}, u32[]{:S(2)}, u32[]{:S(2)}) collective-permute-start(f32[1,64,128]{2,1,0:T(8,128)S(1)} %columns.2.refs_4_.refs_0_), channel_id=1, source_target_pairs={{0,2},{1,3},{2,0},{3,1},{4,6},{5,7},{6,4},{7,5},{8,10},{9,11},{10,... | collective-permute-start | bytes 98312 | tf_op jit(solution)/shard_map/ppermute | solution.py:555
  66.7 4.0 %collective-permute-start.9 = (f32[1,64,128]{2,1,0:T(8,128)S(1)}, f32[1,64,128]{2,1,0:T(8,128)S(1)}, u32[]{:S(2)}, u32[]{:S(2)}) collective-permute-start(f32[1,64,128]{2,1,0:T(8,128)S(1)} %columns.2.refs_4_.refs_0_), channel_id=1, source_target_pairs={{0,3},{1,0},{2,1},{3,2},{4,7},{5,4},{6,5},{7,6},{8,11},{9,8},{10,9... | collective-permute-start | bytes 98312 | tf_op jit(solution)/shard_map/ppermute | solution.py:555
  73.9 8.8 %all-to-all-start.2 = ((f32[8,8,128]{2,1,0:T(8,128)}), f32[8,8,128]{2,1,0:T(8,128)S(1)}, u32[]{:S(2)}, u32[]{:S(2)}) async-start(f32[8,8,128]{2,1,0:T(8,128)} %rows.3.refs_4_), calls=%async_computation.2 | async-start | bytes 65536 | tf_op jit(solution)/shard_map/all_to_all | solution.py:550
  85.1 9.8 %collective-permute-start.14 = (f32[1,64,128]{2,1,0:T(8,128)S(1)}, f32[1,64,128]{2,1,0:T(8,128)S(1)}, u32[]{:S(2)}, u32[]{:S(2)}) collective-permute-start(f32[1,64,128]{2,1,0:T(8,128)S(1)} %columns.3.refs_4_.refs_7_), channel_id=1, source_target_pairs={{0,1},{1,2},{2,3},{3,0},{4,5},{5,6},{6,7},{7,4},{8,9},{9,10},{10,1... | collective-permute-start | bytes 98312 | tf_op jit(solution)/shard_map/ppermute | solution.py:555
  87.6 7.3 %collective-permute-start.13 = (f32[1,64,128]{2,1,0:T(8,128)S(1)}, f32[1,64,128]{2,1,0:T(8,128)S(1)}, u32[]{:S(2)}, u32[]{:S(2)}) collective-permute-start(f32[1,64,128]{2,1,0:T(8,128)S(1)} %columns.3.refs_4_.refs_7_), channel_id=1, source_target_pairs={{0,2},{1,3},{2,0},{3,1},{4,6},{5,7},{6,4},{7,5},{8,10},{9,11},{10,... | collective-permute-start | bytes 98312 | tf_op jit(solution)/shard_map/ppermute | solution.py:555
  90.1 4.8 %collective-permute-start.12 = (f32[1,64,128]{2,1,0:T(8,128)S(1)}, f32[1,64,128]{2,1,0:T(8,128)S(1)}, u32[]{:S(2)}, u32[]{:S(2)}) collective-permute-start(f32[1,64,128]{2,1,0:T(8,128)S(1)} %columns.3.refs_4_.refs_7_), channel_id=1, source_target_pairs={{0,3},{1,0},{2,1},{3,2},{4,7},{5,4},{6,5},{7,6},{8,11},{9,8},{10,9... | collective-permute-start | bytes 98312 | tf_op jit(solution)/shard_map/ppermute | solution.py:555
  112.6 14.6 %all-to-all-start.3 = ((bf16[8,80,512]{2,1,0:T(8,128)(2,1)}), bf16[8,80,512]{2,1,0:T(8,128)(2,1)S(1)}, u32[]{:S(2)}, u32[]{:S(2)}) async-start(bf16[8,80,512]{2,1,0:T(8,128)(2,1)} %get-tuple-element.45.refs_4_), calls=%async_computation.3 | async-start | bytes 1310720 | tf_op jit(solution)/shard_map/all_to_all | solution.py:550
  129.6 19.6 %all-to-all-start.4 = ((f32[8,32,512]{2,1,0:T(8,128)}), f32[8,32,512]{2,1,0:T(8,128)S(1)}, u32[]{:S(2)}, u32[]{:S(2)}) async-start(f32[8,32,512]{2,1,0:T(8,128)} %get-tuple-element.55), calls=%async_computation.4 | async-start | bytes 1048576 | tf_op jit(solution)/shard_map/all_to_all | solution.py:550
  133.1 5.5 %collective-permute-start.17 = (f32[8,128]{1,0:T(8,128)S(1)}, f32[8,128]{1,0:T(8,128)S(1)}, u32[]{:S(2)}, u32[]{:S(2)}) collective-permute-start(f32[8,128]{1,0:T(8,128)S(1)} %get-tuple-element.53.refs_5_), channel_id=1, source_target_pairs={{0,3},{1,2},{2,1},{3,0},{4,7},{5,6},{6,5},{7,4},{8,11},{9,10},{10,... | collective-permute-start | bytes 12296 | tf_op jit(solution)/shard_map/ppermute | solution.py:561
  135.9 4.5 %collective-permute-start.16 = (f32[8,128]{1,0:T(8,128)S(1)}, f32[8,128]{1,0:T(8,128)S(1)}, u32[]{:S(2)}, u32[]{:S(2)}) collective-permute-start(f32[8,128]{1,0:T(8,128)S(1)} %get-tuple-element.53.refs_5_), channel_id=1, source_target_pairs={{0,2},{1,3},{2,0},{3,1},{4,6},{5,7},{6,4},{7,5},{8,10},{9,11},{10,... | collective-permute-start | bytes 12296 | tf_op jit(solution)/shard_map/ppermute | solution.py:561
  135.9 4.5 %collective-permute-start.15 = (f32[8,128]{1,0:T(8,128)S(1)}, f32[8,128]{1,0:T(8,128)S(1)}, u32[]{:S(2)}, u32[]{:S(2)}) collective-permute-start(f32[8,128]{1,0:T(8,128)S(1)} %get-tuple-element.53.refs_5_), channel_id=1, source_target_pairs={{0,1},{1,0},{2,3},{3,2},{4,5},{5,4},{6,7},{7,6},{8,9},{9,8},{10,11... | collective-permute-start | bytes 12296 | tf_op jit(solution)/shard_map/ppermute | solution.py:561
  (4 other events, 26.9 us)

commit v5 on v3

--- a/solution.py
+++ b/solution.py
@@ -16,6 +16,7 @@
 SCALE_STUDENT = LOG2E / TEMP_STUDENT
 LANES = 128
 WIDE = 1024
+SERIES = (0.00093768624, 0.0091820806, 0.055269409, 0.24016587, 0.6931408, 0.99999982)
 TILE = 256
 F32 = jnp.float32
 BF16 = jnp.bfloat16
@@ -69,6 +70,16 @@
 
 def nt_dot(a, b):
     return lax.dot_general(a, b, (((1,), (1,)), ((), ())), preferred_element_type=F32)
+
+
+def exp2_by_squares(x):
+    y = jnp.maximum(x, -127.0) * (1.0 / 128.0)
+    value = SERIES[0]
+    for term in SERIES[1:]:
+        value = value * y + term
+    for _ in range(7):
+        value = value * value
+    return value
 
 
 def add_up(values):
@@ -322,7 +333,11 @@
             unit[...], w_ref[:, columns_of(k, n, TILE)], preferred_element_type=F32
         )
         shift = lse[...]
-        use(n, [jnp.exp2(tile * scale - shift) for tile in lane_tiles(logits)])
+        tiles = [tile * scale - shift for tile in lane_tiles(logits)]
+        if n == 0:
+            use(n, [exp2_by_squares(tiles[0])] + [jnp.exp2(tile) for tile in tiles[1:]])
+        else:
+            use(n, [jnp.exp2(tile) for tile in tiles])
 
 
 def student_kernel(

time: 149 us -> 150 us (level)
  Pallas kernels: 84.1 us -> 87.1 us
    pallas_call x5, Pallas kernels: 18.9 us -> 20.5 us  [student_piece(): pl.pallas_call(functools.partial(student_kernel, log_protos, first, group...]
where the time goes in v5:
time: 150 us; the launch traced here: 149 us
  Pallas kernels  87.1 us (58%)
  starting transfers between devices  45.9 us (31%)
  waiting for transfers between devices  9.03 us (6%)
  local copies, waits for them, and re-layouts  4.62 us (3%)
  between operations  2.68 us (2%)
    all_to_all x6, starting transfers between devices, exchange(): return lax.all_to_all(value, axis, 0, 0)  21.7 us
    pallas_call x5, Pallas kernels, student_piece(): pl.pallas_call(functools.partial(student_kernel, log_protos, first, group...  20.5 us
    ppermute x12, starting transfers between devices, following(): lax.ppermute(value, axis, [(i, (i - s) % n) for i in range(n)])  19.7 us
    pallas_call x1, Pallas kernels, local(): pl.pallas_call(functools.partial(last_kernel, groups), in_specs=[VMEM] +...  19.2 us
    pallas_call x1, Pallas kernels, local(): pl.pallas_call(stats_kernel, in_specs=[ANY] * 3, out_specs=[ANY, ANY, VME...  15.5 us
    all_to_all x6, waiting for transfers between devices, exchange(): return lax.all_to_all(value, axis, 0, 0)  8.99 us
    pallas_call x1, Pallas kernels, local(): pl.pallas_call(functools.partial(grad_kernel, counts, float(protos)), in_...  7.68 us
    pallas_call x2, Pallas kernels, local(): pl.pallas_call(functools.partial(row_kernel, len(cols)), in_specs=[VMEM]...  6.11 us
  transfers between devices with their start and end apart: 21, of which 4 were waited for; matrix products, arithmetic and copies ran while one was open for 0% of the time, Pallas kernels for 38%

profile of v5, /device:TPU:0, one launch (start us, length us, event | category | flops | bytes accessed | tf_op | source)
XLA Modules:
  0.0 149.4 jit_solution(840836845268216498)
XLA Ops:
  0.6 3.1 %collective-permute-start.2 = (bf16[256,512]{1,0:T(8,128)(2,1)}, bf16[256,512]{1,0:T(8,128)(2,1)S(1)}, u32[]{:S(2)}, u32[]{:S(2)}) collective-permute-start(bf16[256,512]{1,0:T(8,128)(2,1)} %s_hbm.3), channel_id=1, source_target_pairs={{0,1},{1,2},{2,3},{3,0},{4,5},{5,6},{6,7},{7,4},{8,9},{9,10},{10,1... | collective-permute-start | bytes 786440 | tf_op jit(solution)/shard_map/ppermute | solution.py:547
  7.6 15.5 %own_rows.1 = (bf16[8,256,1024]{2,1,0:T(8,128)(2,1)}, bf16[8,256,1024]{2,1,0:T(8,128)(2,1)}, f32[8,8,128]{2,1,0:T(8,128)}) custom-call(bf16[256,512]{1,0:T(8,128)(2,1)} %t_ref.1, bf16[256,512]{1,0:T(8,128)(2,1)} %s_hbm.3, bf16[512,8192]{1,0:T(8,128)(2,1)} %w_hbm.15), custom_call_target="tpu_custom_call" | custom-call | flops 4294967296 | bytes 8388608 | tf_op jit(solution)/shard_map/own_rows/pallas_call | solution.py:592
  23.2 3.7 %all-to-all-start = ((f32[8,8,128]{2,1,0:T(8,128)}), f32[8,8,128]{2,1,0:T(8,128)S(1)}, u32[]{:S(2)}, u32[]{:S(2)}) async-start(f32[8,8,128]{2,1,0:T(8,128)} %get-tuple-element.29.before_ref), calls=%async_computation | async-start | bytes 65536 | tf_op jit(solution)/shard_map/all_to_all | solution.py:542
  26.9 5.5 %own_back.1.refs_0_.student_hbm = f32[256,512]{1,0:T(8,128)S(1)} custom-call(f32[8,8,128]{2,1,0:T(8,128)} %get-tuple-element.29.before_ref, bf16[8,256,1024]{2,1,0:T(8,128)(2,1)} %get-tuple-element.30.exp_hbm, bf16[512,8192]{1,0:T(8,128)(2,1)} %w_hbm.15), custom_call_target="tpu_custom_call" | custom-call | flops 2147483648 | bytes 8388608 | tf_op jit(solution)/shard_map/own_back/pallas_call | solution.py:618
  32.5 2.9 %first_columns.1 = (f32[8,128]{1,0:T(8,128)S(1)}, f32[1,72,128]{2,1,0:T(8,128)S(1)}) custom-call(s32[2]{0:T(128)S(1)} %pad_add_fusion.place_ref, f32[8,8,128]{2,1,0:T(8,128)S(1)} %all-to-all-done.stats_ref, bf16[8,256,1024]{2,1,0:T(8,128)(2,1)} %get-tuple-element.28.exp_hbm.refs_5_.refs_2_, f32[256,512]{1,0:T(8,128)S(1)} %own_back.1.refs_0_.student_hbm, ...), custom_call_target="tpu_custom_call" | custom-call | flops 4194304 | bytes 4194304 | tf_op jit(solution)/shard_map/first_columns/pallas_call | solution.py:632
  36.5 2.8 %collective-permute-start.6 = (f32[1,72,128]{2,1,0:T(8,128)S(1)}, f32[1,72,128]{2,1,0:T(8,128)S(1)}, u32[]{:S(2)}, u32[]{:S(2)}) collective-permute-start(f32[1,72,128]{2,1,0:T(8,128)S(1)} %get-tuple-element.32.refs_3_.refs_0_.logs_ref), channel_id=1, source_target_pairs={{0,3},{1,0},{2,1},{3,2},{4,7},{5,4},{6,5},{7,6},{8,11},{9,8},{10,9... | collective-permute-start | bytes 110600 | tf_op jit(solution)/shard_map/ppermute | solution.py:547
  43.5 2.9 %collective-permute-start.3 = (bf16[256,512]{1,0:T(8,128)(2,1)}, bf16[256,512]{1,0:T(8,128)(2,1)S(1)}, u32[]{:S(2)}, u32[]{:S(2)}) collective-permute-start(bf16[256,512]{1,0:T(8,128)(2,1)} %get-tuple-element.33), channel_id=1, source_target_pairs={{0,3},{1,0},{2,1},{3,2},{4,7},{5,4},{6,5},{7,6},{8,11},{9,8},{10,9... | collective-permute-start | bytes 786440 | tf_op jit(solution)/shard_map/ppermute | solution.py:547
  46.4 3.0 %rows.2.refs_4_ = f32[8,8,128]{2,1,0:T(8,128)} custom-call(f32[1,72,128]{2,1,0:T(8,128)S(1)} %get-tuple-element.32.refs_3_.refs_0_.logs_ref, f32[1,72,128]{2,1,0:T(8,128)S(1)} %collective-permute-done.6.refs_1_.refs_4_, f32[1,72,128]{2,1,0:T(8,128)S(1)} %collective-permute-done.7.refs_2_.refs_5_, f32[1,72,128]{2,1,0:T(8,128)S(1)} %collective-permute-done.8.refs_3_.refs_6_, ...), custom_call_target="tpu_custom_call" | custom-call | flops 4194304 | bytes 4194304 | tf_op jit(solution)/shard_map/rows/pallas_call | solution.py:688
  49.5 4.2 %all-to-all-start.1 = ((f32[8,8,128]{2,1,0:T(8,128)}), f32[8,8,128]{2,1,0:T(8,128)S(1)}, u32[]{:S(2)}, u32[]{:S(2)}) async-start(f32[8,8,128]{2,1,0:T(8,128)} %rows.2.refs_4_), calls=%async_computation.1 | async-start | bytes 65536 | tf_op jit(solution)/shard_map/all_to_all | solution.py:542
  53.7 3.1 %student_side.5 = (bf16[128,1024]{1,0:T(8,128)(2,1)S(1)}, f32[8,128]{1,0:T(8,128)S(1)}) custom-call(bf16[768,512]{1,0:T(8,128)(2,1)S(1)} %get-tuple-element.34.refs_6_.unit, bf16[128,1024]{1,0:T(8,128)(2,1)S(1)} %get-tuple-element.35.feat_ref, bf16[128,256]{1,0:T(8,128)(2,1)S(1)} %get-tuple-element.36.scaled_ref, ...), custom_call_target="tpu_custom_call" | custom-call | flops 1342177280 | bytes 1048576 | tf_op jit(solution)/shard_map/student_side/pallas_call | solution.py:666
  58.5 3.0 %columns.2.refs_4_ = f32[4,64,128]{2,1,0:T(8,128)} custom-call(f32[8,8,128]{2,1,0:T(8,128)S(1)} %all-to-all-done.1.sums_ref, f32[8,128]{1,0:T(8,128)S(1)} %get-tuple-element.31.factor_ref.refs_4_.refs_1_, bf16[8,256,1024]{2,1,0:T(8,128)(2,1)} %get-tuple-element.28.exp_hbm.refs_5_.refs_2_, f32[8,128]{1,0:T(8,128)S(1)} %get-tuple-element.37.refs_0_), custom_call_target="tpu_custom_call" | custom-call | flops 4194304 | bytes 4194304 | tf_op jit(solution)/shard_map/columns/pallas_call | solution.py:701
  61.5 3.3 %all-to-all-start.2 = ((f32[4,64,128]{2,1,0:T(8,128)}), f32[4,64,128]{2,1,0:T(8,128)S(1)}, u32[]{:S(2)}, u32[]{:S(2)}) async-start(f32[4,64,128]{2,1,0:T(8,128)} %columns.2.refs_4_), calls=%async_computation.2 | async-start | bytes 262144 | tf_op jit(solution)/shard_map/all_to_all | solution.py:542
  64.8 3.1 %student_side.6 = (bf16[128,1024]{1,0:T(8,128)(2,1)S(1)}, f32[8,128]{1,0:T(8,128)S(1)}) custom-call(bf16[768,512]{1,0:T(8,128)(2,1)S(1)} %get-tuple-element.34.refs_6_.unit, bf16[128,1024]{1,0:T(8,128)(2,1)S(1)} %get-tuple-element.35.feat_ref, bf16[128,256]{1,0:T(8,128)(2,1)S(1)} %get-tuple-element.36.scaled_ref, ...), custom_call_target="tpu_custom_call" | custom-call | flops 1342177280 | bytes 1048576 | tf_op jit(solution)/shard_map/student_side/pallas_call | solution.py:666
  67.9 3.2 %all-to-all-done.2.refs_0_ = f32[4,64,128]{2,1,0:T(8,128)S(1)} async-done(((f32[4,64,128]{2,1,0:T(8,128)}), f32[4,64,128]{2,1,0:T(8,128)S(1)}, u32[]{:S(2)}, u32[]{:S(2)}) %all-to-all-start.2) | async-done | bytes 131104 | tf_op jit(solution)/shard_map/all_to_all | solution.py:542
  71.2 3.1 %rows.3.refs_4_ = f32[8,8,128]{2,1,0:T(8,128)} custom-call(f32[4,64,128]{2,1,0:T(8,128)S(1)} %all-to-all-done.2.refs_0_, f32[8,128]{1,0:T(8,128)S(1)} %get-tuple-element.31.factor_ref.refs_4_.refs_1_, bf16[8,256,1024]{2,1,0:T(8,128)(2,1)} %get-tuple-element.28.exp_hbm.refs_5_.refs_2_, f32[8,128]{1,0:T(8,128)S(1)} %get-tuple-element.38.refs_3_, ...), custom_call_target="tpu_custom_call" | custom-call | flops 4194304 | bytes 4194304 | tf_op jit(solution)/shard_map/rows/pallas_call | solution.py:688
  74.3 3.4 %all-to-all-start.3 = ((f32[8,8,128]{2,1,0:T(8,128)}), f32[8,8,128]{2,1,0:T(8,128)S(1)}, u32[]{:S(2)}, u32[]{:S(2)}) async-start(f32[8,8,128]{2,1,0:T(8,128)} %rows.3.refs_4_), calls=%async_computation.3 | async-start | bytes 65536 | tf_op jit(solution)/shard_map/all_to_all | solution.py:542
  77.6 3.1 %student_side.7 = (bf16[128,1024]{1,0:T(8,128)(2,1)S(1)}, f32[8,128]{1,0:T(8,128)S(1)}) custom-call(bf16[768,512]{1,0:T(8,128)(2,1)S(1)} %get-tuple-element.34.refs_6_.unit, bf16[128,1024]{1,0:T(8,128)(2,1)S(1)} %get-tuple-element.35.feat_ref, bf16[128,256]{1,0:T(8,128)(2,1)S(1)} %get-tuple-element.36.scaled_ref, ...), custom_call_target="tpu_custom_call" | custom-call | flops 1342177280 | bytes 1048576 | tf_op jit(solution)/shard_map/student_side/pallas_call | solution.py:666
  88.7 3.1 %student_side.8 = (bf16[128,1024]{1,0:T(8,128)(2,1)S(1)}, f32[8,128]{1,0:T(8,128)S(1)}) custom-call(bf16[768,512]{1,0:T(8,128)(2,1)S(1)} %get-tuple-element.34.refs_6_.unit, bf16[128,1024]{1,0:T(8,128)(2,1)S(1)} %get-tuple-element.35.feat_ref, bf16[128,256]{1,0:T(8,128)(2,1)S(1)} %get-tuple-element.36.scaled_ref, ...), custom_call_target="tpu_custom_call" | custom-call | flops 1342177280 | bytes 1048576 | tf_op jit(solution)/shard_map/student_side/pallas_call | solution.py:666
  92.5 19.2 %last_rows.1 = (bf16[8,768,1024]{2,1,0:T(8,128)(2,1)}, f32[64,128]{1,0:T(8,128)S(1)}, bf16[8,80,512]{2,1,0:T(8,128)(2,1)}) custom-call(f32[8,128]{1,0:T(8,128)S(1)} %get-tuple-element.31.factor_ref.refs_4_.refs_1_, bf16[256,512]{1,0:T(8,128)(2,1)} %s_hbm.3, f32[256,512]{1,0:T(8,128)} %copy-done, ...), custom_call_target="tpu_custom_call" | custom-call | flops 8589934592 | bytes 12582912 | tf_op jit(solution)/shard_map/last_rows/pallas_call | solution.py:719
  111.7 3.6 %all-to-all-start.4 = ((bf16[8,80,512]{2,1,0:T(8,128)(2,1)}), bf16[8,80,512]{2,1,0:T(8,128)(2,1)S(1)}, u32[]{:S(2)}, u32[]{:S(2)}) async-start(bf16[8,80,512]{2,1,0:T(8,128)(2,1)} %get-tuple-element.43.refs_4_), calls=%async_computation.4 | async-start | bytes 1310720 | tf_op jit(solution)/shard_map/all_to_all | solution.py:542
  115.2 8.1 %student_side.9 = (bf16[128,4096]{1,0:T(8,128)(2,1)S(1)}, f32[8,128]{1,0:T(8,128)S(1)}) custom-call(bf16[768,512]{1,0:T(8,128)(2,1)S(1)} %get-tuple-element.34.refs_6_.unit, bf16[128,1024]{1,0:T(8,128)(2,1)S(1)} %get-tuple-element.35.feat_ref, bf16[128,256]{1,0:T(8,128)(2,1)S(1)} %get-tuple-element.36.scaled_ref, ...), custom_call_target="tpu_custom_call" | custom-call | flops 5368709120 | bytes 4194304 | tf_op jit(solution)/shard_map/student_side/pallas_call | solution.py:666
  123.4 2.9 %all-to-all-done.4.message_ref = bf16[8,80,512]{2,1,0:T(8,128)(2,1)S(1)} async-done(((bf16[8,80,512]{2,1,0:T(8,128)(2,1)}), bf16[8,80,512]{2,1,0:T(8,128)(2,1)S(1)}, u32[]{:S(2)}, u32[]{:S(2)}) %all-to-all-start.4) | async-done | bytes 655392 | tf_op jit(solution)/shard_map/all_to_all | solution.py:542
  128.6 3.5 %all-to-all-start.5 = ((f32[8,32,512]{2,1,0:T(8,128)}), f32[8,32,512]{2,1,0:T(8,128)S(1)}, u32[]{:S(2)}, u32[]{:S(2)}) async-start(f32[8,32,512]{2,1,0:T(8,128)} %get-tuple-element.51), calls=%async_computation.5 | async-start | bytes 1048576 | tf_op jit(solution)/shard_map/all_to_all | solution.py:542
  138.5 7.7 %weight_grads.1 = bf16[128,8192]{1,0:T(8,128)(2,1)} custom-call(bf16[8,256,1024]{2,1,0:T(8,128)(2,1)} %get-tuple-element.28.exp_hbm.refs_5_.refs_2_, bf16[8,768,1024]{2,1,0:T(8,128)(2,1)} %get-tuple-element.41.prob_hbm, bf16[128,1024]{1,0:T(8,128)(2,1)S(1)} %get-tuple-element.35.feat_ref, f32[64,128]{1,0:T(8,128)S(1)} %get-tuple-element.42.scale_ref, ...), custom_call_target="tpu_custom_call" | custom-call | flops 2147483648 | bytes 12582912 | tf_op jit(solution)/shard_map/weight_grads/pallas_call | solution.py:765
  (52 shorter events, 29.6 us)
Async XLA Ops:
  0.6 31.9 %collective-permute-start.2 = (bf16[256,512]{1,0:T(8,128)(2,1)}, bf16[256,512]{1,0:T(8,128)(2,1)S(1)}, u32[]{:S(2)}, u32[]{:S(2)}) collective-permute-start(bf16[256,512]{1,0:T(8,128)(2,1)} %s_hbm.3), channel_id=1, source_target_pairs={{0,1},{1,2},{2,3},{3,0},{4,5},{5,6},{6,7},{7,4},{8,9},{9,10},{10,1... | collective-permute-start | bytes 786440 | tf_op jit(solution)/shard_map/ppermute | solution.py:547
  3.7 28.8 %collective-permute-start.1 = (bf16[256,512]{1,0:T(8,128)(2,1)}, bf16[256,512]{1,0:T(8,128)(2,1)S(1)}, u32[]{:S(2)}, u32[]{:S(2)}) collective-permute-start(bf16[256,512]{1,0:T(8,128)(2,1)} %s_hbm.3), channel_id=1, source_target_pairs={{0,2},{1,3},{2,0},{3,1},{4,6},{5,7},{6,4},{7,5},{8,10},{9,11},{10,... | collective-permute-start | bytes 786440 | tf_op jit(solution)/shard_map/ppermute | solution.py:547
  6.3 26.2 %collective-permute-start = (bf16[256,512]{1,0:T(8,128)(2,1)}, bf16[256,512]{1,0:T(8,128)(2,1)S(1)}, u32[]{:S(2)}, u32[]{:S(2)}) collective-permute-start(bf16[256,512]{1,0:T(8,128)(2,1)} %s_hbm.3), channel_id=1, source_target_pairs={{0,3},{1,0},{2,1},{3,2},{4,7},{5,4},{6,5},{7,6},{8,11},{9,8},{10,9... | collective-permute-start | bytes 786440 | tf_op jit(solution)/shard_map/ppermute | solution.py:547
  23.2 9.3 %all-to-all-start = ((f32[8,8,128]{2,1,0:T(8,128)}), f32[8,8,128]{2,1,0:T(8,128)S(1)}, u32[]{:S(2)}, u32[]{:S(2)}) async-start(f32[8,8,128]{2,1,0:T(8,128)} %get-tuple-element.29.before_ref), calls=%async_computation | async-start | bytes 65536 | tf_op jit(solution)/shard_map/all_to_all | solution.py:542
  32.4 17.1 %copy-start = (f32[256,512]{1,0:T(8,128)}, f32[256,512]{1,0:T(8,128)S(1)}, u32[]{:S(2)}) copy-start(f32[256,512]{1,0:T(8,128)S(1)} %own_back.1.refs_0_.student_hbm) | copy-start | bytes 1572868
  32.4 6.9 %copy-start.1 = (bf16[256,512]{1,0:T(8,128)(2,1)S(1)}, bf16[256,512]{1,0:T(8,128)(2,1)}, u32[]{:S(2)}) copy-start(bf16[256,512]{1,0:T(8,128)(2,1)} %s_hbm.3) | copy-start | bytes 786436
  32.4 6.9 %copy-start.6 = (bf16[256,512]{1,0:T(8,128)(2,1)S(1)}, bf16[256,512]{1,0:T(8,128)(2,1)}, u32[]{:S(2)}) copy-start(bf16[256,512]{1,0:T(8,128)(2,1)} %t_ref.1) | copy-start | bytes 786436
  35.5 8.0 %collective-permute-start.8 = (f32[1,72,128]{2,1,0:T(8,128)S(1)}, f32[1,72,128]{2,1,0:T(8,128)S(1)}, u32[]{:S(2)}, u32[]{:S(2)}) collective-permute-start(f32[1,72,128]{2,1,0:T(8,128)S(1)} %get-tuple-element.32.refs_3_.refs_0_.logs_ref), channel_id=1, source_target_pairs={{0,1},{1,2},{2,3},{3,0},{4,5},{5,6},{6,7},{7,4},{8,9},{9,10},{10,1... | collective-permute-start | bytes 110600 | tf_op jit(solution)/shard_map/ppermute | solution.py:547
  36.2 10.2 %collective-permute-start.7 = (f32[1,72,128]{2,1,0:T(8,128)S(1)}, f32[1,72,128]{2,1,0:T(8,128)S(1)}, u32[]{:S(2)}, u32[]{:S(2)}) collective-permute-start(f32[1,72,128]{2,1,0:T(8,128)S(1)} %get-tuple-element.32.refs_3_.refs_0_.logs_ref), channel_id=1, source_target_pairs={{0,2},{1,3},{2,0},{3,1},{4,6},{5,7},{6,4},{7,5},{8,10},{9,11},{10,... | collective-permute-start | bytes 110600 | tf_op jit(solution)/shard_map/ppermute | solution.py:547
  36.5 9.9 %collective-permute-start.6 = (f32[1,72,128]{2,1,0:T(8,128)S(1)}, f32[1,72,128]{2,1,0:T(8,128)S(1)}, u32[]{:S(2)}, u32[]{:S(2)}) collective-permute-start(f32[1,72,128]{2,1,0:T(8,128)S(1)} %get-tuple-element.32.refs_3_.refs_0_.logs_ref), channel_id=1, source_target_pairs={{0,3},{1,0},{2,1},{3,2},{4,7},{5,4},{6,5},{7,6},{8,11},{9,8},{10,9... | collective-permute-start | bytes 110600 | tf_op jit(solution)/shard_map/ppermute | solution.py:547
  41.4 29.8 %collective-permute-start.5 = (bf16[256,512]{1,0:T(8,128)(2,1)}, bf16[256,512]{1,0:T(8,128)(2,1)S(1)}, u32[]{:S(2)}, u32[]{:S(2)}) collective-permute-start(bf16[256,512]{1,0:T(8,128)(2,1)} %get-tuple-element.33), channel_id=1, source_target_pairs={{0,1},{1,2},{2,3},{3,0},{4,5},{5,6},{6,7},{7,4},{8,9},{9,10},{10,1... | collective-permute-start | bytes 786440 | tf_op jit(solution)/shard_map/ppermute | solution.py:547
  42.0 29.2 %collective-permute-start.4 = (bf16[256,512]{1,0:T(8,128)(2,1)}, bf16[256,512]{1,0:T(8,128)(2,1)S(1)}, u32[]{:S(2)}, u32[]{:S(2)}) collective-permute-start(bf16[256,512]{1,0:T(8,128)(2,1)} %get-tuple-element.33), channel_id=1, source_target_pairs={{0,2},{1,3},{2,0},{3,1},{4,6},{5,7},{6,4},{7,5},{8,10},{9,11},{10,... | collective-permute-start | bytes 786440 | tf_op jit(solution)/shard_map/ppermute | solution.py:547
  43.5 27.7 %collective-permute-start.3 = (bf16[256,512]{1,0:T(8,128)(2,1)}, bf16[256,512]{1,0:T(8,128)(2,1)S(1)}, u32[]{:S(2)}, u32[]{:S(2)}) collective-permute-start(bf16[256,512]{1,0:T(8,128)(2,1)} %get-tuple-element.33), channel_id=1, source_target_pairs={{0,3},{1,0},{2,1},{3,2},{4,7},{5,4},{6,5},{7,6},{8,11},{9,8},{10,9... | collective-permute-start | bytes 786440 | tf_op jit(solution)/shard_map/ppermute | solution.py:547
  49.5 9.0 %all-to-all-start.1 = ((f32[8,8,128]{2,1,0:T(8,128)}), f32[8,8,128]{2,1,0:T(8,128)S(1)}, u32[]{:S(2)}, u32[]{:S(2)}) async-start(f32[8,8,128]{2,1,0:T(8,128)} %rows.2.refs_4_), calls=%async_computation.1 | async-start | bytes 65536 | tf_op jit(solution)/shard_map/all_to_all | solution.py:542
  61.5 9.7 %all-to-all-start.2 = ((f32[4,64,128]{2,1,0:T(8,128)}), f32[4,64,128]{2,1,0:T(8,128)S(1)}, u32[]{:S(2)}, u32[]{:S(2)}) async-start(f32[4,64,128]{2,1,0:T(8,128)} %columns.2.refs_4_), calls=%async_computation.2 | async-start | bytes 262144 | tf_op jit(solution)/shard_map/all_to_all | solution.py:542
  74.3 8.2 %all-to-all-start.3 = ((f32[8,8,128]{2,1,0:T(8,128)}), f32[8,8,128]{2,1,0:T(8,128)S(1)}, u32[]{:S(2)}, u32[]{:S(2)}) async-start(f32[8,8,128]{2,1,0:T(8,128)} %rows.3.refs_4_), calls=%async_computation.3 | async-start | bytes 65536 | tf_op jit(solution)/shard_map/all_to_all | solution.py:542
  84.8 7.7 %collective-permute-start.11 = (f32[1,64,128]{2,1,0:T(8,128)S(1)}, f32[1,64,128]{2,1,0:T(8,128)S(1)}, u32[]{:S(2)}, u32[]{:S(2)}) collective-permute-start(f32[1,64,128]{2,1,0:T(8,128)S(1)} %columns.3.refs_4_.refs_7_), channel_id=1, source_target_pairs={{0,1},{1,2},{2,3},{3,0},{4,5},{5,6},{6,7},{7,4},{8,9},{9,10},{10,1... | collective-permute-start | bytes 98312 | tf_op jit(solution)/shard_map/ppermute | solution.py:547
  85.7 6.8 %collective-permute-start.10 = (f32[1,64,128]{2,1,0:T(8,128)S(1)}, f32[1,64,128]{2,1,0:T(8,128)S(1)}, u32[]{:S(2)}, u32[]{:S(2)}) collective-permute-start(f32[1,64,128]{2,1,0:T(8,128)S(1)} %columns.3.refs_4_.refs_7_), channel_id=1, source_target_pairs={{0,2},{1,3},{2,0},{3,1},{4,6},{5,7},{6,4},{7,5},{8,10},{9,11},{10,... | collective-permute-start | bytes 98312 | tf_op jit(solution)/shard_map/ppermute | solution.py:547
  87.0 5.5 %collective-permute-start.9 = (f32[1,64,128]{2,1,0:T(8,128)S(1)}, f32[1,64,128]{2,1,0:T(8,128)S(1)}, u32[]{:S(2)}, u32[]{:S(2)}) collective-permute-start(f32[1,64,128]{2,1,0:T(8,128)S(1)} %columns.3.refs_4_.refs_7_), channel_id=1, source_target_pairs={{0,3},{1,0},{2,1},{3,2},{4,7},{5,4},{6,5},{7,6},{8,11},{9,8},{10,9... | collective-permute-start | bytes 98312 | tf_op jit(solution)/shard_map/ppermute | solution.py:547
  111.7 14.6 %all-to-all-start.4 = ((bf16[8,80,512]{2,1,0:T(8,128)(2,1)}), bf16[8,80,512]{2,1,0:T(8,128)(2,1)S(1)}, u32[]{:S(2)}, u32[]{:S(2)}) async-start(bf16[8,80,512]{2,1,0:T(8,128)(2,1)} %get-tuple-element.43.refs_4_), calls=%async_computation.4 | async-start | bytes 1310720 | tf_op jit(solution)/shard_map/all_to_all | solution.py:542
  128.6 18.8 %all-to-all-start.5 = ((f32[8,32,512]{2,1,0:T(8,128)}), f32[8,32,512]{2,1,0:T(8,128)S(1)}, u32[]{:S(2)}, u32[]{:S(2)}) async-start(f32[8,32,512]{2,1,0:T(8,128)} %get-tuple-element.51), calls=%async_computation.5 | async-start | bytes 1048576 | tf_op jit(solution)/shard_map/all_to_all | solution.py:542
  132.2 14.0 %collective-permute-start.14 = (f32[8,128]{1,0:T(8,128)S(1)}, f32[8,128]{1,0:T(8,128)S(1)}, u32[]{:S(2)}, u32[]{:S(2)}) collective-permute-start(f32[8,128]{1,0:T(8,128)S(1)} %get-tuple-element.52), channel_id=1, source_target_pairs={{0,3},{1,2},{2,1},{3,0},{4,7},{5,6},{6,5},{7,4},{8,11},{9,10},{10,... | collective-permute-start | bytes 12296 | tf_op jit(solution)/shard_map/ppermute | solution.py:553
  134.1 12.1 %collective-permute-start.13 = (f32[8,128]{1,0:T(8,128)S(1)}, f32[8,128]{1,0:T(8,128)S(1)}, u32[]{:S(2)}, u32[]{:S(2)}) collective-permute-start(f32[8,128]{1,0:T(8,128)S(1)} %get-tuple-element.52), channel_id=1, source_target_pairs={{0,2},{1,3},{2,0},{3,1},{4,6},{5,7},{6,4},{7,5},{8,10},{9,11},{10,... | collective-permute-start | bytes 12296 | tf_op jit(solution)/shard_map/ppermute | solution.py:553
  134.4 11.9 %collective-permute-start.12 = (f32[8,128]{1,0:T(8,128)S(1)}, f32[8,128]{1,0:T(8,128)S(1)}, u32[]{:S(2)}, u32[]{:S(2)}) collective-permute-start(f32[8,128]{1,0:T(8,128)S(1)} %get-tuple-element.52), channel_id=1, source_target_pairs={{0,1},{1,0},{2,3},{3,2},{4,5},{5,4},{6,7},{7,6},{8,9},{9,8},{10,11... | collective-permute-start | bytes 12296 | tf_op jit(solution)/shard_map/ppermute | solution.py:553
  (4 other events, 3.3 us)

commit v6 on v3

--- a/solution.py
+++ b/solution.py
@@ -17,6 +17,7 @@
 LANES = 128
 WIDE = 1024
 TILE = 256
+FAR = (2, 3)
 F32 = jnp.float32
 BF16 = jnp.bfloat16
 
@@ -158,8 +159,8 @@
     def _(k):
         for which, (half, out, sem) in enumerate(zip(halves, (t_out, s_out), (t_sem, s_sem))):
             shift = top[half, :]
-            for n in range(0, WIDE, TILE):
-                tiles = lane_tiles(logits[half, columns_of(k, n, TILE)])
+            for n in range(0, WIDE, 2 * TILE):
+                tiles = lane_tiles(logits[half, columns_of(k, n, 2 * TILE)])
                 tiles = [jnp.exp2(tile - shift) for tile in tiles]
                 for t, tile in enumerate(tiles):
                     lanes = slice(n + t * LANES, n + (t + 1) * LANES)
@@ -466,21 +467,32 @@
     total = total - paired * (weight[mine, :1] * protos)
     load.wait()
     unit, length = unit_rows(s_ref[...])
-    out_ref[0] = (total - unit * jnp.sum(unit * total, axis=-1, keepdims=True)) / length
+    total = (total - unit * jnp.sum(unit * total, axis=-1, keepdims=True)) / length
+    out_ref[0] = total.astype(BF16)
     repeat(out_ref)
     height = logs_ref.shape[1] - 8
     logs = logs_ref[0, height + quarter : height + 2 * quarter, :]
     terms = logs / LOG2E - totals[tiles : tiles + quarter, :] * scale / TEMP_STUDENT
-    loss_ref[...] = jnp.broadcast_to(jnp.sum(terms), loss_ref.shape)
+    loss_ref[...] = jnp.broadcast_to(jnp.sum(terms) / (tiles * LANES), loss_ref.shape)
 
 
 def grad_kernel(counts, protos, exp_hbm, prob_hbm, feat_ref, scale_ref, sums_ref, factor_ref, *refs):
     parts = refs[: len(counts)]
-    out_hbm, scaled, exp_ref, prob_ref, out, exp_sem, prob_sem, sem = refs[-8:]
+    out_hbm, scaled, exp_ref, prob_ref, out, part_ref, exp_sem, prob_sem, sem, part_sem = refs[-10:]
+    part_loads, where = {}, []
+    for i, (count, part) in enumerate(zip(counts, parts)):
+        for k in range(count):
+            if i in FAR:
+                slot = len(part_loads)
+                part_loads[len(where)] = copy_of(part, part_ref, part_sem, slot, k - slot)
+                where.append((part_ref, slot))
+            else:
+                where.append((part, k))
     exp_loads = copies(exp_hbm, exp_ref, exp_sem)
     prob_loads = copies(prob_hbm, prob_ref, prob_sem)
-    start(exp_loads, prob_loads)
-    where = [(part, k) for count, part in zip(counts, parts) for k in range(count)]
+    start(exp_loads[:2], prob_loads[:2])
+    start(list(part_loads.values()))
+    start(exp_loads[2:], prob_loads[2:])
     own = exp_ref.shape[1]
     tiles = (own + prob_ref.shape[1]) // LANES
     rows = protos / sums_ref[:tiles, :]
@@ -500,6 +512,8 @@
             scaled[:, own:], prob_ref[k], preferred_element_type=F32
         )
         part, there = where[k]
+        if k in part_loads:
+            part_loads[k].wait()
         for t, tile in enumerate(lane_tiles(paired)):
             lanes = slice(k * WIDE + t * LANES, k * WIDE + (t + 1) * LANES)
             scale = scale_ref[lanes.start // LANES : lanes.stop // LANES, :]
@@ -739,17 +753,19 @@
         functools.partial(rows_kernel, tiles, float(protos)),
         in_specs=[SMEM, ANY, VMEM, VMEM, ANY],
         out_specs=[VMEM] * 3,
-        out_shape=[struct((parts, share, width), F32), token, struct((sum_rows, LANES), F32)],
+        out_shape=[struct((parts, share, width), BF16), token, struct((sum_rows, LANES), F32)],
         scratch_shapes=[spread, pltpu.VMEM((share, width), BF16), pltpu.SemaphoreType.DMA],
         compiler_params=params(0),
         name="row_grads",
     )(place, student_rows, message, logs[0], done)
-    grad_rows = exchange(grad_rows, "proto").reshape(own, width)
-    loss = tree_sum(loss_part, "batch")[0, 0] / rows
+    grad_rows = exchange(grad_rows, "proto").reshape(own, width).astype(F32)
+    loss = tree_sum(loss_part, "batch")[0, 0]
 
     grad_weight = pl.pallas_call(
         functools.partial(grad_kernel, counts, float(protos)),
-        in_specs=[ANY] * 2 + [VMEM] * (4 + len(counts)),
+        in_specs=[ANY] * 2
+        + [VMEM] * 4
+        + [ANY if i in FAR else VMEM for i in range(len(counts))],
         out_specs=ANY,
         out_shape=struct((feats, local_protos), BF16),
         scratch_shapes=[
@@ -757,12 +773,13 @@
             exp_buffer,
             pltpu.VMEM((chunks, others, WIDE), BF16),
             pltpu.VMEM((feats, local_protos), BF16),
-            sems, sems, sems,
+            pltpu.VMEM((feats, sum(counts[i] for i in FAR) * WIDE), BF16),
+            sems, sems, sems, sems,
         ],
         compiler_params=params(exp_bytes + others_bytes + 4 * feats * local_protos),
         cost_estimate=cost(2 * feats * rows * local_protos, others_bytes),
         name="weight_grads",
-    )(t_exp, far(prob), feat, col_scale, sums, factor, *grad_parts)
+    )(t_exp, far(prob), feat, col_scale, sums, factor, *[far(x) if i in FAR else x for i, x in enumerate(grad_parts)])
     return grad_weight, grad_rows, loss
 
 

time: 149 us -> 145 us (0.973)
  local copies, waits for them, and re-layouts: 4.62 us -> 1.92 us
  between operations: 2.68 us -> 0.9 us
    unnamed x15 -> x10, local copies, waits for them, and re-layouts: 4.1 us -> 1.4 us
  transfers between devices with their start and end apart: 21 -> 21, of which waited for: 4 -> 4; matrix products, arithmetic and copies ran while one was open for 0% -> 0% of each run, Pallas kernels for 38% -> 39%
where the time goes in v6:
time: 145 us
  Pallas kernels  84.7 us (58%)
  starting transfers between devices  45.8 us (32%)
  waiting for transfers between devices  10.4 us (7%)
  local copies, waits for them, and re-layouts  1.92 us (1%)
    all_to_all x6, starting transfers between devices, exchange(): return lax.all_to_all(value, axis, 0, 0)  21.6 us
    ppermute x12, starting transfers between devices, following(): lax.ppermute(value, axis, [(i, (i - s) % n) for i in range(n)])  19.7 us
    pallas_call x5, Pallas kernels, student_piece(): pl.pallas_call(functools.partial(student_kernel, log_protos, first, group...  18.9 us
    pallas_call x1, Pallas kernels, local(): pl.pallas_call(functools.partial(last_kernel, groups), in_specs=[VMEM] +...  17.7 us
    pallas_call x1, Pallas kernels, local(): pl.pallas_call(stats_kernel, in_specs=[ANY] * 3, out_specs=[ANY, ANY, VME...  15.6 us
    all_to_all x6, waiting for transfers between devices, exchange(): return lax.all_to_all(value, axis, 0, 0)  10.3 us
    pallas_call x1, Pallas kernels, local(): pl.pallas_call(functools.partial(grad_kernel, counts, float(protos)), in_...  8.38 us
    pallas_call x2, Pallas kernels, local(): pl.pallas_call(functools.partial(row_kernel, len(cols)), in_specs=[VMEM]...  6.12 us
  transfers between devices with their start and end apart: 21, of which 4 were waited for; matrix products, arithmetic and copies ran while one was open for 0% of the time, Pallas kernels for 39%

profile of v6, /device:TPU:0, one launch (start us, length us, event | category | flops | bytes accessed | tf_op | source)
XLA Modules:
  0.0 144.6 jit_solution(4875358216168958602)
XLA Ops:
  0.6 3.1 %collective-permute-start.2 = (bf16[256,512]{1,0:T(8,128)(2,1)}, bf16[256,512]{1,0:T(8,128)(2,1)S(1)}, u32[]{:S(2)}, u32[]{:S(2)}) collective-permute-start(bf16[256,512]{1,0:T(8,128)(2,1)} %s_hbm.3), channel_id=1, source_target_pairs={{0,1},{1,2},{2,3},{3,0},{4,5},{5,6},{6,7},{7,4},{8,9},{9,10},{10,1... | collective-permute-start | bytes 786440 | tf_op jit(solution)/shard_map/ppermute | solution.py:546
  7.6 15.6 %own_rows.1 = (bf16[8,256,1024]{2,1,0:T(8,128)(2,1)}, bf16[8,256,1024]{2,1,0:T(8,128)(2,1)}, f32[8,8,128]{2,1,0:T(8,128)}) custom-call(bf16[256,512]{1,0:T(8,128)(2,1)} %t_ref.1, bf16[256,512]{1,0:T(8,128)(2,1)} %s_hbm.3, bf16[512,8192]{1,0:T(8,128)(2,1)} %w_hbm.15), custom_call_target="tpu_custom_call" | custom-call | flops 4294967296 | bytes 8388608 | tf_op jit(solution)/shard_map/own_rows/pallas_call | solution.py:591
  23.3 3.7 %all-to-all-start = ((f32[8,8,128]{2,1,0:T(8,128)}), f32[8,8,128]{2,1,0:T(8,128)S(1)}, u32[]{:S(2)}, u32[]{:S(2)}) async-start(f32[8,8,128]{2,1,0:T(8,128)} %get-tuple-element.29.before_ref), calls=%async_computation | async-start | bytes 65536 | tf_op jit(solution)/shard_map/all_to_all | solution.py:541
  27.0 5.5 %own_back.1.refs_0_.student_hbm = f32[256,512]{1,0:T(8,128)S(1)} custom-call(f32[8,8,128]{2,1,0:T(8,128)} %get-tuple-element.29.before_ref, bf16[8,256,1024]{2,1,0:T(8,128)(2,1)} %get-tuple-element.30.exp_hbm, bf16[512,8192]{1,0:T(8,128)(2,1)} %w_hbm.15), custom_call_target="tpu_custom_call" | custom-call | flops 2147483648 | bytes 8388608 | tf_op jit(solution)/shard_map/own_back/pallas_call | solution.py:617
  32.6 2.9 %first_columns.1 = (f32[8,128]{1,0:T(8,128)S(1)}, f32[1,72,128]{2,1,0:T(8,128)S(1)}) custom-call(s32[2]{0:T(128)S(1)} %pad_add_fusion.place_ref, f32[8,8,128]{2,1,0:T(8,128)S(1)} %all-to-all-done.stats_ref, bf16[8,256,1024]{2,1,0:T(8,128)(2,1)} %get-tuple-element.28.exp_hbm.refs_5_.refs_2_, f32[256,512]{1,0:T(8,128)S(1)} %own_back.1.refs_0_.student_hbm, ...), custom_call_target="tpu_custom_call" | custom-call | flops 4194304 | bytes 4194304 | tf_op jit(solution)/shard_map/first_columns/pallas_call | solution.py:631
  36.6 2.8 %collective-permute-start.6 = (f32[1,72,128]{2,1,0:T(8,128)S(1)}, f32[1,72,128]{2,1,0:T(8,128)S(1)}, u32[]{:S(2)}, u32[]{:S(2)}) collective-permute-start(f32[1,72,128]{2,1,0:T(8,128)S(1)} %get-tuple-element.32.refs_3_.refs_0_.logs_ref), channel_id=1, source_target_pairs={{0,3},{1,0},{2,1},{3,2},{4,7},{5,4},{6,5},{7,6},{8,11},{9,8},{10,9... | collective-permute-start | bytes 110600 | tf_op jit(solution)/shard_map/ppermute | solution.py:546
  43.5 2.9 %collective-permute-start.3 = (bf16[256,512]{1,0:T(8,128)(2,1)}, bf16[256,512]{1,0:T(8,128)(2,1)S(1)}, u32[]{:S(2)}, u32[]{:S(2)}) collective-permute-start(bf16[256,512]{1,0:T(8,128)(2,1)} %get-tuple-element.33), channel_id=1, source_target_pairs={{0,3},{1,0},{2,1},{3,2},{4,7},{5,4},{6,5},{7,6},{8,11},{9,8},{10,9... | collective-permute-start | bytes 786440 | tf_op jit(solution)/shard_map/ppermute | solution.py:546
  46.5 3.1 %rows.2.refs_4_ = f32[8,8,128]{2,1,0:T(8,128)} custom-call(f32[1,72,128]{2,1,0:T(8,128)S(1)} %get-tuple-element.32.refs_3_.refs_0_.logs_ref, f32[1,72,128]{2,1,0:T(8,128)S(1)} %collective-permute-done.6.refs_1_.refs_4_, f32[1,72,128]{2,1,0:T(8,128)S(1)} %collective-permute-done.7.refs_2_.refs_5_, f32[1,72,128]{2,1,0:T(8,128)S(1)} %collective-permute-done.8.refs_3_.refs_6_, ...), custom_call_target="tpu_custom_call" | custom-call | flops 4194304 | bytes 4194304 | tf_op jit(solution)/shard_map/rows/pallas_call | solution.py:687
  49.5 4.2 %all-to-all-start.1 = ((f32[8,8,128]{2,1,0:T(8,128)}), f32[8,8,128]{2,1,0:T(8,128)S(1)}, u32[]{:S(2)}, u32[]{:S(2)}) async-start(f32[8,8,128]{2,1,0:T(8,128)} %rows.2.refs_4_), calls=%async_computation.1 | async-start | bytes 65536 | tf_op jit(solution)/shard_map/all_to_all | solution.py:541
  53.8 2.9 %student_side.5 = (bf16[128,1024]{1,0:T(8,128)(2,1)S(1)}, f32[8,128]{1,0:T(8,128)S(1)}) custom-call(bf16[768,512]{1,0:T(8,128)(2,1)S(1)} %get-tuple-element.34.refs_6_.unit, bf16[128,1024]{1,0:T(8,128)(2,1)S(1)} %get-tuple-element.35.feat_ref, bf16[128,256]{1,0:T(8,128)(2,1)S(1)} %get-tuple-element.36.scaled_ref, ...), custom_call_target="tpu_custom_call" | custom-call | flops 1342177280 | bytes 1048576 | tf_op jit(solution)/shard_map/student_side/pallas_call | solution.py:665
  58.6 3.0 %columns.2.refs_4_ = f32[4,64,128]{2,1,0:T(8,128)} custom-call(f32[8,8,128]{2,1,0:T(8,128)S(1)} %all-to-all-done.1.sums_ref, f32[8,128]{1,0:T(8,128)S(1)} %get-tuple-element.31.factor_ref.refs_4_.refs_1_, bf16[8,256,1024]{2,1,0:T(8,128)(2,1)} %get-tuple-element.28.exp_hbm.refs_5_.refs_2_, f32[8,128]{1,0:T(8,128)S(1)} %get-tuple-element.37.refs_0_), custom_call_target="tpu_custom_call" | custom-call | flops 4194304 | bytes 4194304 | tf_op jit(solution)/shard_map/columns/pallas_call | solution.py:700
  61.6 3.3 %all-to-all-start.2 = ((f32[4,64,128]{2,1,0:T(8,128)}), f32[4,64,128]{2,1,0:T(8,128)S(1)}, u32[]{:S(2)}, u32[]{:S(2)}) async-start(f32[4,64,128]{2,1,0:T(8,128)} %columns.2.refs_4_), calls=%async_computation.2 | async-start | bytes 262144 | tf_op jit(solution)/shard_map/all_to_all | solution.py:541
  64.9 2.9 %student_side.6 = (bf16[128,1024]{1,0:T(8,128)(2,1)S(1)}, f32[8,128]{1,0:T(8,128)S(1)}) custom-call(bf16[768,512]{1,0:T(8,128)(2,1)S(1)} %get-tuple-element.34.refs_6_.unit, bf16[128,1024]{1,0:T(8,128)(2,1)S(1)} %get-tuple-element.35.feat_ref, bf16[128,256]{1,0:T(8,128)(2,1)S(1)} %get-tuple-element.36.scaled_ref, ...), custom_call_target="tpu_custom_call" | custom-call | flops 1342177280 | bytes 1048576 | tf_op jit(solution)/shard_map/student_side/pallas_call | solution.py:665
  67.8 3.4 %all-to-all-done.2.refs_0_ = f32[4,64,128]{2,1,0:T(8,128)S(1)} async-done(((f32[4,64,128]{2,1,0:T(8,128)}), f32[4,64,128]{2,1,0:T(8,128)S(1)}, u32[]{:S(2)}, u32[]{:S(2)}) %all-to-all-start.2) | async-done | bytes 131104 | tf_op jit(solution)/shard_map/all_to_all | solution.py:541
  71.3 3.1 %rows.3.refs_4_ = f32[8,8,128]{2,1,0:T(8,128)} custom-call(f32[4,64,128]{2,1,0:T(8,128)S(1)} %all-to-all-done.2.refs_0_, f32[8,128]{1,0:T(8,128)S(1)} %get-tuple-element.31.factor_ref.refs_4_.refs_1_, bf16[8,256,1024]{2,1,0:T(8,128)(2,1)} %get-tuple-element.28.exp_hbm.refs_5_.refs_2_, f32[8,128]{1,0:T(8,128)S(1)} %get-tuple-element.38.refs_3_, ...), custom_call_target="tpu_custom_call" | custom-call | flops 4194304 | bytes 4194304 | tf_op jit(solution)/shard_map/rows/pallas_call | solution.py:687
  74.4 3.4 %all-to-all-start.3 = ((f32[8,8,128]{2,1,0:T(8,128)}), f32[8,8,128]{2,1,0:T(8,128)S(1)}, u32[]{:S(2)}, u32[]{:S(2)}) async-start(f32[8,8,128]{2,1,0:T(8,128)} %rows.3.refs_4_), calls=%async_computation.3 | async-start | bytes 65536 | tf_op jit(solution)/shard_map/all_to_all | solution.py:541
  77.7 2.9 %student_side.7 = (bf16[128,1024]{1,0:T(8,128)(2,1)S(1)}, f32[8,128]{1,0:T(8,128)S(1)}) custom-call(bf16[768,512]{1,0:T(8,128)(2,1)S(1)} %get-tuple-element.34.refs_6_.unit, bf16[128,1024]{1,0:T(8,128)(2,1)S(1)} %get-tuple-element.35.feat_ref, bf16[128,256]{1,0:T(8,128)(2,1)S(1)} %get-tuple-element.36.scaled_ref, ...), custom_call_target="tpu_custom_call" | custom-call | flops 1342177280 | bytes 1048576 | tf_op jit(solution)/shard_map/student_side/pallas_call | solution.py:665
  88.8 2.9 %student_side.8 = (bf16[128,1024]{1,0:T(8,128)(2,1)S(1)}, f32[8,128]{1,0:T(8,128)S(1)}) custom-call(bf16[768,512]{1,0:T(8,128)(2,1)S(1)} %get-tuple-element.34.refs_6_.unit, bf16[128,1024]{1,0:T(8,128)(2,1)S(1)} %get-tuple-element.35.feat_ref, bf16[128,256]{1,0:T(8,128)(2,1)S(1)} %get-tuple-element.36.scaled_ref, ...), custom_call_target="tpu_custom_call" | custom-call | flops 1342177280 | bytes 1048576 | tf_op jit(solution)/shard_map/student_side/pallas_call | solution.py:665
  92.4 17.7 %last_rows.1 = (bf16[8,768,1024]{2,1,0:T(8,128)(2,1)}, f32[64,128]{1,0:T(8,128)S(1)}, bf16[8,80,512]{2,1,0:T(8,128)(2,1)}) custom-call(f32[8,128]{1,0:T(8,128)S(1)} %get-tuple-element.31.factor_ref.refs_4_.refs_1_, bf16[256,512]{1,0:T(8,128)(2,1)} %s_hbm.3, f32[256,512]{1,0:T(8,128)} %copy-done, ...), custom_call_target="tpu_custom_call" | custom-call | flops 8589934592 | bytes 12582912 | tf_op jit(solution)/shard_map/last_rows/pallas_call | solution.py:718
  110.1 3.6 %all-to-all-start.4 = ((bf16[8,80,512]{2,1,0:T(8,128)(2,1)}), bf16[8,80,512]{2,1,0:T(8,128)(2,1)S(1)}, u32[]{:S(2)}, u32[]{:S(2)}) async-start(bf16[8,80,512]{2,1,0:T(8,128)(2,1)} %get-tuple-element.43.refs_4_), calls=%async_computation.4 | async-start | bytes 1310720 | tf_op jit(solution)/shard_map/all_to_all | solution.py:541
  113.6 7.4 %student_side.9 = (bf16[128,4096]{1,0:T(8,128)(2,1)S(1)}, f32[8,128]{1,0:T(8,128)S(1)}) custom-call(bf16[768,512]{1,0:T(8,128)(2,1)S(1)} %get-tuple-element.34.refs_6_.unit, bf16[128,1024]{1,0:T(8,128)(2,1)S(1)} %get-tuple-element.35.feat_ref, bf16[128,256]{1,0:T(8,128)(2,1)S(1)} %get-tuple-element.36.scaled_ref, ...), custom_call_target="tpu_custom_call" | custom-call | flops 5368709120 | bytes 4194304 | tf_op jit(solution)/shard_map/student_side/pallas_call | solution.py:665
  121.0 3.7 %all-to-all-done.4.message_ref = bf16[8,80,512]{2,1,0:T(8,128)(2,1)S(1)} async-done(((bf16[8,80,512]{2,1,0:T(8,128)(2,1)}), bf16[8,80,512]{2,1,0:T(8,128)(2,1)S(1)}, u32[]{:S(2)}, u32[]{:S(2)}) %all-to-all-start.4) | async-done | bytes 655392 | tf_op jit(solution)/shard_map/all_to_all | solution.py:541
  131.4 3.4 %all-to-all-start.5 = ((bf16[8,32,512]{2,1,0:T(8,128)(2,1)}), bf16[8,32,512]{2,1,0:T(8,128)(2,1)S(1)}, u32[]{:S(2)}, u32[]{:S(2)}) async-start(bf16[8,32,512]{2,1,0:T(8,128)(2,1)} %get-tuple-element.51), calls=%async_computation.5 | async-start | bytes 524288 | tf_op jit(solution)/shard_map/all_to_all | solution.py:541
  134.8 8.4 %weight_grads.1 = bf16[128,8192]{1,0:T(8,128)(2,1)} custom-call(bf16[8,256,1024]{2,1,0:T(8,128)(2,1)} %get-tuple-element.28.exp_hbm.refs_5_.refs_2_, bf16[8,768,1024]{2,1,0:T(8,128)(2,1)} %get-tuple-element.41.prob_hbm, bf16[128,1024]{1,0:T(8,128)(2,1)S(1)} %get-tuple-element.35.feat_ref, f32[64,128]{1,0:T(8,128)S(1)} %get-tuple-element.42.scale_ref, ...), custom_call_target="tpu_custom_call" | custom-call | flops 2147483648 | bytes 12582912 | tf_op jit(solution)/shard_map/weight_grads/pallas_call | solution.py:764
  (48 shorter events, 28.1 us)
Async XLA Ops:
  0.6 32.0 %collective-permute-start.2 = (bf16[256,512]{1,0:T(8,128)(2,1)}, bf16[256,512]{1,0:T(8,128)(2,1)S(1)}, u32[]{:S(2)}, u32[]{:S(2)}) collective-permute-start(bf16[256,512]{1,0:T(8,128)(2,1)} %s_hbm.3), channel_id=1, source_target_pairs={{0,1},{1,2},{2,3},{3,0},{4,5},{5,6},{6,7},{7,4},{8,9},{9,10},{10,1... | collective-permute-start | bytes 786440 | tf_op jit(solution)/shard_map/ppermute | solution.py:546
  3.7 28.9 %collective-permute-start.1 = (bf16[256,512]{1,0:T(8,128)(2,1)}, bf16[256,512]{1,0:T(8,128)(2,1)S(1)}, u32[]{:S(2)}, u32[]{:S(2)}) collective-permute-start(bf16[256,512]{1,0:T(8,128)(2,1)} %s_hbm.3), channel_id=1, source_target_pairs={{0,2},{1,3},{2,0},{3,1},{4,6},{5,7},{6,4},{7,5},{8,10},{9,11},{10,... | collective-permute-start | bytes 786440 | tf_op jit(solution)/shard_map/ppermute | solution.py:546
  6.3 26.3 %collective-permute-start = (bf16[256,512]{1,0:T(8,128)(2,1)}, bf16[256,512]{1,0:T(8,128)(2,1)S(1)}, u32[]{:S(2)}, u32[]{:S(2)}) collective-permute-start(bf16[256,512]{1,0:T(8,128)(2,1)} %s_hbm.3), channel_id=1, source_target_pairs={{0,3},{1,0},{2,1},{3,2},{4,7},{5,4},{6,5},{7,6},{8,11},{9,8},{10,9... | collective-permute-start | bytes 786440 | tf_op jit(solution)/shard_map/ppermute | solution.py:546
  23.3 9.3 %all-to-all-start = ((f32[8,8,128]{2,1,0:T(8,128)}), f32[8,8,128]{2,1,0:T(8,128)S(1)}, u32[]{:S(2)}, u32[]{:S(2)}) async-start(f32[8,8,128]{2,1,0:T(8,128)} %get-tuple-element.29.before_ref), calls=%async_computation | async-start | bytes 65536 | tf_op jit(solution)/shard_map/all_to_all | solution.py:541
  32.5 17.1 %copy-start = (f32[256,512]{1,0:T(8,128)}, f32[256,512]{1,0:T(8,128)S(1)}, u32[]{:S(2)}) copy-start(f32[256,512]{1,0:T(8,128)S(1)} %own_back.1.refs_0_.student_hbm) | copy-start | bytes 1572868
  32.5 6.9 %copy-start.1 = (bf16[256,512]{1,0:T(8,128)(2,1)S(1)}, bf16[256,512]{1,0:T(8,128)(2,1)}, u32[]{:S(2)}) copy-start(bf16[256,512]{1,0:T(8,128)(2,1)} %s_hbm.3) | copy-start | bytes 786436
  32.5 6.9 %copy-start.4 = (bf16[256,512]{1,0:T(8,128)(2,1)S(1)}, bf16[256,512]{1,0:T(8,128)(2,1)}, u32[]{:S(2)}) copy-start(bf16[256,512]{1,0:T(8,128)(2,1)} %t_ref.1) | copy-start | bytes 786436
  35.5 8.0 %collective-permute-start.8 = (f32[1,72,128]{2,1,0:T(8,128)S(1)}, f32[1,72,128]{2,1,0:T(8,128)S(1)}, u32[]{:S(2)}, u32[]{:S(2)}) collective-permute-start(f32[1,72,128]{2,1,0:T(8,128)S(1)} %get-tuple-element.32.refs_3_.refs_0_.logs_ref), channel_id=1, source_target_pairs={{0,1},{1,2},{2,3},{3,0},{4,5},{5,6},{6,7},{7,4},{8,9},{9,10},{10,1... | collective-permute-start | bytes 110600 | tf_op jit(solution)/shard_map/ppermute | solution.py:546
  36.3 10.2 %collective-permute-start.7 = (f32[1,72,128]{2,1,0:T(8,128)S(1)}, f32[1,72,128]{2,1,0:T(8,128)S(1)}, u32[]{:S(2)}, u32[]{:S(2)}) collective-permute-start(f32[1,72,128]{2,1,0:T(8,128)S(1)} %get-tuple-element.32.refs_3_.refs_0_.logs_ref), channel_id=1, source_target_pairs={{0,2},{1,3},{2,0},{3,1},{4,6},{5,7},{6,4},{7,5},{8,10},{9,11},{10,... | collective-permute-start | bytes 110600 | tf_op jit(solution)/shard_map/ppermute | solution.py:546
  36.6 9.9 %collective-permute-start.6 = (f32[1,72,128]{2,1,0:T(8,128)S(1)}, f32[1,72,128]{2,1,0:T(8,128)S(1)}, u32[]{:S(2)}, u32[]{:S(2)}) collective-permute-start(f32[1,72,128]{2,1,0:T(8,128)S(1)} %get-tuple-element.32.refs_3_.refs_0_.logs_ref), channel_id=1, source_target_pairs={{0,3},{1,0},{2,1},{3,2},{4,7},{5,4},{6,5},{7,6},{8,11},{9,8},{10,9... | collective-permute-start | bytes 110600 | tf_op jit(solution)/shard_map/ppermute | solution.py:546
  41.5 29.8 %collective-permute-start.5 = (bf16[256,512]{1,0:T(8,128)(2,1)}, bf16[256,512]{1,0:T(8,128)(2,1)S(1)}, u32[]{:S(2)}, u32[]{:S(2)}) collective-permute-start(bf16[256,512]{1,0:T(8,128)(2,1)} %get-tuple-element.33), channel_id=1, source_target_pairs={{0,1},{1,2},{2,3},{3,0},{4,5},{5,6},{6,7},{7,4},{8,9},{9,10},{10,1... | collective-permute-start | bytes 786440 | tf_op jit(solution)/shard_map/ppermute | solution.py:546
  42.1 29.2 %collective-permute-start.4 = (bf16[256,512]{1,0:T(8,128)(2,1)}, bf16[256,512]{1,0:T(8,128)(2,1)S(1)}, u32[]{:S(2)}, u32[]{:S(2)}) collective-permute-start(bf16[256,512]{1,0:T(8,128)(2,1)} %get-tuple-element.33), channel_id=1, source_target_pairs={{0,2},{1,3},{2,0},{3,1},{4,6},{5,7},{6,4},{7,5},{8,10},{9,11},{10,... | collective-permute-start | bytes 786440 | tf_op jit(solution)/shard_map/ppermute | solution.py:546
  43.5 27.7 %collective-permute-start.3 = (bf16[256,512]{1,0:T(8,128)(2,1)}, bf16[256,512]{1,0:T(8,128)(2,1)S(1)}, u32[]{:S(2)}, u32[]{:S(2)}) collective-permute-start(bf16[256,512]{1,0:T(8,128)(2,1)} %get-tuple-element.33), channel_id=1, source_target_pairs={{0,3},{1,0},{2,1},{3,2},{4,7},{5,4},{6,5},{7,6},{8,11},{9,8},{10,9... | collective-permute-start | bytes 786440 | tf_op jit(solution)/shard_map/ppermute | solution.py:546
  49.5 9.1 %all-to-all-start.1 = ((f32[8,8,128]{2,1,0:T(8,128)}), f32[8,8,128]{2,1,0:T(8,128)S(1)}, u32[]{:S(2)}, u32[]{:S(2)}) async-start(f32[8,8,128]{2,1,0:T(8,128)} %rows.2.refs_4_), calls=%async_computation.1 | async-start | bytes 65536 | tf_op jit(solution)/shard_map/all_to_all | solution.py:541
  61.6 9.7 %all-to-all-start.2 = ((f32[4,64,128]{2,1,0:T(8,128)}), f32[4,64,128]{2,1,0:T(8,128)S(1)}, u32[]{:S(2)}, u32[]{:S(2)}) async-start(f32[4,64,128]{2,1,0:T(8,128)} %columns.2.refs_4_), calls=%async_computation.2 | async-start | bytes 262144 | tf_op jit(solution)/shard_map/all_to_all | solution.py:541
  74.4 8.2 %all-to-all-start.3 = ((f32[8,8,128]{2,1,0:T(8,128)}), f32[8,8,128]{2,1,0:T(8,128)S(1)}, u32[]{:S(2)}, u32[]{:S(2)}) async-start(f32[8,8,128]{2,1,0:T(8,128)} %rows.3.refs_4_), calls=%async_computation.3 | async-start | bytes 65536 | tf_op jit(solution)/shard_map/all_to_all | solution.py:541
  84.9 7.5 %collective-permute-start.11 = (f32[1,64,128]{2,1,0:T(8,128)S(1)}, f32[1,64,128]{2,1,0:T(8,128)S(1)}, u32[]{:S(2)}, u32[]{:S(2)}) collective-permute-start(f32[1,64,128]{2,1,0:T(8,128)S(1)} %columns.3.refs_4_.refs_7_), channel_id=1, source_target_pairs={{0,1},{1,2},{2,3},{3,0},{4,5},{5,6},{6,7},{7,4},{8,9},{9,10},{10,1... | collective-permute-start | bytes 98312 | tf_op jit(solution)/shard_map/ppermute | solution.py:546
  85.8 6.6 %collective-permute-start.10 = (f32[1,64,128]{2,1,0:T(8,128)S(1)}, f32[1,64,128]{2,1,0:T(8,128)S(1)}, u32[]{:S(2)}, u32[]{:S(2)}) collective-permute-start(f32[1,64,128]{2,1,0:T(8,128)S(1)} %columns.3.refs_4_.refs_7_), channel_id=1, source_target_pairs={{0,2},{1,3},{2,0},{3,1},{4,6},{5,7},{6,4},{7,5},{8,10},{9,11},{10,... | collective-permute-start | bytes 98312 | tf_op jit(solution)/shard_map/ppermute | solution.py:546
  87.1 5.3 %collective-permute-start.9 = (f32[1,64,128]{2,1,0:T(8,128)S(1)}, f32[1,64,128]{2,1,0:T(8,128)S(1)}, u32[]{:S(2)}, u32[]{:S(2)}) collective-permute-start(f32[1,64,128]{2,1,0:T(8,128)S(1)} %columns.3.refs_4_.refs_7_), channel_id=1, source_target_pairs={{0,3},{1,0},{2,1},{3,2},{4,7},{5,4},{6,5},{7,6},{8,11},{9,8},{10,9... | collective-permute-start | bytes 98312 | tf_op jit(solution)/shard_map/ppermute | solution.py:546
  110.1 14.6 %all-to-all-start.4 = ((bf16[8,80,512]{2,1,0:T(8,128)(2,1)}), bf16[8,80,512]{2,1,0:T(8,128)(2,1)S(1)}, u32[]{:S(2)}, u32[]{:S(2)}) async-start(bf16[8,80,512]{2,1,0:T(8,128)(2,1)} %get-tuple-element.43.refs_4_), calls=%async_computation.4 | async-start | bytes 1310720 | tf_op jit(solution)/shard_map/all_to_all | solution.py:541
  126.9 16.3 %collective-permute-start.14 = (f32[8,128]{1,0:T(8,128)S(1)}, f32[8,128]{1,0:T(8,128)S(1)}, u32[]{:S(2)}, u32[]{:S(2)}) collective-permute-start(f32[8,128]{1,0:T(8,128)S(1)} %get-tuple-element.52), channel_id=1, source_target_pairs={{0,3},{1,2},{2,1},{3,0},{4,7},{5,6},{6,5},{7,4},{8,11},{9,10},{10,... | collective-permute-start | bytes 12296 | tf_op jit(solution)/shard_map/ppermute | solution.py:552
  129.1 14.1 %collective-permute-start.13 = (f32[8,128]{1,0:T(8,128)S(1)}, f32[8,128]{1,0:T(8,128)S(1)}, u32[]{:S(2)}, u32[]{:S(2)}) collective-permute-start(f32[8,128]{1,0:T(8,128)S(1)} %get-tuple-element.52), channel_id=1, source_target_pairs={{0,2},{1,3},{2,0},{3,1},{4,6},{5,7},{6,4},{7,5},{8,10},{9,11},{10,... | collective-permute-start | bytes 12296 | tf_op jit(solution)/shard_map/ppermute | solution.py:552
  129.3 13.9 %collective-permute-start.12 = (f32[8,128]{1,0:T(8,128)S(1)}, f32[8,128]{1,0:T(8,128)S(1)}, u32[]{:S(2)}, u32[]{:S(2)}) collective-permute-start(f32[8,128]{1,0:T(8,128)S(1)} %get-tuple-element.52), channel_id=1, source_target_pairs={{0,1},{1,0},{2,3},{3,2},{4,5},{5,4},{6,7},{7,6},{8,9},{9,8},{10,11... | collective-permute-start | bytes 12296 | tf_op jit(solution)/shard_map/ppermute | solution.py:552
  131.4 12.4 %all-to-all-start.5 = ((bf16[8,32,512]{2,1,0:T(8,128)(2,1)}), bf16[8,32,512]{2,1,0:T(8,128)(2,1)S(1)}, u32[]{:S(2)}, u32[]{:S(2)}) async-start(bf16[8,32,512]{2,1,0:T(8,128)(2,1)} %get-tuple-element.51), calls=%async_computation.5 | async-start | bytes 524288 | tf_op jit(solution)/shard_map/all_to_all | solution.py:541
  (2 other events, 1.4 us)

commit v7 on v6

--- a/solution.py
+++ b/solution.py
@@ -360,17 +360,19 @@
     return high, middle, (rest - middle.astype(F32)).astype(BF16)
 
 
-def last_kernel(groups, factor_ref, own_hbm, student_hbm, exp_hbm, w_hbm, *refs):
+def last_kernel(groups, factor_ref, own_hbm, student_hbm, exp_hbm, w_hbm, s_hbm, *refs):
     units, refs = refs[: groups - 1], refs[groups - 1 :]
     logs, cols, refs = refs[:groups], refs[groups : 2 * groups], refs[2 * groups :]
     (
         prob_hbm, scale_ref, out_ref, unit, lse, rows, own_rows, back, scaled, sums, prob_ref,
-        exp_ref, w_ref, own_ref, student_ref, prob_sem, exp_sem, w_sem, sem,
-    ) = refs[-19:]
+        exp_ref, w_ref, own_ref, student_ref, s_ref, prob_sem, exp_sem, w_sem, sem, s_sem,
+    ) = refs[-21:]
     w_loads, exp_loads = copies(w_hbm, w_ref, w_sem), copies(exp_hbm, exp_ref, exp_sem)
     late_loads = whole_copies([(own_hbm, own_ref), (student_hbm, student_ref)], sem)
+    half_chunks = s_ref.shape[0]
     start(w_loads, exp_loads)
     start(late_loads)
+    start(copies(s_hbm, s_ref, s_sem, exp_ref.shape[0] - half_chunks, 0, half_chunks))
     slots, others, _ = prob_ref.shape
     own, chunks = exp_ref.shape[1], exp_ref.shape[0]
     tiles = (own + others) // LANES
@@ -387,8 +389,7 @@
     def store(k):
         return pltpu.make_async_copy(prob_ref.at[lax.rem(k, slots)], prob_hbm.at[k], prob_sem.at[k])
 
-    @pl.loop(0, chunks)
-    def _(k):
+    def one_chunk(k):
         copy_of(w_hbm, w_ref, w_sem, k).wait()
         slot = lax.rem(k, slots)
         scale = chunk_scales(scale_ref, k)
@@ -412,11 +413,23 @@
         copy_of(exp_hbm, exp_ref, exp_sem, k).wait()
         add_row_sums(own_rows, exp_ref.at[k], scale)
 
+    @pl.loop(0, chunks - half_chunks)
+    def _(k):
+        one_chunk(k)
+
+    wait(late_loads)
+
+    @pl.loop(chunks - half_chunks, chunks)
+    def _(k):
+        one_chunk(k)
+        j = k - (chunks - half_chunks)
+        copy_of(s_hbm, s_ref, s_sem, j, chunks - half_chunks).wait()
+        student_ref[...] += nt_dot(s_ref[j], w_ref[:, columns_of(k)])
+
     sums[...] = jnp.zeros(sums.shape, F32)
     pack_rows(sums.at[:quarter], jnp.sum(own_rows[...], axis=1, keepdims=True))
     sums[:quarter, :] = sums[:quarter, :] * factor_ref[:quarter, :]
     pack_rows(sums.at[quarter:tiles], jnp.sum(rows[...], axis=1, keepdims=True))
-    wait(late_loads)
     half = unit_rows(own_ref[...])[0].astype(BF16).astype(F32)
     inner = jnp.sum(half * back[...], axis=1, keepdims=True)
     pack_rows(sums.at[tiles : tiles + quarter], inner)
@@ -577,6 +590,7 @@
     w_buffer = pltpu.VMEM((width, local_protos), BF16)
     exp_buffer = pltpu.VMEM((chunks, own, WIDE), BF16)
     sems = pltpu.SemaphoreType.DMA((chunks,))
+    half_chunks = chunks // 2
     log_protos = math.log2(protos)
     token = struct((8, LANES), F32)
 
@@ -619,7 +633,11 @@
         in_specs=[ANY] * 3,
         out_specs=VMEM,
         out_shape=struct((own, width), F32),
-        scratch_shapes=[exp_buffer, w_buffer, sems, sems],
+        scratch_shapes=[
+            pltpu.VMEM((half_chunks, own, WIDE), BF16),
+            pltpu.VMEM((width, half_chunks * WIDE), BF16),
+            sems, sems,
+        ],
         compiler_params=params(weight_bytes + exp_bytes),
         cost_estimate=cost(2 * own * width * local_protos, weight_bytes),
         name="own_back",
@@ -717,7 +735,7 @@
     message_shape = (parts, 2 * share + sum_rows, width)
     prob, col_scale, message = pl.pallas_call(
         functools.partial(last_kernel, groups),
-        in_specs=[VMEM] + [ANY] * 4 + [VMEM] * (3 * groups - 1) + [ANY],
+        in_specs=[VMEM] + [ANY] * 5 + [VMEM] * (3 * groups - 1) + [ANY],
         out_specs=[ANY, VMEM, VMEM],
         out_shape=[
             pltpu.HBM((chunks, others, WIDE), BF16),
@@ -737,14 +755,16 @@
             w_buffer,
             pltpu.VMEM((own, width), BF16),
             pltpu.VMEM((own, width), F32),
+            pltpu.VMEM((chunks - half_chunks, own, WIDE), BF16),
             sems, sems, sems,
             pltpu.SemaphoreType.DMA((2,)),
+            sems,
         ],
-        compiler_params=params(20 * 2**20 + weight_bytes + exp_bytes),
+        compiler_params=params(20 * 2**20 + weight_bytes + 2 * exp_bytes),
         cost_estimate=cost(2 * rows * width * local_protos, others_bytes),
         name="last_rows",
     )(
-        factor, student_rows, far(back_student), t_exp, weight, *t_all, *logs, *cols, done,
+        factor, student_rows, far(back_student), t_exp, weight, s_exp, *t_all, *logs, *cols, done,
     )
     done = student_piece(message)
     message = exchange(message, "proto")

time: 145 us -> 145 us (level)
    pallas_call x1, Pallas kernels: 5.47 us -> 3.9 us  [local(): pl.pallas_call(own_back_kernel, in_specs=[ANY] * 3, out_specs=VMEM, out_s...]
  transfers between devices with their start and end apart: 21 -> 21, of which waited for: 4 -> 5; matrix products, arithmetic and copies ran while one was open for 0% -> 0% of each run, Pallas kernels for 39% -> 38%
where the time goes in v7:
time: 145 us; the launch traced here: 144 us
  Pallas kernels  84.5 us (58%)
  starting transfers between devices  45 us (31%)
  waiting for transfers between devices  11.2 us (8%)
  local copies, waits for them, and re-layouts  1.92 us (1%)
    all_to_all x6, starting transfers between devices, exchange(): return lax.all_to_all(value, axis, 0, 0)  20.8 us
    ppermute x12, starting transfers between devices, following(): lax.ppermute(value, axis, [(i, (i - s) % n) for i in range(n)])  19.7 us
    pallas_call x1, Pallas kernels, local(): pl.pallas_call(functools.partial(last_kernel, groups), in_specs=[VMEM] +...  19.1 us
    pallas_call x5, Pallas kernels, student_piece(): pl.pallas_call(functools.partial(student_kernel, log_protos, first, group...  18.9 us
    pallas_call x1, Pallas kernels, local(): pl.pallas_call(stats_kernel, in_specs=[ANY] * 3, out_specs=[ANY, ANY, VME...  15.6 us
    all_to_all x6, waiting for transfers between devices, exchange(): return lax.all_to_all(value, axis, 0, 0)  11.1 us
    pallas_call x1, Pallas kernels, local(): pl.pallas_call(functools.partial(grad_kernel, counts, float(protos)), in_...  8.38 us
    pallas_call x2, Pallas kernels, local(): pl.pallas_call(functools.partial(row_kernel, len(cols)), in_specs=[VMEM]...  6.12 us
  transfers between devices with their start and end apart: 21, of which 5 were waited for; matrix products, arithmetic and copies ran while one was open for 0% of the time, Pallas kernels for 38%

profile of v7, /device:TPU:0, one launch (start us, length us, event | category | flops | bytes accessed | tf_op | source)
XLA Modules:
  0.0 144.4 jit_solution(7782227870472967972)
XLA Ops:
  0.6 3.1 %collective-permute-start.2 = (bf16[256,512]{1,0:T(8,128)(2,1)}, bf16[256,512]{1,0:T(8,128)(2,1)S(1)}, u32[]{:S(2)}, u32[]{:S(2)}) collective-permute-start(bf16[256,512]{1,0:T(8,128)(2,1)} %s_hbm.3), channel_id=1, source_target_pairs={{0,1},{1,2},{2,3},{3,0},{4,5},{5,6},{6,7},{7,4},{8,9},{9,10},{10,1... | collective-permute-start | bytes 786440 | tf_op jit(solution)/shard_map/ppermute | solution.py:559
  7.6 15.6 %own_rows.1 = (bf16[8,256,1024]{2,1,0:T(8,128)(2,1)}, bf16[8,256,1024]{2,1,0:T(8,128)(2,1)}, f32[8,8,128]{2,1,0:T(8,128)}) custom-call(bf16[256,512]{1,0:T(8,128)(2,1)} %t_ref.1, bf16[256,512]{1,0:T(8,128)(2,1)} %s_hbm.3, bf16[512,8192]{1,0:T(8,128)(2,1)} %w_hbm.15), custom_call_target="tpu_custom_call" | custom-call | flops 4294967296 | bytes 8388608 | tf_op jit(solution)/shard_map/own_rows/pallas_call | solution.py:605
  23.3 3.7 %all-to-all-start = ((f32[8,8,128]{2,1,0:T(8,128)}), f32[8,8,128]{2,1,0:T(8,128)S(1)}, u32[]{:S(2)}, u32[]{:S(2)}) async-start(f32[8,8,128]{2,1,0:T(8,128)} %get-tuple-element.29.before_ref), calls=%async_computation | async-start | bytes 65536 | tf_op jit(solution)/shard_map/all_to_all | solution.py:554
  27.0 3.9 %own_back.1.refs_0_.student_hbm = f32[256,512]{1,0:T(8,128)S(1)} custom-call(f32[8,8,128]{2,1,0:T(8,128)} %get-tuple-element.29.before_ref, bf16[8,256,1024]{2,1,0:T(8,128)(2,1)} %get-tuple-element.30.exp_hbm.s_hbm, bf16[512,8192]{1,0:T(8,128)(2,1)} %w_hbm.15), custom_call_target="tpu_custom_call" | custom-call | flops 2147483648 | bytes 8388608 | tf_op jit(solution)/shard_map/own_back/pallas_call | solution.py:631
  31.9 2.9 %first_columns.1 = (f32[8,128]{1,0:T(8,128)S(1)}, f32[1,72,128]{2,1,0:T(8,128)S(1)}) custom-call(s32[2]{0:T(128)S(1)} %pad_add_fusion.place_ref, f32[8,8,128]{2,1,0:T(8,128)S(1)} %all-to-all-done.stats_ref, bf16[8,256,1024]{2,1,0:T(8,128)(2,1)} %get-tuple-element.28.exp_hbm.refs_5_.refs_2_, f32[256,512]{1,0:T(8,128)S(1)} %own_back.1.refs_0_.student_hbm, ...), custom_call_target="tpu_custom_call" | custom-call | flops 4194304 | bytes 4194304 | tf_op jit(solution)/shard_map/first_columns/pallas_call | solution.py:649
  35.8 2.8 %collective-permute-start.6 = (f32[1,72,128]{2,1,0:T(8,128)S(1)}, f32[1,72,128]{2,1,0:T(8,128)S(1)}, u32[]{:S(2)}, u32[]{:S(2)}) collective-permute-start(f32[1,72,128]{2,1,0:T(8,128)S(1)} %get-tuple-element.32.refs_3_.refs_0_.logs_ref), channel_id=1, source_target_pairs={{0,3},{1,0},{2,1},{3,2},{4,7},{5,4},{6,5},{7,6},{8,11},{9,8},{10,9... | collective-permute-start | bytes 110600 | tf_op jit(solution)/shard_map/ppermute | solution.py:559
  42.8 2.9 %collective-permute-start.3 = (bf16[256,512]{1,0:T(8,128)(2,1)}, bf16[256,512]{1,0:T(8,128)(2,1)S(1)}, u32[]{:S(2)}, u32[]{:S(2)}) collective-permute-start(bf16[256,512]{1,0:T(8,128)(2,1)} %get-tuple-element.33), channel_id=1, source_target_pairs={{0,3},{1,0},{2,1},{3,2},{4,7},{5,4},{6,5},{7,6},{8,11},{9,8},{10,9... | collective-permute-start | bytes 786440 | tf_op jit(solution)/shard_map/ppermute | solution.py:559
  45.7 3.1 %rows.2.refs_4_ = f32[8,8,128]{2,1,0:T(8,128)} custom-call(f32[1,72,128]{2,1,0:T(8,128)S(1)} %get-tuple-element.32.refs_3_.refs_0_.logs_ref, f32[1,72,128]{2,1,0:T(8,128)S(1)} %collective-permute-done.6.refs_1_.refs_4_, f32[1,72,128]{2,1,0:T(8,128)S(1)} %collective-permute-done.7.refs_2_.refs_5_, f32[1,72,128]{2,1,0:T(8,128)S(1)} %collective-permute-done.8.refs_3_.refs_6_, ...), custom_call_target="tpu_custom_call" | custom-call | flops 4194304 | bytes 4194304 | tf_op jit(solution)/shard_map/rows/pallas_call | solution.py:705
  48.8 3.4 %all-to-all-start.1 = ((f32[8,8,128]{2,1,0:T(8,128)}), f32[8,8,128]{2,1,0:T(8,128)S(1)}, u32[]{:S(2)}, u32[]{:S(2)}) async-start(f32[8,8,128]{2,1,0:T(8,128)} %rows.2.refs_4_), calls=%async_computation.1 | async-start | bytes 65536 | tf_op jit(solution)/shard_map/all_to_all | solution.py:554
  52.2 2.9 %student_side.5 = (bf16[128,1024]{1,0:T(8,128)(2,1)S(1)}, f32[8,128]{1,0:T(8,128)S(1)}) custom-call(bf16[768,512]{1,0:T(8,128)(2,1)S(1)} %get-tuple-element.34.refs_6_.unit, bf16[128,1024]{1,0:T(8,128)(2,1)S(1)} %get-tuple-element.35.feat_ref, bf16[128,256]{1,0:T(8,128)(2,1)S(1)} %get-tuple-element.36.scaled_ref, ...), custom_call_target="tpu_custom_call" | custom-call | flops 1342177280 | bytes 1048576 | tf_op jit(solution)/shard_map/student_side/pallas_call | solution.py:683
  57.0 3.0 %columns.2.refs_4_ = f32[4,64,128]{2,1,0:T(8,128)} custom-call(f32[8,8,128]{2,1,0:T(8,128)S(1)} %all-to-all-done.1.sums_ref, f32[8,128]{1,0:T(8,128)S(1)} %get-tuple-element.31.factor_ref.refs_4_.refs_1_, bf16[8,256,1024]{2,1,0:T(8,128)(2,1)} %get-tuple-element.28.exp_hbm.refs_5_.refs_2_, f32[8,128]{1,0:T(8,128)S(1)} %get-tuple-element.37.refs_0_), custom_call_target="tpu_custom_call" | custom-call | flops 4194304 | bytes 4194304 | tf_op jit(solution)/shard_map/columns/pallas_call | solution.py:718
  60.0 3.3 %all-to-all-start.2 = ((f32[4,64,128]{2,1,0:T(8,128)}), f32[4,64,128]{2,1,0:T(8,128)S(1)}, u32[]{:S(2)}, u32[]{:S(2)}) async-start(f32[4,64,128]{2,1,0:T(8,128)} %columns.2.refs_4_), calls=%async_computation.2 | async-start | bytes 262144 | tf_op jit(solution)/shard_map/all_to_all | solution.py:554
  63.4 2.9 %student_side.6 = (bf16[128,1024]{1,0:T(8,128)(2,1)S(1)}, f32[8,128]{1,0:T(8,128)S(1)}) custom-call(bf16[768,512]{1,0:T(8,128)(2,1)S(1)} %get-tuple-element.34.refs_6_.unit, bf16[128,1024]{1,0:T(8,128)(2,1)S(1)} %get-tuple-element.35.feat_ref, bf16[128,256]{1,0:T(8,128)(2,1)S(1)} %get-tuple-element.36.scaled_ref, ...), custom_call_target="tpu_custom_call" | custom-call | flops 1342177280 | bytes 1048576 | tf_op jit(solution)/shard_map/student_side/pallas_call | solution.py:683
  66.3 3.4 %all-to-all-done.2.refs_0_ = f32[4,64,128]{2,1,0:T(8,128)S(1)} async-done(((f32[4,64,128]{2,1,0:T(8,128)}), f32[4,64,128]{2,1,0:T(8,128)S(1)}, u32[]{:S(2)}, u32[]{:S(2)}) %all-to-all-start.2) | async-done | bytes 131104 | tf_op jit(solution)/shard_map/all_to_all | solution.py:554
  69.7 3.1 %rows.3.refs_4_ = f32[8,8,128]{2,1,0:T(8,128)} custom-call(f32[4,64,128]{2,1,0:T(8,128)S(1)} %all-to-all-done.2.refs_0_, f32[8,128]{1,0:T(8,128)S(1)} %get-tuple-element.31.factor_ref.refs_4_.refs_1_, bf16[8,256,1024]{2,1,0:T(8,128)(2,1)} %get-tuple-element.28.exp_hbm.refs_5_.refs_2_, f32[8,128]{1,0:T(8,128)S(1)} %get-tuple-element.38.refs_3_, ...), custom_call_target="tpu_custom_call" | custom-call | flops 4194304 | bytes 4194304 | tf_op jit(solution)/shard_map/rows/pallas_call | solution.py:705
  72.8 3.4 %all-to-all-start.3 = ((f32[8,8,128]{2,1,0:T(8,128)}), f32[8,8,128]{2,1,0:T(8,128)S(1)}, u32[]{:S(2)}, u32[]{:S(2)}) async-start(f32[8,8,128]{2,1,0:T(8,128)} %rows.3.refs_4_), calls=%async_computation.3 | async-start | bytes 65536 | tf_op jit(solution)/shard_map/all_to_all | solution.py:554
  76.1 2.9 %student_side.7 = (bf16[128,1024]{1,0:T(8,128)(2,1)S(1)}, f32[8,128]{1,0:T(8,128)S(1)}) custom-call(bf16[768,512]{1,0:T(8,128)(2,1)S(1)} %get-tuple-element.34.refs_6_.unit, bf16[128,1024]{1,0:T(8,128)(2,1)S(1)} %get-tuple-element.35.feat_ref, bf16[128,256]{1,0:T(8,128)(2,1)S(1)} %get-tuple-element.36.scaled_ref, ...), custom_call_target="tpu_custom_call" | custom-call | flops 1342177280 | bytes 1048576 | tf_op jit(solution)/shard_map/student_side/pallas_call | solution.py:683
  87.2 2.9 %student_side.8 = (bf16[128,1024]{1,0:T(8,128)(2,1)S(1)}, f32[8,128]{1,0:T(8,128)S(1)}) custom-call(bf16[768,512]{1,0:T(8,128)(2,1)S(1)} %get-tuple-element.34.refs_6_.unit, bf16[128,1024]{1,0:T(8,128)(2,1)S(1)} %get-tuple-element.35.feat_ref, bf16[128,256]{1,0:T(8,128)(2,1)S(1)} %get-tuple-element.36.scaled_ref, ...), custom_call_target="tpu_custom_call" | custom-call | flops 1342177280 | bytes 1048576 | tf_op jit(solution)/shard_map/student_side/pallas_call | solution.py:683
  90.8 19.1 %last_rows.1 = (bf16[8,768,1024]{2,1,0:T(8,128)(2,1)}, f32[64,128]{1,0:T(8,128)S(1)}, bf16[8,80,512]{2,1,0:T(8,128)(2,1)}) custom-call(f32[8,128]{1,0:T(8,128)S(1)} %get-tuple-element.31.factor_ref.refs_4_.refs_1_, bf16[256,512]{1,0:T(8,128)(2,1)} %s_hbm.3, f32[256,512]{1,0:T(8,128)} %copy-done, ...), custom_call_target="tpu_custom_call" | custom-call | flops 8589934592 | bytes 12582912 | tf_op jit(solution)/shard_map/last_rows/pallas_call | solution.py:736
  109.9 3.6 %all-to-all-start.4 = ((bf16[8,80,512]{2,1,0:T(8,128)(2,1)}), bf16[8,80,512]{2,1,0:T(8,128)(2,1)S(1)}, u32[]{:S(2)}, u32[]{:S(2)}) async-start(bf16[8,80,512]{2,1,0:T(8,128)(2,1)} %get-tuple-element.43.refs_4_), calls=%async_computation.4 | async-start | bytes 1310720 | tf_op jit(solution)/shard_map/all_to_all | solution.py:554
  113.4 7.4 %student_side.9 = (bf16[128,4096]{1,0:T(8,128)(2,1)S(1)}, f32[8,128]{1,0:T(8,128)S(1)}) custom-call(bf16[768,512]{1,0:T(8,128)(2,1)S(1)} %get-tuple-element.34.refs_6_.unit, bf16[128,1024]{1,0:T(8,128)(2,1)S(1)} %get-tuple-element.35.feat_ref, bf16[128,256]{1,0:T(8,128)(2,1)S(1)} %get-tuple-element.36.scaled_ref, ...), custom_call_target="tpu_custom_call" | custom-call | flops 5368709120 | bytes 4194304 | tf_op jit(solution)/shard_map/student_side/pallas_call | solution.py:683
  120.8 3.7 %all-to-all-done.4.message_ref = bf16[8,80,512]{2,1,0:T(8,128)(2,1)S(1)} async-done(((bf16[8,80,512]{2,1,0:T(8,128)(2,1)}), bf16[8,80,512]{2,1,0:T(8,128)(2,1)S(1)}, u32[]{:S(2)}, u32[]{:S(2)}) %all-to-all-start.4) | async-done | bytes 655392 | tf_op jit(solution)/shard_map/all_to_all | solution.py:554
  131.2 3.4 %all-to-all-start.5 = ((bf16[8,32,512]{2,1,0:T(8,128)(2,1)}), bf16[8,32,512]{2,1,0:T(8,128)(2,1)S(1)}, u32[]{:S(2)}, u32[]{:S(2)}) async-start(bf16[8,32,512]{2,1,0:T(8,128)(2,1)} %get-tuple-element.51), calls=%async_computation.5 | async-start | bytes 524288 | tf_op jit(solution)/shard_map/all_to_all | solution.py:554
  134.6 8.4 %weight_grads.1 = bf16[128,8192]{1,0:T(8,128)(2,1)} custom-call(bf16[8,256,1024]{2,1,0:T(8,128)(2,1)} %get-tuple-element.28.exp_hbm.refs_5_.refs_2_, bf16[8,768,1024]{2,1,0:T(8,128)(2,1)} %get-tuple-element.41.prob_hbm, bf16[128,1024]{1,0:T(8,128)(2,1)S(1)} %get-tuple-element.35.feat_ref, f32[64,128]{1,0:T(8,128)S(1)} %get-tuple-element.42.scale_ref, ...), custom_call_target="tpu_custom_call" | custom-call | flops 2147483648 | bytes 12582912 | tf_op jit(solution)/shard_map/weight_grads/pallas_call | solution.py:784
  (48 shorter events, 28.9 us)
Async XLA Ops:
  0.6 31.2 %collective-permute-start.2 = (bf16[256,512]{1,0:T(8,128)(2,1)}, bf16[256,512]{1,0:T(8,128)(2,1)S(1)}, u32[]{:S(2)}, u32[]{:S(2)}) collective-permute-start(bf16[256,512]{1,0:T(8,128)(2,1)} %s_hbm.3), channel_id=1, source_target_pairs={{0,1},{1,2},{2,3},{3,0},{4,5},{5,6},{6,7},{7,4},{8,9},{9,10},{10,1... | collective-permute-start | bytes 786440 | tf_op jit(solution)/shard_map/ppermute | solution.py:559
  3.7 28.1 %collective-permute-start.1 = (bf16[256,512]{1,0:T(8,128)(2,1)}, bf16[256,512]{1,0:T(8,128)(2,1)S(1)}, u32[]{:S(2)}, u32[]{:S(2)}) collective-permute-start(bf16[256,512]{1,0:T(8,128)(2,1)} %s_hbm.3), channel_id=1, source_target_pairs={{0,2},{1,3},{2,0},{3,1},{4,6},{5,7},{6,4},{7,5},{8,10},{9,11},{10,... | collective-permute-start | bytes 786440 | tf_op jit(solution)/shard_map/ppermute | solution.py:559
  6.3 25.6 %collective-permute-start = (bf16[256,512]{1,0:T(8,128)(2,1)}, bf16[256,512]{1,0:T(8,128)(2,1)S(1)}, u32[]{:S(2)}, u32[]{:S(2)}) collective-permute-start(bf16[256,512]{1,0:T(8,128)(2,1)} %s_hbm.3), channel_id=1, source_target_pairs={{0,3},{1,0},{2,1},{3,2},{4,7},{5,4},{6,5},{7,6},{8,11},{9,8},{10,9... | collective-permute-start | bytes 786440 | tf_op jit(solution)/shard_map/ppermute | solution.py:559
  23.3 8.6 %all-to-all-start = ((f32[8,8,128]{2,1,0:T(8,128)}), f32[8,8,128]{2,1,0:T(8,128)S(1)}, u32[]{:S(2)}, u32[]{:S(2)}) async-start(f32[8,8,128]{2,1,0:T(8,128)} %get-tuple-element.29.before_ref), calls=%async_computation | async-start | bytes 65536 | tf_op jit(solution)/shard_map/all_to_all | solution.py:554
  30.9 17.9 %copy-start = (f32[256,512]{1,0:T(8,128)}, f32[256,512]{1,0:T(8,128)S(1)}, u32[]{:S(2)}) copy-start(f32[256,512]{1,0:T(8,128)S(1)} %own_back.1.refs_0_.student_hbm) | copy-start | bytes 1572868
  30.9 7.7 %copy-start.1 = (bf16[256,512]{1,0:T(8,128)(2,1)S(1)}, bf16[256,512]{1,0:T(8,128)(2,1)}, u32[]{:S(2)}) copy-start(bf16[256,512]{1,0:T(8,128)(2,1)} %s_hbm.3) | copy-start | bytes 786436
  30.9 7.7 %copy-start.4 = (bf16[256,512]{1,0:T(8,128)(2,1)S(1)}, bf16[256,512]{1,0:T(8,128)(2,1)}, u32[]{:S(2)}) copy-start(bf16[256,512]{1,0:T(8,128)(2,1)} %t_ref.1) | copy-start | bytes 786436
  34.8 8.0 %collective-permute-start.8 = (f32[1,72,128]{2,1,0:T(8,128)S(1)}, f32[1,72,128]{2,1,0:T(8,128)S(1)}, u32[]{:S(2)}, u32[]{:S(2)}) collective-permute-start(f32[1,72,128]{2,1,0:T(8,128)S(1)} %get-tuple-element.32.refs_3_.refs_0_.logs_ref), channel_id=1, source_target_pairs={{0,1},{1,2},{2,3},{3,0},{4,5},{5,6},{6,7},{7,4},{8,9},{9,10},{10,1... | collective-permute-start | bytes 110600 | tf_op jit(solution)/shard_map/ppermute | solution.py:559
  35.5 10.2 %collective-permute-start.7 = (f32[1,72,128]{2,1,0:T(8,128)S(1)}, f32[1,72,128]{2,1,0:T(8,128)S(1)}, u32[]{:S(2)}, u32[]{:S(2)}) collective-permute-start(f32[1,72,128]{2,1,0:T(8,128)S(1)} %get-tuple-element.32.refs_3_.refs_0_.logs_ref), channel_id=1, source_target_pairs={{0,2},{1,3},{2,0},{3,1},{4,6},{5,7},{6,4},{7,5},{8,10},{9,11},{10,... | collective-permute-start | bytes 110600 | tf_op jit(solution)/shard_map/ppermute | solution.py:559
  35.8 9.9 %collective-permute-start.6 = (f32[1,72,128]{2,1,0:T(8,128)S(1)}, f32[1,72,128]{2,1,0:T(8,128)S(1)}, u32[]{:S(2)}, u32[]{:S(2)}) collective-permute-start(f32[1,72,128]{2,1,0:T(8,128)S(1)} %get-tuple-element.32.refs_3_.refs_0_.logs_ref), channel_id=1, source_target_pairs={{0,3},{1,0},{2,1},{3,2},{4,7},{5,4},{6,5},{7,6},{8,11},{9,8},{10,9... | collective-permute-start | bytes 110600 | tf_op jit(solution)/shard_map/ppermute | solution.py:559
  40.7 29.0 %collective-permute-start.5 = (bf16[256,512]{1,0:T(8,128)(2,1)}, bf16[256,512]{1,0:T(8,128)(2,1)S(1)}, u32[]{:S(2)}, u32[]{:S(2)}) collective-permute-start(bf16[256,512]{1,0:T(8,128)(2,1)} %get-tuple-element.33), channel_id=1, source_target_pairs={{0,1},{1,2},{2,3},{3,0},{4,5},{5,6},{6,7},{7,4},{8,9},{9,10},{10,1... | collective-permute-start | bytes 786440 | tf_op jit(solution)/shard_map/ppermute | solution.py:559
  41.3 28.4 %collective-permute-start.4 = (bf16[256,512]{1,0:T(8,128)(2,1)}, bf16[256,512]{1,0:T(8,128)(2,1)S(1)}, u32[]{:S(2)}, u32[]{:S(2)}) collective-permute-start(bf16[256,512]{1,0:T(8,128)(2,1)} %get-tuple-element.33), channel_id=1, source_target_pairs={{0,2},{1,3},{2,0},{3,1},{4,6},{5,7},{6,4},{7,5},{8,10},{9,11},{10,... | collective-permute-start | bytes 786440 | tf_op jit(solution)/shard_map/ppermute | solution.py:559
  42.8 26.9 %collective-permute-start.3 = (bf16[256,512]{1,0:T(8,128)(2,1)}, bf16[256,512]{1,0:T(8,128)(2,1)S(1)}, u32[]{:S(2)}, u32[]{:S(2)}) collective-permute-start(bf16[256,512]{1,0:T(8,128)(2,1)} %get-tuple-element.33), channel_id=1, source_target_pairs={{0,3},{1,0},{2,1},{3,2},{4,7},{5,4},{6,5},{7,6},{8,11},{9,8},{10,9... | collective-permute-start | bytes 786440 | tf_op jit(solution)/shard_map/ppermute | solution.py:559
  48.8 8.2 %all-to-all-start.1 = ((f32[8,8,128]{2,1,0:T(8,128)}), f32[8,8,128]{2,1,0:T(8,128)S(1)}, u32[]{:S(2)}, u32[]{:S(2)}) async-start(f32[8,8,128]{2,1,0:T(8,128)} %rows.2.refs_4_), calls=%async_computation.1 | async-start | bytes 65536 | tf_op jit(solution)/shard_map/all_to_all | solution.py:554
  60.0 9.7 %all-to-all-start.2 = ((f32[4,64,128]{2,1,0:T(8,128)}), f32[4,64,128]{2,1,0:T(8,128)S(1)}, u32[]{:S(2)}, u32[]{:S(2)}) async-start(f32[4,64,128]{2,1,0:T(8,128)} %columns.2.refs_4_), calls=%async_computation.2 | async-start | bytes 262144 | tf_op jit(solution)/shard_map/all_to_all | solution.py:554
  72.8 8.2 %all-to-all-start.3 = ((f32[8,8,128]{2,1,0:T(8,128)}), f32[8,8,128]{2,1,0:T(8,128)S(1)}, u32[]{:S(2)}, u32[]{:S(2)}) async-start(f32[8,8,128]{2,1,0:T(8,128)} %rows.3.refs_4_), calls=%async_computation.3 | async-start | bytes 65536 | tf_op jit(solution)/shard_map/all_to_all | solution.py:554
  83.3 7.5 %collective-permute-start.11 = (f32[1,64,128]{2,1,0:T(8,128)S(1)}, f32[1,64,128]{2,1,0:T(8,128)S(1)}, u32[]{:S(2)}, u32[]{:S(2)}) collective-permute-start(f32[1,64,128]{2,1,0:T(8,128)S(1)} %columns.3.refs_4_.refs_7_), channel_id=1, source_target_pairs={{0,1},{1,2},{2,3},{3,0},{4,5},{5,6},{6,7},{7,4},{8,9},{9,10},{10,1... | collective-permute-start | bytes 98312 | tf_op jit(solution)/shard_map/ppermute | solution.py:559
  84.2 6.6 %collective-permute-start.10 = (f32[1,64,128]{2,1,0:T(8,128)S(1)}, f32[1,64,128]{2,1,0:T(8,128)S(1)}, u32[]{:S(2)}, u32[]{:S(2)}) collective-permute-start(f32[1,64,128]{2,1,0:T(8,128)S(1)} %columns.3.refs_4_.refs_7_), channel_id=1, source_target_pairs={{0,2},{1,3},{2,0},{3,1},{4,6},{5,7},{6,4},{7,5},{8,10},{9,11},{10,... | collective-permute-start | bytes 98312 | tf_op jit(solution)/shard_map/ppermute | solution.py:559
  85.5 5.3 %collective-permute-start.9 = (f32[1,64,128]{2,1,0:T(8,128)S(1)}, f32[1,64,128]{2,1,0:T(8,128)S(1)}, u32[]{:S(2)}, u32[]{:S(2)}) collective-permute-start(f32[1,64,128]{2,1,0:T(8,128)S(1)} %columns.3.refs_4_.refs_7_), channel_id=1, source_target_pairs={{0,3},{1,0},{2,1},{3,2},{4,7},{5,4},{6,5},{7,6},{8,11},{9,8},{10,9... | collective-permute-start | bytes 98312 | tf_op jit(solution)/shard_map/ppermute | solution.py:559
  109.9 14.6 %all-to-all-start.4 = ((bf16[8,80,512]{2,1,0:T(8,128)(2,1)}), bf16[8,80,512]{2,1,0:T(8,128)(2,1)S(1)}, u32[]{:S(2)}, u32[]{:S(2)}) async-start(bf16[8,80,512]{2,1,0:T(8,128)(2,1)} %get-tuple-element.43.refs_4_), calls=%async_computation.4 | async-start | bytes 1310720 | tf_op jit(solution)/shard_map/all_to_all | solution.py:554
  126.7 16.3 %collective-permute-start.14 = (f32[8,128]{1,0:T(8,128)S(1)}, f32[8,128]{1,0:T(8,128)S(1)}, u32[]{:S(2)}, u32[]{:S(2)}) collective-permute-start(f32[8,128]{1,0:T(8,128)S(1)} %get-tuple-element.52), channel_id=1, source_target_pairs={{0,3},{1,2},{2,1},{3,0},{4,7},{5,6},{6,5},{7,4},{8,11},{9,10},{10,... | collective-permute-start | bytes 12296 | tf_op jit(solution)/shard_map/ppermute | solution.py:565
  128.9 14.1 %collective-permute-start.13 = (f32[8,128]{1,0:T(8,128)S(1)}, f32[8,128]{1,0:T(8,128)S(1)}, u32[]{:S(2)}, u32[]{:S(2)}) collective-permute-start(f32[8,128]{1,0:T(8,128)S(1)} %get-tuple-element.52), channel_id=1, source_target_pairs={{0,2},{1,3},{2,0},{3,1},{4,6},{5,7},{6,4},{7,5},{8,10},{9,11},{10,... | collective-permute-start | bytes 12296 | tf_op jit(solution)/shard_map/ppermute | solution.py:565
  129.1 13.9 %collective-permute-start.12 = (f32[8,128]{1,0:T(8,128)S(1)}, f32[8,128]{1,0:T(8,128)S(1)}, u32[]{:S(2)}, u32[]{:S(2)}) collective-permute-start(f32[8,128]{1,0:T(8,128)S(1)} %get-tuple-element.52), channel_id=1, source_target_pairs={{0,1},{1,0},{2,3},{3,2},{4,5},{5,4},{6,7},{7,6},{8,9},{9,8},{10,11... | collective-permute-start | bytes 12296 | tf_op jit(solution)/shard_map/ppermute | solution.py:565
  131.2 12.4 %all-to-all-start.5 = ((bf16[8,32,512]{2,1,0:T(8,128)(2,1)}), bf16[8,32,512]{2,1,0:T(8,128)(2,1)S(1)}, u32[]{:S(2)}, u32[]{:S(2)}) async-start(bf16[8,32,512]{2,1,0:T(8,128)(2,1)} %get-tuple-element.51), calls=%async_computation.5 | async-start | bytes 524288 | tf_op jit(solution)/shard_map/all_to_all | solution.py:554
  (2 other events, 1.4 us)

commit v8 on v6

--- a/solution.py
+++ b/solution.py
@@ -17,7 +17,7 @@
 LANES = 128
 WIDE = 1024
 TILE = 256
-FAR = (2, 3)
+FAR = (2,)
 F32 = jnp.float32
 BF16 = jnp.bfloat16
 
@@ -656,7 +656,7 @@
     cols = [cols] + following(cols, "batch")
     logs = cols
 
-    counts = [c * chunks // 8 for c in (1, 1, 1, 1, 4)]
+    counts = [c * chunks // 8 for c in (1, 1, 1, 5)]
     grad_parts = []
 
     def student_piece(before):
@@ -707,7 +707,8 @@
             cost_estimate=cost(2 * own * local_protos, exp_bytes),
             name="columns",
         )(sums, factor, t_exp, done)
-        done = student_piece(cols)
+        if turn < SWEEPS - 2:
+            done = student_piece(cols)
         if middle:
             cols = [exchange(cols, "batch")]
         else:

time: 145 us -> 145 us (level)
  Pallas kernels: 84.7 us -> 83.1 us
    ppermute x12, waiting for transfers between devices: 0.03 us -> 2.85 us  [following(): lax.ppermute(value, axis, [(i, (i - s) % n) for i in range(n)])]
    all_to_all x6, waiting for transfers between devices: 10.3 us -> 7.9 us  [exchange(): return lax.all_to_all(value, axis, 0, 0)]
    pallas_call x5 -> x4, Pallas kernels: 18.9 us -> 17.5 us  [student_piece(): pl.pallas_call(functools.partial(student_kernel, log_protos, first, group...]
  transfers between devices with their start and end apart: 21 -> 21, of which waited for: 4 -> 6; matrix products, arithmetic and copies ran while one was open for 0% -> 0% of each run, Pallas kernels for 39% -> 38%
where the time goes in v8:
time: 145 us
  Pallas kernels  83.1 us (57%)
  starting transfers between devices  46 us (32%)
  waiting for transfers between devices  10.8 us (7%)
  local copies, waits for them, and re-layouts  2.86 us (2%)
    all_to_all x6, starting transfers between devices, exchange(): return lax.all_to_all(value, axis, 0, 0)  21.8 us
    ppermute x12, starting transfers between devices, following(): lax.ppermute(value, axis, [(i, (i - s) % n) for i in range(n)])  19.8 us
    pallas_call x1, Pallas kernels, local(): pl.pallas_call(functools.partial(last_kernel, groups), in_specs=[VMEM] +...  17.7 us
    pallas_call x4, Pallas kernels, student_piece(): pl.pallas_call(functools.partial(student_kernel, log_protos, first, group...  17.5 us
    pallas_call x1, Pallas kernels, local(): pl.pallas_call(stats_kernel, in_specs=[ANY] * 3, out_specs=[ANY, ANY, VME...  15.6 us
    pallas_call x1, Pallas kernels, local(): pl.pallas_call(functools.partial(grad_kernel, counts, float(protos)), in_...  8.76 us
    all_to_all x6, waiting for transfers between devices, exchange(): return lax.all_to_all(value, axis, 0, 0)  7.9 us
    pallas_call x2, Pallas kernels, local(): pl.pallas_call(functools.partial(row_kernel, len(cols)), in_specs=[VMEM]...  6.13 us
  transfers between devices with their start and end apart: 21, of which 6 were waited for; matrix products, arithmetic and copies ran while one was open for 0% of the time, Pallas kernels for 38%

profile of v8, /device:TPU:0, one launch (start us, length us, event | category | flops | bytes accessed | tf_op | source)
XLA Modules:
  0.0 144.6 jit_solution(14999296862401048193)
XLA Ops:
  0.6 3.1 %collective-permute-start.2 = (bf16[256,512]{1,0:T(8,128)(2,1)}, bf16[256,512]{1,0:T(8,128)(2,1)S(1)}, u32[]{:S(2)}, u32[]{:S(2)}) collective-permute-start(bf16[256,512]{1,0:T(8,128)(2,1)} %s_hbm.3), channel_id=1, source_target_pairs={{0,1},{1,2},{2,3},{3,0},{4,5},{5,6},{6,7},{7,4},{8,9},{9,10},{10,1... | collective-permute-start | bytes 786440 | tf_op jit(solution)/shard_map/ppermute | solution.py:546
  3.7 2.6 %collective-permute-start.1 = (bf16[256,512]{1,0:T(8,128)(2,1)}, bf16[256,512]{1,0:T(8,128)(2,1)S(1)}, u32[]{:S(2)}, u32[]{:S(2)}) collective-permute-start(bf16[256,512]{1,0:T(8,128)(2,1)} %s_hbm.3), channel_id=1, source_target_pairs={{0,2},{1,3},{2,0},{3,1},{4,6},{5,7},{6,4},{7,5},{8,10},{9,11},{10,... | collective-permute-start | bytes 786440 | tf_op jit(solution)/shard_map/ppermute | solution.py:546
  7.6 15.6 %own_rows.1 = (bf16[8,256,1024]{2,1,0:T(8,128)(2,1)}, bf16[8,256,1024]{2,1,0:T(8,128)(2,1)}, f32[8,8,128]{2,1,0:T(8,128)}) custom-call(bf16[256,512]{1,0:T(8,128)(2,1)} %t_ref.1, bf16[256,512]{1,0:T(8,128)(2,1)} %s_hbm.3, bf16[512,8192]{1,0:T(8,128)(2,1)} %w_hbm.13), custom_call_target="tpu_custom_call" | custom-call | flops 4294967296 | bytes 8388608 | tf_op jit(solution)/shard_map/own_rows/pallas_call | solution.py:591
  23.3 3.7 %all-to-all-start = ((f32[8,8,128]{2,1,0:T(8,128)}), f32[8,8,128]{2,1,0:T(8,128)S(1)}, u32[]{:S(2)}, u32[]{:S(2)}) async-start(f32[8,8,128]{2,1,0:T(8,128)} %get-tuple-element.27.before_ref), calls=%async_computation | async-start | bytes 65536 | tf_op jit(solution)/shard_map/all_to_all | solution.py:541
  27.0 5.5 %own_back.1.refs_0_.student_hbm = f32[256,512]{1,0:T(8,128)S(1)} custom-call(f32[8,8,128]{2,1,0:T(8,128)} %get-tuple-element.27.before_ref, bf16[8,256,1024]{2,1,0:T(8,128)(2,1)} %get-tuple-element.28.exp_hbm, bf16[512,8192]{1,0:T(8,128)(2,1)} %w_hbm.13), custom_call_target="tpu_custom_call" | custom-call | flops 2147483648 | bytes 8388608 | tf_op jit(solution)/shard_map/own_back/pallas_call | solution.py:617
  32.6 2.9 %first_columns.1 = (f32[8,128]{1,0:T(8,128)S(1)}, f32[1,72,128]{2,1,0:T(8,128)S(1)}) custom-call(s32[2]{0:T(128)S(1)} %pad_add_fusion.place_ref, f32[8,8,128]{2,1,0:T(8,128)S(1)} %all-to-all-done.stats_ref, bf16[8,256,1024]{2,1,0:T(8,128)(2,1)} %get-tuple-element.26.exp_hbm.refs_5_.refs_2_, f32[256,512]{1,0:T(8,128)S(1)} %own_back.1.refs_0_.student_hbm, ...), custom_call_target="tpu_custom_call" | custom-call | flops 4194304 | bytes 4194304 | tf_op jit(solution)/shard_map/first_columns/pallas_call | solution.py:631
  36.6 2.8 %collective-permute-start.6 = (f32[1,72,128]{2,1,0:T(8,128)S(1)}, f32[1,72,128]{2,1,0:T(8,128)S(1)}, u32[]{:S(2)}, u32[]{:S(2)}) collective-permute-start(f32[1,72,128]{2,1,0:T(8,128)S(1)} %get-tuple-element.30.refs_3_.refs_0_.logs_ref), channel_id=1, source_target_pairs={{0,3},{1,0},{2,1},{3,2},{4,7},{5,4},{6,5},{7,6},{8,11},{9,8},{10,9... | collective-permute-start | bytes 110600 | tf_op jit(solution)/shard_map/ppermute | solution.py:546
  43.1 2.8 %collective-permute-start.3 = (bf16[256,512]{1,0:T(8,128)(2,1)S(1)}, bf16[256,512]{1,0:T(8,128)(2,1)S(1)}, u32[]{:S(2)}, u32[]{:S(2)}) collective-permute-start(bf16[256,512]{1,0:T(8,128)(2,1)S(1)} %get-tuple-element.31), channel_id=1, source_target_pairs={{0,3},{1,0},{2,1},{3,2},{4,7},{5,4},{6,5},{7,6},{8,11},{9,8},{10,9... | collective-permute-start | bytes 786440 | tf_op jit(solution)/shard_map/ppermute | solution.py:546
  45.9 3.1 %rows.2.refs_4_ = f32[8,8,128]{2,1,0:T(8,128)} custom-call(f32[1,72,128]{2,1,0:T(8,128)S(1)} %get-tuple-element.30.refs_3_.refs_0_.logs_ref, f32[1,72,128]{2,1,0:T(8,128)S(1)} %collective-permute-done.6.refs_1_.refs_4_, f32[1,72,128]{2,1,0:T(8,128)S(1)} %collective-permute-done.7.refs_2_.refs_5_, f32[1,72,128]{2,1,0:T(8,128)S(1)} %collective-permute-done.8.refs_3_.refs_6_, ...), custom_call_target="tpu_custom_call" | custom-call | flops 4194304 | bytes 4194304 | tf_op jit(solution)/shard_map/rows/pallas_call | solution.py:687
  49.0 4.2 %all-to-all-start.1 = ((f32[8,8,128]{2,1,0:T(8,128)}), f32[8,8,128]{2,1,0:T(8,128)S(1)}, u32[]{:S(2)}, u32[]{:S(2)}) async-start(f32[8,8,128]{2,1,0:T(8,128)} %rows.2.refs_4_), calls=%async_computation.1 | async-start | bytes 65536 | tf_op jit(solution)/shard_map/all_to_all | solution.py:541
  53.2 2.9 %student_side.4 = (bf16[128,1024]{1,0:T(8,128)(2,1)S(1)}, f32[8,128]{1,0:T(8,128)S(1)}) custom-call(bf16[768,512]{1,0:T(8,128)(2,1)S(1)} %get-tuple-element.32.refs_6_.unit, bf16[128,1024]{1,0:T(8,128)(2,1)S(1)} %get-tuple-element.33.feat_ref, bf16[128,256]{1,0:T(8,128)(2,1)S(1)} %get-tuple-element.34.scaled_ref, ...), custom_call_target="tpu_custom_call" | custom-call | flops 1342177280 | bytes 1048576 | tf_op jit(solution)/shard_map/student_side/pallas_call | solution.py:665
  58.1 3.0 %columns.2.refs_4_ = f32[4,64,128]{2,1,0:T(8,128)} custom-call(f32[8,8,128]{2,1,0:T(8,128)S(1)} %all-to-all-done.1.sums_ref, f32[8,128]{1,0:T(8,128)S(1)} %get-tuple-element.29.factor_ref.refs_4_.refs_1_, bf16[8,256,1024]{2,1,0:T(8,128)(2,1)} %get-tuple-element.26.exp_hbm.refs_5_.refs_2_, f32[8,128]{1,0:T(8,128)S(1)} %get-tuple-element.35.refs_0_), custom_call_target="tpu_custom_call" | custom-call | flops 4194304 | bytes 4194304 | tf_op jit(solution)/shard_map/columns/pallas_call | solution.py:700
  61.1 3.3 %all-to-all-start.2 = ((f32[4,64,128]{2,1,0:T(8,128)}), f32[4,64,128]{2,1,0:T(8,128)S(1)}, u32[]{:S(2)}, u32[]{:S(2)}) async-start(f32[4,64,128]{2,1,0:T(8,128)} %columns.2.refs_4_), calls=%async_computation.2 | async-start | bytes 262144 | tf_op jit(solution)/shard_map/all_to_all | solution.py:541
  64.4 2.9 %student_side.5 = (bf16[128,1024]{1,0:T(8,128)(2,1)S(1)}, f32[8,128]{1,0:T(8,128)S(1)}) custom-call(bf16[768,512]{1,0:T(8,128)(2,1)S(1)} %get-tuple-element.32.refs_6_.unit, bf16[128,1024]{1,0:T(8,128)(2,1)S(1)} %get-tuple-element.33.feat_ref, bf16[128,256]{1,0:T(8,128)(2,1)S(1)} %get-tuple-element.34.scaled_ref, ...), custom_call_target="tpu_custom_call" | custom-call | flops 1342177280 | bytes 1048576 | tf_op jit(solution)/shard_map/student_side/pallas_call | solution.py:665
  68.0 2.8 %all-to-all-done.2.refs_0_ = f32[4,64,128]{2,1,0:T(8,128)S(1)} async-done(((f32[4,64,128]{2,1,0:T(8,128)}), f32[4,64,128]{2,1,0:T(8,128)S(1)}, u32[]{:S(2)}, u32[]{:S(2)}) %all-to-all-start.2) | async-done | bytes 131104 | tf_op jit(solution)/shard_map/all_to_all | solution.py:541
  70.8 3.1 %rows.3.refs_4_ = f32[8,8,128]{2,1,0:T(8,128)} custom-call(f32[4,64,128]{2,1,0:T(8,128)S(1)} %all-to-all-done.2.refs_0_, f32[8,128]{1,0:T(8,128)S(1)} %get-tuple-element.29.factor_ref.refs_4_.refs_1_, bf16[8,256,1024]{2,1,0:T(8,128)(2,1)} %get-tuple-element.26.exp_hbm.refs_5_.refs_2_, f32[8,128]{1,0:T(8,128)S(1)} %get-tuple-element.36.refs_3_, ...), custom_call_target="tpu_custom_call" | custom-call | flops 4194304 | bytes 4194304 | tf_op jit(solution)/shard_map/rows/pallas_call | solution.py:687
  73.8 3.4 %all-to-all-start.3 = ((f32[8,8,128]{2,1,0:T(8,128)}), f32[8,8,128]{2,1,0:T(8,128)S(1)}, u32[]{:S(2)}, u32[]{:S(2)}) async-start(f32[8,8,128]{2,1,0:T(8,128)} %rows.3.refs_4_), calls=%async_computation.3 | async-start | bytes 65536 | tf_op jit(solution)/shard_map/all_to_all | solution.py:541
  77.2 2.9 %student_side.6 = (bf16[128,1024]{1,0:T(8,128)(2,1)S(1)}, f32[8,128]{1,0:T(8,128)S(1)}) custom-call(bf16[768,512]{1,0:T(8,128)(2,1)S(1)} %get-tuple-element.32.refs_6_.unit, bf16[128,1024]{1,0:T(8,128)(2,1)S(1)} %get-tuple-element.33.feat_ref, bf16[128,256]{1,0:T(8,128)(2,1)S(1)} %get-tuple-element.34.scaled_ref, ...), custom_call_target="tpu_custom_call" | custom-call | flops 1342177280 | bytes 1048576 | tf_op jit(solution)/shard_map/student_side/pallas_call | solution.py:665
  91.0 17.7 %last_rows.1 = (bf16[8,768,1024]{2,1,0:T(8,128)(2,1)}, f32[64,128]{1,0:T(8,128)S(1)}, bf16[8,80,512]{2,1,0:T(8,128)(2,1)}) custom-call(f32[8,128]{1,0:T(8,128)S(1)} %get-tuple-element.29.factor_ref.refs_4_.refs_1_, bf16[256,512]{1,0:T(8,128)(2,1)} %s_hbm.3, f32[256,512]{1,0:T(8,128)} %copy-done, ...), custom_call_target="tpu_custom_call" | custom-call | flops 8589934592 | bytes 12582912 | tf_op jit(solution)/shard_map/last_rows/pallas_call | solution.py:719
  108.7 3.7 %all-to-all-start.4 = ((bf16[8,80,512]{2,1,0:T(8,128)(2,1)}), bf16[8,80,512]{2,1,0:T(8,128)(2,1)S(1)}, u32[]{:S(2)}, u32[]{:S(2)}) async-start(bf16[8,80,512]{2,1,0:T(8,128)(2,1)} %get-tuple-element.40.refs_4_), calls=%async_computation.4 | async-start | bytes 1310720 | tf_op jit(solution)/shard_map/all_to_all | solution.py:541
  112.5 8.9 %student_side.7 = (bf16[128,5120]{1,0:T(8,128)(2,1)S(1)}, f32[8,128]{1,0:T(8,128)S(1)}) custom-call(bf16[768,512]{1,0:T(8,128)(2,1)S(1)} %get-tuple-element.32.refs_6_.unit, bf16[128,1024]{1,0:T(8,128)(2,1)S(1)} %get-tuple-element.33.feat_ref, bf16[128,256]{1,0:T(8,128)(2,1)S(1)} %get-tuple-element.34.scaled_ref, ...), custom_call_target="tpu_custom_call" | custom-call | flops 6710886400 | bytes 5242880 | tf_op jit(solution)/shard_map/student_side/pallas_call | solution.py:665
  125.6 2.9 %collective-permute-start.14 = (f32[8,128]{1,0:T(8,128)S(1)}, f32[8,128]{1,0:T(8,128)S(1)}, u32[]{:S(2)}, u32[]{:S(2)}) collective-permute-start(f32[8,128]{1,0:T(8,128)S(1)} %get-tuple-element.48), channel_id=1, source_target_pairs={{0,3},{1,2},{2,1},{3,0},{4,7},{5,6},{6,5},{7,4},{8,11},{9,10},{10,... | collective-permute-start | bytes 12296 | tf_op jit(solution)/shard_map/ppermute | solution.py:552
  130.0 3.4 %all-to-all-start.5 = ((bf16[8,32,512]{2,1,0:T(8,128)(2,1)}), bf16[8,32,512]{2,1,0:T(8,128)(2,1)S(1)}, u32[]{:S(2)}, u32[]{:S(2)}) async-start(bf16[8,32,512]{2,1,0:T(8,128)(2,1)} %get-tuple-element.47), calls=%async_computation.5 | async-start | bytes 524288 | tf_op jit(solution)/shard_map/all_to_all | solution.py:541
  134.4 8.8 %weight_grads.1 = bf16[128,8192]{1,0:T(8,128)(2,1)} custom-call(bf16[8,256,1024]{2,1,0:T(8,128)(2,1)} %get-tuple-element.26.exp_hbm.refs_5_.refs_2_, bf16[8,768,1024]{2,1,0:T(8,128)(2,1)} %get-tuple-element.38.prob_hbm, bf16[128,1024]{1,0:T(8,128)(2,1)S(1)} %get-tuple-element.33.feat_ref, f32[64,128]{1,0:T(8,128)S(1)} %get-tuple-element.39.scale_ref, ...), custom_call_target="tpu_custom_call" | custom-call | flops 2147483648 | bytes 12582912 | tf_op jit(solution)/shard_map/weight_grads/pallas_call | solution.py:765
  (49 shorter events, 27.8 us)
Async XLA Ops:
  0.6 32.0 %collective-permute-start.2 = (bf16[256,512]{1,0:T(8,128)(2,1)}, bf16[256,512]{1,0:T(8,128)(2,1)S(1)}, u32[]{:S(2)}, u32[]{:S(2)}) collective-permute-start(bf16[256,512]{1,0:T(8,128)(2,1)} %s_hbm.3), channel_id=1, source_target_pairs={{0,1},{1,2},{2,3},{3,0},{4,5},{5,6},{6,7},{7,4},{8,9},{9,10},{10,1... | collective-permute-start | bytes 786440 | tf_op jit(solution)/shard_map/ppermute | solution.py:546
  3.7 28.9 %collective-permute-start.1 = (bf16[256,512]{1,0:T(8,128)(2,1)}, bf16[256,512]{1,0:T(8,128)(2,1)S(1)}, u32[]{:S(2)}, u32[]{:S(2)}) collective-permute-start(bf16[256,512]{1,0:T(8,128)(2,1)} %s_hbm.3), channel_id=1, source_target_pairs={{0,2},{1,3},{2,0},{3,1},{4,6},{5,7},{6,4},{7,5},{8,10},{9,11},{10,... | collective-permute-start | bytes 786440 | tf_op jit(solution)/shard_map/ppermute | solution.py:546
  6.3 26.3 %collective-permute-start = (bf16[256,512]{1,0:T(8,128)(2,1)}, bf16[256,512]{1,0:T(8,128)(2,1)S(1)}, u32[]{:S(2)}, u32[]{:S(2)}) collective-permute-start(bf16[256,512]{1,0:T(8,128)(2,1)} %s_hbm.3), channel_id=1, source_target_pairs={{0,3},{1,0},{2,1},{3,2},{4,7},{5,4},{6,5},{7,6},{8,11},{9,8},{10,9... | collective-permute-start | bytes 786440 | tf_op jit(solution)/shard_map/ppermute | solution.py:546
  23.3 9.3 %all-to-all-start = ((f32[8,8,128]{2,1,0:T(8,128)}), f32[8,8,128]{2,1,0:T(8,128)S(1)}, u32[]{:S(2)}, u32[]{:S(2)}) async-start(f32[8,8,128]{2,1,0:T(8,128)} %get-tuple-element.27.before_ref), calls=%async_computation | async-start | bytes 65536 | tf_op jit(solution)/shard_map/all_to_all | solution.py:541
  32.5 16.5 %copy-start = (f32[256,512]{1,0:T(8,128)}, f32[256,512]{1,0:T(8,128)S(1)}, u32[]{:S(2)}) copy-start(f32[256,512]{1,0:T(8,128)S(1)} %own_back.1.refs_0_.student_hbm) | copy-start | bytes 1572868
  32.5 6.9 %copy-start.1 = (bf16[256,512]{1,0:T(8,128)(2,1)S(1)}, bf16[256,512]{1,0:T(8,128)(2,1)}, u32[]{:S(2)}) copy-start(bf16[256,512]{1,0:T(8,128)(2,1)} %s_hbm.3) | copy-start | bytes 786436
  32.5 6.9 %copy-start.5 = (bf16[256,512]{1,0:T(8,128)(2,1)S(1)}, bf16[256,512]{1,0:T(8,128)(2,1)}, u32[]{:S(2)}) copy-start(bf16[256,512]{1,0:T(8,128)(2,1)} %t_ref.1) | copy-start | bytes 786436
  35.5 7.5 %collective-permute-start.8 = (f32[1,72,128]{2,1,0:T(8,128)S(1)}, f32[1,72,128]{2,1,0:T(8,128)S(1)}, u32[]{:S(2)}, u32[]{:S(2)}) collective-permute-start(f32[1,72,128]{2,1,0:T(8,128)S(1)} %get-tuple-element.30.refs_3_.refs_0_.logs_ref), channel_id=1, source_target_pairs={{0,1},{1,2},{2,3},{3,0},{4,5},{5,6},{6,7},{7,4},{8,9},{9,10},{10,1... | collective-permute-start | bytes 110600 | tf_op jit(solution)/shard_map/ppermute | solution.py:546
  36.3 9.7 %collective-permute-start.7 = (f32[1,72,128]{2,1,0:T(8,128)S(1)}, f32[1,72,128]{2,1,0:T(8,128)S(1)}, u32[]{:S(2)}, u32[]{:S(2)}) collective-permute-start(f32[1,72,128]{2,1,0:T(8,128)S(1)} %get-tuple-element.30.refs_3_.refs_0_.logs_ref), channel_id=1, source_target_pairs={{0,2},{1,3},{2,0},{3,1},{4,6},{5,7},{6,4},{7,5},{8,10},{9,11},{10,... | collective-permute-start | bytes 110600 | tf_op jit(solution)/shard_map/ppermute | solution.py:546
  36.6 9.3 %collective-permute-start.6 = (f32[1,72,128]{2,1,0:T(8,128)S(1)}, f32[1,72,128]{2,1,0:T(8,128)S(1)}, u32[]{:S(2)}, u32[]{:S(2)}) collective-permute-start(f32[1,72,128]{2,1,0:T(8,128)S(1)} %get-tuple-element.30.refs_3_.refs_0_.logs_ref), channel_id=1, source_target_pairs={{0,3},{1,0},{2,1},{3,2},{4,7},{5,4},{6,5},{7,6},{8,11},{9,8},{10,9... | collective-permute-start | bytes 110600 | tf_op jit(solution)/shard_map/ppermute | solution.py:546
  40.9 29.8 %collective-permute-start.5 = (bf16[256,512]{1,0:T(8,128)(2,1)S(1)}, bf16[256,512]{1,0:T(8,128)(2,1)S(1)}, u32[]{:S(2)}, u32[]{:S(2)}) collective-permute-start(bf16[256,512]{1,0:T(8,128)(2,1)S(1)} %get-tuple-element.31), channel_id=1, source_target_pairs={{0,1},{1,2},{2,3},{3,0},{4,5},{5,6},{6,7},{7,4},{8,9},{9,10},{10,1... | collective-permute-start | bytes 786440 | tf_op jit(solution)/shard_map/ppermute | solution.py:546
  41.5 29.2 %collective-permute-start.4 = (bf16[256,512]{1,0:T(8,128)(2,1)S(1)}, bf16[256,512]{1,0:T(8,128)(2,1)S(1)}, u32[]{:S(2)}, u32[]{:S(2)}) collective-permute-start(bf16[256,512]{1,0:T(8,128)(2,1)S(1)} %get-tuple-element.31), channel_id=1, source_target_pairs={{0,2},{1,3},{2,0},{3,1},{4,6},{5,7},{6,4},{7,5},{8,10},{9,11},{10,... | collective-permute-start | bytes 786440 | tf_op jit(solution)/shard_map/ppermute | solution.py:546
  43.1 27.7 %collective-permute-start.3 = (bf16[256,512]{1,0:T(8,128)(2,1)S(1)}, bf16[256,512]{1,0:T(8,128)(2,1)S(1)}, u32[]{:S(2)}, u32[]{:S(2)}) collective-permute-start(bf16[256,512]{1,0:T(8,128)(2,1)S(1)} %get-tuple-element.31), channel_id=1, source_target_pairs={{0,3},{1,0},{2,1},{3,2},{4,7},{5,4},{6,5},{7,6},{8,11},{9,8},{10,9... | collective-permute-start | bytes 786440 | tf_op jit(solution)/shard_map/ppermute | solution.py:546
  49.0 9.1 %all-to-all-start.1 = ((f32[8,8,128]{2,1,0:T(8,128)}), f32[8,8,128]{2,1,0:T(8,128)S(1)}, u32[]{:S(2)}, u32[]{:S(2)}) async-start(f32[8,8,128]{2,1,0:T(8,128)} %rows.2.refs_4_), calls=%async_computation.1 | async-start | bytes 65536 | tf_op jit(solution)/shard_map/all_to_all | solution.py:541
  61.1 9.7 %all-to-all-start.2 = ((f32[4,64,128]{2,1,0:T(8,128)}), f32[4,64,128]{2,1,0:T(8,128)S(1)}, u32[]{:S(2)}, u32[]{:S(2)}) async-start(f32[4,64,128]{2,1,0:T(8,128)} %columns.2.refs_4_), calls=%async_computation.2 | async-start | bytes 262144 | tf_op jit(solution)/shard_map/all_to_all | solution.py:541
  73.8 8.1 %all-to-all-start.3 = ((f32[8,8,128]{2,1,0:T(8,128)}), f32[8,8,128]{2,1,0:T(8,128)S(1)}, u32[]{:S(2)}, u32[]{:S(2)}) async-start(f32[8,8,128]{2,1,0:T(8,128)} %rows.3.refs_4_), calls=%async_computation.3 | async-start | bytes 65536 | tf_op jit(solution)/shard_map/all_to_all | solution.py:541
  84.3 5.9 %collective-permute-start.11 = (f32[1,64,128]{2,1,0:T(8,128)S(1)}, f32[1,64,128]{2,1,0:T(8,128)S(1)}, u32[]{:S(2)}, u32[]{:S(2)}) collective-permute-start(f32[1,64,128]{2,1,0:T(8,128)S(1)} %columns.3.refs_7_), channel_id=1, source_target_pairs={{0,1},{1,2},{2,3},{3,0},{4,5},{5,6},{6,7},{7,4},{8,9},{9,10},{10,1... | collective-permute-start | bytes 98312 | tf_op jit(solution)/shard_map/ppermute | solution.py:546
  85.3 5.7 %collective-permute-start.10 = (f32[1,64,128]{2,1,0:T(8,128)S(1)}, f32[1,64,128]{2,1,0:T(8,128)S(1)}, u32[]{:S(2)}, u32[]{:S(2)}) collective-permute-start(f32[1,64,128]{2,1,0:T(8,128)S(1)} %columns.3.refs_7_), channel_id=1, source_target_pairs={{0,2},{1,3},{2,0},{3,1},{4,6},{5,7},{6,4},{7,5},{8,10},{9,11},{10,... | collective-permute-start | bytes 98312 | tf_op jit(solution)/shard_map/ppermute | solution.py:546
  86.5 4.5 %collective-permute-start.9 = (f32[1,64,128]{2,1,0:T(8,128)S(1)}, f32[1,64,128]{2,1,0:T(8,128)S(1)}, u32[]{:S(2)}, u32[]{:S(2)}) collective-permute-start(f32[1,64,128]{2,1,0:T(8,128)S(1)} %columns.3.refs_7_), channel_id=1, source_target_pairs={{0,3},{1,0},{2,1},{3,2},{4,7},{5,4},{6,5},{7,6},{8,11},{9,8},{10,9... | collective-permute-start | bytes 98312 | tf_op jit(solution)/shard_map/ppermute | solution.py:546
  108.7 14.6 %all-to-all-start.4 = ((bf16[8,80,512]{2,1,0:T(8,128)(2,1)}), bf16[8,80,512]{2,1,0:T(8,128)(2,1)S(1)}, u32[]{:S(2)}, u32[]{:S(2)}) async-start(bf16[8,80,512]{2,1,0:T(8,128)(2,1)} %get-tuple-element.40.refs_4_), calls=%async_computation.4 | async-start | bytes 1310720 | tf_op jit(solution)/shard_map/all_to_all | solution.py:541
  125.6 17.6 %collective-permute-start.14 = (f32[8,128]{1,0:T(8,128)S(1)}, f32[8,128]{1,0:T(8,128)S(1)}, u32[]{:S(2)}, u32[]{:S(2)}) collective-permute-start(f32[8,128]{1,0:T(8,128)S(1)} %get-tuple-element.48), channel_id=1, source_target_pairs={{0,3},{1,2},{2,1},{3,0},{4,7},{5,6},{6,5},{7,4},{8,11},{9,10},{10,... | collective-permute-start | bytes 12296 | tf_op jit(solution)/shard_map/ppermute | solution.py:552
  128.5 14.7 %collective-permute-start.13 = (f32[8,128]{1,0:T(8,128)S(1)}, f32[8,128]{1,0:T(8,128)S(1)}, u32[]{:S(2)}, u32[]{:S(2)}) collective-permute-start(f32[8,128]{1,0:T(8,128)S(1)} %get-tuple-element.48), channel_id=1, source_target_pairs={{0,2},{1,3},{2,0},{3,1},{4,6},{5,7},{6,4},{7,5},{8,10},{9,11},{10,... | collective-permute-start | bytes 12296 | tf_op jit(solution)/shard_map/ppermute | solution.py:552
  128.7 14.4 %collective-permute-start.12 = (f32[8,128]{1,0:T(8,128)S(1)}, f32[8,128]{1,0:T(8,128)S(1)}, u32[]{:S(2)}, u32[]{:S(2)}) collective-permute-start(f32[8,128]{1,0:T(8,128)S(1)} %get-tuple-element.48), channel_id=1, source_target_pairs={{0,1},{1,0},{2,3},{3,2},{4,5},{5,4},{6,7},{7,6},{8,9},{9,8},{10,11... | collective-permute-start | bytes 12296 | tf_op jit(solution)/shard_map/ppermute | solution.py:552
  130.0 13.7 %all-to-all-start.5 = ((bf16[8,32,512]{2,1,0:T(8,128)(2,1)}), bf16[8,32,512]{2,1,0:T(8,128)(2,1)S(1)}, u32[]{:S(2)}, u32[]{:S(2)}) async-start(bf16[8,32,512]{2,1,0:T(8,128)(2,1)} %get-tuple-element.47), calls=%async_computation.5 | async-start | bytes 524288 | tf_op jit(solution)/shard_map/all_to_all | solution.py:541
  (3 other events, 2.4 us)

commit v9 on v8

--- a/solution.py
+++ b/solution.py
@@ -17,7 +17,7 @@
 LANES = 128
 WIDE = 1024
 TILE = 256
-FAR = (2,)
+FAR = (0, 1, 2)
 F32 = jnp.float32
 BF16 = jnp.bfloat16
 
@@ -490,9 +490,9 @@
                 where.append((part, k))
     exp_loads = copies(exp_hbm, exp_ref, exp_sem)
     prob_loads = copies(prob_hbm, prob_ref, prob_sem)
-    start(exp_loads[:2], prob_loads[:2])
+    start(exp_loads[:1], prob_loads[:1])
     start(list(part_loads.values()))
-    start(exp_loads[2:], prob_loads[2:])
+    start(exp_loads[1:], prob_loads[1:])
     own = exp_ref.shape[1]
     tiles = (own + prob_ref.shape[1]) // LANES
     rows = protos / sums_ref[:tiles, :]

time: 145 us -> 145 us (level)
  no operation moved by 1% of the time
where the time goes in v9:
time: 145 us; the launch traced here: 144 us
  Pallas kernels  83.2 us (57%)
  starting transfers between devices  46 us (32%)
  waiting for transfers between devices  10 us (7%)
  local copies, waits for them, and re-layouts  2.63 us (2%)
    all_to_all x6, starting transfers between devices, exchange(): return lax.all_to_all(value, axis, 0, 0)  21.8 us
    ppermute x12, starting transfers between devices, following(): lax.ppermute(value, axis, [(i, (i - s) % n) for i in range(n)])  19.8 us
    pallas_call x1, Pallas kernels, local(): pl.pallas_call(functools.partial(last_kernel, groups), in_specs=[VMEM] +...  17.7 us
    pallas_call x4, Pallas kernels, student_piece(): pl.pallas_call(functools.partial(student_kernel, log_protos, first, group...  17.5 us
    pallas_call x1, Pallas kernels, local(): pl.pallas_call(stats_kernel, in_specs=[ANY] * 3, out_specs=[ANY, ANY, VME...  15.6 us
    pallas_call x1, Pallas kernels, local(): pl.pallas_call(functools.partial(grad_kernel, counts, float(protos)), in_...  8.83 us
    all_to_all x6, waiting for transfers between devices, exchange(): return lax.all_to_all(value, axis, 0, 0)  7.17 us
    pallas_call x2, Pallas kernels, local(): pl.pallas_call(functools.partial(row_kernel, len(cols)), in_specs=[VMEM]...  6.13 us
  transfers between devices with their start and end apart: 21, of which 6 were waited for; matrix products, arithmetic and copies ran while one was open for 0% of the time, Pallas kernels for 38%

profile of v9, /device:TPU:0, one launch (start us, length us, event | category | flops | bytes accessed | tf_op | source)
XLA Modules:
  0.0 143.7 jit_solution(9254393210511217070)
XLA Ops:
  0.6 3.1 %collective-permute-start.2 = (bf16[256,512]{1,0:T(8,128)(2,1)}, bf16[256,512]{1,0:T(8,128)(2,1)S(1)}, u32[]{:S(2)}, u32[]{:S(2)}) collective-permute-start(bf16[256,512]{1,0:T(8,128)(2,1)} %s_hbm.3), channel_id=1, source_target_pairs={{0,1},{1,2},{2,3},{3,0},{4,5},{5,6},{6,7},{7,4},{8,9},{9,10},{10,1... | collective-permute-start | bytes 786440 | tf_op jit(solution)/shard_map/ppermute | solution.py:546
  3.7 2.6 %collective-permute-start.1 = (bf16[256,512]{1,0:T(8,128)(2,1)}, bf16[256,512]{1,0:T(8,128)(2,1)S(1)}, u32[]{:S(2)}, u32[]{:S(2)}) collective-permute-start(bf16[256,512]{1,0:T(8,128)(2,1)} %s_hbm.3), channel_id=1, source_target_pairs={{0,2},{1,3},{2,0},{3,1},{4,6},{5,7},{6,4},{7,5},{8,10},{9,11},{10,... | collective-permute-start | bytes 786440 | tf_op jit(solution)/shard_map/ppermute | solution.py:546
  7.6 15.6 %own_rows.1 = (bf16[8,256,1024]{2,1,0:T(8,128)(2,1)}, bf16[8,256,1024]{2,1,0:T(8,128)(2,1)}, f32[8,8,128]{2,1,0:T(8,128)}) custom-call(bf16[256,512]{1,0:T(8,128)(2,1)} %t_ref.1, bf16[256,512]{1,0:T(8,128)(2,1)} %s_hbm.3, bf16[512,8192]{1,0:T(8,128)(2,1)} %w_hbm.13), custom_call_target="tpu_custom_call" | custom-call | flops 4294967296 | bytes 8388608 | tf_op jit(solution)/shard_map/own_rows/pallas_call | solution.py:591
  23.3 3.7 %all-to-all-start = ((f32[8,8,128]{2,1,0:T(8,128)}), f32[8,8,128]{2,1,0:T(8,128)S(1)}, u32[]{:S(2)}, u32[]{:S(2)}) async-start(f32[8,8,128]{2,1,0:T(8,128)} %get-tuple-element.27.before_ref), calls=%async_computation | async-start | bytes 65536 | tf_op jit(solution)/shard_map/all_to_all | solution.py:541
  27.0 5.5 %own_back.1.refs_0_.student_hbm = f32[256,512]{1,0:T(8,128)S(1)} custom-call(f32[8,8,128]{2,1,0:T(8,128)} %get-tuple-element.27.before_ref, bf16[8,256,1024]{2,1,0:T(8,128)(2,1)} %get-tuple-element.28.exp_hbm, bf16[512,8192]{1,0:T(8,128)(2,1)} %w_hbm.13), custom_call_target="tpu_custom_call" | custom-call | flops 2147483648 | bytes 8388608 | tf_op jit(solution)/shard_map/own_back/pallas_call | solution.py:617
  32.6 2.9 %first_columns.1 = (f32[8,128]{1,0:T(8,128)S(1)}, f32[1,72,128]{2,1,0:T(8,128)S(1)}) custom-call(s32[2]{0:T(128)S(1)} %pad_add_fusion.place_ref, f32[8,8,128]{2,1,0:T(8,128)S(1)} %all-to-all-done.stats_ref, bf16[8,256,1024]{2,1,0:T(8,128)(2,1)} %get-tuple-element.26.exp_hbm.refs_5_.refs_2_, f32[256,512]{1,0:T(8,128)S(1)} %own_back.1.refs_0_.student_hbm, ...), custom_call_target="tpu_custom_call" | custom-call | flops 4194304 | bytes 4194304 | tf_op jit(solution)/shard_map/first_columns/pallas_call | solution.py:631
  36.6 2.8 %collective-permute-start.6 = (f32[1,72,128]{2,1,0:T(8,128)S(1)}, f32[1,72,128]{2,1,0:T(8,128)S(1)}, u32[]{:S(2)}, u32[]{:S(2)}) collective-permute-start(f32[1,72,128]{2,1,0:T(8,128)S(1)} %get-tuple-element.30.refs_3_.refs_0_.logs_ref), channel_id=1, source_target_pairs={{0,3},{1,0},{2,1},{3,2},{4,7},{5,4},{6,5},{7,6},{8,11},{9,8},{10,9... | collective-permute-start | bytes 110600 | tf_op jit(solution)/shard_map/ppermute | solution.py:546
  43.1 2.8 %collective-permute-start.3 = (bf16[256,512]{1,0:T(8,128)(2,1)S(1)}, bf16[256,512]{1,0:T(8,128)(2,1)S(1)}, u32[]{:S(2)}, u32[]{:S(2)}) collective-permute-start(bf16[256,512]{1,0:T(8,128)(2,1)S(1)} %get-tuple-element.31), channel_id=1, source_target_pairs={{0,3},{1,0},{2,1},{3,2},{4,7},{5,4},{6,5},{7,6},{8,11},{9,8},{10,9... | collective-permute-start | bytes 786440 | tf_op jit(solution)/shard_map/ppermute | solution.py:546
  45.9 3.1 %rows.2.refs_4_ = f32[8,8,128]{2,1,0:T(8,128)} custom-call(f32[1,72,128]{2,1,0:T(8,128)S(1)} %get-tuple-element.30.refs_3_.refs_0_.logs_ref, f32[1,72,128]{2,1,0:T(8,128)S(1)} %collective-permute-done.6.refs_1_.refs_4_, f32[1,72,128]{2,1,0:T(8,128)S(1)} %collective-permute-done.7.refs_2_.refs_5_, f32[1,72,128]{2,1,0:T(8,128)S(1)} %collective-permute-done.8.refs_3_.refs_6_, ...), custom_call_target="tpu_custom_call" | custom-call | flops 4194304 | bytes 4194304 | tf_op jit(solution)/shard_map/rows/pallas_call | solution.py:687
  49.0 4.2 %all-to-all-start.1 = ((f32[8,8,128]{2,1,0:T(8,128)}), f32[8,8,128]{2,1,0:T(8,128)S(1)}, u32[]{:S(2)}, u32[]{:S(2)}) async-start(f32[8,8,128]{2,1,0:T(8,128)} %rows.2.refs_4_), calls=%async_computation.1 | async-start | bytes 65536 | tf_op jit(solution)/shard_map/all_to_all | solution.py:541
  53.2 2.9 %student_side.4 = (bf16[128,1024]{1,0:T(8,128)(2,1)S(1)}, f32[8,128]{1,0:T(8,128)S(1)}) custom-call(bf16[768,512]{1,0:T(8,128)(2,1)S(1)} %get-tuple-element.32.refs_6_.unit, bf16[128,1024]{1,0:T(8,128)(2,1)S(1)} %get-tuple-element.33.feat_ref, bf16[128,256]{1,0:T(8,128)(2,1)S(1)} %get-tuple-element.34.scaled_ref, ...), custom_call_target="tpu_custom_call" | custom-call | flops 1342177280 | bytes 1048576 | tf_op jit(solution)/shard_map/student_side/pallas_call | solution.py:665
  58.1 3.0 %columns.2.refs_4_ = f32[4,64,128]{2,1,0:T(8,128)} custom-call(f32[8,8,128]{2,1,0:T(8,128)S(1)} %all-to-all-done.1.sums_ref, f32[8,128]{1,0:T(8,128)S(1)} %get-tuple-element.29.factor_ref.refs_4_.refs_1_, bf16[8,256,1024]{2,1,0:T(8,128)(2,1)} %get-tuple-element.26.exp_hbm.refs_5_.refs_2_, f32[8,128]{1,0:T(8,128)S(1)} %get-tuple-element.35.refs_0_), custom_call_target="tpu_custom_call" | custom-call | flops 4194304 | bytes 4194304 | tf_op jit(solution)/shard_map/columns/pallas_call | solution.py:700
  61.1 3.3 %all-to-all-start.2 = ((f32[4,64,128]{2,1,0:T(8,128)}), f32[4,64,128]{2,1,0:T(8,128)S(1)}, u32[]{:S(2)}, u32[]{:S(2)}) async-start(f32[4,64,128]{2,1,0:T(8,128)} %columns.2.refs_4_), calls=%async_computation.2 | async-start | bytes 262144 | tf_op jit(solution)/shard_map/all_to_all | solution.py:541
  64.4 2.9 %student_side.5 = (bf16[128,1024]{1,0:T(8,128)(2,1)S(1)}, f32[8,128]{1,0:T(8,128)S(1)}) custom-call(bf16[768,512]{1,0:T(8,128)(2,1)S(1)} %get-tuple-element.32.refs_6_.unit, bf16[128,1024]{1,0:T(8,128)(2,1)S(1)} %get-tuple-element.33.feat_ref, bf16[128,256]{1,0:T(8,128)(2,1)S(1)} %get-tuple-element.34.scaled_ref, ...), custom_call_target="tpu_custom_call" | custom-call | flops 1342177280 | bytes 1048576 | tf_op jit(solution)/shard_map/student_side/pallas_call | solution.py:665
  68.0 2.8 %all-to-all-done.2.refs_0_ = f32[4,64,128]{2,1,0:T(8,128)S(1)} async-done(((f32[4,64,128]{2,1,0:T(8,128)}), f32[4,64,128]{2,1,0:T(8,128)S(1)}, u32[]{:S(2)}, u32[]{:S(2)}) %all-to-all-start.2) | async-done | bytes 131104 | tf_op jit(solution)/shard_map/all_to_all | solution.py:541
  70.8 3.1 %rows.3.refs_4_ = f32[8,8,128]{2,1,0:T(8,128)} custom-call(f32[4,64,128]{2,1,0:T(8,128)S(1)} %all-to-all-done.2.refs_0_, f32[8,128]{1,0:T(8,128)S(1)} %get-tuple-element.29.factor_ref.refs_4_.refs_1_, bf16[8,256,1024]{2,1,0:T(8,128)(2,1)} %get-tuple-element.26.exp_hbm.refs_5_.refs_2_, f32[8,128]{1,0:T(8,128)S(1)} %get-tuple-element.36.refs_3_, ...), custom_call_target="tpu_custom_call" | custom-call | flops 4194304 | bytes 4194304 | tf_op jit(solution)/shard_map/rows/pallas_call | solution.py:687
  73.8 3.4 %all-to-all-start.3 = ((f32[8,8,128]{2,1,0:T(8,128)}), f32[8,8,128]{2,1,0:T(8,128)S(1)}, u32[]{:S(2)}, u32[]{:S(2)}) async-start(f32[8,8,128]{2,1,0:T(8,128)} %rows.3.refs_4_), calls=%async_computation.3 | async-start | bytes 65536 | tf_op jit(solution)/shard_map/all_to_all | solution.py:541
  77.2 2.9 %student_side.6 = (bf16[128,1024]{1,0:T(8,128)(2,1)S(1)}, f32[8,128]{1,0:T(8,128)S(1)}) custom-call(bf16[768,512]{1,0:T(8,128)(2,1)S(1)} %get-tuple-element.32.refs_6_.unit, bf16[128,1024]{1,0:T(8,128)(2,1)S(1)} %get-tuple-element.33.feat_ref, bf16[128,256]{1,0:T(8,128)(2,1)S(1)} %get-tuple-element.34.scaled_ref, ...), custom_call_target="tpu_custom_call" | custom-call | flops 1342177280 | bytes 1048576 | tf_op jit(solution)/shard_map/student_side/pallas_call | solution.py:665
  91.0 17.7 %last_rows.1 = (bf16[8,768,1024]{2,1,0:T(8,128)(2,1)}, f32[64,128]{1,0:T(8,128)S(1)}, bf16[8,80,512]{2,1,0:T(8,128)(2,1)}) custom-call(f32[8,128]{1,0:T(8,128)S(1)} %get-tuple-element.29.factor_ref.refs_4_.refs_1_, bf16[256,512]{1,0:T(8,128)(2,1)} %s_hbm.3, f32[256,512]{1,0:T(8,128)} %copy-done, ...), custom_call_target="tpu_custom_call" | custom-call | flops 8589934592 | bytes 12582912 | tf_op jit(solution)/shard_map/last_rows/pallas_call | solution.py:719
  108.7 3.7 %all-to-all-start.4 = ((bf16[8,80,512]{2,1,0:T(8,128)(2,1)}), bf16[8,80,512]{2,1,0:T(8,128)(2,1)S(1)}, u32[]{:S(2)}, u32[]{:S(2)}) async-start(bf16[8,80,512]{2,1,0:T(8,128)(2,1)} %get-tuple-element.40.refs_4_), calls=%async_computation.4 | async-start | bytes 1310720 | tf_op jit(solution)/shard_map/all_to_all | solution.py:541
  112.5 8.9 %student_side.7 = (bf16[128,5120]{1,0:T(8,128)(2,1)S(1)}, f32[8,128]{1,0:T(8,128)S(1)}) custom-call(bf16[768,512]{1,0:T(8,128)(2,1)S(1)} %get-tuple-element.32.refs_6_.unit, bf16[128,1024]{1,0:T(8,128)(2,1)S(1)} %get-tuple-element.33.feat_ref, bf16[128,256]{1,0:T(8,128)(2,1)S(1)} %get-tuple-element.34.scaled_ref, ...), custom_call_target="tpu_custom_call" | custom-call | flops 6710886400 | bytes 5242880 | tf_op jit(solution)/shard_map/student_side/pallas_call | solution.py:665
  125.6 2.9 %collective-permute-start.14 = (f32[8,128]{1,0:T(8,128)S(1)}, f32[8,128]{1,0:T(8,128)S(1)}, u32[]{:S(2)}, u32[]{:S(2)}) collective-permute-start(f32[8,128]{1,0:T(8,128)S(1)} %get-tuple-element.48), channel_id=1, source_target_pairs={{0,3},{1,2},{2,1},{3,0},{4,7},{5,6},{6,5},{7,4},{8,11},{9,10},{10,... | collective-permute-start | bytes 12296 | tf_op jit(solution)/shard_map/ppermute | solution.py:552
  130.0 3.4 %all-to-all-start.5 = ((bf16[8,32,512]{2,1,0:T(8,128)(2,1)}), bf16[8,32,512]{2,1,0:T(8,128)(2,1)S(1)}, u32[]{:S(2)}, u32[]{:S(2)}) async-start(bf16[8,32,512]{2,1,0:T(8,128)(2,1)} %get-tuple-element.47), calls=%async_computation.5 | async-start | bytes 524288 | tf_op jit(solution)/shard_map/all_to_all | solution.py:541
  133.4 8.8 %weight_grads.1 = bf16[128,8192]{1,0:T(8,128)(2,1)} custom-call(bf16[8,256,1024]{2,1,0:T(8,128)(2,1)} %get-tuple-element.26.exp_hbm.refs_5_.refs_2_, bf16[8,768,1024]{2,1,0:T(8,128)(2,1)} %get-tuple-element.38.prob_hbm, bf16[128,1024]{1,0:T(8,128)(2,1)S(1)} %get-tuple-element.33.feat_ref, f32[64,128]{1,0:T(8,128)S(1)} %get-tuple-element.39.scale_ref, ...), custom_call_target="tpu_custom_call" | custom-call | flops 2147483648 | bytes 12582912 | tf_op jit(solution)/shard_map/weight_grads/pallas_call | solution.py:765
  (49 shorter events, 26.8 us)
Async XLA Ops:
  0.6 32.0 %collective-permute-start.2 = (bf16[256,512]{1,0:T(8,128)(2,1)}, bf16[256,512]{1,0:T(8,128)(2,1)S(1)}, u32[]{:S(2)}, u32[]{:S(2)}) collective-permute-start(bf16[256,512]{1,0:T(8,128)(2,1)} %s_hbm.3), channel_id=1, source_target_pairs={{0,1},{1,2},{2,3},{3,0},{4,5},{5,6},{6,7},{7,4},{8,9},{9,10},{10,1... | collective-permute-start | bytes 786440 | tf_op jit(solution)/shard_map/ppermute | solution.py:546
  3.7 28.9 %collective-permute-start.1 = (bf16[256,512]{1,0:T(8,128)(2,1)}, bf16[256,512]{1,0:T(8,128)(2,1)S(1)}, u32[]{:S(2)}, u32[]{:S(2)}) collective-permute-start(bf16[256,512]{1,0:T(8,128)(2,1)} %s_hbm.3), channel_id=1, source_target_pairs={{0,2},{1,3},{2,0},{3,1},{4,6},{5,7},{6,4},{7,5},{8,10},{9,11},{10,... | collective-permute-start | bytes 786440 | tf_op jit(solution)/shard_map/ppermute | solution.py:546
  6.3 26.3 %collective-permute-start = (bf16[256,512]{1,0:T(8,128)(2,1)}, bf16[256,512]{1,0:T(8,128)(2,1)S(1)}, u32[]{:S(2)}, u32[]{:S(2)}) collective-permute-start(bf16[256,512]{1,0:T(8,128)(2,1)} %s_hbm.3), channel_id=1, source_target_pairs={{0,3},{1,0},{2,1},{3,2},{4,7},{5,4},{6,5},{7,6},{8,11},{9,8},{10,9... | collective-permute-start | bytes 786440 | tf_op jit(solution)/shard_map/ppermute | solution.py:546
  23.3 9.3 %all-to-all-start = ((f32[8,8,128]{2,1,0:T(8,128)}), f32[8,8,128]{2,1,0:T(8,128)S(1)}, u32[]{:S(2)}, u32[]{:S(2)}) async-start(f32[8,8,128]{2,1,0:T(8,128)} %get-tuple-element.27.before_ref), calls=%async_computation | async-start | bytes 65536 | tf_op jit(solution)/shard_map/all_to_all | solution.py:541
  32.5 16.5 %copy-start = (f32[256,512]{1,0:T(8,128)}, f32[256,512]{1,0:T(8,128)S(1)}, u32[]{:S(2)}) copy-start(f32[256,512]{1,0:T(8,128)S(1)} %own_back.1.refs_0_.student_hbm) | copy-start | bytes 1572868
  32.5 6.9 %copy-start.1 = (bf16[256,512]{1,0:T(8,128)(2,1)S(1)}, bf16[256,512]{1,0:T(8,128)(2,1)}, u32[]{:S(2)}) copy-start(bf16[256,512]{1,0:T(8,128)(2,1)} %s_hbm.3) | copy-start | bytes 786436
  32.5 6.9 %copy-start.5 = (bf16[256,512]{1,0:T(8,128)(2,1)S(1)}, bf16[256,512]{1,0:T(8,128)(2,1)}, u32[]{:S(2)}) copy-start(bf16[256,512]{1,0:T(8,128)(2,1)} %t_ref.1) | copy-start | bytes 786436
  35.5 7.5 %collective-permute-start.8 = (f32[1,72,128]{2,1,0:T(8,128)S(1)}, f32[1,72,128]{2,1,0:T(8,128)S(1)}, u32[]{:S(2)}, u32[]{:S(2)}) collective-permute-start(f32[1,72,128]{2,1,0:T(8,128)S(1)} %get-tuple-element.30.refs_3_.refs_0_.logs_ref), channel_id=1, source_target_pairs={{0,1},{1,2},{2,3},{3,0},{4,5},{5,6},{6,7},{7,4},{8,9},{9,10},{10,1... | collective-permute-start | bytes 110600 | tf_op jit(solution)/shard_map/ppermute | solution.py:546
  36.3 9.7 %collective-permute-start.7 = (f32[1,72,128]{2,1,0:T(8,128)S(1)}, f32[1,72,128]{2,1,0:T(8,128)S(1)}, u32[]{:S(2)}, u32[]{:S(2)}) collective-permute-start(f32[1,72,128]{2,1,0:T(8,128)S(1)} %get-tuple-element.30.refs_3_.refs_0_.logs_ref), channel_id=1, source_target_pairs={{0,2},{1,3},{2,0},{3,1},{4,6},{5,7},{6,4},{7,5},{8,10},{9,11},{10,... | collective-permute-start | bytes 110600 | tf_op jit(solution)/shard_map/ppermute | solution.py:546
  36.6 9.3 %collective-permute-start.6 = (f32[1,72,128]{2,1,0:T(8,128)S(1)}, f32[1,72,128]{2,1,0:T(8,128)S(1)}, u32[]{:S(2)}, u32[]{:S(2)}) collective-permute-start(f32[1,72,128]{2,1,0:T(8,128)S(1)} %get-tuple-element.30.refs_3_.refs_0_.logs_ref), channel_id=1, source_target_pairs={{0,3},{1,0},{2,1},{3,2},{4,7},{5,4},{6,5},{7,6},{8,11},{9,8},{10,9... | collective-permute-start | bytes 110600 | tf_op jit(solution)/shard_map/ppermute | solution.py:546
  40.9 29.8 %collective-permute-start.5 = (bf16[256,512]{1,0:T(8,128)(2,1)S(1)}, bf16[256,512]{1,0:T(8,128)(2,1)S(1)}, u32[]{:S(2)}, u32[]{:S(2)}) collective-permute-start(bf16[256,512]{1,0:T(8,128)(2,1)S(1)} %get-tuple-element.31), channel_id=1, source_target_pairs={{0,1},{1,2},{2,3},{3,0},{4,5},{5,6},{6,7},{7,4},{8,9},{9,10},{10,1... | collective-permute-start | bytes 786440 | tf_op jit(solution)/shard_map/ppermute | solution.py:546
  41.5 29.2 %collective-permute-start.4 = (bf16[256,512]{1,0:T(8,128)(2,1)S(1)}, bf16[256,512]{1,0:T(8,128)(2,1)S(1)}, u32[]{:S(2)}, u32[]{:S(2)}) collective-permute-start(bf16[256,512]{1,0:T(8,128)(2,1)S(1)} %get-tuple-element.31), channel_id=1, source_target_pairs={{0,2},{1,3},{2,0},{3,1},{4,6},{5,7},{6,4},{7,5},{8,10},{9,11},{10,... | collective-permute-start | bytes 786440 | tf_op jit(solution)/shard_map/ppermute | solution.py:546
  43.1 27.7 %collective-permute-start.3 = (bf16[256,512]{1,0:T(8,128)(2,1)S(1)}, bf16[256,512]{1,0:T(8,128)(2,1)S(1)}, u32[]{:S(2)}, u32[]{:S(2)}) collective-permute-start(bf16[256,512]{1,0:T(8,128)(2,1)S(1)} %get-tuple-element.31), channel_id=1, source_target_pairs={{0,3},{1,0},{2,1},{3,2},{4,7},{5,4},{6,5},{7,6},{8,11},{9,8},{10,9... | collective-permute-start | bytes 786440 | tf_op jit(solution)/shard_map/ppermute | solution.py:546
  49.0 9.1 %all-to-all-start.1 = ((f32[8,8,128]{2,1,0:T(8,128)}), f32[8,8,128]{2,1,0:T(8,128)S(1)}, u32[]{:S(2)}, u32[]{:S(2)}) async-start(f32[8,8,128]{2,1,0:T(8,128)} %rows.2.refs_4_), calls=%async_computation.1 | async-start | bytes 65536 | tf_op jit(solution)/shard_map/all_to_all | solution.py:541
  61.1 9.7 %all-to-all-start.2 = ((f32[4,64,128]{2,1,0:T(8,128)}), f32[4,64,128]{2,1,0:T(8,128)S(1)}, u32[]{:S(2)}, u32[]{:S(2)}) async-start(f32[4,64,128]{2,1,0:T(8,128)} %columns.2.refs_4_), calls=%async_computation.2 | async-start | bytes 262144 | tf_op jit(solution)/shard_map/all_to_all | solution.py:541
  73.8 8.1 %all-to-all-start.3 = ((f32[8,8,128]{2,1,0:T(8,128)}), f32[8,8,128]{2,1,0:T(8,128)S(1)}, u32[]{:S(2)}, u32[]{:S(2)}) async-start(f32[8,8,128]{2,1,0:T(8,128)} %rows.3.refs_4_), calls=%async_computation.3 | async-start | bytes 65536 | tf_op jit(solution)/shard_map/all_to_all | solution.py:541
  84.3 5.9 %collective-permute-start.11 = (f32[1,64,128]{2,1,0:T(8,128)S(1)}, f32[1,64,128]{2,1,0:T(8,128)S(1)}, u32[]{:S(2)}, u32[]{:S(2)}) collective-permute-start(f32[1,64,128]{2,1,0:T(8,128)S(1)} %columns.3.refs_7_), channel_id=1, source_target_pairs={{0,1},{1,2},{2,3},{3,0},{4,5},{5,6},{6,7},{7,4},{8,9},{9,10},{10,1... | collective-permute-start | bytes 98312 | tf_op jit(solution)/shard_map/ppermute | solution.py:546
  85.3 5.7 %collective-permute-start.10 = (f32[1,64,128]{2,1,0:T(8,128)S(1)}, f32[1,64,128]{2,1,0:T(8,128)S(1)}, u32[]{:S(2)}, u32[]{:S(2)}) collective-permute-start(f32[1,64,128]{2,1,0:T(8,128)S(1)} %columns.3.refs_7_), channel_id=1, source_target_pairs={{0,2},{1,3},{2,0},{3,1},{4,6},{5,7},{6,4},{7,5},{8,10},{9,11},{10,... | collective-permute-start | bytes 98312 | tf_op jit(solution)/shard_map/ppermute | solution.py:546
  86.5 4.5 %collective-permute-start.9 = (f32[1,64,128]{2,1,0:T(8,128)S(1)}, f32[1,64,128]{2,1,0:T(8,128)S(1)}, u32[]{:S(2)}, u32[]{:S(2)}) collective-permute-start(f32[1,64,128]{2,1,0:T(8,128)S(1)} %columns.3.refs_7_), channel_id=1, source_target_pairs={{0,3},{1,0},{2,1},{3,2},{4,7},{5,4},{6,5},{7,6},{8,11},{9,8},{10,9... | collective-permute-start | bytes 98312 | tf_op jit(solution)/shard_map/ppermute | solution.py:546
  108.7 14.6 %all-to-all-start.4 = ((bf16[8,80,512]{2,1,0:T(8,128)(2,1)}), bf16[8,80,512]{2,1,0:T(8,128)(2,1)S(1)}, u32[]{:S(2)}, u32[]{:S(2)}) async-start(bf16[8,80,512]{2,1,0:T(8,128)(2,1)} %get-tuple-element.40.refs_4_), calls=%async_computation.4 | async-start | bytes 1310720 | tf_op jit(solution)/shard_map/all_to_all | solution.py:541
  125.6 16.7 %collective-permute-start.14 = (f32[8,128]{1,0:T(8,128)S(1)}, f32[8,128]{1,0:T(8,128)S(1)}, u32[]{:S(2)}, u32[]{:S(2)}) collective-permute-start(f32[8,128]{1,0:T(8,128)S(1)} %get-tuple-element.48), channel_id=1, source_target_pairs={{0,3},{1,2},{2,1},{3,0},{4,7},{5,6},{6,5},{7,4},{8,11},{9,10},{10,... | collective-permute-start | bytes 12296 | tf_op jit(solution)/shard_map/ppermute | solution.py:552
  128.5 13.8 %collective-permute-start.13 = (f32[8,128]{1,0:T(8,128)S(1)}, f32[8,128]{1,0:T(8,128)S(1)}, u32[]{:S(2)}, u32[]{:S(2)}) collective-permute-start(f32[8,128]{1,0:T(8,128)S(1)} %get-tuple-element.48), channel_id=1, source_target_pairs={{0,2},{1,3},{2,0},{3,1},{4,6},{5,7},{6,4},{7,5},{8,10},{9,11},{10,... | collective-permute-start | bytes 12296 | tf_op jit(solution)/shard_map/ppermute | solution.py:552
  128.8 13.5 %collective-permute-start.12 = (f32[8,128]{1,0:T(8,128)S(1)}, f32[8,128]{1,0:T(8,128)S(1)}, u32[]{:S(2)}, u32[]{:S(2)}) collective-permute-start(f32[8,128]{1,0:T(8,128)S(1)} %get-tuple-element.48), channel_id=1, source_target_pairs={{0,1},{1,0},{2,3},{3,2},{4,5},{5,4},{6,7},{7,6},{8,9},{9,8},{10,11... | collective-permute-start | bytes 12296 | tf_op jit(solution)/shard_map/ppermute | solution.py:552
  130.0 12.8 %all-to-all-start.5 = ((bf16[8,32,512]{2,1,0:T(8,128)(2,1)}), bf16[8,32,512]{2,1,0:T(8,128)(2,1)S(1)}, u32[]{:S(2)}, u32[]{:S(2)}) async-start(bf16[8,32,512]{2,1,0:T(8,128)(2,1)} %get-tuple-element.47), calls=%async_computation.5 | async-start | bytes 524288 | tf_op jit(solution)/shard_map/all_to_all | solution.py:541
  (3 other events, 2.1 us)

commit v10 on v9

--- a/solution.py
+++ b/solution.py
@@ -16,7 +16,7 @@
 SCALE_STUDENT = LOG2E / TEMP_STUDENT
 LANES = 128
 WIDE = 1024
-TILE = 256
+TILE = 512
 FAR = (0, 1, 2)
 F32 = jnp.float32
 BF16 = jnp.bfloat16

time: 145 us -> 144 us (level)
  no operation moved by 1% of the time
where the time goes in v10:
time: 144 us; the launch traced here: 143 us
  Pallas kernels  82.2 us (57%)
  starting transfers between devices  46 us (32%)
  waiting for transfers between devices  10.1 us (7%)
  local copies, waits for them, and re-layouts  2.63 us (2%)
    all_to_all x6, starting transfers between devices, exchange(): return lax.all_to_all(value, axis, 0, 0)  21.8 us
    ppermute x12, starting transfers between devices, following(): lax.ppermute(value, axis, [(i, (i - s) % n) for i in range(n)])  19.8 us
    pallas_call x4, Pallas kernels, student_piece(): pl.pallas_call(functools.partial(student_kernel, log_protos, first, group...  17.5 us
    pallas_call x1, Pallas kernels, local(): pl.pallas_call(functools.partial(last_kernel, groups), in_specs=[VMEM] +...  17.4 us
    pallas_call x1, Pallas kernels, local(): pl.pallas_call(stats_kernel, in_specs=[ANY] * 3, out_specs=[ANY, ANY, VME...  14.9 us
    pallas_call x1, Pallas kernels, local(): pl.pallas_call(functools.partial(grad_kernel, counts, float(protos)), in_...  8.82 us
    all_to_all x6, waiting for transfers between devices, exchange(): return lax.all_to_all(value, axis, 0, 0)  7.23 us
    pallas_call x2, Pallas kernels, local(): pl.pallas_call(functools.partial(row_kernel, len(cols)), in_specs=[VMEM]...  6.13 us
  transfers between devices with their start and end apart: 21, of which 6 were waited for; matrix products, arithmetic and copies ran while one was open for 0% of the time, Pallas kernels for 38%

profile of v10, /device:TPU:0, one launch (start us, length us, event | category | flops | bytes accessed | tf_op | source)
XLA Modules:
  0.0 142.8 jit_solution(7747029339924268514)
XLA Ops:
  0.6 3.1 %collective-permute-start.2 = (bf16[256,512]{1,0:T(8,128)(2,1)}, bf16[256,512]{1,0:T(8,128)(2,1)S(1)}, u32[]{:S(2)}, u32[]{:S(2)}) collective-permute-start(bf16[256,512]{1,0:T(8,128)(2,1)} %s_hbm.3), channel_id=1, source_target_pairs={{0,1},{1,2},{2,3},{3,0},{4,5},{5,6},{6,7},{7,4},{8,9},{9,10},{10,1... | collective-permute-start | bytes 786440 | tf_op jit(solution)/shard_map/ppermute | solution.py:546
  3.7 2.6 %collective-permute-start.1 = (bf16[256,512]{1,0:T(8,128)(2,1)}, bf16[256,512]{1,0:T(8,128)(2,1)S(1)}, u32[]{:S(2)}, u32[]{:S(2)}) collective-permute-start(bf16[256,512]{1,0:T(8,128)(2,1)} %s_hbm.3), channel_id=1, source_target_pairs={{0,2},{1,3},{2,0},{3,1},{4,6},{5,7},{6,4},{7,5},{8,10},{9,11},{10,... | collective-permute-start | bytes 786440 | tf_op jit(solution)/shard_map/ppermute | solution.py:546
  7.6 14.9 %own_rows.1 = (bf16[8,256,1024]{2,1,0:T(8,128)(2,1)}, bf16[8,256,1024]{2,1,0:T(8,128)(2,1)}, f32[8,8,128]{2,1,0:T(8,128)}) custom-call(bf16[256,512]{1,0:T(8,128)(2,1)} %t_ref.1, bf16[256,512]{1,0:T(8,128)(2,1)} %s_hbm.3, bf16[512,8192]{1,0:T(8,128)(2,1)} %w_hbm.13), custom_call_target="tpu_custom_call" | custom-call | flops 4294967296 | bytes 8388608 | tf_op jit(solution)/shard_map/own_rows/pallas_call | solution.py:591
  22.5 3.7 %all-to-all-start = ((f32[8,8,128]{2,1,0:T(8,128)}), f32[8,8,128]{2,1,0:T(8,128)S(1)}, u32[]{:S(2)}, u32[]{:S(2)}) async-start(f32[8,8,128]{2,1,0:T(8,128)} %get-tuple-element.27.before_ref), calls=%async_computation | async-start | bytes 65536 | tf_op jit(solution)/shard_map/all_to_all | solution.py:541
  26.3 5.5 %own_back.1.refs_0_.student_hbm = f32[256,512]{1,0:T(8,128)S(1)} custom-call(f32[8,8,128]{2,1,0:T(8,128)} %get-tuple-element.27.before_ref, bf16[8,256,1024]{2,1,0:T(8,128)(2,1)} %get-tuple-element.28.exp_hbm, bf16[512,8192]{1,0:T(8,128)(2,1)} %w_hbm.13), custom_call_target="tpu_custom_call" | custom-call | flops 2147483648 | bytes 8388608 | tf_op jit(solution)/shard_map/own_back/pallas_call | solution.py:617
  31.9 2.9 %first_columns.1 = (f32[8,128]{1,0:T(8,128)S(1)}, f32[1,72,128]{2,1,0:T(8,128)S(1)}) custom-call(s32[2]{0:T(128)S(1)} %pad_add_fusion.place_ref, f32[8,8,128]{2,1,0:T(8,128)S(1)} %all-to-all-done.stats_ref, bf16[8,256,1024]{2,1,0:T(8,128)(2,1)} %get-tuple-element.26.exp_hbm.refs_5_.refs_2_, f32[256,512]{1,0:T(8,128)S(1)} %own_back.1.refs_0_.student_hbm, ...), custom_call_target="tpu_custom_call" | custom-call | flops 4194304 | bytes 4194304 | tf_op jit(solution)/shard_map/first_columns/pallas_call | solution.py:631
  35.9 2.8 %collective-permute-start.6 = (f32[1,72,128]{2,1,0:T(8,128)S(1)}, f32[1,72,128]{2,1,0:T(8,128)S(1)}, u32[]{:S(2)}, u32[]{:S(2)}) collective-permute-start(f32[1,72,128]{2,1,0:T(8,128)S(1)} %get-tuple-element.30.refs_3_.refs_0_.logs_ref), channel_id=1, source_target_pairs={{0,3},{1,0},{2,1},{3,2},{4,7},{5,4},{6,5},{7,6},{8,11},{9,8},{10,9... | collective-permute-start | bytes 110600 | tf_op jit(solution)/shard_map/ppermute | solution.py:546
  42.4 2.8 %collective-permute-start.3 = (bf16[256,512]{1,0:T(8,128)(2,1)S(1)}, bf16[256,512]{1,0:T(8,128)(2,1)S(1)}, u32[]{:S(2)}, u32[]{:S(2)}) collective-permute-start(bf16[256,512]{1,0:T(8,128)(2,1)S(1)} %get-tuple-element.31), channel_id=1, source_target_pairs={{0,3},{1,0},{2,1},{3,2},{4,7},{5,4},{6,5},{7,6},{8,11},{9,8},{10,9... | collective-permute-start | bytes 786440 | tf_op jit(solution)/shard_map/ppermute | solution.py:546
  45.2 3.1 %rows.2.refs_4_ = f32[8,8,128]{2,1,0:T(8,128)} custom-call(f32[1,72,128]{2,1,0:T(8,128)S(1)} %get-tuple-element.30.refs_3_.refs_0_.logs_ref, f32[1,72,128]{2,1,0:T(8,128)S(1)} %collective-permute-done.6.refs_1_.refs_4_, f32[1,72,128]{2,1,0:T(8,128)S(1)} %collective-permute-done.7.refs_2_.refs_5_, f32[1,72,128]{2,1,0:T(8,128)S(1)} %collective-permute-done.8.refs_3_.refs_6_, ...), custom_call_target="tpu_custom_call" | custom-call | flops 4194304 | bytes 4194304 | tf_op jit(solution)/shard_map/rows/pallas_call | solution.py:687
  48.3 4.2 %all-to-all-start.1 = ((f32[8,8,128]{2,1,0:T(8,128)}), f32[8,8,128]{2,1,0:T(8,128)S(1)}, u32[]{:S(2)}, u32[]{:S(2)}) async-start(f32[8,8,128]{2,1,0:T(8,128)} %rows.2.refs_4_), calls=%async_computation.1 | async-start | bytes 65536 | tf_op jit(solution)/shard_map/all_to_all | solution.py:541
  52.5 2.9 %student_side.4 = (bf16[128,1024]{1,0:T(8,128)(2,1)S(1)}, f32[8,128]{1,0:T(8,128)S(1)}) custom-call(bf16[768,512]{1,0:T(8,128)(2,1)S(1)} %get-tuple-element.32.refs_6_.unit, bf16[128,1024]{1,0:T(8,128)(2,1)S(1)} %get-tuple-element.33.feat_ref, bf16[128,256]{1,0:T(8,128)(2,1)S(1)} %get-tuple-element.34.scaled_ref, ...), custom_call_target="tpu_custom_call" | custom-call | flops 1342177280 | bytes 1048576 | tf_op jit(solution)/shard_map/student_side/pallas_call | solution.py:665
  57.4 3.0 %columns.2.refs_4_ = f32[4,64,128]{2,1,0:T(8,128)} custom-call(f32[8,8,128]{2,1,0:T(8,128)S(1)} %all-to-all-done.1.sums_ref, f32[8,128]{1,0:T(8,128)S(1)} %get-tuple-element.29.factor_ref.refs_4_.refs_1_, bf16[8,256,1024]{2,1,0:T(8,128)(2,1)} %get-tuple-element.26.exp_hbm.refs_5_.refs_2_, f32[8,128]{1,0:T(8,128)S(1)} %get-tuple-element.35.refs_0_), custom_call_target="tpu_custom_call" | custom-call | flops 4194304 | bytes 4194304 | tf_op jit(solution)/shard_map/columns/pallas_call | solution.py:700
  60.3 3.3 %all-to-all-start.2 = ((f32[4,64,128]{2,1,0:T(8,128)}), f32[4,64,128]{2,1,0:T(8,128)S(1)}, u32[]{:S(2)}, u32[]{:S(2)}) async-start(f32[4,64,128]{2,1,0:T(8,128)} %columns.2.refs_4_), calls=%async_computation.2 | async-start | bytes 262144 | tf_op jit(solution)/shard_map/all_to_all | solution.py:541
  63.7 2.9 %student_side.5 = (bf16[128,1024]{1,0:T(8,128)(2,1)S(1)}, f32[8,128]{1,0:T(8,128)S(1)}) custom-call(bf16[768,512]{1,0:T(8,128)(2,1)S(1)} %get-tuple-element.32.refs_6_.unit, bf16[128,1024]{1,0:T(8,128)(2,1)S(1)} %get-tuple-element.33.feat_ref, bf16[128,256]{1,0:T(8,128)(2,1)S(1)} %get-tuple-element.34.scaled_ref, ...), custom_call_target="tpu_custom_call" | custom-call | flops 1342177280 | bytes 1048576 | tf_op jit(solution)/shard_map/student_side/pallas_call | solution.py:665
  67.3 2.8 %all-to-all-done.2.refs_0_ = f32[4,64,128]{2,1,0:T(8,128)S(1)} async-done(((f32[4,64,128]{2,1,0:T(8,128)}), f32[4,64,128]{2,1,0:T(8,128)S(1)}, u32[]{:S(2)}, u32[]{:S(2)}) %all-to-all-start.2) | async-done | bytes 131104 | tf_op jit(solution)/shard_map/all_to_all | solution.py:541
  70.1 3.1 %rows.3.refs_4_ = f32[8,8,128]{2,1,0:T(8,128)} custom-call(f32[4,64,128]{2,1,0:T(8,128)S(1)} %all-to-all-done.2.refs_0_, f32[8,128]{1,0:T(8,128)S(1)} %get-tuple-element.29.factor_ref.refs_4_.refs_1_, bf16[8,256,1024]{2,1,0:T(8,128)(2,1)} %get-tuple-element.26.exp_hbm.refs_5_.refs_2_, f32[8,128]{1,0:T(8,128)S(1)} %get-tuple-element.36.refs_3_, ...), custom_call_target="tpu_custom_call" | custom-call | flops 4194304 | bytes 4194304 | tf_op jit(solution)/shard_map/rows/pallas_call | solution.py:687
  73.1 3.4 %all-to-all-start.3 = ((f32[8,8,128]{2,1,0:T(8,128)}), f32[8,8,128]{2,1,0:T(8,128)S(1)}, u32[]{:S(2)}, u32[]{:S(2)}) async-start(f32[8,8,128]{2,1,0:T(8,128)} %rows.3.refs_4_), calls=%async_computation.3 | async-start | bytes 65536 | tf_op jit(solution)/shard_map/all_to_all | solution.py:541
  76.5 2.9 %student_side.6 = (bf16[128,1024]{1,0:T(8,128)(2,1)S(1)}, f32[8,128]{1,0:T(8,128)S(1)}) custom-call(bf16[768,512]{1,0:T(8,128)(2,1)S(1)} %get-tuple-element.32.refs_6_.unit, bf16[128,1024]{1,0:T(8,128)(2,1)S(1)} %get-tuple-element.33.feat_ref, bf16[128,256]{1,0:T(8,128)(2,1)S(1)} %get-tuple-element.34.scaled_ref, ...), custom_call_target="tpu_custom_call" | custom-call | flops 1342177280 | bytes 1048576 | tf_op jit(solution)/shard_map/student_side/pallas_call | solution.py:665
  90.3 17.4 %last_rows.1 = (bf16[8,768,1024]{2,1,0:T(8,128)(2,1)}, f32[64,128]{1,0:T(8,128)S(1)}, bf16[8,80,512]{2,1,0:T(8,128)(2,1)}) custom-call(f32[8,128]{1,0:T(8,128)S(1)} %get-tuple-element.29.factor_ref.refs_4_.refs_1_, bf16[256,512]{1,0:T(8,128)(2,1)} %s_hbm.3, f32[256,512]{1,0:T(8,128)} %copy-done, ...), custom_call_target="tpu_custom_call" | custom-call | flops 8589934592 | bytes 12582912 | tf_op jit(solution)/shard_map/last_rows/pallas_call | solution.py:719
  107.8 3.7 %all-to-all-start.4 = ((bf16[8,80,512]{2,1,0:T(8,128)(2,1)}), bf16[8,80,512]{2,1,0:T(8,128)(2,1)S(1)}, u32[]{:S(2)}, u32[]{:S(2)}) async-start(bf16[8,80,512]{2,1,0:T(8,128)(2,1)} %get-tuple-element.40.refs_4_), calls=%async_computation.4 | async-start | bytes 1310720 | tf_op jit(solution)/shard_map/all_to_all | solution.py:541
  111.5 8.8 %student_side.7 = (bf16[128,5120]{1,0:T(8,128)(2,1)S(1)}, f32[8,128]{1,0:T(8,128)S(1)}) custom-call(bf16[768,512]{1,0:T(8,128)(2,1)S(1)} %get-tuple-element.32.refs_6_.unit, bf16[128,1024]{1,0:T(8,128)(2,1)S(1)} %get-tuple-element.33.feat_ref, bf16[128,256]{1,0:T(8,128)(2,1)S(1)} %get-tuple-element.34.scaled_ref, ...), custom_call_target="tpu_custom_call" | custom-call | flops 6710886400 | bytes 5242880 | tf_op jit(solution)/shard_map/student_side/pallas_call | solution.py:665
  124.6 2.9 %collective-permute-start.14 = (f32[8,128]{1,0:T(8,128)S(1)}, f32[8,128]{1,0:T(8,128)S(1)}, u32[]{:S(2)}, u32[]{:S(2)}) collective-permute-start(f32[8,128]{1,0:T(8,128)S(1)} %get-tuple-element.48), channel_id=1, source_target_pairs={{0,3},{1,2},{2,1},{3,0},{4,7},{5,6},{6,5},{7,4},{8,11},{9,10},{10,... | collective-permute-start | bytes 12296 | tf_op jit(solution)/shard_map/ppermute | solution.py:552
  129.1 3.4 %all-to-all-start.5 = ((bf16[8,32,512]{2,1,0:T(8,128)(2,1)}), bf16[8,32,512]{2,1,0:T(8,128)(2,1)S(1)}, u32[]{:S(2)}, u32[]{:S(2)}) async-start(bf16[8,32,512]{2,1,0:T(8,128)(2,1)} %get-tuple-element.47), calls=%async_computation.5 | async-start | bytes 524288 | tf_op jit(solution)/shard_map/all_to_all | solution.py:541
  132.5 8.8 %weight_grads.1 = bf16[128,8192]{1,0:T(8,128)(2,1)} custom-call(bf16[8,256,1024]{2,1,0:T(8,128)(2,1)} %get-tuple-element.26.exp_hbm.refs_5_.refs_2_, bf16[8,768,1024]{2,1,0:T(8,128)(2,1)} %get-tuple-element.38.prob_hbm, bf16[128,1024]{1,0:T(8,128)(2,1)S(1)} %get-tuple-element.33.feat_ref, f32[64,128]{1,0:T(8,128)S(1)} %get-tuple-element.39.scale_ref, ...), custom_call_target="tpu_custom_call" | custom-call | flops 2147483648 | bytes 12582912 | tf_op jit(solution)/shard_map/weight_grads/pallas_call | solution.py:765
  (49 shorter events, 26.9 us)
Async XLA Ops:
  0.6 31.3 %collective-permute-start.2 = (bf16[256,512]{1,0:T(8,128)(2,1)}, bf16[256,512]{1,0:T(8,128)(2,1)S(1)}, u32[]{:S(2)}, u32[]{:S(2)}) collective-permute-start(bf16[256,512]{1,0:T(8,128)(2,1)} %s_hbm.3), channel_id=1, source_target_pairs={{0,1},{1,2},{2,3},{3,0},{4,5},{5,6},{6,7},{7,4},{8,9},{9,10},{10,1... | collective-permute-start | bytes 786440 | tf_op jit(solution)/shard_map/ppermute | solution.py:546
  3.7 28.2 %collective-permute-start.1 = (bf16[256,512]{1,0:T(8,128)(2,1)}, bf16[256,512]{1,0:T(8,128)(2,1)S(1)}, u32[]{:S(2)}, u32[]{:S(2)}) collective-permute-start(bf16[256,512]{1,0:T(8,128)(2,1)} %s_hbm.3), channel_id=1, source_target_pairs={{0,2},{1,3},{2,0},{3,1},{4,6},{5,7},{6,4},{7,5},{8,10},{9,11},{10,... | collective-permute-start | bytes 786440 | tf_op jit(solution)/shard_map/ppermute | solution.py:546
  6.3 25.6 %collective-permute-start = (bf16[256,512]{1,0:T(8,128)(2,1)}, bf16[256,512]{1,0:T(8,128)(2,1)S(1)}, u32[]{:S(2)}, u32[]{:S(2)}) collective-permute-start(bf16[256,512]{1,0:T(8,128)(2,1)} %s_hbm.3), channel_id=1, source_target_pairs={{0,3},{1,0},{2,1},{3,2},{4,7},{5,4},{6,5},{7,6},{8,11},{9,8},{10,9... | collective-permute-start | bytes 786440 | tf_op jit(solution)/shard_map/ppermute | solution.py:546
  22.5 9.3 %all-to-all-start = ((f32[8,8,128]{2,1,0:T(8,128)}), f32[8,8,128]{2,1,0:T(8,128)S(1)}, u32[]{:S(2)}, u32[]{:S(2)}) async-start(f32[8,8,128]{2,1,0:T(8,128)} %get-tuple-element.27.before_ref), calls=%async_computation | async-start | bytes 65536 | tf_op jit(solution)/shard_map/all_to_all | solution.py:541
  31.8 16.5 %copy-start = (f32[256,512]{1,0:T(8,128)}, f32[256,512]{1,0:T(8,128)S(1)}, u32[]{:S(2)}) copy-start(f32[256,512]{1,0:T(8,128)S(1)} %own_back.1.refs_0_.student_hbm) | copy-start | bytes 1572868
  31.8 6.9 %copy-start.1 = (bf16[256,512]{1,0:T(8,128)(2,1)S(1)}, bf16[256,512]{1,0:T(8,128)(2,1)}, u32[]{:S(2)}) copy-start(bf16[256,512]{1,0:T(8,128)(2,1)} %s_hbm.3) | copy-start | bytes 786436
  31.8 6.9 %copy-start.5 = (bf16[256,512]{1,0:T(8,128)(2,1)S(1)}, bf16[256,512]{1,0:T(8,128)(2,1)}, u32[]{:S(2)}) copy-start(bf16[256,512]{1,0:T(8,128)(2,1)} %t_ref.1) | copy-start | bytes 786436
  34.8 7.5 %collective-permute-start.8 = (f32[1,72,128]{2,1,0:T(8,128)S(1)}, f32[1,72,128]{2,1,0:T(8,128)S(1)}, u32[]{:S(2)}, u32[]{:S(2)}) collective-permute-start(f32[1,72,128]{2,1,0:T(8,128)S(1)} %get-tuple-element.30.refs_3_.refs_0_.logs_ref), channel_id=1, source_target_pairs={{0,1},{1,2},{2,3},{3,0},{4,5},{5,6},{6,7},{7,4},{8,9},{9,10},{10,1... | collective-permute-start | bytes 110600 | tf_op jit(solution)/shard_map/ppermute | solution.py:546
  35.6 9.7 %collective-permute-start.7 = (f32[1,72,128]{2,1,0:T(8,128)S(1)}, f32[1,72,128]{2,1,0:T(8,128)S(1)}, u32[]{:S(2)}, u32[]{:S(2)}) collective-permute-start(f32[1,72,128]{2,1,0:T(8,128)S(1)} %get-tuple-element.30.refs_3_.refs_0_.logs_ref), channel_id=1, source_target_pairs={{0,2},{1,3},{2,0},{3,1},{4,6},{5,7},{6,4},{7,5},{8,10},{9,11},{10,... | collective-permute-start | bytes 110600 | tf_op jit(solution)/shard_map/ppermute | solution.py:546
  35.9 9.3 %collective-permute-start.6 = (f32[1,72,128]{2,1,0:T(8,128)S(1)}, f32[1,72,128]{2,1,0:T(8,128)S(1)}, u32[]{:S(2)}, u32[]{:S(2)}) collective-permute-start(f32[1,72,128]{2,1,0:T(8,128)S(1)} %get-tuple-element.30.refs_3_.refs_0_.logs_ref), channel_id=1, source_target_pairs={{0,3},{1,0},{2,1},{3,2},{4,7},{5,4},{6,5},{7,6},{8,11},{9,8},{10,9... | collective-permute-start | bytes 110600 | tf_op jit(solution)/shard_map/ppermute | solution.py:546
  40.2 29.8 %collective-permute-start.5 = (bf16[256,512]{1,0:T(8,128)(2,1)S(1)}, bf16[256,512]{1,0:T(8,128)(2,1)S(1)}, u32[]{:S(2)}, u32[]{:S(2)}) collective-permute-start(bf16[256,512]{1,0:T(8,128)(2,1)S(1)} %get-tuple-element.31), channel_id=1, source_target_pairs={{0,1},{1,2},{2,3},{3,0},{4,5},{5,6},{6,7},{7,4},{8,9},{9,10},{10,1... | collective-permute-start | bytes 786440 | tf_op jit(solution)/shard_map/ppermute | solution.py:546
  40.8 29.2 %collective-permute-start.4 = (bf16[256,512]{1,0:T(8,128)(2,1)S(1)}, bf16[256,512]{1,0:T(8,128)(2,1)S(1)}, u32[]{:S(2)}, u32[]{:S(2)}) collective-permute-start(bf16[256,512]{1,0:T(8,128)(2,1)S(1)} %get-tuple-element.31), channel_id=1, source_target_pairs={{0,2},{1,3},{2,0},{3,1},{4,6},{5,7},{6,4},{7,5},{8,10},{9,11},{10,... | collective-permute-start | bytes 786440 | tf_op jit(solution)/shard_map/ppermute | solution.py:546
  42.4 27.7 %collective-permute-start.3 = (bf16[256,512]{1,0:T(8,128)(2,1)S(1)}, bf16[256,512]{1,0:T(8,128)(2,1)S(1)}, u32[]{:S(2)}, u32[]{:S(2)}) collective-permute-start(bf16[256,512]{1,0:T(8,128)(2,1)S(1)} %get-tuple-element.31), channel_id=1, source_target_pairs={{0,3},{1,0},{2,1},{3,2},{4,7},{5,4},{6,5},{7,6},{8,11},{9,8},{10,9... | collective-permute-start | bytes 786440 | tf_op jit(solution)/shard_map/ppermute | solution.py:546
  48.3 9.1 %all-to-all-start.1 = ((f32[8,8,128]{2,1,0:T(8,128)}), f32[8,8,128]{2,1,0:T(8,128)S(1)}, u32[]{:S(2)}, u32[]{:S(2)}) async-start(f32[8,8,128]{2,1,0:T(8,128)} %rows.2.refs_4_), calls=%async_computation.1 | async-start | bytes 65536 | tf_op jit(solution)/shard_map/all_to_all | solution.py:541
  60.3 9.7 %all-to-all-start.2 = ((f32[4,64,128]{2,1,0:T(8,128)}), f32[4,64,128]{2,1,0:T(8,128)S(1)}, u32[]{:S(2)}, u32[]{:S(2)}) async-start(f32[4,64,128]{2,1,0:T(8,128)} %columns.2.refs_4_), calls=%async_computation.2 | async-start | bytes 262144 | tf_op jit(solution)/shard_map/all_to_all | solution.py:541
  73.1 8.1 %all-to-all-start.3 = ((f32[8,8,128]{2,1,0:T(8,128)}), f32[8,8,128]{2,1,0:T(8,128)S(1)}, u32[]{:S(2)}, u32[]{:S(2)}) async-start(f32[8,8,128]{2,1,0:T(8,128)} %rows.3.refs_4_), calls=%async_computation.3 | async-start | bytes 65536 | tf_op jit(solution)/shard_map/all_to_all | solution.py:541
  83.6 5.9 %collective-permute-start.11 = (f32[1,64,128]{2,1,0:T(8,128)S(1)}, f32[1,64,128]{2,1,0:T(8,128)S(1)}, u32[]{:S(2)}, u32[]{:S(2)}) collective-permute-start(f32[1,64,128]{2,1,0:T(8,128)S(1)} %columns.3.refs_7_), channel_id=1, source_target_pairs={{0,1},{1,2},{2,3},{3,0},{4,5},{5,6},{6,7},{7,4},{8,9},{9,10},{10,1... | collective-permute-start | bytes 98312 | tf_op jit(solution)/shard_map/ppermute | solution.py:546
  84.6 5.7 %collective-permute-start.10 = (f32[1,64,128]{2,1,0:T(8,128)S(1)}, f32[1,64,128]{2,1,0:T(8,128)S(1)}, u32[]{:S(2)}, u32[]{:S(2)}) collective-permute-start(f32[1,64,128]{2,1,0:T(8,128)S(1)} %columns.3.refs_7_), channel_id=1, source_target_pairs={{0,2},{1,3},{2,0},{3,1},{4,6},{5,7},{6,4},{7,5},{8,10},{9,11},{10,... | collective-permute-start | bytes 98312 | tf_op jit(solution)/shard_map/ppermute | solution.py:546
  85.8 4.5 %collective-permute-start.9 = (f32[1,64,128]{2,1,0:T(8,128)S(1)}, f32[1,64,128]{2,1,0:T(8,128)S(1)}, u32[]{:S(2)}, u32[]{:S(2)}) collective-permute-start(f32[1,64,128]{2,1,0:T(8,128)S(1)} %columns.3.refs_7_), channel_id=1, source_target_pairs={{0,3},{1,0},{2,1},{3,2},{4,7},{5,4},{6,5},{7,6},{8,11},{9,8},{10,9... | collective-permute-start | bytes 98312 | tf_op jit(solution)/shard_map/ppermute | solution.py:546
  107.8 14.6 %all-to-all-start.4 = ((bf16[8,80,512]{2,1,0:T(8,128)(2,1)}), bf16[8,80,512]{2,1,0:T(8,128)(2,1)S(1)}, u32[]{:S(2)}, u32[]{:S(2)}) async-start(bf16[8,80,512]{2,1,0:T(8,128)(2,1)} %get-tuple-element.40.refs_4_), calls=%async_computation.4 | async-start | bytes 1310720 | tf_op jit(solution)/shard_map/all_to_all | solution.py:541
  124.6 16.7 %collective-permute-start.14 = (f32[8,128]{1,0:T(8,128)S(1)}, f32[8,128]{1,0:T(8,128)S(1)}, u32[]{:S(2)}, u32[]{:S(2)}) collective-permute-start(f32[8,128]{1,0:T(8,128)S(1)} %get-tuple-element.48), channel_id=1, source_target_pairs={{0,3},{1,2},{2,1},{3,0},{4,7},{5,6},{6,5},{7,4},{8,11},{9,10},{10,... | collective-permute-start | bytes 12296 | tf_op jit(solution)/shard_map/ppermute | solution.py:552
  127.6 13.8 %collective-permute-start.13 = (f32[8,128]{1,0:T(8,128)S(1)}, f32[8,128]{1,0:T(8,128)S(1)}, u32[]{:S(2)}, u32[]{:S(2)}) collective-permute-start(f32[8,128]{1,0:T(8,128)S(1)} %get-tuple-element.48), channel_id=1, source_target_pairs={{0,2},{1,3},{2,0},{3,1},{4,6},{5,7},{6,4},{7,5},{8,10},{9,11},{10,... | collective-permute-start | bytes 12296 | tf_op jit(solution)/shard_map/ppermute | solution.py:552
  127.8 13.6 %collective-permute-start.12 = (f32[8,128]{1,0:T(8,128)S(1)}, f32[8,128]{1,0:T(8,128)S(1)}, u32[]{:S(2)}, u32[]{:S(2)}) collective-permute-start(f32[8,128]{1,0:T(8,128)S(1)} %get-tuple-element.48), channel_id=1, source_target_pairs={{0,1},{1,0},{2,3},{3,2},{4,5},{5,4},{6,7},{7,6},{8,9},{9,8},{10,11... | collective-permute-start | bytes 12296 | tf_op jit(solution)/shard_map/ppermute | solution.py:552
  129.1 12.8 %all-to-all-start.5 = ((bf16[8,32,512]{2,1,0:T(8,128)(2,1)}), bf16[8,32,512]{2,1,0:T(8,128)(2,1)S(1)}, u32[]{:S(2)}, u32[]{:S(2)}) async-start(bf16[8,32,512]{2,1,0:T(8,128)(2,1)} %get-tuple-element.47), calls=%async_computation.5 | async-start | bytes 524288 | tf_op jit(solution)/shard_map/all_to_all | solution.py:541
  (3 other events, 2.1 us)

commit v11 on v10

--- a/solution.py
+++ b/solution.py
@@ -16,7 +16,7 @@
 SCALE_STUDENT = LOG2E / TEMP_STUDENT
 LANES = 128
 WIDE = 1024
-TILE = 512
+TILE = 1024
 FAR = (0, 1, 2)
 F32 = jnp.float32
 BF16 = jnp.bfloat16
@@ -159,8 +159,8 @@
     def _(k):
         for which, (half, out, sem) in enumerate(zip(halves, (t_out, s_out), (t_sem, s_sem))):
             shift = top[half, :]
-            for n in range(0, WIDE, 2 * TILE):
-                tiles = lane_tiles(logits[half, columns_of(k, n, 2 * TILE)])
+            for n in range(0, WIDE, TILE):
+                tiles = lane_tiles(logits[half, columns_of(k, n, TILE)])
                 tiles = [jnp.exp2(tile - shift) for tile in tiles]
                 for t, tile in enumerate(tiles):
                     lanes = slice(n + t * LANES, n + (t + 1) * LANES)

time: 144 us -> 144 us (level)
  no operation moved by 1% of the time
where the time goes in v11:
time: 144 us; the launch traced here: 143 us
  Pallas kernels  82.2 us (57%)
  starting transfers between devices  46 us (32%)
  waiting for transfers between devices  10.1 us (7%)
  local copies, waits for them, and re-layouts  2.63 us (2%)
    all_to_all x6, starting transfers between devices, exchange(): return lax.all_to_all(value, axis, 0, 0)  21.8 us
    ppermute x12, starting transfers between devices, following(): lax.ppermute(value, axis, [(i, (i - s) % n) for i in range(n)])  19.8 us
    pallas_call x1, Pallas kernels, local(): pl.pallas_call(functools.partial(last_kernel, groups), in_specs=[VMEM] +...  17.5 us
    pallas_call x4, Pallas kernels, student_piece(): pl.pallas_call(functools.partial(student_kernel, log_protos, first, group...  17.5 us
    pallas_call x1, Pallas kernels, local(): pl.pallas_call(stats_kernel, in_specs=[ANY] * 3, out_specs=[ANY, ANY, VME...  14.9 us
    pallas_call x1, Pallas kernels, local(): pl.pallas_call(functools.partial(grad_kernel, counts, float(protos)), in_...  8.82 us
    all_to_all x6, waiting for transfers between devices, exchange(): return lax.all_to_all(value, axis, 0, 0)  7.24 us
    pallas_call x2, Pallas kernels, local(): pl.pallas_call(functools.partial(row_kernel, len(cols)), in_specs=[VMEM]...  6.13 us
  transfers between devices with their start and end apart: 21, of which 6 were waited for; matrix products, arithmetic and copies ran while one was open for 0% of the time, Pallas kernels for 38%

profile of v11, /device:TPU:0, one launch (start us, length us, event | category | flops | bytes accessed | tf_op | source)
XLA Modules:
  0.0 142.8 jit_solution(15830372467015141611)
XLA Ops:
  0.6 3.1 %collective-permute-start.2 = (bf16[256,512]{1,0:T(8,128)(2,1)}, bf16[256,512]{1,0:T(8,128)(2,1)S(1)}, u32[]{:S(2)}, u32[]{:S(2)}) collective-permute-start(bf16[256,512]{1,0:T(8,128)(2,1)} %s_hbm.3), channel_id=1, source_target_pairs={{0,1},{1,2},{2,3},{3,0},{4,5},{5,6},{6,7},{7,4},{8,9},{9,10},{10,1... | collective-permute-start | bytes 786440 | tf_op jit(solution)/shard_map/ppermute | solution.py:546
  3.7 2.6 %collective-permute-start.1 = (bf16[256,512]{1,0:T(8,128)(2,1)}, bf16[256,512]{1,0:T(8,128)(2,1)S(1)}, u32[]{:S(2)}, u32[]{:S(2)}) collective-permute-start(bf16[256,512]{1,0:T(8,128)(2,1)} %s_hbm.3), channel_id=1, source_target_pairs={{0,2},{1,3},{2,0},{3,1},{4,6},{5,7},{6,4},{7,5},{8,10},{9,11},{10,... | collective-permute-start | bytes 786440 | tf_op jit(solution)/shard_map/ppermute | solution.py:546
  7.6 14.9 %own_rows.1 = (bf16[8,256,1024]{2,1,0:T(8,128)(2,1)}, bf16[8,256,1024]{2,1,0:T(8,128)(2,1)}, f32[8,8,128]{2,1,0:T(8,128)}) custom-call(bf16[256,512]{1,0:T(8,128)(2,1)} %t_ref.1, bf16[256,512]{1,0:T(8,128)(2,1)} %s_hbm.3, bf16[512,8192]{1,0:T(8,128)(2,1)} %w_hbm.13), custom_call_target="tpu_custom_call" | custom-call | flops 4294967296 | bytes 8388608 | tf_op jit(solution)/shard_map/own_rows/pallas_call | solution.py:591
  22.5 3.7 %all-to-all-start = ((f32[8,8,128]{2,1,0:T(8,128)}), f32[8,8,128]{2,1,0:T(8,128)S(1)}, u32[]{:S(2)}, u32[]{:S(2)}) async-start(f32[8,8,128]{2,1,0:T(8,128)} %get-tuple-element.27.before_ref), calls=%async_computation | async-start | bytes 65536 | tf_op jit(solution)/shard_map/all_to_all | solution.py:541
  26.3 5.5 %own_back.1.refs_0_.student_hbm = f32[256,512]{1,0:T(8,128)S(1)} custom-call(f32[8,8,128]{2,1,0:T(8,128)} %get-tuple-element.27.before_ref, bf16[8,256,1024]{2,1,0:T(8,128)(2,1)} %get-tuple-element.28.exp_hbm, bf16[512,8192]{1,0:T(8,128)(2,1)} %w_hbm.13), custom_call_target="tpu_custom_call" | custom-call | flops 2147483648 | bytes 8388608 | tf_op jit(solution)/shard_map/own_back/pallas_call | solution.py:617
  31.9 2.9 %first_columns.1 = (f32[8,128]{1,0:T(8,128)S(1)}, f32[1,72,128]{2,1,0:T(8,128)S(1)}) custom-call(s32[2]{0:T(128)S(1)} %pad_add_fusion.place_ref, f32[8,8,128]{2,1,0:T(8,128)S(1)} %all-to-all-done.stats_ref, bf16[8,256,1024]{2,1,0:T(8,128)(2,1)} %get-tuple-element.26.exp_hbm.refs_5_.refs_2_, f32[256,512]{1,0:T(8,128)S(1)} %own_back.1.refs_0_.student_hbm, ...), custom_call_target="tpu_custom_call" | custom-call | flops 4194304 | bytes 4194304 | tf_op jit(solution)/shard_map/first_columns/pallas_call | solution.py:631
  35.9 2.8 %collective-permute-start.6 = (f32[1,72,128]{2,1,0:T(8,128)S(1)}, f32[1,72,128]{2,1,0:T(8,128)S(1)}, u32[]{:S(2)}, u32[]{:S(2)}) collective-permute-start(f32[1,72,128]{2,1,0:T(8,128)S(1)} %get-tuple-element.30.refs_3_.refs_0_.logs_ref), channel_id=1, source_target_pairs={{0,3},{1,0},{2,1},{3,2},{4,7},{5,4},{6,5},{7,6},{8,11},{9,8},{10,9... | collective-permute-start | bytes 110600 | tf_op jit(solution)/shard_map/ppermute | solution.py:546
  42.4 2.8 %collective-permute-start.3 = (bf16[256,512]{1,0:T(8,128)(2,1)S(1)}, bf16[256,512]{1,0:T(8,128)(2,1)S(1)}, u32[]{:S(2)}, u32[]{:S(2)}) collective-permute-start(bf16[256,512]{1,0:T(8,128)(2,1)S(1)} %get-tuple-element.31), channel_id=1, source_target_pairs={{0,3},{1,0},{2,1},{3,2},{4,7},{5,4},{6,5},{7,6},{8,11},{9,8},{10,9... | collective-permute-start | bytes 786440 | tf_op jit(solution)/shard_map/ppermute | solution.py:546
  45.2 3.1 %rows.2.refs_4_ = f32[8,8,128]{2,1,0:T(8,128)} custom-call(f32[1,72,128]{2,1,0:T(8,128)S(1)} %get-tuple-element.30.refs_3_.refs_0_.logs_ref, f32[1,72,128]{2,1,0:T(8,128)S(1)} %collective-permute-done.6.refs_1_.refs_4_, f32[1,72,128]{2,1,0:T(8,128)S(1)} %collective-permute-done.7.refs_2_.refs_5_, f32[1,72,128]{2,1,0:T(8,128)S(1)} %collective-permute-done.8.refs_3_.refs_6_, ...), custom_call_target="tpu_custom_call" | custom-call | flops 4194304 | bytes 4194304 | tf_op jit(solution)/shard_map/rows/pallas_call | solution.py:687
  48.3 4.2 %all-to-all-start.1 = ((f32[8,8,128]{2,1,0:T(8,128)}), f32[8,8,128]{2,1,0:T(8,128)S(1)}, u32[]{:S(2)}, u32[]{:S(2)}) async-start(f32[8,8,128]{2,1,0:T(8,128)} %rows.2.refs_4_), calls=%async_computation.1 | async-start | bytes 65536 | tf_op jit(solution)/shard_map/all_to_all | solution.py:541
  52.5 2.9 %student_side.4 = (bf16[128,1024]{1,0:T(8,128)(2,1)S(1)}, f32[8,128]{1,0:T(8,128)S(1)}) custom-call(bf16[768,512]{1,0:T(8,128)(2,1)S(1)} %get-tuple-element.32.refs_6_.unit, bf16[128,1024]{1,0:T(8,128)(2,1)S(1)} %get-tuple-element.33.feat_ref, bf16[128,256]{1,0:T(8,128)(2,1)S(1)} %get-tuple-element.34.scaled_ref, ...), custom_call_target="tpu_custom_call" | custom-call | flops 1342177280 | bytes 1048576 | tf_op jit(solution)/shard_map/student_side/pallas_call | solution.py:665
  57.4 3.0 %columns.2.refs_4_ = f32[4,64,128]{2,1,0:T(8,128)} custom-call(f32[8,8,128]{2,1,0:T(8,128)S(1)} %all-to-all-done.1.sums_ref, f32[8,128]{1,0:T(8,128)S(1)} %get-tuple-element.29.factor_ref.refs_4_.refs_1_, bf16[8,256,1024]{2,1,0:T(8,128)(2,1)} %get-tuple-element.26.exp_hbm.refs_5_.refs_2_, f32[8,128]{1,0:T(8,128)S(1)} %get-tuple-element.35.refs_0_), custom_call_target="tpu_custom_call" | custom-call | flops 4194304 | bytes 4194304 | tf_op jit(solution)/shard_map/columns/pallas_call | solution.py:700
  60.3 3.3 %all-to-all-start.2 = ((f32[4,64,128]{2,1,0:T(8,128)}), f32[4,64,128]{2,1,0:T(8,128)S(1)}, u32[]{:S(2)}, u32[]{:S(2)}) async-start(f32[4,64,128]{2,1,0:T(8,128)} %columns.2.refs_4_), calls=%async_computation.2 | async-start | bytes 262144 | tf_op jit(solution)/shard_map/all_to_all | solution.py:541
  63.7 2.9 %student_side.5 = (bf16[128,1024]{1,0:T(8,128)(2,1)S(1)}, f32[8,128]{1,0:T(8,128)S(1)}) custom-call(bf16[768,512]{1,0:T(8,128)(2,1)S(1)} %get-tuple-element.32.refs_6_.unit, bf16[128,1024]{1,0:T(8,128)(2,1)S(1)} %get-tuple-element.33.feat_ref, bf16[128,256]{1,0:T(8,128)(2,1)S(1)} %get-tuple-element.34.scaled_ref, ...), custom_call_target="tpu_custom_call" | custom-call | flops 1342177280 | bytes 1048576 | tf_op jit(solution)/shard_map/student_side/pallas_call | solution.py:665
  67.3 2.8 %all-to-all-done.2.refs_0_ = f32[4,64,128]{2,1,0:T(8,128)S(1)} async-done(((f32[4,64,128]{2,1,0:T(8,128)}), f32[4,64,128]{2,1,0:T(8,128)S(1)}, u32[]{:S(2)}, u32[]{:S(2)}) %all-to-all-start.2) | async-done | bytes 131104 | tf_op jit(solution)/shard_map/all_to_all | solution.py:541
  70.1 3.1 %rows.3.refs_4_ = f32[8,8,128]{2,1,0:T(8,128)} custom-call(f32[4,64,128]{2,1,0:T(8,128)S(1)} %all-to-all-done.2.refs_0_, f32[8,128]{1,0:T(8,128)S(1)} %get-tuple-element.29.factor_ref.refs_4_.refs_1_, bf16[8,256,1024]{2,1,0:T(8,128)(2,1)} %get-tuple-element.26.exp_hbm.refs_5_.refs_2_, f32[8,128]{1,0:T(8,128)S(1)} %get-tuple-element.36.refs_3_, ...), custom_call_target="tpu_custom_call" | custom-call | flops 4194304 | bytes 4194304 | tf_op jit(solution)/shard_map/rows/pallas_call | solution.py:687
  73.1 3.4 %all-to-all-start.3 = ((f32[8,8,128]{2,1,0:T(8,128)}), f32[8,8,128]{2,1,0:T(8,128)S(1)}, u32[]{:S(2)}, u32[]{:S(2)}) async-start(f32[8,8,128]{2,1,0:T(8,128)} %rows.3.refs_4_), calls=%async_computation.3 | async-start | bytes 65536 | tf_op jit(solution)/shard_map/all_to_all | solution.py:541
  76.5 2.9 %student_side.6 = (bf16[128,1024]{1,0:T(8,128)(2,1)S(1)}, f32[8,128]{1,0:T(8,128)S(1)}) custom-call(bf16[768,512]{1,0:T(8,128)(2,1)S(1)} %get-tuple-element.32.refs_6_.unit, bf16[128,1024]{1,0:T(8,128)(2,1)S(1)} %get-tuple-element.33.feat_ref, bf16[128,256]{1,0:T(8,128)(2,1)S(1)} %get-tuple-element.34.scaled_ref, ...), custom_call_target="tpu_custom_call" | custom-call | flops 1342177280 | bytes 1048576 | tf_op jit(solution)/shard_map/student_side/pallas_call | solution.py:665
  90.3 17.5 %last_rows.1 = (bf16[8,768,1024]{2,1,0:T(8,128)(2,1)}, f32[64,128]{1,0:T(8,128)S(1)}, bf16[8,80,512]{2,1,0:T(8,128)(2,1)}) custom-call(f32[8,128]{1,0:T(8,128)S(1)} %get-tuple-element.29.factor_ref.refs_4_.refs_1_, bf16[256,512]{1,0:T(8,128)(2,1)} %s_hbm.3, f32[256,512]{1,0:T(8,128)} %copy-done, ...), custom_call_target="tpu_custom_call" | custom-call | flops 8589934592 | bytes 12582912 | tf_op jit(solution)/shard_map/last_rows/pallas_call | solution.py:719
  107.8 3.7 %all-to-all-start.4 = ((bf16[8,80,512]{2,1,0:T(8,128)(2,1)}), bf16[8,80,512]{2,1,0:T(8,128)(2,1)S(1)}, u32[]{:S(2)}, u32[]{:S(2)}) async-start(bf16[8,80,512]{2,1,0:T(8,128)(2,1)} %get-tuple-element.40.refs_4_), calls=%async_computation.4 | async-start | bytes 1310720 | tf_op jit(solution)/shard_map/all_to_all | solution.py:541
  111.6 8.8 %student_side.7 = (bf16[128,5120]{1,0:T(8,128)(2,1)S(1)}, f32[8,128]{1,0:T(8,128)S(1)}) custom-call(bf16[768,512]{1,0:T(8,128)(2,1)S(1)} %get-tuple-element.32.refs_6_.unit, bf16[128,1024]{1,0:T(8,128)(2,1)S(1)} %get-tuple-element.33.feat_ref, bf16[128,256]{1,0:T(8,128)(2,1)S(1)} %get-tuple-element.34.scaled_ref, ...), custom_call_target="tpu_custom_call" | custom-call | flops 6710886400 | bytes 5242880 | tf_op jit(solution)/shard_map/student_side/pallas_call | solution.py:665
  124.7 2.9 %collective-permute-start.14 = (f32[8,128]{1,0:T(8,128)S(1)}, f32[8,128]{1,0:T(8,128)S(1)}, u32[]{:S(2)}, u32[]{:S(2)}) collective-permute-start(f32[8,128]{1,0:T(8,128)S(1)} %get-tuple-element.48), channel_id=1, source_target_pairs={{0,3},{1,2},{2,1},{3,0},{4,7},{5,6},{6,5},{7,4},{8,11},{9,10},{10,... | collective-permute-start | bytes 12296 | tf_op jit(solution)/shard_map/ppermute | solution.py:552
  129.1 3.4 %all-to-all-start.5 = ((bf16[8,32,512]{2,1,0:T(8,128)(2,1)}), bf16[8,32,512]{2,1,0:T(8,128)(2,1)S(1)}, u32[]{:S(2)}, u32[]{:S(2)}) async-start(bf16[8,32,512]{2,1,0:T(8,128)(2,1)} %get-tuple-element.47), calls=%async_computation.5 | async-start | bytes 524288 | tf_op jit(solution)/shard_map/all_to_all | solution.py:541
  132.6 8.8 %weight_grads.1 = bf16[128,8192]{1,0:T(8,128)(2,1)} custom-call(bf16[8,256,1024]{2,1,0:T(8,128)(2,1)} %get-tuple-element.26.exp_hbm.refs_5_.refs_2_, bf16[8,768,1024]{2,1,0:T(8,128)(2,1)} %get-tuple-element.38.prob_hbm, bf16[128,1024]{1,0:T(8,128)(2,1)S(1)} %get-tuple-element.33.feat_ref, f32[64,128]{1,0:T(8,128)S(1)} %get-tuple-element.39.scale_ref, ...), custom_call_target="tpu_custom_call" | custom-call | flops 2147483648 | bytes 12582912 | tf_op jit(solution)/shard_map/weight_grads/pallas_call | solution.py:765
  (49 shorter events, 26.9 us)
Async XLA Ops:
  0.6 31.3 %collective-permute-start.2 = (bf16[256,512]{1,0:T(8,128)(2,1)}, bf16[256,512]{1,0:T(8,128)(2,1)S(1)}, u32[]{:S(2)}, u32[]{:S(2)}) collective-permute-start(bf16[256,512]{1,0:T(8,128)(2,1)} %s_hbm.3), channel_id=1, source_target_pairs={{0,1},{1,2},{2,3},{3,0},{4,5},{5,6},{6,7},{7,4},{8,9},{9,10},{10,1... | collective-permute-start | bytes 786440 | tf_op jit(solution)/shard_map/ppermute | solution.py:546
  3.7 28.2 %collective-permute-start.1 = (bf16[256,512]{1,0:T(8,128)(2,1)}, bf16[256,512]{1,0:T(8,128)(2,1)S(1)}, u32[]{:S(2)}, u32[]{:S(2)}) collective-permute-start(bf16[256,512]{1,0:T(8,128)(2,1)} %s_hbm.3), channel_id=1, source_target_pairs={{0,2},{1,3},{2,0},{3,1},{4,6},{5,7},{6,4},{7,5},{8,10},{9,11},{10,... | collective-permute-start | bytes 786440 | tf_op jit(solution)/shard_map/ppermute | solution.py:546
  6.3 25.6 %collective-permute-start = (bf16[256,512]{1,0:T(8,128)(2,1)}, bf16[256,512]{1,0:T(8,128)(2,1)S(1)}, u32[]{:S(2)}, u32[]{:S(2)}) collective-permute-start(bf16[256,512]{1,0:T(8,128)(2,1)} %s_hbm.3), channel_id=1, source_target_pairs={{0,3},{1,0},{2,1},{3,2},{4,7},{5,4},{6,5},{7,6},{8,11},{9,8},{10,9... | collective-permute-start | bytes 786440 | tf_op jit(solution)/shard_map/ppermute | solution.py:546
  22.5 9.3 %all-to-all-start = ((f32[8,8,128]{2,1,0:T(8,128)}), f32[8,8,128]{2,1,0:T(8,128)S(1)}, u32[]{:S(2)}, u32[]{:S(2)}) async-start(f32[8,8,128]{2,1,0:T(8,128)} %get-tuple-element.27.before_ref), calls=%async_computation | async-start | bytes 65536 | tf_op jit(solution)/shard_map/all_to_all | solution.py:541
  31.8 16.5 %copy-start = (f32[256,512]{1,0:T(8,128)}, f32[256,512]{1,0:T(8,128)S(1)}, u32[]{:S(2)}) copy-start(f32[256,512]{1,0:T(8,128)S(1)} %own_back.1.refs_0_.student_hbm) | copy-start | bytes 1572868
  31.8 6.9 %copy-start.1 = (bf16[256,512]{1,0:T(8,128)(2,1)S(1)}, bf16[256,512]{1,0:T(8,128)(2,1)}, u32[]{:S(2)}) copy-start(bf16[256,512]{1,0:T(8,128)(2,1)} %s_hbm.3) | copy-start | bytes 786436
  31.8 6.9 %copy-start.5 = (bf16[256,512]{1,0:T(8,128)(2,1)S(1)}, bf16[256,512]{1,0:T(8,128)(2,1)}, u32[]{:S(2)}) copy-start(bf16[256,512]{1,0:T(8,128)(2,1)} %t_ref.1) | copy-start | bytes 786436
  34.8 7.5 %collective-permute-start.8 = (f32[1,72,128]{2,1,0:T(8,128)S(1)}, f32[1,72,128]{2,1,0:T(8,128)S(1)}, u32[]{:S(2)}, u32[]{:S(2)}) collective-permute-start(f32[1,72,128]{2,1,0:T(8,128)S(1)} %get-tuple-element.30.refs_3_.refs_0_.logs_ref), channel_id=1, source_target_pairs={{0,1},{1,2},{2,3},{3,0},{4,5},{5,6},{6,7},{7,4},{8,9},{9,10},{10,1... | collective-permute-start | bytes 110600 | tf_op jit(solution)/shard_map/ppermute | solution.py:546
  35.6 9.7 %collective-permute-start.7 = (f32[1,72,128]{2,1,0:T(8,128)S(1)}, f32[1,72,128]{2,1,0:T(8,128)S(1)}, u32[]{:S(2)}, u32[]{:S(2)}) collective-permute-start(f32[1,72,128]{2,1,0:T(8,128)S(1)} %get-tuple-element.30.refs_3_.refs_0_.logs_ref), channel_id=1, source_target_pairs={{0,2},{1,3},{2,0},{3,1},{4,6},{5,7},{6,4},{7,5},{8,10},{9,11},{10,... | collective-permute-start | bytes 110600 | tf_op jit(solution)/shard_map/ppermute | solution.py:546
  35.9 9.3 %collective-permute-start.6 = (f32[1,72,128]{2,1,0:T(8,128)S(1)}, f32[1,72,128]{2,1,0:T(8,128)S(1)}, u32[]{:S(2)}, u32[]{:S(2)}) collective-permute-start(f32[1,72,128]{2,1,0:T(8,128)S(1)} %get-tuple-element.30.refs_3_.refs_0_.logs_ref), channel_id=1, source_target_pairs={{0,3},{1,0},{2,1},{3,2},{4,7},{5,4},{6,5},{7,6},{8,11},{9,8},{10,9... | collective-permute-start | bytes 110600 | tf_op jit(solution)/shard_map/ppermute | solution.py:546
  40.2 29.8 %collective-permute-start.5 = (bf16[256,512]{1,0:T(8,128)(2,1)S(1)}, bf16[256,512]{1,0:T(8,128)(2,1)S(1)}, u32[]{:S(2)}, u32[]{:S(2)}) collective-permute-start(bf16[256,512]{1,0:T(8,128)(2,1)S(1)} %get-tuple-element.31), channel_id=1, source_target_pairs={{0,1},{1,2},{2,3},{3,0},{4,5},{5,6},{6,7},{7,4},{8,9},{9,10},{10,1... | collective-permute-start | bytes 786440 | tf_op jit(solution)/shard_map/ppermute | solution.py:546
  40.8 29.2 %collective-permute-start.4 = (bf16[256,512]{1,0:T(8,128)(2,1)S(1)}, bf16[256,512]{1,0:T(8,128)(2,1)S(1)}, u32[]{:S(2)}, u32[]{:S(2)}) collective-permute-start(bf16[256,512]{1,0:T(8,128)(2,1)S(1)} %get-tuple-element.31), channel_id=1, source_target_pairs={{0,2},{1,3},{2,0},{3,1},{4,6},{5,7},{6,4},{7,5},{8,10},{9,11},{10,... | collective-permute-start | bytes 786440 | tf_op jit(solution)/shard_map/ppermute | solution.py:546
  42.4 27.7 %collective-permute-start.3 = (bf16[256,512]{1,0:T(8,128)(2,1)S(1)}, bf16[256,512]{1,0:T(8,128)(2,1)S(1)}, u32[]{:S(2)}, u32[]{:S(2)}) collective-permute-start(bf16[256,512]{1,0:T(8,128)(2,1)S(1)} %get-tuple-element.31), channel_id=1, source_target_pairs={{0,3},{1,0},{2,1},{3,2},{4,7},{5,4},{6,5},{7,6},{8,11},{9,8},{10,9... | collective-permute-start | bytes 786440 | tf_op jit(solution)/shard_map/ppermute | solution.py:546
  48.3 9.1 %all-to-all-start.1 = ((f32[8,8,128]{2,1,0:T(8,128)}), f32[8,8,128]{2,1,0:T(8,128)S(1)}, u32[]{:S(2)}, u32[]{:S(2)}) async-start(f32[8,8,128]{2,1,0:T(8,128)} %rows.2.refs_4_), calls=%async_computation.1 | async-start | bytes 65536 | tf_op jit(solution)/shard_map/all_to_all | solution.py:541
  60.3 9.7 %all-to-all-start.2 = ((f32[4,64,128]{2,1,0:T(8,128)}), f32[4,64,128]{2,1,0:T(8,128)S(1)}, u32[]{:S(2)}, u32[]{:S(2)}) async-start(f32[4,64,128]{2,1,0:T(8,128)} %columns.2.refs_4_), calls=%async_computation.2 | async-start | bytes 262144 | tf_op jit(solution)/shard_map/all_to_all | solution.py:541
  73.1 8.1 %all-to-all-start.3 = ((f32[8,8,128]{2,1,0:T(8,128)}), f32[8,8,128]{2,1,0:T(8,128)S(1)}, u32[]{:S(2)}, u32[]{:S(2)}) async-start(f32[8,8,128]{2,1,0:T(8,128)} %rows.3.refs_4_), calls=%async_computation.3 | async-start | bytes 65536 | tf_op jit(solution)/shard_map/all_to_all | solution.py:541
  83.6 5.9 %collective-permute-start.11 = (f32[1,64,128]{2,1,0:T(8,128)S(1)}, f32[1,64,128]{2,1,0:T(8,128)S(1)}, u32[]{:S(2)}, u32[]{:S(2)}) collective-permute-start(f32[1,64,128]{2,1,0:T(8,128)S(1)} %columns.3.refs_7_), channel_id=1, source_target_pairs={{0,1},{1,2},{2,3},{3,0},{4,5},{5,6},{6,7},{7,4},{8,9},{9,10},{10,1... | collective-permute-start | bytes 98312 | tf_op jit(solution)/shard_map/ppermute | solution.py:546
  84.6 5.7 %collective-permute-start.10 = (f32[1,64,128]{2,1,0:T(8,128)S(1)}, f32[1,64,128]{2,1,0:T(8,128)S(1)}, u32[]{:S(2)}, u32[]{:S(2)}) collective-permute-start(f32[1,64,128]{2,1,0:T(8,128)S(1)} %columns.3.refs_7_), channel_id=1, source_target_pairs={{0,2},{1,3},{2,0},{3,1},{4,6},{5,7},{6,4},{7,5},{8,10},{9,11},{10,... | collective-permute-start | bytes 98312 | tf_op jit(solution)/shard_map/ppermute | solution.py:546
  85.8 4.5 %collective-permute-start.9 = (f32[1,64,128]{2,1,0:T(8,128)S(1)}, f32[1,64,128]{2,1,0:T(8,128)S(1)}, u32[]{:S(2)}, u32[]{:S(2)}) collective-permute-start(f32[1,64,128]{2,1,0:T(8,128)S(1)} %columns.3.refs_7_), channel_id=1, source_target_pairs={{0,3},{1,0},{2,1},{3,2},{4,7},{5,4},{6,5},{7,6},{8,11},{9,8},{10,9... | collective-permute-start | bytes 98312 | tf_op jit(solution)/shard_map/ppermute | solution.py:546
  107.8 14.6 %all-to-all-start.4 = ((bf16[8,80,512]{2,1,0:T(8,128)(2,1)}), bf16[8,80,512]{2,1,0:T(8,128)(2,1)S(1)}, u32[]{:S(2)}, u32[]{:S(2)}) async-start(bf16[8,80,512]{2,1,0:T(8,128)(2,1)} %get-tuple-element.40.refs_4_), calls=%async_computation.4 | async-start | bytes 1310720 | tf_op jit(solution)/shard_map/all_to_all | solution.py:541
  124.7 16.7 %collective-permute-start.14 = (f32[8,128]{1,0:T(8,128)S(1)}, f32[8,128]{1,0:T(8,128)S(1)}, u32[]{:S(2)}, u32[]{:S(2)}) collective-permute-start(f32[8,128]{1,0:T(8,128)S(1)} %get-tuple-element.48), channel_id=1, source_target_pairs={{0,3},{1,2},{2,1},{3,0},{4,7},{5,6},{6,5},{7,4},{8,11},{9,10},{10,... | collective-permute-start | bytes 12296 | tf_op jit(solution)/shard_map/ppermute | solution.py:552
  127.6 13.8 %collective-permute-start.13 = (f32[8,128]{1,0:T(8,128)S(1)}, f32[8,128]{1,0:T(8,128)S(1)}, u32[]{:S(2)}, u32[]{:S(2)}) collective-permute-start(f32[8,128]{1,0:T(8,128)S(1)} %get-tuple-element.48), channel_id=1, source_target_pairs={{0,2},{1,3},{2,0},{3,1},{4,6},{5,7},{6,4},{7,5},{8,10},{9,11},{10,... | collective-permute-start | bytes 12296 | tf_op jit(solution)/shard_map/ppermute | solution.py:552
  127.9 13.6 %collective-permute-start.12 = (f32[8,128]{1,0:T(8,128)S(1)}, f32[8,128]{1,0:T(8,128)S(1)}, u32[]{:S(2)}, u32[]{:S(2)}) collective-permute-start(f32[8,128]{1,0:T(8,128)S(1)} %get-tuple-element.48), channel_id=1, source_target_pairs={{0,1},{1,0},{2,3},{3,2},{4,5},{5,4},{6,7},{7,6},{8,9},{9,8},{10,11... | collective-permute-start | bytes 12296 | tf_op jit(solution)/shard_map/ppermute | solution.py:552
  129.1 12.8 %all-to-all-start.5 = ((bf16[8,32,512]{2,1,0:T(8,128)(2,1)}), bf16[8,32,512]{2,1,0:T(8,128)(2,1)S(1)}, u32[]{:S(2)}, u32[]{:S(2)}) async-start(bf16[8,32,512]{2,1,0:T(8,128)(2,1)} %get-tuple-element.47), calls=%async_computation.5 | async-start | bytes 524288 | tf_op jit(solution)/shard_map/all_to_all | solution.py:541
  (3 other events, 2.1 us)
